TPU v7x, 32 devices: a whole 2x2x4 slice. The times are simulated.
32 devices in a mesh: groups: 1, expert: 32 (over z, y, x, core).
Axes of the slice: x: 2, y: 2, z: 4, core: 2. Of those that a mesh axis runs over, the one named last changes fastest.
Arguments:
- tokens: bfloat16 [2048, 4096], P(('groups', 'expert')), may hold values from -6 to 6
- route_ids: int32 [2048, 8], P(('groups', 'expert')), may hold values from 0 to 15, all different within a row; in each aligned block of 64 rows (0 to 63, 64 to 127, ...) at most 40 rows name the same one
- route_gates: float32 [2048, 8], P(('groups', 'expert')), may hold values from 0.05 to 1
- gate_weight: bfloat16 [4096, 12288], P(None, 'expert'), may hold values from -0.09375 to 0.09375
- up_weight: bfloat16 [4096, 12288], P(None, 'expert'), may hold values from -0.09375 to 0.09375
- down_weight: bfloat16 [12288, 4096], P('expert'), may hold values from -0.4375 to 0.4375
- kv_pages: bfloat16 [1024, 16, 1024], P(('groups', 'expert')), may hold values from -6 to 6
- page_target: int32 [1024], P(('groups', 'expert')), may hold values from 0 to 1023, as said below
Outputs:
- combined: bfloat16 [2048, 4096], P(('groups', 'expert'))
- handed_pages: bfloat16 [1024, 16, 1024], P(('groups', 'expert'))
Inputs may be any that keep to these rules, and one draw needn't show every extreme that they name: `route_ids`: each row names 8 different experts; the rows of one device name one expert at most 40 times, a bound that some block reaches. A permutation; page p goes to device page_target[p] // 32. Every device receives exactly 32 pages, at most 1 of them from one device and exactly 1 from some device; the distances from source to destination device, modulo the axis, form the same multiset on every device.
All inputs are finite; a program needn't handle non-finite values.
Results may differ from a plain program's by a relative error of at most 0.0064.
Values may be sent and summed in bfloat16 or wider, within the bound.
No kernel may reach another device: no remote copies, remote signals or barrier semaphores. Data moves between devices by JAX's collectives and lax.ppermute only.
A program may use at most 128 MiB of HBM per device.

v0:
```python
import jax
import jax.numpy as jnp
from jax import lax
from jax.sharding import PartitionSpec as P

PCAP = 1


def partner(x, axis, stride):
    return lax.ppermute(x, axis, [(i, i ^ 1 << stride) for i in range(lax.axis_size(axis))])


def slot_ranks(labels, count):
    onehot = (labels[:, None] == jnp.arange(count, dtype=jnp.int32)[None, :]).astype(jnp.int32)
    earlier = jnp.cumsum(onehot, axis=0) - onehot
    return jnp.sum(earlier * onehot, axis=1)


def place_pages(arrived, arrived_labels, page_count, page_shape):
    picking = (
        arrived_labels.astype(jnp.float32)[None, :]
        == jnp.arange(page_count, dtype=jnp.float32)[:, None]
    ).astype(jnp.bfloat16)
    landed = jnp.dot(picking, arrived, preferred_element_type=jnp.float32)
    return landed.astype(jnp.bfloat16).reshape(page_shape)


def hand_pages(kv_pages, page_target):
    page_count = kv_pages.shape[0]
    owners = lax.axis_size("expert")
    target_dev = page_target // page_count
    target_slot = page_target % page_count
    flat_pages = kv_pages.reshape(page_count, -1)
    position = target_dev * PCAP + slot_ranks(target_dev, owners)
    placing = position[:, None] == jnp.arange(owners * PCAP, dtype=jnp.int32)[None, :]
    outgoing = lax.dot_general(
        placing.astype(jnp.bfloat16),
        flat_pages,
        (((0,), (0,)), ((), ())),
        preferred_element_type=jnp.float32,
    ).astype(jnp.bfloat16)
    labels = jnp.sum(jnp.where(placing, target_slot[:, None] + 1, 0), axis=0) - 1
    arrived, arrived_labels = (
        lax.all_to_all(outgoing, "expert", split_axis=0, concat_axis=0, tiled=True),
        lax.all_to_all(
            labels.astype(jnp.bfloat16), "expert", split_axis=0, concat_axis=0, tiled=True
        ),
    )
    return place_pages(arrived, arrived_labels, page_count, kv_pages.shape)


def local(
    tokens, route_ids, route_gates, gate_weight, up_weight, down_weight, kv_pages, page_target
):
    tok_rows, width = tokens.shape
    half = width // 2
    chosen = route_ids.shape[1]
    owners = lax.axis_size("expert")
    experts = owners // 2
    capacity = min(tok_rows, 5 * tok_rows * chosen // (4 * experts))
    parity = lax.axis_index("expert") % 2
    handed = hand_pages(kv_pages, page_target)
    flat_ids = route_ids.reshape(-1)
    position = flat_ids * capacity + slot_ranks(flat_ids, experts)
    hits = (position[:, None] == jnp.arange(experts * capacity, dtype=jnp.int32)[None, :]).reshape(
        tok_rows, chosen, experts * capacity
    )
    placing = jnp.any(hits, axis=1).astype(jnp.bfloat16)
    shares = route_gates / jnp.sum(route_gates, axis=1, keepdims=True)
    mixing = shares.astype(jnp.bfloat16)
    blend = jnp.sum(jnp.where(hits, mixing.astype(jnp.float32)[:, :, None], 0.0), axis=1).astype(
        jnp.bfloat16
    )
    outgoing = lax.dot_general(
        placing, tokens, (((0,), (0,)), ((), ())), preferred_element_type=jnp.float32
    ).astype(jnp.bfloat16)
    outgoing = jnp.broadcast_to(
        outgoing.reshape(experts, 1, capacity, width), (experts, 2, capacity, width)
    ).reshape(owners, capacity, width)
    received = lax.all_to_all(outgoing, "expert", split_axis=0, concat_axis=0, tiled=True)
    sources, held, cols = received.shape
    rows = received.reshape(sources * held, cols)
    gate = jnp.dot(rows, gate_weight, preferred_element_type=jnp.float32)
    up = jnp.dot(rows, up_weight, preferred_element_type=jnp.float32)
    hidden = (jax.nn.silu(gate) * up).astype(jnp.bfloat16)
    partial_value = jnp.dot(hidden, down_weight, preferred_element_type=jnp.float32)
    keep = lax.dynamic_slice_in_dim(partial_value, parity * half, half, 1)
    give = lax.dynamic_slice_in_dim(partial_value, (1 - parity) * half, half, 1)
    summed = keep + partner(give, "expert", 0)
    back = summed.astype(jnp.bfloat16).reshape(sources, held, half)
    returned = lax.all_to_all(back, "expert", split_axis=0, concat_axis=0, tiled=True)
    expert_out = returned.reshape(experts, 2, capacity, half)
    combined = jnp.einsum(
        "tec,ehcf->thf",
        blend.reshape(tok_rows, experts, capacity),
        expert_out,
        preferred_element_type=jnp.float32,
    )
    combined = combined.reshape(tok_rows, width).astype(jnp.bfloat16)
    return (combined, handed)


def solution(mesh):
    placed = (
        P(("groups", "expert"), None),
        P(("groups", "expert"), None),
        P(("groups", "expert"), None),
        P(None, "expert"),
        P(None, "expert"),
        P("expert", None),
        P(("groups", "expert"), None, None),
        P(("groups", "expert")),
    )
    return jax.shard_map(
        local,
        mesh=mesh,
        in_specs=placed,
        out_specs=(P(("groups", "expert"), None), P(("groups", "expert"), None, None)),
        check_vma=False,
    )
```

profile of v0, /device:TPU:0, one launch (start us, length us, event | category | flops | bytes accessed | tf_op | source)
XLA Modules:
  0.0 485.7 jit_solution(15276891868457884090)
XLA Ops:
  0.6 0.9 copy.58
  1.8 1.2 reduce-window.6
  4.7 5.0 %convolution_convert_fusion.2 = bf16[640,4096]{1,0:T(8,128)(2,1)} fusion(pred[64,640]{1,0:T(8,128)(4,1)S(1)} %fusion.9, bf16[64,4096]{1,0:T(8,128)(2,1)} %param.8), kind=kOutput, calls=%fused_computation.4 | convolution fusion | flops 338165760 | bytes 5808128 | tf_op jit(solution)/shard_map/dot_general | solution.py:74
  9.7 7.9 %broadcast_in_dim.29 = bf16[16,2,40,4096]{3,2,1,0:T(8,128)(2,1)} broadcast(bf16[16,40,4096]{2,1,0:T(8,128)(2,1)} %bitcast.56), dimensions={0,2,3} | broadcast | bytes 15728640 | tf_op jit(solution)/shard_map/broadcast_in_dim | solution.py:77
  17.6 7.4 %all-to-all-start = ((bf16[32,40,4096]{2,1,0:T(8,128)(2,1)}), bf16[32,40,4096]{2,1,0:T(8,128)(2,1)}, u32[]{:S(2)}, u32[]{:S(2)}) async-start(bf16[32,40,4096]{2,1,0:T(8,128)(2,1)} %bitcast.55), calls=%async_computation | async-start | bytes 20971520 | tf_op jit(solution)/shard_map/all_to_all | solution.py:80
  25.0 232.3 %all-to-all-done = bf16[32,40,4096]{2,1,0:T(8,128)(2,1)} async-done(((bf16[32,40,4096]{2,1,0:T(8,128)(2,1)}), bf16[32,40,4096]{2,1,0:T(8,128)(2,1)}, u32[]{:S(2)}, u32[]{:S(2)}) %all-to-all-start) | async-done | bytes 10485792 | tf_op jit(solution)/shard_map/all_to_all | solution.py:80
  257.3 10.2 %fusion.23 = f32[1280,384]{1,0:T(8,128)} fusion(bf16[1280,4096]{1,0:T(8,128)(2,1)} %bitcast.4, bf16[4096,384]{1,0:T(8,128)(2,1)} %param.11), kind=kOutput, calls=%fused_computation.52 | convolution fusion | flops 4026531840 | bytes 15597568 | tf_op jit(solution)/shard_map/dot_general | solution.py:83
  267.5 18.8 %fusion.3 = f32[1280,4096]{1,0:T(8,128)} fusion(bf16[384,4096]{1,0:T(8,128)(2,1)S(1)} %copy-done, bf16[1280,4096]{1,0:T(8,128)(2,1)} %bitcast.4, bf16[4096,384]{1,0:T(8,128)(2,1)} %param.12, f32[1280,384]{1,0:T(8,128)} %fusion.23), kind=kOutput, calls=%fused_computation.10 | convolution fusion | flops 8056012800 | bytes 39714816 | tf_op jit(solution)/shard_map/dot_general | solution.py:86
  286.3 9.5 %constant_dynamic-slice_fusion = f32[1280,2048]{1,0:T(8,128)} fusion(f32[1280,4096]{1,0:T(8,128)} %fusion.3, s32[]{:T(128)S(6)} %select_n.35), kind=kLoop, calls=%fused_computation.50 | loop fusion | bytes 20971524 | tf_op jit(solution)/shard_map/dynamic_slice | solution.py:88
  297.0 2.5 all-to-all-start.2
  301.2 1.4 reduce.4
  302.6 1.6 reshape.105
  304.2 7.8 %all-to-all-done.2 = bf16[32,1,1]{2,1,0:T(2,128)(2,1)S(1)} async-done(((bf16[32,1,1]{2,1,0:T(2,128)(2,1)}), bf16[32,1,1]{2,1,0:T(2,128)(2,1)S(1)}, u32[]{:S(2)}, u32[]{:S(2)}) %all-to-all-start.2) | async-done | bytes 96 | tf_op jit(solution)/shard_map/all_to_all | solution.py:45
  312.1 2.8 all-to-all-start.3
  314.9 11.1 %add_convert_fusion = bf16[1280,2048]{1,0:T(8,128)(2,1)} fusion(f32[1280,2048]{1,0:T(8,128)} %collective-permute-done, f32[1280,4096]{1,0:T(8,128)} %fusion.3, s32[]{:T(128)S(6)} %select_n.34), kind=kLoop, calls=%fused_computation.3 | loop fusion | flops 5242880 | bytes 26214404 | tf_op jit(solution)/shard_map/convert_element_type | solution.py:90
  326.0 15.1 %all-to-all-done.3 = bf16[32,2,8192]{2,1,0:T(2,128)(2,1)S(1)} async-done(((bf16[32,2,8192]{2,1,0:T(2,128)(2,1)}), bf16[32,2,8192]{2,1,0:T(2,128)(2,1)S(1)}, u32[]{:S(2)}, u32[]{:S(2)}) %all-to-all-start.3) | async-done | bytes 1048608 | tf_op jit(solution)/shard_map/all_to_all | solution.py:44
  341.1 3.7 all-to-all-start.1
  345.9 1.0 reshape.106
  347.0 1.4 convolution_convert_fusion
  348.4 1.6 copy.71
  350.0 111.6 %all-to-all-done.1 = bf16[32,40,2048]{2,1,0:T(8,128)(2,1)} async-done(((bf16[32,40,2048]{2,1,0:T(8,128)(2,1)}), bf16[32,40,2048]{2,1,0:T(8,128)(2,1)}, u32[]{:S(2)}, u32[]{:S(2)}) %all-to-all-start.1) | async-done | bytes 5242912 | tf_op jit(solution)/shard_map/all_to_all | solution.py:91
  461.5 10.3 %copy.78 = bf16[16,2,40,2048]{3,1,2,0:T(2,128)(2,1)} copy(bf16[16,2,40,2048]{3,2,1,0:T(8,128)(2,1)} %bitcast.6) | data formatting | bytes 10485760 | tf_op jit(solution)/shard_map/reshape | solution.py:92
  471.8 9.6 %dot_general.30 = bf16[4096,40,16]{0,1,2:T(8,128)(2,1)} reshape(bf16[2,2048,40,16]{1,0,2,3:T(2,128)(2,1)} %bitcast.57) | data formatting | bytes 10485760 | tf_op jit(solution)/shard_map/tec,ehcf->thf/dot_general | solution.py:93
  481.4 4.3 fusion.1
  (41 shorter events, 5.8 us)
Async XLA Ops:
  0.6 266.8 %copy-start = (bf16[384,4096]{1,0:T(8,128)(2,1)S(1)}, bf16[384,4096]{1,0:T(8,128)(2,1)}, u32[]{:S(2)}) copy-start(bf16[384,4096]{1,0:T(8,128)(2,1)} %param.13) | copy-start | bytes 9437188
  17.6 239.7 %all-to-all-start = ((bf16[32,40,4096]{2,1,0:T(8,128)(2,1)}), bf16[32,40,4096]{2,1,0:T(8,128)(2,1)}, u32[]{:S(2)}, u32[]{:S(2)}) async-start(bf16[32,40,4096]{2,1,0:T(8,128)(2,1)} %bitcast.55), calls=%async_computation | async-start | bytes 20971520 | tf_op jit(solution)/shard_map/all_to_all | solution.py:80
  286.3 9.5 %copy-start.4 = (s32[32]{0:T(128)S(1)}, s32[32]{0:T(128)}, u32[]{:S(2)}) copy-start(s32[32]{0:T(128)} %param.15) | copy-start | bytes 388
  286.3 13.3 %copy-start.2 = (bf16[32,16,1024]{2,1,0:T(8,128)(2,1)S(1)}, bf16[32,16,1024]{2,1,0:T(8,128)(2,1)}, u32[]{:S(2)}) copy-start(bf16[32,16,1024]{2,1,0:T(8,128)(2,1)} %param.14) | copy-start | bytes 3145732
  295.8 19.1 %collective-permute-start = (f32[1280,2048]{1,0:T(8,128)}, f32[1280,2048]{1,0:T(8,128)}, u32[]{:S(2)}, u32[]{:S(2)}) collective-permute-start(f32[1280,2048]{1,0:T(8,128)} %constant_dynamic-slice_fusion), channel_id=1, source_target_pairs={{0,1},{1,0},{2,3},{3,2},{4,5},{5,4},{6,7},{7,6},{8,9},{9,8},{10,11... | collective-permute-start | bytes 31457288 | tf_op jit(solution)/shard_map/ppermute | solution.py:10
  297.0 15.1 %all-to-all-start.2 = ((bf16[32,1,1]{2,1,0:T(2,128)(2,1)}), bf16[32,1,1]{2,1,0:T(2,128)(2,1)S(1)}, u32[]{:S(2)}, u32[]{:S(2)}) async-start(bf16[32,1,1]{2,1,0:T(2,128)(2,1)} %copy.66), calls=%async_computation.2 | async-start | bytes 32768 | tf_op jit(solution)/shard_map/all_to_all | solution.py:45
  312.1 29.1 %all-to-all-start.3 = ((bf16[32,2,8192]{2,1,0:T(2,128)(2,1)}), bf16[32,2,8192]{2,1,0:T(2,128)(2,1)S(1)}, u32[]{:S(2)}, u32[]{:S(2)}) async-start(bf16[32,2,8192]{2,1,0:T(2,128)(2,1)} %reshape.105), calls=%async_computation.3 | async-start | bytes 2097152 | tf_op jit(solution)/shard_map/all_to_all | solution.py:44
  341.1 3.7 copy-start.3
  341.1 120.4 %all-to-all-start.1 = ((bf16[32,40,2048]{2,1,0:T(8,128)(2,1)}), bf16[32,40,2048]{2,1,0:T(8,128)(2,1)}, u32[]{:S(2)}, u32[]{:S(2)}) async-start(bf16[32,40,2048]{2,1,0:T(8,128)(2,1)} %bitcast.58), calls=%async_computation.1 | async-start | bytes 10485760 | tf_op jit(solution)/shard_map/all_to_all | solution.py:91
  471.8 13.9 %copy-start.1 = (bf16[384,4096]{1,0:T(8,128)(2,1)S(1)}, bf16[384,4096]{1,0:T(8,128)(2,1)}, u32[]{:S(2)}) copy-start(bf16[384,4096]{1,0:T(8,128)(2,1)} %param.13) | copy-start | bytes 9437188
where the time goes:
time: 486 us
  waiting for transfers between devices  367 us (76%)
  local copies, waits for them, and re-layouts  45.2 us (9%)
  matrix products  40.2 us (8%)
  starting transfers between devices  16.5 us (3%)
  other arithmetic  16.2 us (3%)
    all_to_all x1, waiting for transfers between devices, local(): lax.all_to_all(outgoing, 'expert', split_axis=0, concat_axis=0, tiled=True)  232 us
    all_to_all x1, waiting for transfers between devices, local(): lax.all_to_all(back, 'expert', split_axis=0, concat_axis=0, tiled=True)  112 us
    dot_general x1, matrix products, local(): jnp.dot(hidden, down_weight, preferred_element_type=jnp.float32)  18.8 us
    all_to_all x1, waiting for transfers between devices, hand_pages(): lax.all_to_all(outgoing, 'expert', split_axis=0, concat_axis=0, tiled=True)  15.1 us
    convert_element_type x1, other arithmetic, local(): back = summed.astype(jnp.bfloat16).reshape(sources, held, half)  11.1 us
    reshape x1, local copies, waits for them, and re-layouts, local(): expert_out = returned.reshape(experts, 2, capacity, half)  10.3 us
    dot_general x1, matrix products, local(): gate = jnp.dot(rows, gate_weight, preferred_element_type=jnp.float32)  10.2 us
  transfers between devices with their start and end apart: 5, of which 4 were waited for; matrix products, arithmetic and copies ran while one was open for 5% of the time, Pallas kernels for 0%

commit v1 on v0

v1 whole, which is shorter than its diff:
```python
import jax
import jax.numpy as jnp
from jax import lax
from jax.sharding import PartitionSpec as P

PCAP = 1
PLANE = 4


def slot_ranks(labels, count):
    onehot = (labels[:, None] == jnp.arange(count, dtype=jnp.int32)[None, :]).astype(jnp.int32)
    earlier = jnp.cumsum(onehot, axis=0) - onehot
    return jnp.sum(earlier * onehot, axis=1)


def place_pages(arrived, arrived_labels, page_count, page_shape):
    picking = (
        arrived_labels.astype(jnp.float32)[None, :]
        == jnp.arange(page_count, dtype=jnp.float32)[:, None]
    ).astype(jnp.bfloat16)
    landed = jnp.dot(picking, arrived, preferred_element_type=jnp.float32)
    return landed.astype(jnp.bfloat16).reshape(page_shape)


def hand_pages(kv_pages, page_target):
    page_count = kv_pages.shape[0]
    owners = lax.axis_size("expert")
    target_dev = page_target // page_count
    target_slot = page_target % page_count
    flat_pages = kv_pages.reshape(page_count, -1)
    position = target_dev * PCAP + slot_ranks(target_dev, owners)
    placing = position[:, None] == jnp.arange(owners * PCAP, dtype=jnp.int32)[None, :]
    outgoing = lax.dot_general(
        placing.astype(jnp.bfloat16),
        flat_pages,
        (((0,), (0,)), ((), ())),
        preferred_element_type=jnp.float32,
    ).astype(jnp.bfloat16)
    labels = jnp.sum(jnp.where(placing, target_slot[:, None] + 1, 0), axis=0) - 1
    arrived, arrived_labels = (
        lax.all_to_all(outgoing, "expert", split_axis=0, concat_axis=0, tiled=True),
        lax.all_to_all(
            labels.astype(jnp.bfloat16), "expert", split_axis=0, concat_axis=0, tiled=True
        ),
    )
    return place_pages(arrived, arrived_labels, page_count, kv_pages.shape)


def send(x, step=None, flip=None):
    count = lax.axis_size("expert")
    if flip is not None:
        pairs = [(i, i ^ flip) for i in range(count)]
    else:
        pairs = [(i, (i + step) % count) for i in range(count)]
    return lax.ppermute(x, "expert", pairs)


def mixing_table(route_ids, route_gates, experts):
    shares = route_gates / jnp.sum(route_gates, axis=1, keepdims=True)
    mixing = shares.astype(jnp.bfloat16).astype(jnp.float32)
    hits = route_ids[:, :, None] == jnp.arange(experts, dtype=jnp.int32)
    return jnp.sum(jnp.where(hits, mixing[:, :, None], 0.0), axis=1).astype(jnp.bfloat16)


def plane_slots(table, nearby, capacity):
    rows = table.shape[0]
    weight = jnp.dot(table, nearby, preferred_element_type=jnp.float32)
    named = weight > 0
    below = jnp.arange(rows)[:, None] > jnp.arange(rows)[None, :]
    rank = jnp.dot(
        below.astype(jnp.bfloat16), named.astype(jnp.bfloat16), preferred_element_type=jnp.float32
    )
    hits = (rank[:, :, None] == jnp.arange(capacity, dtype=jnp.float32)) & named[:, :, None]
    placing = hits.astype(jnp.bfloat16)
    blend = jnp.where(hits, weight[:, :, None], 0.0).astype(jnp.bfloat16)
    return placing, blend


def local(
    tokens, route_ids, route_gates, gate_weight, up_weight, down_weight, kv_pages, page_target
):
    tok_rows, width = tokens.shape
    chosen = route_ids.shape[1]
    owners = lax.axis_size("expert")
    experts = owners // 2
    planes = experts // PLANE
    stride = 2 * PLANE
    capacity = min(tok_rows, 5 * tok_rows * chosen // (4 * experts))
    chip = lax.axis_index("expert") // 2
    near = (chip // PLANE) * PLANE + ((chip % PLANE) ^ jnp.arange(PLANE, dtype=jnp.int32))
    nearby = (jnp.arange(experts, dtype=jnp.int32)[:, None] == near[None, :]).astype(jnp.bfloat16)

    blocks = [tokens]
    for _ in range(1, planes):
        blocks.append(send(blocks[-1], step=stride))
    table = mixing_table(route_ids, route_gates, experts)
    tables = [table] + [send(table, step=stride * s) for s in range(1, planes)]

    gate_all = jnp.concatenate([gate_weight, send(gate_weight, flip=1)], axis=1)
    up_all = jnp.concatenate([up_weight, send(up_weight, flip=1)], axis=1)
    down_all = jnp.concatenate([down_weight, send(down_weight, flip=1)], axis=0)

    held, blends = [], []
    for s in range(planes):
        placing, blend = plane_slots(tables[s], nearby, capacity)
        blends.append(blend.reshape(tok_rows, PLANE * capacity))
        for j in range(PLANE):
            picked = lax.dot_general(
                placing[:, j],
                blocks[s],
                (((0,), (0,)), ((), ())),
                preferred_element_type=jnp.float32,
            ).astype(jnp.bfloat16)
            held.append(send(picked, flip=2 * j) if j else picked)

    outs = []
    group = 2
    for first in range(0, planes, group):
        rows = jnp.concatenate(held[first * PLANE : (first + group) * PLANE], axis=0)
        gate = jnp.dot(rows, gate_all, preferred_element_type=jnp.float32)
        up = jnp.dot(rows, up_all, preferred_element_type=jnp.float32)
        hidden = (jax.nn.silu(gate) * up).astype(jnp.bfloat16)
        out = jnp.dot(hidden, down_all, preferred_element_type=jnp.float32).astype(jnp.bfloat16)
        outs.extend(jnp.split(out, group * PLANE, axis=0))

    def returned(s):
        mine = outs[s * PLANE : (s + 1) * PLANE]
        back = [mine[0]] + [send(mine[j], flip=2 * j) for j in range(1, PLANE)]
        return jnp.dot(
            blends[s], jnp.concatenate(back, axis=0), preferred_element_type=jnp.float32
        )

    total = returned(1).astype(jnp.bfloat16)
    for s in list(range(2, planes)) + [0]:
        arrived = send(total, step=stride)
        total = (returned(s) + arrived.astype(jnp.float32)).astype(jnp.bfloat16)
    handed = hand_pages(kv_pages, page_target)
    return (total, handed)


def solution(mesh):
    placed = (
        P(("groups", "expert"), None),
        P(("groups", "expert"), None),
        P(("groups", "expert"), None),
        P(None, "expert"),
        P(None, "expert"),
        P("expert", None),
        P(("groups", "expert"), None, None),
        P(("groups", "expert")),
    )
    return jax.shard_map(
        local,
        mesh=mesh,
        in_specs=placed,
        out_specs=(P(("groups", "expert"), None), P(("groups", "expert"), None, None)),
        check_vma=False,
    )
```

time: 486 us -> 252 us (0.52)
  waiting for transfers between devices: 367 us -> 112 us
  starting transfers between devices: 16.5 us -> 54.5 us
  local copies, waits for them, and re-layouts: 45.2 us -> 28.3 us
  other arithmetic: 16.2 us -> 5.93 us
  matrix products: 40.2 us -> 49.4 us
    all_to_all x2 -> x0, waiting for transfers between devices: 344 us -> none  [the longest x1 232 us: local(): lax.all_to_all(outgoing, 'expert', split_axis=0, concat_axis=0, tiled=True)]
    ppermute x1 -> x36, waiting for transfers between devices: 0.01 us -> 112 us  [send(): return lax.ppermute(x, 'expert', pairs)]
    ppermute x1 -> x36, starting transfers between devices: 0.01 us -> 44.7 us  [send(): return lax.ppermute(x, 'expert', pairs)]
    all_to_all x1, waiting for transfers between devices: 15.1 us -> 0.01 us  [hand_pages(): lax.all_to_all(outgoing, 'expert', split_axis=0, concat_axis=0, tiled=True)]
    unnamed x15 -> x47, local copies, waits for them, and re-layouts: 5.71 us -> 17 us
    all_to_all x2 -> x0, starting transfers between devices: 11.1 us -> none  [the longest x1 7.41 us: local(): lax.all_to_all(outgoing, 'expert', split_axis=0, concat_axis=0, tiled=True)]
    reshape x1 -> x0, local copies, waits for them, and re-layouts: 10.3 us -> none  [local(): expert_out = returned.reshape(experts, 2, capacity, half)]
    convert_element_type x2, other arithmetic: 11.1 us -> 1.49 us  [the longest x1 0.8 us: plane_slots(): blend = jnp.where(hits, weight[:, :, None], 0.0).astype(jnp.bfloat16)]
  transfers between devices with their start and end apart: 5 -> 38, of which waited for: 4 -> 18; matrix products, arithmetic and copies ran while one was open for 5% -> 31% of each run, Pallas kernels for 0% -> 0%
where the time goes in v1:
time: 252 us; the launch traced here: 251 us
  waiting for transfers between devices  112 us (44%)
  starting transfers between devices  54.5 us (22%)
  matrix products  49.4 us (20%)
  local copies, waits for them, and re-layouts  28.3 us (11%)
  other arithmetic  5.93 us (2%)
    ppermute x36, waiting for transfers between devices, send(): return lax.ppermute(x, 'expert', pairs)  112 us
    ppermute x36, starting transfers between devices, send(): return lax.ppermute(x, 'expert', pairs)  44.7 us
    dot_general x2, matrix products, local(): jnp.dot(hidden, down_all, preferred_element_type=jnp.float32)  24.2 us
    unnamed x47, local copies, waits for them, and re-layouts  17 us
    dot_general x16, matrix products, local(): lax.dot_general(placing[:, j], blocks[s], (((0,), (0,)), ((), ())), prefe...  9.24 us
    dot_general x4, matrix products, returned(): jnp.dot(blends[s], jnp.concatenate(back, axis=0), preferred_element_type=...  6.36 us
    dot_general x2, matrix products, local(): gate = jnp.dot(rows, gate_all, preferred_element_type=jnp.float32)  6.34 us
    all_to_all x1, starting transfers between devices, hand_pages(): lax.all_to_all(labels.astype(jnp.bfloat16), 'expert', split_axis=0, conca...  5.62 us
  transfers between devices with their start and end apart: 38, of which 18 were waited for; matrix products, arithmetic and copies ran while one was open for 31% of the time, Pallas kernels for 0%

profile of v1, /device:TPU:0, one launch (start us, length us, event | category | flops | bytes accessed | tf_op | source)
XLA Modules:
  0.0 251.4 jit_solution(13620406066491712582)
XLA Ops:
  2.8 5.1 %collective-permute-start.14 = (bf16[64,16]{0,1:T(8,128)(2,1)S(1)}, bf16[64,16]{0,1:T(8,128)(2,1)S(1)}, u32[]{:S(2)}, u32[]{:S(2)}) collective-permute-start(bf16[64,16]{0,1:T(8,128)(2,1)S(1)} %select_reduce_fusion), channel_id=1, source_target_pairs={{0,24},{1,25},{2,26},{3,27},{4,28},{5,29},{6,30},{7,31},{8,0},{9,1... | collective-permute-start | bytes 6152 | tf_op jit(solution)/shard_map/ppermute | solution.py:55
  10.7 5.6 %all-to-all-start = ((bf16[32,1,1]{2,1,0:T(2,128)(2,1)}), bf16[32,1,1]{2,1,0:T(2,128)(2,1)S(1)}, u32[]{:S(2)}, u32[]{:S(2)}) async-start(bf16[32,1,1]{2,1,0:T(2,128)(2,1)} %copy.34), calls=%async_computation | async-start | bytes 32768 | tf_op jit(solution)/shard_map/all_to_all | solution.py:42
  40.8 7.7 %collective-permute-done = bf16[40,4096]{1,0:T(8,128)(2,1)S(1)} collective-permute-done((bf16[40,4096]{1,0:T(8,128)(2,1)}, bf16[40,4096]{1,0:T(8,128)(2,1)S(1)}, u32[]{:S(2)}, u32[]{:S(2)}) %collective-permute-start) | collective-permute-done | bytes 327712 | tf_op jit(solution)/shard_map/ppermute | solution.py:55
  50.8 7.1 %collective-permute-done.1 = bf16[40,4096]{1,0:T(8,128)(2,1)S(1)} collective-permute-done((bf16[40,4096]{1,0:T(8,128)(2,1)S(1)}, bf16[40,4096]{1,0:T(8,128)(2,1)S(1)}, u32[]{:S(2)}, u32[]{:S(2)}) %collective-permute-start.1) | collective-permute-done | bytes 327712 | tf_op jit(solution)/shard_map/ppermute | solution.py:55
  61.0 6.2 %collective-permute-done.2 = bf16[40,4096]{1,0:T(8,128)(2,1)S(1)} collective-permute-done((bf16[40,4096]{1,0:T(8,128)(2,1)S(1)}, bf16[40,4096]{1,0:T(8,128)(2,1)S(1)}, u32[]{:S(2)}, u32[]{:S(2)}) %collective-permute-start.2) | collective-permute-done | bytes 327712 | tf_op jit(solution)/shard_map/ppermute | solution.py:55
  72.7 3.1 %collective-permute-done.5 = bf16[40,4096]{1,0:T(8,128)(2,1)S(1)} collective-permute-done((bf16[40,4096]{1,0:T(8,128)(2,1)S(1)}, bf16[40,4096]{1,0:T(8,128)(2,1)S(1)}, u32[]{:S(2)}, u32[]{:S(2)}) %collective-permute-start.5) | collective-permute-done | bytes 327712 | tf_op jit(solution)/shard_map/ppermute | solution.py:55
  79.3 5.0 %collective-permute-done.6 = bf16[40,4096]{1,0:T(8,128)(2,1)S(1)} collective-permute-done((bf16[40,4096]{1,0:T(8,128)(2,1)S(1)}, bf16[40,4096]{1,0:T(8,128)(2,1)S(1)}, u32[]{:S(2)}, u32[]{:S(2)}) %collective-permute-start.6) | collective-permute-done | bytes 327712 | tf_op jit(solution)/shard_map/ppermute | solution.py:55
  87.3 8.0 %collective-permute-done.16 = bf16[64,4096]{1,0:T(8,128)(2,1)S(1)} collective-permute-done((bf16[64,4096]{1,0:T(8,128)(2,1)S(1)}, bf16[64,4096]{1,0:T(8,128)(2,1)S(1)}, u32[]{:S(2)}, u32[]{:S(2)}) %collective-permute-start.16) | collective-permute-done | bytes 524320 | tf_op jit(solution)/shard_map/ppermute | solution.py:55
  97.9 4.8 %collective-permute-done.17 = bf16[40,4096]{1,0:T(8,128)(2,1)S(1)} collective-permute-done((bf16[40,4096]{1,0:T(8,128)(2,1)S(1)}, bf16[40,4096]{1,0:T(8,128)(2,1)S(1)}, u32[]{:S(2)}, u32[]{:S(2)}) %collective-permute-start.17) | collective-permute-done | bytes 327712 | tf_op jit(solution)/shard_map/ppermute | solution.py:55
  104.3 9.8 %collective-permute-done.19 = bf16[40,4096]{1,0:T(8,128)(2,1)S(1)} collective-permute-done((bf16[40,4096]{1,0:T(8,128)(2,1)S(1)}, bf16[40,4096]{1,0:T(8,128)(2,1)S(1)}, u32[]{:S(2)}, u32[]{:S(2)}) %collective-permute-start.19) | collective-permute-done | bytes 327712 | tf_op jit(solution)/shard_map/ppermute | solution.py:55
  118.5 5.3 %collective-permute-done.21 = bf16[40,4096]{1,0:T(8,128)(2,1)S(1)} collective-permute-done((bf16[40,4096]{1,0:T(8,128)(2,1)S(1)}, bf16[40,4096]{1,0:T(8,128)(2,1)S(1)}, u32[]{:S(2)}, u32[]{:S(2)}) %collective-permute-start.21) | collective-permute-done | bytes 327712 | tf_op jit(solution)/shard_map/ppermute | solution.py:55
  124.5 7.3 %collective-permute-done.23 = bf16[40,4096]{1,0:T(8,128)(2,1)S(1)} collective-permute-done((bf16[40,4096]{1,0:T(8,128)(2,1)S(1)}, bf16[40,4096]{1,0:T(8,128)(2,1)S(1)}, u32[]{:S(2)}, u32[]{:S(2)}) %collective-permute-start.23) | collective-permute-done | bytes 327712 | tf_op jit(solution)/shard_map/ppermute | solution.py:55
  131.9 3.4 %constant_dynamic-update-slice_fusion.6 = bf16[4096,768]{1,0:T(8,128)(2,1)S(1)} fusion(bf16[4096,768]{1,0:T(8,128)(2,1)S(1)} %bitcast.167, bf16[4096,384]{1,0:T(8,128)(2,1)} %collective-permute-done.8), kind=kLoop, calls=%fused_computation.98 | loop fusion | bytes 6291456 | tf_op jit(solution)/shard_map/concatenate | solution.py:99
  136.0 3.1 %fusion.79 = f32[320,768]{1,0:T(8,128)} fusion(bf16[320,4096]{1,0:T(8,128)(2,1)S(1)} %constant_dynamic-update-slice_fusion.12, bf16[4096,768]{1,0:T(8,128)(2,1)S(1)} %constant_dynamic-update-slice_fusion.6), kind=kOutput, calls=%fused_computation.173 | convolution fusion | flops 2013265920 | bytes 9895936 | tf_op jit(solution)/shard_map/dot_general | solution.py:120
  139.7 3.2 %fusion.77 = f32[320,768]{1,0:T(8,128)} fusion(bf16[320,4096]{1,0:T(8,128)(2,1)S(1)} %copy-done.6, bf16[4096,768]{1,0:T(8,128)(2,1)S(1)} %constant_dynamic-update-slice_fusion.6), kind=kOutput, calls=%fused_computation.171 | convolution fusion | flops 2013265920 | bytes 9895936 | tf_op jit(solution)/shard_map/dot_general | solution.py:120
  144.9 11.2 %convolution_convert_fusion.3 = bf16[320,4096]{1,0:T(8,128)(2,1)S(1)} fusion(bf16[768,4096]{1,0:T(8,128)(2,1)} %constant_dynamic-update-slice_fusion.10, f32[320,768]{1,0:T(8,128)} %fusion.77, bf16[320,4096]{1,0:T(8,128)(2,1)} %constant_dynamic-update-slice_fusion, bf16[4096,768]{1,0:T(8,128)(2,1)} %copy-done.4), kind=kOutput, calls=%fused_computation.4 | convolution fusion | flops 4029317120 | bytes 18808832 | tf_op jit(solution)/shard_map/dot_general | solution.py:123
  160.9 12.9 %convolution_convert_fusion.2 = bf16[320,4096]{1,0:T(8,128)(2,1)} fusion(bf16[768,4096]{1,0:T(8,128)(2,1)} %constant_dynamic-update-slice_fusion.10, f32[320,768]{1,0:T(8,128)} %fusion.79, bf16[320,4096]{1,0:T(8,128)(2,1)} %copy-done.7, bf16[4096,768]{1,0:T(8,128)(2,1)} %copy-done.4), kind=kOutput, calls=%fused_computation.3 | convolution fusion | flops 4029317120 | bytes 18808832 | tf_op jit(solution)/shard_map/dot_general | solution.py:123
  175.1 4.2 %all-to-all-start.1 = ((bf16[32,2,8192]{2,1,0:T(2,128)(2,1)}), bf16[32,2,8192]{2,1,0:T(2,128)(2,1)S(1)}, u32[]{:S(2)}, u32[]{:S(2)}) async-start(bf16[32,2,8192]{2,1,0:T(2,128)(2,1)} %reshape.82), calls=%async_computation.1 | async-start | bytes 2097152 | tf_op jit(solution)/shard_map/all_to_all | solution.py:41
  184.7 16.0 %collective-permute-done.29 = bf16[40,4096]{1,0:T(8,128)(2,1)S(1)} collective-permute-done((bf16[40,4096]{1,0:T(8,128)(2,1)S(1)}, bf16[40,4096]{1,0:T(8,128)(2,1)S(1)}, u32[]{:S(2)}, u32[]{:S(2)}) %collective-permute-start.29) | collective-permute-done | bytes 327712 | tf_op jit(solution)/shard_map/ppermute | solution.py:55
  200.8 7.5 %collective-permute-done.28 = bf16[40,4096]{1,0:T(8,128)(2,1)S(1)} collective-permute-done((bf16[40,4096]{1,0:T(8,128)(2,1)S(1)}, bf16[40,4096]{1,0:T(8,128)(2,1)S(1)}, u32[]{:S(2)}, u32[]{:S(2)}) %collective-permute-start.28) | collective-permute-done | bytes 327712 | tf_op jit(solution)/shard_map/ppermute | solution.py:55
  214.9 8.1 %collective-permute-done.26 = bf16[40,4096]{1,0:T(8,128)(2,1)S(1)} collective-permute-done((bf16[40,4096]{1,0:T(8,128)(2,1)S(1)}, bf16[40,4096]{1,0:T(8,128)(2,1)S(1)}, u32[]{:S(2)}, u32[]{:S(2)}) %collective-permute-start.26) | collective-permute-done | bytes 327712 | tf_op jit(solution)/shard_map/ppermute | solution.py:55
  222.9 5.2 %collective-permute-done.25 = bf16[40,4096]{1,0:T(8,128)(2,1)S(1)} collective-permute-done((bf16[40,4096]{1,0:T(8,128)(2,1)S(1)}, bf16[40,4096]{1,0:T(8,128)(2,1)S(1)}, u32[]{:S(2)}, u32[]{:S(2)}) %collective-permute-start.25) | collective-permute-done | bytes 327712 | tf_op jit(solution)/shard_map/ppermute | solution.py:55
  239.1 4.0 %collective-permute-done.13 = bf16[40,4096]{1,0:T(8,128)(2,1)} collective-permute-done((bf16[40,4096]{1,0:T(8,128)(2,1)}, bf16[40,4096]{1,0:T(8,128)(2,1)}, u32[]{:S(2)}, u32[]{:S(2)}) %collective-permute-start.13) | collective-permute-done | bytes 327712 | tf_op jit(solution)/shard_map/ppermute | solution.py:55
  243.1 5.7 %collective-permute-done.12 = bf16[40,4096]{1,0:T(8,128)(2,1)} collective-permute-done((bf16[40,4096]{1,0:T(8,128)(2,1)}, bf16[40,4096]{1,0:T(8,128)(2,1)}, u32[]{:S(2)}, u32[]{:S(2)}) %collective-permute-start.12) | collective-permute-done | bytes 327712 | tf_op jit(solution)/shard_map/ppermute | solution.py:55
  (164 shorter events, 90.4 us)
Async XLA Ops:
  2.8 35.3 %collective-permute-start.14 = (bf16[64,16]{0,1:T(8,128)(2,1)S(1)}, bf16[64,16]{0,1:T(8,128)(2,1)S(1)}, u32[]{:S(2)}, u32[]{:S(2)}) collective-permute-start(bf16[64,16]{0,1:T(8,128)(2,1)S(1)} %select_reduce_fusion), channel_id=1, source_target_pairs={{0,24},{1,25},{2,26},{3,27},{4,28},{5,29},{6,30},{7,31},{8,0},{9,1... | collective-permute-start | bytes 6152 | tf_op jit(solution)/shard_map/ppermute | solution.py:55
  7.9 28.9 %collective-permute-start.3 = (bf16[64,16]{0,1:T(8,128)(2,1)S(1)}, bf16[64,16]{0,1:T(8,128)(2,1)S(1)}, u32[]{:S(2)}, u32[]{:S(2)}) collective-permute-start(bf16[64,16]{0,1:T(8,128)(2,1)S(1)} %select_reduce_fusion), channel_id=1, source_target_pairs={{0,8},{1,9},{2,10},{3,11},{4,12},{5,13},{6,14},{7,15},{8,16},{9,17... | collective-permute-start | bytes 6152 | tf_op jit(solution)/shard_map/ppermute | solution.py:55
  7.9 29.8 %collective-permute-start.15 = (bf16[64,16]{0,1:T(8,128)(2,1)S(1)}, bf16[64,16]{0,1:T(8,128)(2,1)S(1)}, u32[]{:S(2)}, u32[]{:S(2)}) collective-permute-start(bf16[64,16]{0,1:T(8,128)(2,1)S(1)} %select_reduce_fusion), channel_id=1, source_target_pairs={{0,16},{1,17},{2,18},{3,19},{4,20},{5,21},{6,22},{7,23},{8,24},{9,... | collective-permute-start | bytes 6152 | tf_op jit(solution)/shard_map/ppermute | solution.py:55
  10.7 164.4 %all-to-all-start = ((bf16[32,1,1]{2,1,0:T(2,128)(2,1)}), bf16[32,1,1]{2,1,0:T(2,128)(2,1)S(1)}, u32[]{:S(2)}, u32[]{:S(2)}) async-start(bf16[32,1,1]{2,1,0:T(2,128)(2,1)} %copy.34), calls=%async_computation | async-start | bytes 32768 | tf_op jit(solution)/shard_map/all_to_all | solution.py:42
  16.3 51.6 %collective-permute-start.4 = (bf16[64,4096]{1,0:T(8,128)(2,1)}, bf16[64,4096]{1,0:T(8,128)(2,1)S(1)}, u32[]{:S(2)}, u32[]{:S(2)}) collective-permute-start(bf16[64,4096]{1,0:T(8,128)(2,1)} %param.8), channel_id=1, source_target_pairs={{0,8},{1,9},{2,10},{3,11},{4,12},{5,13},{6,14},{7,15},{8,16},{9,17... | collective-permute-start | bytes 1572872 | tf_op jit(solution)/shard_map/ppermute | solution.py:55
  18.2 113.7 %collective-permute-start.8 = (bf16[4096,384]{1,0:T(8,128)(2,1)}, bf16[4096,384]{1,0:T(8,128)(2,1)}, u32[]{:S(2)}, u32[]{:S(2)}) collective-permute-start(bf16[4096,384]{1,0:T(8,128)(2,1)} %param.11), channel_id=1, source_target_pairs={{0,1},{1,0},{2,3},{3,2},{4,5},{5,4},{6,7},{7,6},{8,9},{9,8},{10,11... | collective-permute-start | bytes 9437192 | tf_op jit(solution)/shard_map/ppermute | solution.py:55
  36.9 98.5 %collective-permute-start.9 = (bf16[4096,384]{1,0:T(8,128)(2,1)}, bf16[4096,384]{1,0:T(8,128)(2,1)S(1)}, u32[]{:S(2)}, u32[]{:S(2)}) collective-permute-start(bf16[4096,384]{1,0:T(8,128)(2,1)} %param.12), channel_id=1, source_target_pairs={{0,1},{1,0},{2,3},{3,2},{4,5},{5,4},{6,7},{7,6},{8,9},{9,8},{10,11... | collective-permute-start | bytes 9437192 | tf_op jit(solution)/shard_map/ppermute | solution.py:55
  37.7 105.2 %collective-permute-start.10 = (bf16[384,4096]{1,0:T(8,128)(2,1)}, bf16[384,4096]{1,0:T(8,128)(2,1)S(1)}, u32[]{:S(2)}, u32[]{:S(2)}) collective-permute-start(bf16[384,4096]{1,0:T(8,128)(2,1)} %param.13), channel_id=1, source_target_pairs={{0,1},{1,0},{2,3},{3,2},{4,5},{5,4},{6,7},{7,6},{8,9},{9,8},{10,11... | collective-permute-start | bytes 9437192 | tf_op jit(solution)/shard_map/ppermute | solution.py:55
  70.0 14.3 %collective-permute-start.6 = (bf16[40,4096]{1,0:T(8,128)(2,1)S(1)}, bf16[40,4096]{1,0:T(8,128)(2,1)S(1)}, u32[]{:S(2)}, u32[]{:S(2)}) collective-permute-start(bf16[40,4096]{1,0:T(8,128)(2,1)S(1)} %convolution_convert_fusion.14), channel_id=1, source_target_pairs={{0,4},{1,5},{2,6},{3,7},{4,0},{5,1},{6,2},{7,3},{8,12},{9,13},{10,... | collective-permute-start | bytes 983048 | tf_op jit(solution)/shard_map/ppermute | solution.py:55
  157.5 16.4 %collective-permute-start.32 = (bf16[40,4096]{1,0:T(8,128)(2,1)}, bf16[40,4096]{1,0:T(8,128)(2,1)S(1)}, u32[]{:S(2)}, u32[]{:S(2)}) collective-permute-start(bf16[40,4096]{1,0:T(8,128)(2,1)} %get-tuple-element.3), channel_id=1, source_target_pairs={{0,6},{1,7},{2,4},{3,5},{4,2},{5,3},{6,0},{7,1},{8,14},{9,15},{10,... | collective-permute-start | bytes 983048 | tf_op jit(solution)/shard_map/ppermute | solution.py:55
  158.0 15.8 %collective-permute-start.31 = (bf16[40,4096]{1,0:T(8,128)(2,1)}, bf16[40,4096]{1,0:T(8,128)(2,1)S(1)}, u32[]{:S(2)}, u32[]{:S(2)}) collective-permute-start(bf16[40,4096]{1,0:T(8,128)(2,1)} %get-tuple-element.4), channel_id=1, source_target_pairs={{0,4},{1,5},{2,6},{3,7},{4,0},{5,1},{6,2},{7,3},{8,12},{9,13},{10,... | collective-permute-start | bytes 983048 | tf_op jit(solution)/shard_map/ppermute | solution.py:55
  159.3 14.6 %collective-permute-start.30 = (bf16[40,4096]{1,0:T(8,128)(2,1)}, bf16[40,4096]{1,0:T(8,128)(2,1)S(1)}, u32[]{:S(2)}, u32[]{:S(2)}) collective-permute-start(bf16[40,4096]{1,0:T(8,128)(2,1)} %get-tuple-element.5), channel_id=1, source_target_pairs={{0,2},{1,3},{2,0},{3,1},{4,6},{5,7},{6,4},{7,5},{8,10},{9,11},{10,... | collective-permute-start | bytes 983048 | tf_op jit(solution)/shard_map/ppermute | solution.py:55
  175.1 33.2 %collective-permute-start.33 = (bf16[64,4096]{1,0:T(8,128)(2,1)}, bf16[64,4096]{1,0:T(8,128)(2,1)}, u32[]{:S(2)}, u32[]{:S(2)}) collective-permute-start(bf16[64,4096]{1,0:T(8,128)(2,1)} %convolution_convert_fusion.4), channel_id=1, source_target_pairs={{0,8},{1,9},{2,10},{3,11},{4,12},{5,13},{6,14},{7,15},{8,16},{9,17... | collective-permute-start | bytes 1572872 | tf_op jit(solution)/shard_map/ppermute | solution.py:55
  175.1 59.9 %all-to-all-start.1 = ((bf16[32,2,8192]{2,1,0:T(2,128)(2,1)}), bf16[32,2,8192]{2,1,0:T(2,128)(2,1)S(1)}, u32[]{:S(2)}, u32[]{:S(2)}) async-start(bf16[32,2,8192]{2,1,0:T(2,128)(2,1)} %reshape.82), calls=%async_computation.1 | async-start | bytes 2097152 | tf_op jit(solution)/shard_map/all_to_all | solution.py:41
  181.2 19.6 %collective-permute-start.29 = (bf16[40,4096]{1,0:T(8,128)(2,1)S(1)}, bf16[40,4096]{1,0:T(8,128)(2,1)S(1)}, u32[]{:S(2)}, u32[]{:S(2)}) collective-permute-start(bf16[40,4096]{1,0:T(8,128)(2,1)S(1)} %get-tuple-element.11), channel_id=1, source_target_pairs={{0,6},{1,7},{2,4},{3,5},{4,2},{5,3},{6,0},{7,1},{8,14},{9,15},{10,... | collective-permute-start | bytes 983048 | tf_op jit(solution)/shard_map/ppermute | solution.py:55
  183.9 24.4 %collective-permute-start.28 = (bf16[40,4096]{1,0:T(8,128)(2,1)S(1)}, bf16[40,4096]{1,0:T(8,128)(2,1)S(1)}, u32[]{:S(2)}, u32[]{:S(2)}) collective-permute-start(bf16[40,4096]{1,0:T(8,128)(2,1)S(1)} %get-tuple-element.12), channel_id=1, source_target_pairs={{0,4},{1,5},{2,6},{3,7},{4,0},{5,1},{6,2},{7,3},{8,12},{9,13},{10,... | collective-permute-start | bytes 983048 | tf_op jit(solution)/shard_map/ppermute | solution.py:55
  184.5 23.8 %collective-permute-start.27 = (bf16[40,4096]{1,0:T(8,128)(2,1)S(1)}, bf16[40,4096]{1,0:T(8,128)(2,1)S(1)}, u32[]{:S(2)}, u32[]{:S(2)}) collective-permute-start(bf16[40,4096]{1,0:T(8,128)(2,1)S(1)} %get-tuple-element.13), channel_id=1, source_target_pairs={{0,2},{1,3},{2,0},{3,1},{4,6},{5,7},{6,4},{7,5},{8,10},{9,11},{10,... | collective-permute-start | bytes 983048 | tf_op jit(solution)/shard_map/ppermute | solution.py:55
  209.7 18.4 %collective-permute-start.34 = (bf16[64,4096]{1,0:T(8,128)(2,1)S(1)}, bf16[64,4096]{1,0:T(8,128)(2,1)S(1)}, u32[]{:S(2)}, u32[]{:S(2)}) collective-permute-start(bf16[64,4096]{1,0:T(8,128)(2,1)S(1)} %fusion.3), channel_id=1, source_target_pairs={{0,8},{1,9},{2,10},{3,11},{4,12},{5,13},{6,14},{7,15},{8,16},{9,17... | collective-permute-start | bytes 1572872 | tf_op jit(solution)/shard_map/ppermute | solution.py:55
  212.5 15.7 %collective-permute-start.25 = (bf16[40,4096]{1,0:T(8,128)(2,1)S(1)}, bf16[40,4096]{1,0:T(8,128)(2,1)S(1)}, u32[]{:S(2)}, u32[]{:S(2)}) collective-permute-start(bf16[40,4096]{1,0:T(8,128)(2,1)S(1)} %get-tuple-element.15), channel_id=1, source_target_pairs={{0,4},{1,5},{2,6},{3,7},{4,0},{5,1},{6,2},{7,3},{8,12},{9,13},{10,... | collective-permute-start | bytes 983048 | tf_op jit(solution)/shard_map/ppermute | solution.py:55
  213.3 14.8 %collective-permute-start.24 = (bf16[40,4096]{1,0:T(8,128)(2,1)S(1)}, bf16[40,4096]{1,0:T(8,128)(2,1)S(1)}, u32[]{:S(2)}, u32[]{:S(2)}) collective-permute-start(bf16[40,4096]{1,0:T(8,128)(2,1)S(1)} %get-tuple-element.16), channel_id=1, source_target_pairs={{0,2},{1,3},{2,0},{3,1},{4,6},{5,7},{6,4},{7,5},{8,10},{9,11},{10,... | collective-permute-start | bytes 983048 | tf_op jit(solution)/shard_map/ppermute | solution.py:55
  229.4 19.4 %collective-permute-start.35 = (bf16[64,4096]{1,0:T(8,128)(2,1)}, bf16[64,4096]{1,0:T(8,128)(2,1)}, u32[]{:S(2)}, u32[]{:S(2)}) collective-permute-start(bf16[64,4096]{1,0:T(8,128)(2,1)} %fusion.2), channel_id=1, source_target_pairs={{0,8},{1,9},{2,10},{3,11},{4,12},{5,13},{6,14},{7,15},{8,16},{9,17... | collective-permute-start | bytes 1572872 | tf_op jit(solution)/shard_map/ppermute | solution.py:55
  231.2 11.9 %collective-permute-start.13 = (bf16[40,4096]{1,0:T(8,128)(2,1)}, bf16[40,4096]{1,0:T(8,128)(2,1)}, u32[]{:S(2)}, u32[]{:S(2)}) collective-permute-start(bf16[40,4096]{1,0:T(8,128)(2,1)} %get-tuple-element.6), channel_id=1, source_target_pairs={{0,6},{1,7},{2,4},{3,5},{4,2},{5,3},{6,0},{7,1},{8,14},{9,15},{10,... | collective-permute-start | bytes 983048 | tf_op jit(solution)/shard_map/ppermute | solution.py:55
  232.5 16.4 %collective-permute-start.12 = (bf16[40,4096]{1,0:T(8,128)(2,1)}, bf16[40,4096]{1,0:T(8,128)(2,1)}, u32[]{:S(2)}, u32[]{:S(2)}) collective-permute-start(bf16[40,4096]{1,0:T(8,128)(2,1)} %get-tuple-element.7), channel_id=1, source_target_pairs={{0,4},{1,5},{2,6},{3,7},{4,0},{5,1},{6,2},{7,3},{8,12},{9,13},{10,... | collective-permute-start | bytes 983048 | tf_op jit(solution)/shard_map/ppermute | solution.py:55
  233.4 15.5 %collective-permute-start.11 = (bf16[40,4096]{1,0:T(8,128)(2,1)}, bf16[40,4096]{1,0:T(8,128)(2,1)}, u32[]{:S(2)}, u32[]{:S(2)}) collective-permute-start(bf16[40,4096]{1,0:T(8,128)(2,1)} %get-tuple-element.8), channel_id=1, source_target_pairs={{0,2},{1,3},{2,0},{3,1},{4,6},{5,7},{6,4},{7,5},{8,10},{9,11},{10,... | collective-permute-start | bytes 983048 | tf_op jit(solution)/shard_map/ppermute | solution.py:55
  (29 other events, 419.6 us)

commit v2 on v1

--- a/solution.py
+++ b/solution.py
@@ -22,7 +22,7 @@
     return landed.astype(jnp.bfloat16).reshape(page_shape)
 
 
-def hand_pages(kv_pages, page_target):
+def hand_pages(kv_pages, page_target, earlier):
     page_count = kv_pages.shape[0]
     owners = lax.axis_size("expert")
     target_dev = page_target // page_count
@@ -38,7 +38,7 @@
     ).astype(jnp.bfloat16)
     labels = jnp.sum(jnp.where(placing, target_slot[:, None] + 1, 0), axis=0) - 1
     arrived, arrived_labels = (
-        lax.all_to_all(outgoing, "expert", split_axis=0, concat_axis=0, tiled=True),
+        lax.all_to_all(after(outgoing, earlier), "expert", split_axis=0, concat_axis=0, tiled=True),
         lax.all_to_all(
             labels.astype(jnp.bfloat16), "expert", split_axis=0, concat_axis=0, tiled=True
         ),
@@ -53,6 +53,10 @@
     else:
         pairs = [(i, (i + step) % count) for i in range(count)]
     return lax.ppermute(x, "expert", pairs)
+
+
+def after(x, *earlier):
+    return lax.optimization_barrier((x, *earlier))[0]
 
 
 def mixing_table(route_ids, route_gates, experts):
@@ -76,6 +80,16 @@
     return placing, blend
 
 
+def apply(held, gate_weight, up_weight, down_weight):
+    pieces = [piece for arrived in held for piece in arrived]
+    rows = jnp.concatenate(pieces, axis=0)
+    gate = jnp.dot(rows, gate_weight, preferred_element_type=jnp.float32)
+    up = jnp.dot(rows, up_weight, preferred_element_type=jnp.float32)
+    hidden = lax.optimization_barrier((jax.nn.silu(gate) * up).astype(jnp.bfloat16))
+    out = jnp.dot(hidden, down_weight, preferred_element_type=jnp.float32)
+    return jnp.split(out.astype(jnp.bfloat16), len(pieces), axis=0)
+
+
 def local(
     tokens, route_ids, route_gates, gate_weight, up_weight, down_weight, kv_pages, page_target
 ):
@@ -90,51 +104,60 @@
     near = (chip // PLANE) * PLANE + ((chip % PLANE) ^ jnp.arange(PLANE, dtype=jnp.int32))
     nearby = (jnp.arange(experts, dtype=jnp.int32)[:, None] == near[None, :]).astype(jnp.bfloat16)
 
-    blocks = [tokens]
-    for _ in range(1, planes):
-        blocks.append(send(blocks[-1], step=stride))
     table = mixing_table(route_ids, route_gates, experts)
-    tables = [table] + [send(table, step=stride * s) for s in range(1, planes)]
-
-    gate_all = jnp.concatenate([gate_weight, send(gate_weight, flip=1)], axis=1)
-    up_all = jnp.concatenate([up_weight, send(up_weight, flip=1)], axis=1)
-    down_all = jnp.concatenate([down_weight, send(down_weight, flip=1)], axis=0)
-
-    held, blends = [], []
+    lanes = jnp.pad(table, ((0, 0), (0, -experts % 128)))
+    block = jnp.concatenate([tokens, lanes], axis=1)
+    weights = (gate_weight, up_weight, down_weight)
+    group = 2
+    swapped, blends, got, outs = [], [], [], []
     for s in range(planes):
-        placing, blend = plane_slots(tables[s], nearby, capacity)
+        placing, blend = plane_slots(block[:, width : width + experts], nearby, capacity)
         blends.append(blend.reshape(tok_rows, PLANE * capacity))
+        if s < 3:
+            swapped.append(send(after(weights[s], *swapped), flip=1))
+        arrived = []
         for j in range(PLANE):
             picked = lax.dot_general(
                 placing[:, j],
-                blocks[s],
+                block[:, :width],
                 (((0,), (0,)), ((), ())),
                 preferred_element_type=jnp.float32,
             ).astype(jnp.bfloat16)
-            held.append(send(picked, flip=2 * j) if j else picked)
+            if j:
+                if s:
+                    picked = after(picked, got[s - 1][j])
+                picked = send(picked, flip=2 * j)
+            arrived.append(picked)
+        if s + 1 < planes:
+            block = send(block, step=stride)
+        got.append(arrived)
+    gate_all = jnp.concatenate([gate_weight, swapped[0]], axis=1)
+    up_all = jnp.concatenate([up_weight, swapped[1]], axis=1)
+    down_all = jnp.concatenate([down_weight, swapped[2]], axis=0)
+    for first in range(0, planes, group):
+        held = got[first : first + group]
+        if outs:
+            held[0][0] = after(held[0][0], *outs)
+        outs.extend(apply(held, gate_all, up_all, down_all))
 
-    outs = []
-    group = 2
-    for first in range(0, planes, group):
-        rows = jnp.concatenate(held[first * PLANE : (first + group) * PLANE], axis=0)
-        gate = jnp.dot(rows, gate_all, preferred_element_type=jnp.float32)
-        up = jnp.dot(rows, up_all, preferred_element_type=jnp.float32)
-        hidden = (jax.nn.silu(gate) * up).astype(jnp.bfloat16)
-        out = jnp.dot(hidden, down_all, preferred_element_type=jnp.float32).astype(jnp.bfloat16)
-        outs.extend(jnp.split(out, group * PLANE, axis=0))
-
-    def returned(s):
+    order = list(range(1, planes)) + [0]
+    sent = {}
+    previous = None
+    for i, s in enumerate(order):
         mine = outs[s * PLANE : (s + 1) * PLANE]
-        back = [mine[0]] + [send(mine[j], flip=2 * j) for j in range(1, PLANE)]
-        return jnp.dot(
-            blends[s], jnp.concatenate(back, axis=0), preferred_element_type=jnp.float32
+        back = [mine[0]]
+        for j in range(1, PLANE):
+            back.append(send(after(mine[j], previous[j]) if previous else mine[j], flip=2 * j))
+        sent[s] = previous = back
+    handed = hand_pages(kv_pages, page_target, got[-2][1])
+    total = None
+    for s in order:
+        part = jnp.dot(
+            blends[s], jnp.concatenate(sent[s], axis=0), preferred_element_type=jnp.float32
         )
-
-    total = returned(1).astype(jnp.bfloat16)
-    for s in list(range(2, planes)) + [0]:
-        arrived = send(total, step=stride)
-        total = (returned(s) + arrived.astype(jnp.float32)).astype(jnp.bfloat16)
-    handed = hand_pages(kv_pages, page_target)
+        if total is not None:
+            part = part + send(total, step=stride).astype(jnp.float32)
+        total = part.astype(jnp.bfloat16)
     return (total, handed)
 
 

time: 252 us -> 192 us (0.76)
  waiting for transfers between devices: 112 us -> 66.9 us
  matrix products: 49.4 us -> 38 us
  starting transfers between devices: 54.5 us -> 47.3 us
  local copies, waits for them, and re-layouts: 28.3 us -> 31.4 us
    ppermute x36 -> x33, waiting for transfers between devices: 112 us -> 66.9 us  [send(): return lax.ppermute(x, 'expert', pairs)]
    dot_general x24 -> x26, matrix products: 46.1 us -> 34.7 us  [the longest x16 10.5 us: local(): lax.dot_general(placing[:, j], block[:, :width], (((0,), (0,)), ((), ()))...]
    ppermute x36 -> x33, starting transfers between devices: 44.7 us -> 37.6 us  [send(): return lax.ppermute(x, 'expert', pairs)]
    unnamed x47 -> x53, local copies, waits for them, and re-layouts: 17 us -> 19.8 us
  transfers between devices with their start and end apart: 38 -> 35, of which waited for: 18 -> 13; matrix products, arithmetic and copies ran while one was open for 31% -> 35% of each run, Pallas kernels for 0% -> 0%
where the time goes in v2:
time: 192 us; the launch traced here: 191 us
  waiting for transfers between devices  66.9 us (35%)
  starting transfers between devices  47.3 us (25%)
  matrix products  38 us (20%)
  local copies, waits for them, and re-layouts  31.4 us (16%)
  other arithmetic  5.92 us (3%)
    ppermute x33, waiting for transfers between devices, send(): return lax.ppermute(x, 'expert', pairs)  66.9 us
    ppermute x33, starting transfers between devices, send(): return lax.ppermute(x, 'expert', pairs)  37.6 us
    unnamed x53, local copies, waits for them, and re-layouts  19.8 us
    dot_general x16, matrix products, local(): lax.dot_general(placing[:, j], block[:, :width], (((0,), (0,)), ((), ()))...  10.5 us
    dot_general x2, matrix products, apply(): gate = jnp.dot(rows, gate_weight, preferred_element_type=jnp.float32)  7.32 us
    dot_general x4, matrix products, local(): jnp.dot(blends[s], jnp.concatenate(sent[s], axis=0), preferred_element_ty...  6.36 us
    dot_general x2, matrix products, apply(): out = jnp.dot(hidden, down_weight, preferred_element_type=jnp.float32)  6.13 us
    all_to_all x1, starting transfers between devices, hand_pages(): lax.all_to_all(labels.astype(jnp.bfloat16), 'expert', split_axis=0, conca...  4.95 us
  transfers between devices with their start and end apart: 35, of which 13 were waited for; matrix products, arithmetic and copies ran while one was open for 35% of the time, Pallas kernels for 0%

profile of v2, /device:TPU:0, one launch (start us, length us, event | category | flops | bytes accessed | tf_op | source)
XLA Modules:
  0.0 190.8 jit_solution(17252680936756836846)
XLA Ops:
  5.2 2.9 %collective-permute-start = (bf16[40,4096]{1,0:T(8,128)(2,1)}, bf16[40,4096]{1,0:T(8,128)(2,1)}, u32[]{:S(2)}, u32[]{:S(2)}) collective-permute-start(bf16[40,4096]{1,0:T(8,128)(2,1)} %convolution_convert_fusion.19), channel_id=1, source_target_pairs={{0,2},{1,3},{2,0},{3,1},{4,6},{5,7},{6,4},{7,5},{8,10},{9,11},{10,... | collective-permute-start | bytes 983048 | tf_op jit(solution)/shard_map/ppermute | solution.py:55
  16.4 4.9 %all-to-all-start = ((bf16[32,1,1]{2,1,0:T(2,128)(2,1)}), bf16[32,1,1]{2,1,0:T(2,128)(2,1)S(1)}, u32[]{:S(2)}, u32[]{:S(2)}) async-start(bf16[32,1,1]{2,1,0:T(2,128)(2,1)} %copy.35), calls=%async_computation | async-start | bytes 32768 | tf_op jit(solution)/shard_map/all_to_all | solution.py:42
  21.4 4.0 %constant_dynamic-update-slice_fusion.7 = bf16[4096,768]{1,0:T(8,128)(2,1)} fusion(bf16[4096,384]{1,0:T(8,128)(2,1)} %param.11), kind=kLoop, calls=%fused_computation.110 | loop fusion | bytes 6291456
  25.3 4.1 %constant_dynamic-update-slice_fusion.9 = bf16[4096,768]{1,0:T(8,128)(2,1)} fusion(bf16[4096,384]{1,0:T(8,128)(2,1)} %param.12), kind=kLoop, calls=%fused_computation.112 | loop fusion | bytes 6291456
  43.1 4.4 %collective-permute-done.4 = bf16[40,4096]{1,0:T(8,128)(2,1)S(1)} collective-permute-done((bf16[40,4096]{1,0:T(8,128)(2,1)S(1)}, bf16[40,4096]{1,0:T(8,128)(2,1)S(1)}, u32[]{:S(2)}, u32[]{:S(2)}) %collective-permute-start.4) | collective-permute-done | bytes 327712 | tf_op jit(solution)/shard_map/ppermute | solution.py:55
  47.7 7.9 %collective-permute-done.5 = bf16[40,4096]{1,0:T(8,128)(2,1)S(1)} collective-permute-done((bf16[40,4096]{1,0:T(8,128)(2,1)S(1)}, bf16[40,4096]{1,0:T(8,128)(2,1)S(1)}, u32[]{:S(2)}, u32[]{:S(2)}) %collective-permute-start.5) | collective-permute-done | bytes 327712 | tf_op jit(solution)/shard_map/ppermute | solution.py:55
  63.5 3.6 %collective-permute-done.11 = bf16[40,4096]{1,0:T(8,128)(2,1)S(1)} collective-permute-done((bf16[40,4096]{1,0:T(8,128)(2,1)S(1)}, bf16[40,4096]{1,0:T(8,128)(2,1)S(1)}, u32[]{:S(2)}, u32[]{:S(2)}) %collective-permute-start.11) | collective-permute-done | bytes 327712 | tf_op jit(solution)/shard_map/ppermute | solution.py:55
  69.7 2.6 %reshape.82 = bf16[32,2,8192]{2,1,0:T(2,128)(2,1)} reshape(bf16[32,16384]{1,0:T(8,128)(2,1)} %reduce.2) | data formatting | bytes 2097152
  78.5 4.2 %constant_dynamic-update-slice_fusion.6 = bf16[4096,768]{1,0:T(8,128)(2,1)} fusion(bf16[4096,768]{1,0:T(8,128)(2,1)} %constant_dynamic-update-slice_fusion.7, bf16[4096,384]{1,0:T(8,128)(2,1)} %collective-permute-done.7), kind=kLoop, calls=%fused_computation.109 | loop fusion | bytes 6291456 | tf_op jit(solution)/shard_map/concatenate | solution.py:134
  82.7 5.1 %fusion.88 = f32[320,768]{1,0:T(8,128)S(1)} fusion(bf16[320,4096]{1,0:T(8,128)(2,1)S(1)} %copy-done.7, bf16[4096,768]{1,0:T(8,128)(2,1)} %constant_dynamic-update-slice_fusion.6), kind=kOutput, calls=%fused_computation.184 | convolution fusion | flops 2013265920 | bytes 9895936 | tf_op jit(solution)/shard_map/dot_general | solution.py:86
  87.9 2.7 %constant_dynamic-update-slice_fusion.8 = bf16[4096,768]{1,0:T(8,128)(2,1)S(1)} fusion(bf16[4096,768]{1,0:T(8,128)(2,1)S(1)} %bitcast.138, bf16[4096,384]{1,0:T(8,128)(2,1)} %collective-permute-done.8), kind=kLoop, calls=%fused_computation.111 | loop fusion | bytes 6291456 | tf_op jit(solution)/shard_map/concatenate | solution.py:135
  103.8 2.2 %multiply_convert_fusion = bf16[320,768]{1,0:T(8,128)(2,1)S(1)} fusion(f32[320,768]{1,0:T(8,128)S(1)} %fusion.89, bf16[320,4096]{1,0:T(8,128)(2,1)S(1)} %constant_dynamic-update-slice_fusion.12, bf16[4096,768]{1,0:T(8,128)(2,1)S(1)} %constant_dynamic-update-slice_fusion.8), kind=kOutput, calls=%fused_computation.62 | convolution fusion | flops 2014740480 | bytes 10387456 | tf_op jit(solution)/shard_map/dot_general | solution.py:87
  106.1 3.9 %convolution_convert_fusion.2 = bf16[320,4096]{1,0:T(8,128)(2,1)} fusion(bf16[320,768]{1,0:T(8,128)(2,1)S(1)} %multiply_convert_fusion, bf16[768,4096]{1,0:T(8,128)(2,1)S(1)} %constant_dynamic-update-slice_fusion.10), kind=kOutput, calls=%fused_computation.2 | convolution fusion | flops 2014576640 | bytes 9404416 | tf_op jit(solution)/shard_map/dot_general | solution.py:89
  110.0 4.4 %collective-permute-done.22 = bf16[40,4096]{1,0:T(8,128)(2,1)S(1)} collective-permute-done((bf16[40,4096]{1,0:T(8,128)(2,1)S(1)}, bf16[40,4096]{1,0:T(8,128)(2,1)S(1)}, u32[]{:S(2)}, u32[]{:S(2)}) %collective-permute-start.22) | collective-permute-done | bytes 327712 | tf_op jit(solution)/shard_map/ppermute | solution.py:55
  115.7 4.8 %all-to-all-start.1 = ((bf16[32,2,8192]{2,1,0:T(2,128)(2,1)}), bf16[32,2,8192]{2,1,0:T(2,128)(2,1)S(1)}, u32[]{:S(2)}, u32[]{:S(2)}) async-start(bf16[32,2,8192]{2,1,0:T(2,128)(2,1)} %reshape.82), calls=%async_computation.1 | async-start | bytes 2097152 | tf_op jit(solution)/shard_map/all_to_all | solution.py:41
  126.0 11.3 %collective-permute-done.19 = bf16[40,4096]{1,0:T(8,128)(2,1)S(1)} collective-permute-done((bf16[40,4096]{1,0:T(8,128)(2,1)S(1)}, bf16[40,4096]{1,0:T(8,128)(2,1)S(1)}, u32[]{:S(2)}, u32[]{:S(2)}) %collective-permute-start.19) | collective-permute-done | bytes 327712 | tf_op jit(solution)/shard_map/ppermute | solution.py:55
  137.2 3.5 %collective-permute-done.23 = bf16[40,4096]{1,0:T(8,128)(2,1)S(1)} collective-permute-done((bf16[40,4096]{1,0:T(8,128)(2,1)S(1)}, bf16[40,4096]{1,0:T(8,128)(2,1)S(1)}, u32[]{:S(2)}, u32[]{:S(2)}) %collective-permute-start.23) | collective-permute-done | bytes 327712 | tf_op jit(solution)/shard_map/ppermute | solution.py:55
  140.7 10.2 %collective-permute-done.27 = bf16[40,4096]{1,0:T(8,128)(2,1)S(1)} collective-permute-done((bf16[40,4096]{1,0:T(8,128)(2,1)S(1)}, bf16[40,4096]{1,0:T(8,128)(2,1)S(1)}, u32[]{:S(2)}, u32[]{:S(2)}) %collective-permute-start.27) | collective-permute-done | bytes 327712 | tf_op jit(solution)/shard_map/ppermute | solution.py:55
  156.0 7.2 %collective-permute-done.20 = bf16[40,4096]{1,0:T(8,128)(2,1)S(1)} collective-permute-done((bf16[40,4096]{1,0:T(8,128)(2,1)S(1)}, bf16[40,4096]{1,0:T(8,128)(2,1)S(1)}, u32[]{:S(2)}, u32[]{:S(2)}) %collective-permute-start.20) | collective-permute-done | bytes 327712 | tf_op jit(solution)/shard_map/ppermute | solution.py:55
  163.1 5.4 %collective-permute-done.24 = bf16[40,4096]{1,0:T(8,128)(2,1)S(1)} collective-permute-done((bf16[40,4096]{1,0:T(8,128)(2,1)S(1)}, bf16[40,4096]{1,0:T(8,128)(2,1)S(1)}, u32[]{:S(2)}, u32[]{:S(2)}) %collective-permute-start.24) | collective-permute-done | bytes 327712 | tf_op jit(solution)/shard_map/ppermute | solution.py:55
  169.7 3.1 %collective-permute-start.32 = (bf16[64,4096]{1,0:T(8,128)(2,1)}, bf16[64,4096]{1,0:T(8,128)(2,1)}, u32[]{:S(2)}, u32[]{:S(2)}) collective-permute-start(bf16[64,4096]{1,0:T(8,128)(2,1)} %fusion.1), channel_id=1, source_target_pairs={{0,8},{1,9},{2,10},{3,11},{4,12},{5,13},{6,14},{7,15},{8,16},{9,17... | collective-permute-start | bytes 1572872 | tf_op jit(solution)/shard_map/ppermute | solution.py:55
  180.7 2.3 %collective-permute-done.21 = bf16[40,4096]{1,0:T(8,128)(2,1)} collective-permute-done((bf16[40,4096]{1,0:T(8,128)(2,1)}, bf16[40,4096]{1,0:T(8,128)(2,1)}, u32[]{:S(2)}, u32[]{:S(2)}) %collective-permute-start.21) | collective-permute-done | bytes 327712 | tf_op jit(solution)/shard_map/ppermute | solution.py:55
  183.0 5.3 %collective-permute-done.25 = bf16[40,4096]{1,0:T(8,128)(2,1)} collective-permute-done((bf16[40,4096]{1,0:T(8,128)(2,1)}, bf16[40,4096]{1,0:T(8,128)(2,1)}, u32[]{:S(2)}, u32[]{:S(2)}) %collective-permute-start.25) | collective-permute-done | bytes 327712 | tf_op jit(solution)/shard_map/ppermute | solution.py:55
  188.3 2.5 %fusion = bf16[64,4096]{1,0:T(8,128)(2,1)} fusion(bf16[64,160]{0,1:T(8,128)(2,1)S(1)} %get-tuple-element.65, bf16[40,4096]{1,0:T(8,128)(2,1)} %collective-permute-done.29, bf16[40,4096]{1,0:T(8,128)(2,1)} %collective-permute-done.25, bf16[40,4096]{1,0:T(8,128)(2,1)} %collective-permute-done.21, bf16[40,4096]{1,0:T(8,128)(2,1)S(1)} %get-tuple-element.61, ...), kind=kOutput, calls=%fused_computation.7 | convolution fusion | flops 89915392 | bytes 2379776 | tf_op jit(solution)/shard_map/dot_general | solution.py:155
  (168 shorter events, 76.9 us)
Async XLA Ops:
  5.2 28.5 %collective-permute-start = (bf16[40,4096]{1,0:T(8,128)(2,1)}, bf16[40,4096]{1,0:T(8,128)(2,1)}, u32[]{:S(2)}, u32[]{:S(2)}) collective-permute-start(bf16[40,4096]{1,0:T(8,128)(2,1)} %convolution_convert_fusion.19), channel_id=1, source_target_pairs={{0,2},{1,3},{2,0},{3,1},{4,6},{5,7},{6,4},{7,5},{8,10},{9,11},{10,... | collective-permute-start | bytes 983048 | tf_op jit(solution)/shard_map/ppermute | solution.py:55
  10.2 25.1 %collective-permute-start.1 = (bf16[40,4096]{1,0:T(8,128)(2,1)}, bf16[40,4096]{1,0:T(8,128)(2,1)}, u32[]{:S(2)}, u32[]{:S(2)}) collective-permute-start(bf16[40,4096]{1,0:T(8,128)(2,1)} %convolution_convert_fusion.18), channel_id=1, source_target_pairs={{0,4},{1,5},{2,6},{3,7},{4,0},{5,1},{6,2},{7,3},{8,12},{9,13},{10,... | collective-permute-start | bytes 983048 | tf_op jit(solution)/shard_map/ppermute | solution.py:55
  12.9 23.3 %collective-permute-start.2 = (bf16[40,4096]{1,0:T(8,128)(2,1)S(1)}, bf16[40,4096]{1,0:T(8,128)(2,1)S(1)}, u32[]{:S(2)}, u32[]{:S(2)}) collective-permute-start(bf16[40,4096]{1,0:T(8,128)(2,1)S(1)} %convolution_convert_fusion.17), channel_id=1, source_target_pairs={{0,6},{1,7},{2,4},{3,5},{4,2},{5,3},{6,0},{7,1},{8,14},{9,15},{10,... | collective-permute-start | bytes 983048 | tf_op jit(solution)/shard_map/ppermute | solution.py:55
  13.2 23.1 %collective-permute-start.3 = (bf16[64,4224]{1,0:T(8,128)(2,1)S(1)}, bf16[64,4224]{1,0:T(8,128)(2,1)S(1)}, u32[]{:S(2)}, u32[]{:S(2)}) collective-permute-start(bf16[64,4224]{1,0:T(8,128)(2,1)S(1)} %fusion.37), channel_id=1, source_target_pairs={{0,8},{1,9},{2,10},{3,11},{4,12},{5,13},{6,14},{7,15},{8,16},{9,17... | collective-permute-start | bytes 1622024 | tf_op jit(solution)/shard_map/ppermute | solution.py:55
  15.3 32.3 %collective-permute-start.7 = (bf16[4096,384]{1,0:T(8,128)(2,1)}, bf16[4096,384]{1,0:T(8,128)(2,1)}, u32[]{:S(2)}, u32[]{:S(2)}) collective-permute-start(bf16[4096,384]{1,0:T(8,128)(2,1)} %param.11), channel_id=1, source_target_pairs={{0,1},{1,0},{2,3},{3,2},{4,5},{5,4},{6,7},{7,6},{8,9},{9,8},{10,11... | collective-permute-start | bytes 9437192 | tf_op jit(solution)/shard_map/ppermute | solution.py:55
  16.4 99.3 %all-to-all-start = ((bf16[32,1,1]{2,1,0:T(2,128)(2,1)}), bf16[32,1,1]{2,1,0:T(2,128)(2,1)S(1)}, u32[]{:S(2)}, u32[]{:S(2)}) async-start(bf16[32,1,1]{2,1,0:T(2,128)(2,1)} %copy.35), calls=%async_computation | async-start | bytes 32768 | tf_op jit(solution)/shard_map/all_to_all | solution.py:42
  39.0 16.6 %collective-permute-start.5 = (bf16[40,4096]{1,0:T(8,128)(2,1)S(1)}, bf16[40,4096]{1,0:T(8,128)(2,1)S(1)}, u32[]{:S(2)}, u32[]{:S(2)}) collective-permute-start(bf16[40,4096]{1,0:T(8,128)(2,1)S(1)} %convolution_convert_fusion.14), channel_id=1, source_target_pairs={{0,4},{1,5},{2,6},{3,7},{4,0},{5,1},{6,2},{7,3},{8,12},{9,13},{10,... | collective-permute-start | bytes 983048 | tf_op jit(solution)/shard_map/ppermute | solution.py:55
  40.8 14.8 %collective-permute-start.6 = (bf16[40,4096]{1,0:T(8,128)(2,1)S(1)}, bf16[40,4096]{1,0:T(8,128)(2,1)S(1)}, u32[]{:S(2)}, u32[]{:S(2)}) collective-permute-start(bf16[40,4096]{1,0:T(8,128)(2,1)S(1)} %convolution_convert_fusion.13), channel_id=1, source_target_pairs={{0,6},{1,7},{2,4},{3,5},{4,2},{5,3},{6,0},{7,1},{8,14},{9,15},{10,... | collective-permute-start | bytes 983048 | tf_op jit(solution)/shard_map/ppermute | solution.py:55
  41.1 15.4 %collective-permute-start.10 = (bf16[64,4224]{1,0:T(8,128)(2,1)S(1)}, bf16[64,4224]{1,0:T(8,128)(2,1)S(1)}, u32[]{:S(2)}, u32[]{:S(2)}) collective-permute-start(bf16[64,4224]{1,0:T(8,128)(2,1)S(1)} %collective-permute-done.3), channel_id=1, source_target_pairs={{0,8},{1,9},{2,10},{3,11},{4,12},{5,13},{6,14},{7,15},{8,16},{9,17... | collective-permute-start | bytes 1622024 | tf_op jit(solution)/shard_map/ppermute | solution.py:55
  47.6 25.7 %collective-permute-start.8 = (bf16[4096,384]{1,0:T(8,128)(2,1)}, bf16[4096,384]{1,0:T(8,128)(2,1)}, u32[]{:S(2)}, u32[]{:S(2)}) collective-permute-start(bf16[4096,384]{1,0:T(8,128)(2,1)} %param.12), channel_id=1, source_target_pairs={{0,1},{1,0},{2,3},{3,2},{4,5},{5,4},{6,7},{7,6},{8,9},{9,8},{10,11... | collective-permute-start | bytes 9437192 | tf_op jit(solution)/shard_map/ppermute | solution.py:55
  59.8 15.9 %collective-permute-start.12 = (bf16[40,4096]{1,0:T(8,128)(2,1)}, bf16[40,4096]{1,0:T(8,128)(2,1)S(1)}, u32[]{:S(2)}, u32[]{:S(2)}) collective-permute-start(bf16[40,4096]{1,0:T(8,128)(2,1)} %convolution_convert_fusion.10), channel_id=1, source_target_pairs={{0,4},{1,5},{2,6},{3,7},{4,0},{5,1},{6,2},{7,3},{8,12},{9,13},{10,... | collective-permute-start | bytes 983048 | tf_op jit(solution)/shard_map/ppermute | solution.py:55
  62.2 15.1 %collective-permute-start.13 = (bf16[40,4096]{1,0:T(8,128)(2,1)}, bf16[40,4096]{1,0:T(8,128)(2,1)}, u32[]{:S(2)}, u32[]{:S(2)}) collective-permute-start(bf16[40,4096]{1,0:T(8,128)(2,1)} %convolution_convert_fusion.9), channel_id=1, source_target_pairs={{0,6},{1,7},{2,4},{3,5},{4,2},{5,3},{6,0},{7,1},{8,14},{9,15},{10,... | collective-permute-start | bytes 983048 | tf_op jit(solution)/shard_map/ppermute | solution.py:55
  73.3 19.5 %collective-permute-start.9 = (bf16[384,4096]{1,0:T(8,128)(2,1)}, bf16[384,4096]{1,0:T(8,128)(2,1)S(1)}, u32[]{:S(2)}, u32[]{:S(2)}) collective-permute-start(bf16[384,4096]{1,0:T(8,128)(2,1)} %param.13), channel_id=1, source_target_pairs={{0,1},{1,0},{2,3},{3,2},{4,5},{5,4},{6,7},{7,6},{8,9},{9,8},{10,11... | collective-permute-start | bytes 9437192 | tf_op jit(solution)/shard_map/ppermute | solution.py:55
  73.6 27.5 %collective-permute-start.15 = (bf16[40,4096]{1,0:T(8,128)(2,1)S(1)}, bf16[40,4096]{1,0:T(8,128)(2,1)S(1)}, u32[]{:S(2)}, u32[]{:S(2)}) collective-permute-start(bf16[40,4096]{1,0:T(8,128)(2,1)S(1)} %convolution_convert_fusion.7), channel_id=1, source_target_pairs={{0,2},{1,3},{2,0},{3,1},{4,6},{5,7},{6,4},{7,5},{8,10},{9,11},{10,... | collective-permute-start | bytes 983048 | tf_op jit(solution)/shard_map/ppermute | solution.py:55
  75.7 25.8 %collective-permute-start.16 = (bf16[40,4096]{1,0:T(8,128)(2,1)S(1)}, bf16[40,4096]{1,0:T(8,128)(2,1)S(1)}, u32[]{:S(2)}, u32[]{:S(2)}) collective-permute-start(bf16[40,4096]{1,0:T(8,128)(2,1)S(1)} %convolution_convert_fusion.6), channel_id=1, source_target_pairs={{0,4},{1,5},{2,6},{3,7},{4,0},{5,1},{6,2},{7,3},{8,12},{9,13},{10,... | collective-permute-start | bytes 983048 | tf_op jit(solution)/shard_map/ppermute | solution.py:55
  77.4 24.1 %collective-permute-start.17 = (bf16[40,4096]{1,0:T(8,128)(2,1)S(1)}, bf16[40,4096]{1,0:T(8,128)(2,1)S(1)}, u32[]{:S(2)}, u32[]{:S(2)}) collective-permute-start(bf16[40,4096]{1,0:T(8,128)(2,1)S(1)} %convolution_convert_fusion.5), channel_id=1, source_target_pairs={{0,6},{1,7},{2,4},{3,5},{4,2},{5,3},{6,0},{7,1},{8,14},{9,15},{10,... | collective-permute-start | bytes 983048 | tf_op jit(solution)/shard_map/ppermute | solution.py:55
  98.3 16.0 %collective-permute-start.22 = (bf16[40,4096]{1,0:T(8,128)(2,1)S(1)}, bf16[40,4096]{1,0:T(8,128)(2,1)S(1)}, u32[]{:S(2)}, u32[]{:S(2)}) collective-permute-start(bf16[40,4096]{1,0:T(8,128)(2,1)S(1)} %get-tuple-element.55), channel_id=1, source_target_pairs={{0,4},{1,5},{2,6},{3,7},{4,0},{5,1},{6,2},{7,3},{8,12},{9,13},{10,... | collective-permute-start | bytes 983048 | tf_op jit(solution)/shard_map/ppermute | solution.py:55
  115.6 35.3 %collective-permute-start.30 = (bf16[64,4096]{1,0:T(8,128)(2,1)}, bf16[64,4096]{1,0:T(8,128)(2,1)}, u32[]{:S(2)}, u32[]{:S(2)}) collective-permute-start(bf16[64,4096]{1,0:T(8,128)(2,1)} %convolution_convert_fusion.4), channel_id=1, source_target_pairs={{0,8},{1,9},{2,10},{3,11},{4,12},{5,13},{6,14},{7,15},{8,16},{9,17... | collective-permute-start | bytes 1572872 | tf_op jit(solution)/shard_map/ppermute | solution.py:55
  115.7 60.9 %all-to-all-start.1 = ((bf16[32,2,8192]{2,1,0:T(2,128)(2,1)}), bf16[32,2,8192]{2,1,0:T(2,128)(2,1)S(1)}, u32[]{:S(2)}, u32[]{:S(2)}) async-start(bf16[32,2,8192]{2,1,0:T(2,128)(2,1)} %reshape.82), calls=%async_computation.1 | async-start | bytes 2097152 | tf_op jit(solution)/shard_map/all_to_all | solution.py:41
  124.3 16.5 %collective-permute-start.23 = (bf16[40,4096]{1,0:T(8,128)(2,1)S(1)}, bf16[40,4096]{1,0:T(8,128)(2,1)S(1)}, u32[]{:S(2)}, u32[]{:S(2)}) collective-permute-start(bf16[40,4096]{1,0:T(8,128)(2,1)S(1)} %get-tuple-element.39), channel_id=1, source_target_pairs={{0,4},{1,5},{2,6},{3,7},{4,0},{5,1},{6,2},{7,3},{8,12},{9,13},{10,... | collective-permute-start | bytes 983048 | tf_op jit(solution)/shard_map/ppermute | solution.py:55
  125.7 25.2 %collective-permute-start.27 = (bf16[40,4096]{1,0:T(8,128)(2,1)S(1)}, bf16[40,4096]{1,0:T(8,128)(2,1)S(1)}, u32[]{:S(2)}, u32[]{:S(2)}) collective-permute-start(bf16[40,4096]{1,0:T(8,128)(2,1)S(1)} %get-tuple-element.42), channel_id=1, source_target_pairs={{0,6},{1,7},{2,4},{3,5},{4,2},{5,3},{6,0},{7,1},{8,14},{9,15},{10,... | collective-permute-start | bytes 983048 | tf_op jit(solution)/shard_map/ppermute | solution.py:55
  152.3 16.1 %collective-permute-start.31 = (bf16[64,4096]{1,0:T(8,128)(2,1)S(1)}, bf16[64,4096]{1,0:T(8,128)(2,1)S(1)}, u32[]{:S(2)}, u32[]{:S(2)}) collective-permute-start(bf16[64,4096]{1,0:T(8,128)(2,1)S(1)} %fusion.2), channel_id=1, source_target_pairs={{0,8},{1,9},{2,10},{3,11},{4,12},{5,13},{6,14},{7,15},{8,16},{9,17... | collective-permute-start | bytes 1572872 | tf_op jit(solution)/shard_map/ppermute | solution.py:55
  153.1 15.4 %collective-permute-start.24 = (bf16[40,4096]{1,0:T(8,128)(2,1)S(1)}, bf16[40,4096]{1,0:T(8,128)(2,1)S(1)}, u32[]{:S(2)}, u32[]{:S(2)}) collective-permute-start(bf16[40,4096]{1,0:T(8,128)(2,1)S(1)} %get-tuple-element.40), channel_id=1, source_target_pairs={{0,4},{1,5},{2,6},{3,7},{4,0},{5,1},{6,2},{7,3},{8,12},{9,13},{10,... | collective-permute-start | bytes 983048 | tf_op jit(solution)/shard_map/ppermute | solution.py:55
  169.7 18.6 %collective-permute-start.32 = (bf16[64,4096]{1,0:T(8,128)(2,1)}, bf16[64,4096]{1,0:T(8,128)(2,1)}, u32[]{:S(2)}, u32[]{:S(2)}) collective-permute-start(bf16[64,4096]{1,0:T(8,128)(2,1)} %fusion.1), channel_id=1, source_target_pairs={{0,8},{1,9},{2,10},{3,11},{4,12},{5,13},{6,14},{7,15},{8,16},{9,17... | collective-permute-start | bytes 1572872 | tf_op jit(solution)/shard_map/ppermute | solution.py:55
  (28 other events, 318.7 us)

commit v3 on v2

--- a/solution.py
+++ b/solution.py
@@ -1,6 +1,10 @@
+import functools
+
 import jax
 import jax.numpy as jnp
 from jax import lax
+from jax.experimental import pallas as pl
+from jax.experimental.pallas import tpu as pltpu
 from jax.sharding import PartitionSpec as P
 
 PCAP = 1
@@ -66,28 +70,177 @@
     return jnp.sum(jnp.where(hits, mixing[:, :, None], 0.0), axis=1).astype(jnp.bfloat16)
 
 
-def plane_slots(table, nearby, capacity):
-    rows = table.shape[0]
-    weight = jnp.dot(table, nearby, preferred_element_type=jnp.float32)
+def spread(experts, capacity, chip):
+    lane = lax.broadcasted_iota(jnp.int32, (experts, PLANE * capacity), 1)
+    near = sum((lane >= capacity * j).astype(jnp.int32) for j in range(1, PLANE))
+    near = (chip // PLANE) * PLANE + ((chip % PLANE) ^ near)
+    expert = lax.broadcasted_iota(jnp.int32, (experts, PLANE * capacity), 0)
+    return (expert == near).astype(jnp.float32).astype(jnp.bfloat16)
+
+
+def slots_of(table, capacity, chip):
+    rows, experts = table.shape
+    weight = jnp.dot(table, spread(experts, capacity, chip), preferred_element_type=jnp.float32)
     named = weight > 0
-    below = jnp.arange(rows)[:, None] > jnp.arange(rows)[None, :]
+    row = lax.broadcasted_iota(jnp.int32, (rows, rows), 0)
+    below = (row > lax.broadcasted_iota(jnp.int32, (rows, rows), 1)).astype(jnp.float32)
     rank = jnp.dot(
-        below.astype(jnp.bfloat16), named.astype(jnp.bfloat16), preferred_element_type=jnp.float32
-    )
-    hits = (rank[:, :, None] == jnp.arange(capacity, dtype=jnp.float32)) & named[:, :, None]
-    placing = hits.astype(jnp.bfloat16)
-    blend = jnp.where(hits, weight[:, :, None], 0.0).astype(jnp.bfloat16)
+        below.astype(jnp.bfloat16),
+        named.astype(jnp.float32).astype(jnp.bfloat16),
+        preferred_element_type=jnp.float32,
+    )
+    lane = lax.broadcasted_iota(jnp.int32, (rows, PLANE * capacity), 1)
+    slot = lane - capacity * sum((lane >= capacity * j).astype(jnp.int32) for j in range(1, PLANE))
+    hits = (rank == slot.astype(jnp.float32)) & named
+    placing = jnp.where(hits, 1.0, 0.0).astype(jnp.bfloat16)
+    blend = jnp.where(hits, weight, 0.0).astype(jnp.bfloat16)
     return placing, blend
 
 
-def apply(held, gate_weight, up_weight, down_weight):
+def pick(placing, rows):
+    return lax.dot_general(
+        placing, rows, (((0,), (0,)), ((), ())), preferred_element_type=jnp.float32
+    )
+
+
+def pick_kernel(experts, capacity, step, chip_ref, block_ref, *outs):
+    width = outs[0].shape[1]
+    blend_ref = outs[PLANE]
+    placing, blend = slots_of(block_ref[:, width : width + experts], capacity, chip_ref[0])
+    blend_ref[...] = blend
+    for at in range(0, width, step):
+        found = pick(placing, block_ref[:, at : at + step])
+        for j in range(PLANE):
+            outs[j][:, at : at + step] = found[capacity * j : capacity * (j + 1)].astype(
+                jnp.bfloat16
+            )
+
+
+def first_kernel(experts, capacity, step, chip_ref, tokens_ref, ids_ref, gates_ref, *outs):
+    rows, width = tokens_ref.shape
+    block_ref = outs[PLANE + 1]
+    gates = gates_ref[...]
+    shares = gates / jnp.sum(gates, axis=1, keepdims=True)
+    mixing = shares.astype(jnp.bfloat16).astype(jnp.float32)
+    lane = lax.broadcasted_iota(jnp.int32, (rows, block_ref.shape[1] - width), 1)
+    table = jnp.zeros(lane.shape, jnp.float32)
+    for k in range(gates.shape[1]):
+        table = table + jnp.where(ids_ref[:, k : k + 1] == lane, mixing[:, k : k + 1], 0.0)
+    block_ref[:, width:] = table.astype(jnp.bfloat16)
+    block_ref[:, :width] = tokens_ref[...]
+    pick_kernel(experts, capacity, step, chip_ref, block_ref, *outs[: PLANE + 1])
+
+
+def pick_pieces(chip, block, width, experts, capacity, routing=None):
+    rows = block.shape[0]
+    piece = jax.ShapeDtypeStruct((capacity, width), jnp.bfloat16)
+    outs = [piece] * PLANE + [jax.ShapeDtypeStruct((rows, PLANE * capacity), jnp.bfloat16)]
+    if routing:
+        lanes = experts + -experts % 128
+        outs.append(jax.ShapeDtypeStruct((rows, width + lanes), jnp.bfloat16))
+    body = first_kernel if routing else pick_kernel
+    operands = (block, *routing) if routing else (block,)
+    return pl.pallas_call(
+        functools.partial(body, experts, capacity, 512),
+        out_shape=outs,
+        in_specs=[pl.BlockSpec(memory_space=pltpu.SMEM)]
+        + [pl.BlockSpec(memory_space=pltpu.VMEM)] * len(operands),
+        out_specs=[pl.BlockSpec(memory_space=pltpu.VMEM)] * len(outs),
+        compiler_params=pltpu.CompilerParams(vmem_limit_bytes=16 * 2**20),
+        cost_estimate=pl.CostEstimate(
+            flops=2 * rows * PLANE * capacity * width,
+            bytes_accessed=2 * width * (rows + PLANE * capacity),
+            transcendentals=0,
+        ),
+    )(jnp.reshape(chip, (1,)), *operands)
+
+
+def expert_kernel(pieces, steps, *refs):
+    rows_in, weights = refs[:pieces], refs[pieces : pieces + 6]
+    outs, hidden = refs[pieces + 6 : 2 * pieces + 6], refs[2 * pieces + 6]
+    sums = refs[2 * pieces + 7 :]
+    i = pl.program_id(0)
+    half = hidden.shape[1] // 2
+
+    @pl.when(i == 0)
+    def _():
+        for total in sums:
+            total[...] = jnp.zeros_like(total)
+
+    @pl.when(i < steps)
+    def _():
+        rows = jnp.concatenate([ref[...].astype(jnp.float32) for ref in rows_in], axis=0)
+        rows = rows.astype(jnp.bfloat16)
+        for total, weight in zip(sums, weights[:4]):
+            total[...] += jnp.dot(rows, weight[...], preferred_element_type=jnp.float32)
+
+    @pl.when(i == steps - 1)
+    def _():
+        for n in range(2):
+            gate = sums[n][...]
+            value = gate / (1.0 + jnp.exp(-gate)) * sums[2 + n][...]
+            hidden[:, n * half : (n + 1) * half] = value.astype(jnp.bfloat16)
+
+    @pl.when(i >= steps)
+    def _():
+        down = jnp.concatenate([weights[4][...], weights[5][...]], axis=0)
+        out = jnp.dot(hidden[...], down, preferred_element_type=jnp.float32)
+        each = out.shape[0] // pieces
+        for n in range(pieces):
+            outs[n][...] = out[n * each : (n + 1) * each].astype(jnp.bfloat16)
+
+
+def apply(held, gate, up, down):
+    pieces = [piece for arrived in held for piece in arrived]
+    each, width = pieces[0].shape
+    rows, half = each * len(pieces), gate[0].shape[1]
+    step = 1024
+    steps = width // step
+    read = lambda i: jnp.minimum(i, steps - 1)
+    write = lambda i: jnp.maximum(i - steps, 0)
+    piece_in = pl.BlockSpec((each, step), lambda i: (0, read(i)))
+    piece_out = pl.BlockSpec((each, step), lambda i: (0, write(i)))
+    wide = pl.BlockSpec((step, half), lambda i: (read(i), 0))
+    tall = pl.BlockSpec((half, step), lambda i: (0, write(i)))
+    return pl.pallas_call(
+        functools.partial(expert_kernel, len(pieces), steps),
+        grid=(2 * steps,),
+        out_shape=[jax.ShapeDtypeStruct((each, width), jnp.bfloat16)] * len(pieces),
+        in_specs=[piece_in] * len(pieces) + [wide] * 4 + [tall] * 2,
+        out_specs=[piece_out] * len(pieces),
+        scratch_shapes=[pltpu.VMEM((rows, 2 * half), jnp.bfloat16)]
+        + [pltpu.VMEM((rows, half), jnp.float32)] * 4,
+        compiler_params=pltpu.CompilerParams(
+            dimension_semantics=("arbitrary",), vmem_limit_bytes=60 * 2**20
+        ),
+        cost_estimate=pl.CostEstimate(
+            flops=12 * rows * width * half,
+            bytes_accessed=12 * width * half + 4 * rows * width,
+            transcendentals=2 * rows * half,
+        ),
+    )(*pieces, *gate, *up, *down)
+
+
+def apply_plain(held, gate, up, down):
     pieces = [piece for arrived in held for piece in arrived]
     rows = jnp.concatenate(pieces, axis=0)
-    gate = jnp.dot(rows, gate_weight, preferred_element_type=jnp.float32)
-    up = jnp.dot(rows, up_weight, preferred_element_type=jnp.float32)
-    hidden = lax.optimization_barrier((jax.nn.silu(gate) * up).astype(jnp.bfloat16))
-    out = jnp.dot(hidden, down_weight, preferred_element_type=jnp.float32)
-    return jnp.split(out.astype(jnp.bfloat16), len(pieces), axis=0)
+    total = 0.0
+    for n in range(2):
+        left = jnp.dot(rows, gate[n], preferred_element_type=jnp.float32)
+        right = jnp.dot(rows, up[n], preferred_element_type=jnp.float32)
+        hidden = (jax.nn.silu(left) * right).astype(jnp.bfloat16)
+        total = total + jnp.dot(hidden, down[n], preferred_element_type=jnp.float32)
+    return jnp.split(total.astype(jnp.bfloat16), len(pieces), axis=0)
+
+
+def pick_plain(chip, block, width, experts, capacity, routing=None):
+    if routing:
+        lanes = jnp.pad(mixing_table(*routing, experts), ((0, 0), (0, -experts % 128)))
+        block = jnp.concatenate([block, lanes], axis=1)
+    placing, blend = slots_of(block[:, width : width + experts], capacity, chip)
+    found = pick(placing, block[:, :width]).astype(jnp.bfloat16)
+    outs = jnp.split(found, PLANE, axis=0) + [blend]
+    return outs + [block] if routing else outs
 
 
 def local(
@@ -101,44 +254,36 @@
     stride = 2 * PLANE
     capacity = min(tok_rows, 5 * tok_rows * chosen // (4 * experts))
     chip = lax.axis_index("expert") // 2
-    near = (chip // PLANE) * PLANE + ((chip % PLANE) ^ jnp.arange(PLANE, dtype=jnp.int32))
-    nearby = (jnp.arange(experts, dtype=jnp.int32)[:, None] == near[None, :]).astype(jnp.bfloat16)
-
-    table = mixing_table(route_ids, route_gates, experts)
-    lanes = jnp.pad(table, ((0, 0), (0, -experts % 128)))
-    block = jnp.concatenate([tokens, lanes], axis=1)
+    whole = capacity % 8 == 0 and width % 1024 == 0
+    choose, work = (pick_pieces, apply) if whole else (pick_plain, apply_plain)
     weights = (gate_weight, up_weight, down_weight)
     group = 2
     swapped, blends, got, outs = [], [], [], []
+    block = tokens
     for s in range(planes):
-        placing, blend = plane_slots(block[:, width : width + experts], nearby, capacity)
-        blends.append(blend.reshape(tok_rows, PLANE * capacity))
+        if s:
+            *pieces, blend = choose(chip, block, width, experts, capacity)
+        else:
+            *pieces, blend, block = choose(
+                chip, tokens, width, experts, capacity, (route_ids, route_gates)
+            )
+        blends.append(blend)
         if s < 3:
-            swapped.append(send(after(weights[s], *swapped), flip=1))
-        arrived = []
-        for j in range(PLANE):
-            picked = lax.dot_general(
-                placing[:, j],
-                block[:, :width],
-                (((0,), (0,)), ((), ())),
-                preferred_element_type=jnp.float32,
-            ).astype(jnp.bfloat16)
-            if j:
-                if s:
-                    picked = after(picked, got[s - 1][j])
-                picked = send(picked, flip=2 * j)
-            arrived.append(picked)
+            earlier = [block] + (got[s - 1][1:] if s else [])
+            swapped.append(send(after(weights[s], *swapped, *earlier), flip=1))
+        for j in range(1, PLANE):
+            piece = after(pieces[j], got[s - 1][j]) if s else pieces[j]
+            pieces[j] = send(piece, flip=2 * j)
+        got.append(pieces)
         if s + 1 < planes:
             block = send(block, step=stride)
-        got.append(arrived)
-    gate_all = jnp.concatenate([gate_weight, swapped[0]], axis=1)
-    up_all = jnp.concatenate([up_weight, swapped[1]], axis=1)
-    down_all = jnp.concatenate([down_weight, swapped[2]], axis=0)
+
+    pairs = [(own, other) for own, other in zip(weights, swapped)]
     for first in range(0, planes, group):
         held = got[first : first + group]
         if outs:
             held[0][0] = after(held[0][0], *outs)
-        outs.extend(apply(held, gate_all, up_all, down_all))
+        outs.extend(work(held, *pairs))
 
     order = list(range(1, planes)) + [0]
     sent = {}

time: 192 us -> 180 us (0.938)
  Pallas kernels: 0 us -> 34.2 us
  matrix products: 38 us -> 8.65 us
  local copies, waits for them, and re-layouts: 31.4 us -> 14.9 us
  waiting for transfers between devices: 66.9 us -> 70.3 us
  other arithmetic: 5.92 us -> 2.84 us
    pallas_call x0 -> x6, Pallas kernels: none -> 34.2 us  [the longest x2 30.8 us: apply(): pl.pallas_call(functools.partial(expert_kernel, len(pieces), steps), grid...]
    dot_general x30 -> x0, matrix products: 29.6 us -> none  [the longest x16 10.5 us: local(): lax.dot_general(placing[:, j], block[:, :width], (((0,), (0,)), ((), ()))...]
    concatenate x5 -> x0, local copies, waits for them, and re-layouts: 7.22 us -> none  [the longest x1 4.16 us: local(): gate_all = jnp.concatenate([gate_weight, swapped[0]], axis=1)]
    unnamed x53 -> x52, local copies, waits for them, and re-layouts: 19.8 us -> 13.7 us
    ppermute x33, waiting for transfers between devices: 66.9 us -> 70.3 us  [send(): return lax.ppermute(x, 'expert', pairs)]
    split x2 -> x0, local copies, waits for them, and re-layouts: 2.99 us -> none  [apply(): return jnp.split(out.astype(jnp.bfloat16), len(pieces), axis=0)]
  transfers between devices with their start and end apart: 35 -> 35, of which waited for: 13 -> 12; matrix products, arithmetic and copies ran while one was open for 35% -> 8% of each run, Pallas kernels for 0% -> 18%
where the time goes in v3:
time: 180 us
  waiting for transfers between devices  70.3 us (39%)
  starting transfers between devices  47.7 us (26%)
  Pallas kernels  34.2 us (19%)
  local copies, waits for them, and re-layouts  14.9 us (8%)
  matrix products  8.65 us (5%)
  other arithmetic  2.84 us (2%)
    ppermute x33, waiting for transfers between devices, send(): return lax.ppermute(x, 'expert', pairs)  70.3 us
    ppermute x33, starting transfers between devices, send(): return lax.ppermute(x, 'expert', pairs)  39.3 us
    pallas_call x2, Pallas kernels, apply(): pl.pallas_call(functools.partial(expert_kernel, len(pieces), steps), grid...  30.8 us
    unnamed x52, local copies, waits for them, and re-layouts  13.7 us
    dot_general x4, matrix products, local(): jnp.dot(blends[s], jnp.concatenate(sent[s], axis=0), preferred_element_ty...  6.67 us
    all_to_all x1, starting transfers between devices, hand_pages(): lax.all_to_all(after(outgoing, earlier), 'expert', split_axis=0, concat_a...  4.8 us
  transfers between devices with their start and end apart: 35, of which 12 were waited for; matrix products, arithmetic and copies ran while one was open for 8% of the time, Pallas kernels for 18%

profile of v3, /device:TPU:0, one launch (start us, length us, event | category | flops | bytes accessed | tf_op | source)
XLA Modules:
  0.0 179.6 jit_solution(9742694786040703932)
XLA Ops:
  5.5 2.6 %collective-permute-start.3 = (bf16[64,4224]{1,0:T(8,128)(2,1)S(1)}, bf16[64,4224]{1,0:T(8,128)(2,1)S(1)}, u32[]{:S(2)}, u32[]{:S(2)}) collective-permute-start(bf16[64,4224]{1,0:T(8,128)(2,1)S(1)} %get-tuple-element.67), channel_id=1, source_target_pairs={{0,8},{1,9},{2,10},{3,11},{4,12},{5,13},{6,14},{7,15},{8,16},{9,17... | collective-permute-start | bytes 1622024 | tf_op jit(solution)/shard_map/ppermute | solution.py:59
  11.5 7.1 %collective-permute-done.refs_1_ = bf16[40,4096]{1,0:T(8,128)(2,1)S(1)} collective-permute-done((bf16[40,4096]{1,0:T(8,128)(2,1)S(1)}, bf16[40,4096]{1,0:T(8,128)(2,1)S(1)}, u32[]{:S(2)}, u32[]{:S(2)}) %collective-permute-start) | collective-permute-done | bytes 327712 | tf_op jit(solution)/shard_map/ppermute | solution.py:59
  18.6 7.5 %collective-permute-done.1.refs_2_ = bf16[40,4096]{1,0:T(8,128)(2,1)S(1)} collective-permute-done((bf16[40,4096]{1,0:T(8,128)(2,1)S(1)}, bf16[40,4096]{1,0:T(8,128)(2,1)S(1)}, u32[]{:S(2)}, u32[]{:S(2)}) %collective-permute-start.1) | collective-permute-done | bytes 327712 | tf_op jit(solution)/shard_map/ppermute | solution.py:59
  34.5 7.2 %collective-permute-done.4.refs_5_ = bf16[40,4096]{1,0:T(8,128)(2,1)S(1)} collective-permute-done((bf16[40,4096]{1,0:T(8,128)(2,1)S(1)}, bf16[40,4096]{1,0:T(8,128)(2,1)S(1)}, u32[]{:S(2)}, u32[]{:S(2)}) %collective-permute-start.4) | collective-permute-done | bytes 327712 | tf_op jit(solution)/shard_map/ppermute | solution.py:59
  41.7 6.0 %collective-permute-done.5.refs_6_ = bf16[40,4096]{1,0:T(8,128)(2,1)S(1)} collective-permute-done((bf16[40,4096]{1,0:T(8,128)(2,1)S(1)}, bf16[40,4096]{1,0:T(8,128)(2,1)S(1)}, u32[]{:S(2)}, u32[]{:S(2)}) %collective-permute-start.5) | collective-permute-done | bytes 327712 | tf_op jit(solution)/shard_map/ppermute | solution.py:59
  57.0 15.4 %shard_map.97 = (bf16[40,4096]{1,0:T(8,128)(2,1)}, bf16[40,4096]{1,0:T(8,128)(2,1)}, bf16[40,4096]{1,0:T(8,128)(2,1)}, bf16[40,4096]{1,0:T(8,128)(2,1)}, bf16[40...) custom-call(bf16[40,4096]{1,0:T(8,128)(2,1)} %copy-done.2, ...), custom_call_target="tpu_custom_call" | custom-call | flops 6039797760 | bytes 24117248 | tf_op jit(solution)/shard_map/pallas_call | solution.py:205
  76.9 3.6 %all-to-all-start = ((bf16[32,1,1]{2,1,0:T(2,128)(2,1)}), bf16[32,1,1]{2,1,0:T(2,128)(2,1)S(1)}, u32[]{:S(2)}, u32[]{:S(2)}) async-start(bf16[32,1,1]{2,1,0:T(2,128)(2,1)} %copy.18), calls=%async_computation | async-start | bytes 32768 | tf_op jit(solution)/shard_map/all_to_all | solution.py:46
  82.6 1.8 collective-permute-start.15
  88.6 1.6 reshape.49
  90.4 1.6 convolution_convert_fusion.2
  92.0 1.7 collective-permute-start.30
  93.7 4.8 %all-to-all-start.1 = ((bf16[32,2,8192]{2,1,0:T(2,128)(2,1)}), bf16[32,2,8192]{2,1,0:T(2,128)(2,1)S(1)}, u32[]{:S(2)}, u32[]{:S(2)}) async-start(bf16[32,2,8192]{2,1,0:T(2,128)(2,1)} %reshape.49), calls=%async_computation.1 | async-start | bytes 2097152 | tf_op jit(solution)/shard_map/all_to_all | solution.py:45
  98.5 5.3 %collective-permute-done.17.refs_7_ = bf16[40,4096]{1,0:T(8,128)(2,1)} collective-permute-done((bf16[40,4096]{1,0:T(8,128)(2,1)S(1)}, bf16[40,4096]{1,0:T(8,128)(2,1)}, u32[]{:S(2)}, u32[]{:S(2)}) %collective-permute-start.17) | collective-permute-done | bytes 327712 | tf_op jit(solution)/shard_map/ppermute | solution.py:59
  103.8 15.4 %shard_map.100 = (bf16[40,4096]{1,0:T(8,128)(2,1)}, bf16[40,4096]{1,0:T(8,128)(2,1)}, bf16[40,4096]{1,0:T(8,128)(2,1)}, bf16[40,4096]{1,0:T(8,128)(2,1)}, bf16[4...) custom-call(bf16[40,4096]{1,0:T(8,128)(2,1)} %copy-done.1, ...), custom_call_target="tpu_custom_call" | custom-call | flops 6039797760 | bytes 24117248 | tf_op jit(solution)/shard_map/pallas_call | solution.py:205
  119.2 2.3 %collective-permute-start.27 = (bf16[40,4096]{1,0:T(8,128)(2,1)}, bf16[40,4096]{1,0:T(8,128)(2,1)S(1)}, u32[]{:S(2)}, u32[]{:S(2)}) collective-permute-start(bf16[40,4096]{1,0:T(8,128)(2,1)} %get-tuple-element.113), channel_id=1, source_target_pairs={{0,6},{1,7},{2,4},{3,5},{4,2},{5,3},{6,0},{7,1},{8,14},{9,15},{10,... | collective-permute-start | bytes 983048 | tf_op jit(solution)/shard_map/ppermute | solution.py:59
  122.8 10.5 %collective-permute-done.27 = bf16[40,4096]{1,0:T(8,128)(2,1)S(1)} collective-permute-done((bf16[40,4096]{1,0:T(8,128)(2,1)}, bf16[40,4096]{1,0:T(8,128)(2,1)S(1)}, u32[]{:S(2)}, u32[]{:S(2)}) %collective-permute-start.27) | collective-permute-done | bytes 327712 | tf_op jit(solution)/shard_map/ppermute | solution.py:59
  133.3 3.9 %collective-permute-done.23 = bf16[40,4096]{1,0:T(8,128)(2,1)S(1)} collective-permute-done((bf16[40,4096]{1,0:T(8,128)(2,1)}, bf16[40,4096]{1,0:T(8,128)(2,1)S(1)}, u32[]{:S(2)}, u32[]{:S(2)}) %collective-permute-start.23) | collective-permute-done | bytes 327712 | tf_op jit(solution)/shard_map/ppermute | solution.py:59
  138.7 2.2 %collective-permute-start.31 = (bf16[64,4096]{1,0:T(8,128)(2,1)S(1)}, bf16[64,4096]{1,0:T(8,128)(2,1)S(1)}, u32[]{:S(2)}, u32[]{:S(2)}) collective-permute-start(bf16[64,4096]{1,0:T(8,128)(2,1)S(1)} %fusion.2), channel_id=1, source_target_pairs={{0,8},{1,9},{2,10},{3,11},{4,12},{5,13},{6,14},{7,15},{8,16},{9,17... | collective-permute-start | bytes 1572872 | tf_op jit(solution)/shard_map/ppermute | solution.py:59
  142.4 1.9 %collective-permute-start.20 = (bf16[40,4096]{1,0:T(8,128)(2,1)S(1)}, bf16[40,4096]{1,0:T(8,128)(2,1)S(1)}, u32[]{:S(2)}, u32[]{:S(2)}) collective-permute-start(bf16[40,4096]{1,0:T(8,128)(2,1)S(1)} %copy-done.18), channel_id=1, source_target_pairs={{0,2},{1,3},{2,0},{3,1},{4,6},{5,7},{6,4},{7,5},{8,10},{9,11},{10,... | collective-permute-start | bytes 983048 | tf_op jit(solution)/shard_map/ppermute | solution.py:59
  144.3 8.0 %collective-permute-done.28 = bf16[40,4096]{1,0:T(8,128)(2,1)S(1)} collective-permute-done((bf16[40,4096]{1,0:T(8,128)(2,1)S(1)}, bf16[40,4096]{1,0:T(8,128)(2,1)S(1)}, u32[]{:S(2)}, u32[]{:S(2)}) %collective-permute-start.28) | collective-permute-done | bytes 327712 | tf_op jit(solution)/shard_map/ppermute | solution.py:59
  152.3 5.0 %collective-permute-done.24 = bf16[40,4096]{1,0:T(8,128)(2,1)S(1)} collective-permute-done((bf16[40,4096]{1,0:T(8,128)(2,1)S(1)}, bf16[40,4096]{1,0:T(8,128)(2,1)S(1)}, u32[]{:S(2)}, u32[]{:S(2)}) %collective-permute-start.24) | collective-permute-done | bytes 327712 | tf_op jit(solution)/shard_map/ppermute | solution.py:59
  167.5 4.0 %collective-permute-done.29 = bf16[40,4096]{1,0:T(8,128)(2,1)} collective-permute-done((bf16[40,4096]{1,0:T(8,128)(2,1)}, bf16[40,4096]{1,0:T(8,128)(2,1)}, u32[]{:S(2)}, u32[]{:S(2)}) %collective-permute-start.29) | collective-permute-done | bytes 327712 | tf_op jit(solution)/shard_map/ppermute | solution.py:59
  171.5 5.7 %collective-permute-done.25 = bf16[40,4096]{1,0:T(8,128)(2,1)} collective-permute-done((bf16[40,4096]{1,0:T(8,128)(2,1)}, bf16[40,4096]{1,0:T(8,128)(2,1)}, u32[]{:S(2)}, u32[]{:S(2)}) %collective-permute-start.25) | collective-permute-done | bytes 327712 | tf_op jit(solution)/shard_map/ppermute | solution.py:59
  177.1 2.5 %fusion = bf16[64,4096]{1,0:T(8,128)(2,1)} fusion(bf16[64,160]{1,0:T(8,128)(2,1)S(1)} %get-tuple-element.62, bf16[40,4096]{1,0:T(8,128)(2,1)} %collective-permute-done.29, bf16[40,4096]{1,0:T(8,128)(2,1)} %collective-permute-done.25, bf16[40,4096]{1,0:T(8,128)(2,1)} %collective-permute-done.21, bf16[40,4096]{1,0:T(8,128)(2,1)S(1)} %copy-done.21, ...), kind=kOutput, calls=%fused_computation.5 | convolution fusion | flops 89915392 | bytes 2379776 | tf_op jit(solution)/shard_map/dot_general | solution.py:300
  (121 shorter events, 51.3 us)
Async XLA Ops:
  5.0 21.1 %collective-permute-start.7 = (bf16[4096,384]{1,0:T(8,128)(2,1)}, bf16[4096,384]{1,0:T(8,128)(2,1)S(1)}, u32[]{:S(2)}, u32[]{:S(2)}) collective-permute-start(bf16[4096,384]{1,0:T(8,128)(2,1)} %refs_8_.3), channel_id=1, source_target_pairs={{0,1},{1,0},{2,3},{3,2},{4,5},{5,4},{6,7},{7,6},{8,9},{9,8},{10,11... | collective-permute-start | bytes 9437192 | tf_op jit(solution)/shard_map/ppermute | solution.py:59
  5.5 20.7 %collective-permute-start.3 = (bf16[64,4224]{1,0:T(8,128)(2,1)S(1)}, bf16[64,4224]{1,0:T(8,128)(2,1)S(1)}, u32[]{:S(2)}, u32[]{:S(2)}) collective-permute-start(bf16[64,4224]{1,0:T(8,128)(2,1)S(1)} %get-tuple-element.67), channel_id=1, source_target_pairs={{0,8},{1,9},{2,10},{3,11},{4,12},{5,13},{6,14},{7,15},{8,16},{9,17... | collective-permute-start | bytes 1622024 | tf_op jit(solution)/shard_map/ppermute | solution.py:59
  9.5 16.6 %collective-permute-start.1 = (bf16[40,4096]{1,0:T(8,128)(2,1)S(1)}, bf16[40,4096]{1,0:T(8,128)(2,1)S(1)}, u32[]{:S(2)}, u32[]{:S(2)}) collective-permute-start(bf16[40,4096]{1,0:T(8,128)(2,1)S(1)} %get-tuple-element.65), channel_id=1, source_target_pairs={{0,4},{1,5},{2,6},{3,7},{4,0},{5,1},{6,2},{7,3},{8,12},{9,13},{10,... | collective-permute-start | bytes 983048 | tf_op jit(solution)/shard_map/ppermute | solution.py:59
  26.1 21.5 %collective-permute-start.8 = (bf16[4096,384]{1,0:T(8,128)(2,1)}, bf16[4096,384]{1,0:T(8,128)(2,1)S(1)}, u32[]{:S(2)}, u32[]{:S(2)}) collective-permute-start(bf16[4096,384]{1,0:T(8,128)(2,1)} %refs_10_.3), channel_id=1, source_target_pairs={{0,1},{1,0},{2,3},{3,2},{4,5},{5,4},{6,7},{7,6},{8,9},{9,8},{10,11... | collective-permute-start | bytes 9437192 | tf_op jit(solution)/shard_map/ppermute | solution.py:59
  27.9 19.7 %collective-permute-start.9 = (bf16[64,4224]{1,0:T(8,128)(2,1)S(1)}, bf16[64,4224]{1,0:T(8,128)(2,1)S(1)}, u32[]{:S(2)}, u32[]{:S(2)}) collective-permute-start(bf16[64,4224]{1,0:T(8,128)(2,1)S(1)} %collective-permute-done.3.block_ref), channel_id=1, source_target_pairs={{0,8},{1,9},{2,10},{3,11},{4,12},{5,13},{6,14},{7,15},{8,16},{9,17... | collective-permute-start | bytes 1622024 | tf_op jit(solution)/shard_map/ppermute | solution.py:59
  32.2 15.5 %collective-permute-start.5 = (bf16[40,4096]{1,0:T(8,128)(2,1)S(1)}, bf16[40,4096]{1,0:T(8,128)(2,1)S(1)}, u32[]{:S(2)}, u32[]{:S(2)}) collective-permute-start(bf16[40,4096]{1,0:T(8,128)(2,1)S(1)} %get-tuple-element.72), channel_id=1, source_target_pairs={{0,4},{1,5},{2,6},{3,7},{4,0},{5,1},{6,2},{7,3},{8,12},{9,13},{10,... | collective-permute-start | bytes 983048 | tf_op jit(solution)/shard_map/ppermute | solution.py:59
  51.9 22.2 %collective-permute-start.11 = (bf16[40,4096]{1,0:T(8,128)(2,1)S(1)}, bf16[40,4096]{1,0:T(8,128)(2,1)S(1)}, u32[]{:S(2)}, u32[]{:S(2)}) collective-permute-start(bf16[40,4096]{1,0:T(8,128)(2,1)S(1)} %get-tuple-element.89), channel_id=1, source_target_pairs={{0,2},{1,3},{2,0},{3,1},{4,6},{5,7},{6,4},{7,5},{8,10},{9,11},{10,... | collective-permute-start | bytes 983048 | tf_op jit(solution)/shard_map/ppermute | solution.py:59
  52.5 30.1 %collective-permute-start.12 = (bf16[40,4096]{1,0:T(8,128)(2,1)S(1)}, bf16[40,4096]{1,0:T(8,128)(2,1)}, u32[]{:S(2)}, u32[]{:S(2)}) collective-permute-start(bf16[40,4096]{1,0:T(8,128)(2,1)S(1)} %get-tuple-element.91), channel_id=1, source_target_pairs={{0,4},{1,5},{2,6},{3,7},{4,0},{5,1},{6,2},{7,3},{8,12},{9,13},{10,... | collective-permute-start | bytes 983048 | tf_op jit(solution)/shard_map/ppermute | solution.py:59
  54.0 30.4 %collective-permute-start.13 = (bf16[40,4096]{1,0:T(8,128)(2,1)S(1)}, bf16[40,4096]{1,0:T(8,128)(2,1)}, u32[]{:S(2)}, u32[]{:S(2)}) collective-permute-start(bf16[40,4096]{1,0:T(8,128)(2,1)S(1)} %get-tuple-element.93), channel_id=1, source_target_pairs={{0,6},{1,7},{2,4},{3,5},{4,2},{5,3},{6,0},{7,1},{8,14},{9,15},{10,... | collective-permute-start | bytes 983048 | tf_op jit(solution)/shard_map/ppermute | solution.py:59
  55.4 19.3 %collective-permute-start.14 = (bf16[64,4224]{1,0:T(8,128)(2,1)S(1)}, bf16[64,4224]{1,0:T(8,128)(2,1)S(1)}, u32[]{:S(2)}, u32[]{:S(2)}) collective-permute-start(bf16[64,4224]{1,0:T(8,128)(2,1)S(1)} %collective-permute-done.9.block_ref), channel_id=1, source_target_pairs={{0,8},{1,9},{2,10},{3,11},{4,12},{5,13},{6,14},{7,15},{8,16},{9,17... | collective-permute-start | bytes 1622024 | tf_op jit(solution)/shard_map/ppermute | solution.py:59
  74.1 16.1 %collective-permute-start.22 = (bf16[40,4096]{1,0:T(8,128)(2,1)}, bf16[40,4096]{1,0:T(8,128)(2,1)}, u32[]{:S(2)}, u32[]{:S(2)}) collective-permute-start(bf16[40,4096]{1,0:T(8,128)(2,1)} %get-tuple-element.85), channel_id=1, source_target_pairs={{0,4},{1,5},{2,6},{3,7},{4,0},{5,1},{6,2},{7,3},{8,12},{9,13},{10,... | collective-permute-start | bytes 983048 | tf_op jit(solution)/shard_map/ppermute | solution.py:59
  74.7 15.6 %collective-permute-start.18 = (bf16[40,4096]{1,0:T(8,128)(2,1)}, bf16[40,4096]{1,0:T(8,128)(2,1)}, u32[]{:S(2)}, u32[]{:S(2)}) collective-permute-start(bf16[40,4096]{1,0:T(8,128)(2,1)} %get-tuple-element.84), channel_id=1, source_target_pairs={{0,2},{1,3},{2,0},{3,1},{4,6},{5,7},{6,4},{7,5},{8,10},{9,11},{10,... | collective-permute-start | bytes 983048 | tf_op jit(solution)/shard_map/ppermute | solution.py:59
  76.9 16.8 %all-to-all-start = ((bf16[32,1,1]{2,1,0:T(2,128)(2,1)}), bf16[32,1,1]{2,1,0:T(2,128)(2,1)S(1)}, u32[]{:S(2)}, u32[]{:S(2)}) async-start(bf16[32,1,1]{2,1,0:T(2,128)(2,1)} %copy.18), calls=%async_computation | async-start | bytes 32768 | tf_op jit(solution)/shard_map/all_to_all | solution.py:46
  82.6 15.9 %collective-permute-start.15 = (bf16[40,4096]{1,0:T(8,128)(2,1)S(1)}, bf16[40,4096]{1,0:T(8,128)(2,1)S(1)}, u32[]{:S(2)}, u32[]{:S(2)}) collective-permute-start(bf16[40,4096]{1,0:T(8,128)(2,1)S(1)} %get-tuple-element.96), channel_id=1, source_target_pairs={{0,2},{1,3},{2,0},{3,1},{4,6},{5,7},{6,4},{7,5},{8,10},{9,11},{10,... | collective-permute-start | bytes 983048 | tf_op jit(solution)/shard_map/ppermute | solution.py:59
  85.9 18.0 %collective-permute-start.17 = (bf16[40,4096]{1,0:T(8,128)(2,1)S(1)}, bf16[40,4096]{1,0:T(8,128)(2,1)}, u32[]{:S(2)}, u32[]{:S(2)}) collective-permute-start(bf16[40,4096]{1,0:T(8,128)(2,1)S(1)} %get-tuple-element.100), channel_id=1, source_target_pairs={{0,6},{1,7},{2,4},{3,5},{4,2},{5,3},{6,0},{7,1},{8,14},{9,15},{10,... | collective-permute-start | bytes 983048 | tf_op jit(solution)/shard_map/ppermute | solution.py:59
  92.0 45.2 %collective-permute-start.30 = (bf16[64,4096]{1,0:T(8,128)(2,1)S(1)}, bf16[64,4096]{1,0:T(8,128)(2,1)S(1)}, u32[]{:S(2)}, u32[]{:S(2)}) collective-permute-start(bf16[64,4096]{1,0:T(8,128)(2,1)S(1)} %convolution_convert_fusion.2), channel_id=1, source_target_pairs={{0,8},{1,9},{2,10},{3,11},{4,12},{5,13},{6,14},{7,15},{8,16},{9,17... | collective-permute-start | bytes 1572872 | tf_op jit(solution)/shard_map/ppermute | solution.py:59
  93.7 69.7 %all-to-all-start.1 = ((bf16[32,2,8192]{2,1,0:T(2,128)(2,1)}), bf16[32,2,8192]{2,1,0:T(2,128)(2,1)S(1)}, u32[]{:S(2)}, u32[]{:S(2)}) async-start(bf16[32,2,8192]{2,1,0:T(2,128)(2,1)} %reshape.49), calls=%async_computation.1 | async-start | bytes 2097152 | tf_op jit(solution)/shard_map/all_to_all | solution.py:45
  121.5 15.7 %collective-permute-start.23 = (bf16[40,4096]{1,0:T(8,128)(2,1)}, bf16[40,4096]{1,0:T(8,128)(2,1)S(1)}, u32[]{:S(2)}, u32[]{:S(2)}) collective-permute-start(bf16[40,4096]{1,0:T(8,128)(2,1)} %get-tuple-element.108), channel_id=1, source_target_pairs={{0,4},{1,5},{2,6},{3,7},{4,0},{5,1},{6,2},{7,3},{8,12},{9,13},{10,... | collective-permute-start | bytes 983048 | tf_op jit(solution)/shard_map/ppermute | solution.py:59
  121.5 15.7 %collective-permute-start.19 = (bf16[40,4096]{1,0:T(8,128)(2,1)}, bf16[40,4096]{1,0:T(8,128)(2,1)S(1)}, u32[]{:S(2)}, u32[]{:S(2)}) collective-permute-start(bf16[40,4096]{1,0:T(8,128)(2,1)} %get-tuple-element.103), channel_id=1, source_target_pairs={{0,2},{1,3},{2,0},{3,1},{4,6},{5,7},{6,4},{7,5},{8,10},{9,11},{10,... | collective-permute-start | bytes 983048 | tf_op jit(solution)/shard_map/ppermute | solution.py:59
  138.7 18.6 %collective-permute-start.31 = (bf16[64,4096]{1,0:T(8,128)(2,1)S(1)}, bf16[64,4096]{1,0:T(8,128)(2,1)S(1)}, u32[]{:S(2)}, u32[]{:S(2)}) collective-permute-start(bf16[64,4096]{1,0:T(8,128)(2,1)S(1)} %fusion.2), channel_id=1, source_target_pairs={{0,8},{1,9},{2,10},{3,11},{4,12},{5,13},{6,14},{7,15},{8,16},{9,17... | collective-permute-start | bytes 1572872 | tf_op jit(solution)/shard_map/ppermute | solution.py:59
  141.7 15.6 %collective-permute-start.24 = (bf16[40,4096]{1,0:T(8,128)(2,1)S(1)}, bf16[40,4096]{1,0:T(8,128)(2,1)S(1)}, u32[]{:S(2)}, u32[]{:S(2)}) collective-permute-start(bf16[40,4096]{1,0:T(8,128)(2,1)S(1)} %copy-done.19), channel_id=1, source_target_pairs={{0,4},{1,5},{2,6},{3,7},{4,0},{5,1},{6,2},{7,3},{8,12},{9,13},{10,... | collective-permute-start | bytes 983048 | tf_op jit(solution)/shard_map/ppermute | solution.py:59
  158.5 18.7 %collective-permute-start.32 = (bf16[64,4096]{1,0:T(8,128)(2,1)}, bf16[64,4096]{1,0:T(8,128)(2,1)}, u32[]{:S(2)}, u32[]{:S(2)}) collective-permute-start(bf16[64,4096]{1,0:T(8,128)(2,1)} %fusion.1), channel_id=1, source_target_pairs={{0,8},{1,9},{2,10},{3,11},{4,12},{5,13},{6,14},{7,15},{8,16},{9,17... | collective-permute-start | bytes 1572872 | tf_op jit(solution)/shard_map/ppermute | solution.py:59
  160.8 16.4 %collective-permute-start.25 = (bf16[40,4096]{1,0:T(8,128)(2,1)}, bf16[40,4096]{1,0:T(8,128)(2,1)}, u32[]{:S(2)}, u32[]{:S(2)}) collective-permute-start(bf16[40,4096]{1,0:T(8,128)(2,1)} %get-tuple-element.110), channel_id=1, source_target_pairs={{0,4},{1,5},{2,6},{3,7},{4,0},{5,1},{6,2},{7,3},{8,12},{9,13},{10,... | collective-permute-start | bytes 983048 | tf_op jit(solution)/shard_map/ppermute | solution.py:59
  162.0 15.1 %collective-permute-start.21 = (bf16[40,4096]{1,0:T(8,128)(2,1)}, bf16[40,4096]{1,0:T(8,128)(2,1)}, u32[]{:S(2)}, u32[]{:S(2)}) collective-permute-start(bf16[40,4096]{1,0:T(8,128)(2,1)} %get-tuple-element.105), channel_id=1, source_target_pairs={{0,2},{1,3},{2,0},{3,1},{4,6},{5,7},{6,4},{7,5},{8,10},{9,11},{10,... | collective-permute-start | bytes 983048 | tf_op jit(solution)/shard_map/ppermute | solution.py:59
  (34 other events, 323.7 us)

commit v4 on v3

--- a/solution.py
+++ b/solution.py
@@ -17,16 +17,16 @@
     return jnp.sum(earlier * onehot, axis=1)
 
 
-def place_pages(arrived, arrived_labels, page_count, page_shape):
+def place_pages(arrived, page_count, page_shape):
     picking = (
-        arrived_labels.astype(jnp.float32)[None, :]
+        arrived[:, -1].astype(jnp.float32)[None, :]
         == jnp.arange(page_count, dtype=jnp.float32)[:, None]
     ).astype(jnp.bfloat16)
-    landed = jnp.dot(picking, arrived, preferred_element_type=jnp.float32)
+    landed = jnp.dot(picking, arrived[:, :-128], preferred_element_type=jnp.float32)
     return landed.astype(jnp.bfloat16).reshape(page_shape)
 
 
-def hand_pages(kv_pages, page_target, earlier):
+def sort_pages(kv_pages, page_target):
     page_count = kv_pages.shape[0]
     owners = lax.axis_size("expert")
     target_dev = page_target // page_count
@@ -41,13 +41,12 @@
         preferred_element_type=jnp.float32,
     ).astype(jnp.bfloat16)
     labels = jnp.sum(jnp.where(placing, target_slot[:, None] + 1, 0), axis=0) - 1
-    arrived, arrived_labels = (
-        lax.all_to_all(after(outgoing, earlier), "expert", split_axis=0, concat_axis=0, tiled=True),
-        lax.all_to_all(
-            labels.astype(jnp.bfloat16), "expert", split_axis=0, concat_axis=0, tiled=True
-        ),
-    )
-    return place_pages(arrived, arrived_labels, page_count, kv_pages.shape)
+    labels = jnp.broadcast_to(labels.astype(jnp.bfloat16)[:, None], (owners * PCAP, 128))
+    return jnp.concatenate([outgoing, labels], axis=1)
+
+
+def exchange(x):
+    return lax.all_to_all(x, "expert", split_axis=0, concat_axis=0, tiled=True)
 
 
 def send(x, step=None, flip=None):
@@ -259,6 +258,7 @@
     weights = (gate_weight, up_weight, down_weight)
     group = 2
     swapped, blends, got, outs = [], [], [], []
+    outgoing = sort_pages(kv_pages, page_target)
     block = tokens
     for s in range(planes):
         if s:
@@ -280,21 +280,23 @@
 
     pairs = [(own, other) for own, other in zip(weights, swapped)]
     for first in range(0, planes, group):
-        held = got[first : first + group]
-        if outs:
-            held[0][0] = after(held[0][0], *outs)
+        held = [list(pieces) for pieces in got[first : first + group]]
+        following = got[first + group][1:] if first + group < planes else []
+        held[0][0] = after(held[0][0], *outs, *following)
         outs.extend(work(held, *pairs))
 
+    arrived = exchange(after(outgoing, *got[-2][1:], block))
     order = list(range(1, planes)) + [0]
-    sent = {}
-    previous = None
-    for i, s in enumerate(order):
+    sent, landed = {}, got[-1][1:]
+    for s in order:
         mine = outs[s * PLANE : (s + 1) * PLANE]
-        back = [mine[0]]
+        sent[s] = [mine[0]]
         for j in range(1, PLANE):
-            back.append(send(after(mine[j], previous[j]) if previous else mine[j], flip=2 * j))
-        sent[s] = previous = back
-    handed = hand_pages(kv_pages, page_target, got[-2][1])
+            waits = [landed[-3 if s == 1 else -4]] + ([arrived] if s == order[-2] else [])
+            landed.append(send(after(mine[j], *waits), flip=2 * j))
+            sent[s].append(landed[-1])
+    handed = place_pages(arrived, kv_pages.shape[0], kv_pages.shape)
+    sent[1][0] = after(sent[1][0], outs[-1])
     total = None
     for s in order:
         part = jnp.dot(

time: 180 us -> 178 us (0.989)
  matrix products: 8.65 us -> 3.16 us
  starting transfers between devices: 47.7 us -> 42.4 us
  local copies, waits for them, and re-layouts: 14.9 us -> 19.1 us
  waiting for transfers between devices: 70.3 us -> 74.4 us
    all_to_all x2 -> x1, starting transfers between devices: 8.37 us -> 3.38 us  [exchange(): return lax.all_to_all(x, 'expert', split_axis=0, concat_axis=0, tiled=True)]
    unnamed x52 -> x65, local copies, waits for them, and re-layouts: 13.7 us -> 18.5 us
    dot_general x4, matrix products: 6.67 us -> 2.19 us  [local(): jnp.dot(blends[s], jnp.concatenate(sent[s], axis=0), preferred_element_ty...]
    ppermute x33, waiting for transfers between devices: 70.3 us -> 74.4 us  [send(): return lax.ppermute(x, 'expert', pairs)]
  transfers between devices with their start and end apart: 35 -> 34, of which waited for: 12 -> 17; matrix products, arithmetic and copies ran while one was open for 8% -> 8% of each run, Pallas kernels for 18% -> 19%
where the time goes in v4:
time: 178 us; the launch traced here: 177 us
  waiting for transfers between devices  74.4 us (42%)
  starting transfers between devices  42.4 us (24%)
  Pallas kernels  34.1 us (19%)
  local copies, waits for them, and re-layouts  19.1 us (11%)
  matrix products  3.16 us (2%)
  other arithmetic  2.8 us (2%)
    ppermute x33, waiting for transfers between devices, send(): return lax.ppermute(x, 'expert', pairs)  74.4 us
    ppermute x33, starting transfers between devices, send(): return lax.ppermute(x, 'expert', pairs)  39 us
    pallas_call x2, Pallas kernels, apply(): pl.pallas_call(functools.partial(expert_kernel, len(pieces), steps), grid...  30.7 us
    unnamed x65, local copies, waits for them, and re-layouts  18.5 us
  transfers between devices with their start and end apart: 34, of which 17 were waited for; matrix products, arithmetic and copies ran while one was open for 8% of the time, Pallas kernels for 19%

profile of v4, /device:TPU:0, one launch (start us, length us, event | category | flops | bytes accessed | tf_op | source)
XLA Modules:
  0.0 177.0 jit_solution(1512849847945212964)
XLA Ops:
  5.5 2.6 %collective-permute-start = (bf16[64,4224]{1,0:T(8,128)(2,1)S(1)}, bf16[64,4224]{1,0:T(8,128)(2,1)S(1)}, u32[]{:S(2)}, u32[]{:S(2)}) collective-permute-start(bf16[64,4224]{1,0:T(8,128)(2,1)S(1)} %get-tuple-element.69), channel_id=1, source_target_pairs={{0,8},{1,9},{2,10},{3,11},{4,12},{5,13},{6,14},{7,15},{8,16},{9,17... | collective-permute-start | bytes 1622024 | tf_op jit(solution)/shard_map/ppermute | solution.py:58
  11.5 7.1 %collective-permute-done.2.refs_1_ = bf16[40,4096]{1,0:T(8,128)(2,1)S(1)} collective-permute-done((bf16[40,4096]{1,0:T(8,128)(2,1)S(1)}, bf16[40,4096]{1,0:T(8,128)(2,1)S(1)}, u32[]{:S(2)}, u32[]{:S(2)}) %collective-permute-start.2) | collective-permute-done | bytes 327712 | tf_op jit(solution)/shard_map/ppermute | solution.py:58
  18.6 7.5 %collective-permute-done.5.refs_2_ = bf16[40,4096]{1,0:T(8,128)(2,1)S(1)} collective-permute-done((bf16[40,4096]{1,0:T(8,128)(2,1)S(1)}, bf16[40,4096]{1,0:T(8,128)(2,1)S(1)}, u32[]{:S(2)}, u32[]{:S(2)}) %collective-permute-start.5) | collective-permute-done | bytes 327712 | tf_op jit(solution)/shard_map/ppermute | solution.py:58
  34.5 7.2 %collective-permute-done.3.refs_5_ = bf16[40,4096]{1,0:T(8,128)(2,1)S(1)} collective-permute-done((bf16[40,4096]{1,0:T(8,128)(2,1)S(1)}, bf16[40,4096]{1,0:T(8,128)(2,1)S(1)}, u32[]{:S(2)}, u32[]{:S(2)}) %collective-permute-start.3) | collective-permute-done | bytes 327712 | tf_op jit(solution)/shard_map/ppermute | solution.py:58
  41.7 6.0 %collective-permute-done.6.refs_6_ = bf16[40,4096]{1,0:T(8,128)(2,1)S(1)} collective-permute-done((bf16[40,4096]{1,0:T(8,128)(2,1)S(1)}, bf16[40,4096]{1,0:T(8,128)(2,1)S(1)}, u32[]{:S(2)}, u32[]{:S(2)}) %collective-permute-start.6) | collective-permute-done | bytes 327712 | tf_op jit(solution)/shard_map/ppermute | solution.py:58
  49.7 1.8 %copy.21 = bf16[4,8,16,1024]{3,1,2,0:T(8,128)(2,1)S(1)} copy(bf16[4,8,16,1024]{3,2,1,0:T(8,128)(2,1)} %bitcast.19) | data formatting | bytes 2097152
  58.3 5.4 %collective-permute-done.4.refs_1_ = bf16[40,4096]{1,0:T(8,128)(2,1)S(1)} collective-permute-done((bf16[40,4096]{1,0:T(8,128)(2,1)S(1)}, bf16[40,4096]{1,0:T(8,128)(2,1)S(1)}, u32[]{:S(2)}, u32[]{:S(2)}) %collective-permute-start.4) | collective-permute-done | bytes 327712 | tf_op jit(solution)/shard_map/ppermute | solution.py:58
  63.7 5.8 %collective-permute-done.7.refs_2_ = bf16[40,4096]{1,0:T(8,128)(2,1)S(1)} collective-permute-done((bf16[40,4096]{1,0:T(8,128)(2,1)S(1)}, bf16[40,4096]{1,0:T(8,128)(2,1)S(1)}, u32[]{:S(2)}, u32[]{:S(2)}) %collective-permute-start.7) | collective-permute-done | bytes 327712 | tf_op jit(solution)/shard_map/ppermute | solution.py:58
  78.2 1.6 reshape.38
  79.8 3.4 %all-to-all-start = ((bf16[32,2,8256]{2,1,0:T(2,128)(2,1)}), bf16[32,2,8256]{2,1,0:T(2,128)(2,1)}, u32[]{:S(2)}, u32[]{:S(2)}) async-start(bf16[32,2,8256]{2,1,0:T(2,128)(2,1)} %reshape.38), calls=%async_computation | async-start | bytes 2129920 | tf_op jit(solution)/shard_map/all_to_all | solution.py:49
  83.2 15.4 %shard_map.98 = (bf16[40,4096]{1,0:T(8,128)(2,1)}, bf16[40,4096]{1,0:T(8,128)(2,1)}, bf16[40,4096]{1,0:T(8,128)(2,1)}, bf16[40,4096]{1,0:T(8,128)(2,1)}, bf16[40...) custom-call(bf16[40,4096]{1,0:T(8,128)(2,1)} %copy-done.1, ...), custom_call_target="tpu_custom_call" | custom-call | flops 6039797760 | bytes 24117248 | tf_op jit(solution)/shard_map/pallas_call | solution.py:204
  98.6 2.6 %collective-permute-start.21 = (bf16[40,4096]{1,0:T(8,128)(2,1)}, bf16[40,4096]{1,0:T(8,128)(2,1)S(1)}, u32[]{:S(2)}, u32[]{:S(2)}) collective-permute-start(bf16[40,4096]{1,0:T(8,128)(2,1)} %get-tuple-element.112), channel_id=1, source_target_pairs={{0,6},{1,7},{2,4},{3,5},{4,2},{5,3},{6,0},{7,1},{8,14},{9,15},{10,... | collective-permute-start | bytes 983048 | tf_op jit(solution)/shard_map/ppermute | solution.py:58
  102.2 15.4 %shard_map.100 = (bf16[40,4096]{1,0:T(8,128)(2,1)}, bf16[40,4096]{1,0:T(8,128)(2,1)}, bf16[40,4096]{1,0:T(8,128)(2,1)}, bf16[40,4096]{1,0:T(8,128)(2,1)}, bf16[4...) custom-call(bf16[40,4096]{1,0:T(8,128)(2,1)} %copy-done.3, ...), custom_call_target="tpu_custom_call" | custom-call | flops 6039797760 | bytes 24117248 | tf_op jit(solution)/shard_map/pallas_call | solution.py:204
  119.1 2.2 %collective-permute-start.30 = (bf16[64,4096]{1,0:T(8,128)(2,1)S(1)}, bf16[64,4096]{1,0:T(8,128)(2,1)S(1)}, u32[]{:S(2)}, u32[]{:S(2)}) collective-permute-start(bf16[64,4096]{1,0:T(8,128)(2,1)S(1)} %convolution_convert_fusion.2), channel_id=1, source_target_pairs={{0,8},{1,9},{2,10},{3,11},{4,12},{5,13},{6,14},{7,15},{8,16},{9,17... | collective-permute-start | bytes 1572872 | tf_op jit(solution)/shard_map/ppermute | solution.py:58
  121.9 1.7 collective-permute-start.19
  124.8 7.2 %collective-permute-done.24 = bf16[40,4096]{1,0:T(8,128)(2,1)S(1)} collective-permute-done((bf16[40,4096]{1,0:T(8,128)(2,1)S(1)}, bf16[40,4096]{1,0:T(8,128)(2,1)S(1)}, u32[]{:S(2)}, u32[]{:S(2)}) %collective-permute-start.24) | collective-permute-done | bytes 327712 | tf_op jit(solution)/shard_map/ppermute | solution.py:58
  132.0 6.0 %collective-permute-done.19 = bf16[40,4096]{1,0:T(8,128)(2,1)S(1)} collective-permute-done((bf16[40,4096]{1,0:T(8,128)(2,1)S(1)}, bf16[40,4096]{1,0:T(8,128)(2,1)S(1)}, u32[]{:S(2)}, u32[]{:S(2)}) %collective-permute-start.19) | collective-permute-done | bytes 327712 | tf_op jit(solution)/shard_map/ppermute | solution.py:58
  140.7 4.4 %reshape.39 = bf16[32,1,16512]{2,1,0:T(2,128)(2,1)S(1)} reshape(bf16[32,2,8256]{2,1,0:T(2,128)(2,1)} %all-to-all-done) | data formatting | bytes 2113536
  146.1 1.7 collective-permute-start.25
  149.6 6.6 %collective-permute-done.25 = bf16[40,4096]{1,0:T(8,128)(2,1)S(1)} collective-permute-done((bf16[40,4096]{1,0:T(8,128)(2,1)S(1)}, bf16[40,4096]{1,0:T(8,128)(2,1)S(1)}, u32[]{:S(2)}, u32[]{:S(2)}) %collective-permute-start.25) | collective-permute-done | bytes 327712 | tf_op jit(solution)/shard_map/ppermute | solution.py:58
  156.2 1.6 collective-permute-done.22
  157.8 3.3 %collective-permute-done.29 = bf16[40,4096]{1,0:T(8,128)(2,1)S(1)} collective-permute-done((bf16[40,4096]{1,0:T(8,128)(2,1)S(1)}, bf16[40,4096]{1,0:T(8,128)(2,1)S(1)}, u32[]{:S(2)}, u32[]{:S(2)}) %collective-permute-start.29) | collective-permute-done | bytes 327712 | tf_op jit(solution)/shard_map/ppermute | solution.py:58
  168.7 3.8 %collective-permute-done.26 = bf16[40,4096]{1,0:T(8,128)(2,1)S(1)} collective-permute-done((bf16[40,4096]{1,0:T(8,128)(2,1)S(1)}, bf16[40,4096]{1,0:T(8,128)(2,1)S(1)}, u32[]{:S(2)}, u32[]{:S(2)}) %collective-permute-start.26) | collective-permute-done | bytes 327712 | tf_op jit(solution)/shard_map/ppermute | solution.py:58
  172.5 3.4 %collective-permute-done.23 = bf16[40,4096]{1,0:T(8,128)(2,1)S(1)} collective-permute-done((bf16[40,4096]{1,0:T(8,128)(2,1)S(1)}, bf16[40,4096]{1,0:T(8,128)(2,1)S(1)}, u32[]{:S(2)}, u32[]{:S(2)}) %collective-permute-start.23) | collective-permute-done | bytes 327712 | tf_op jit(solution)/shard_map/ppermute | solution.py:58
  (133 shorter events, 52.4 us)
Async XLA Ops:
  5.0 21.1 %collective-permute-start.11 = (bf16[4096,384]{1,0:T(8,128)(2,1)}, bf16[4096,384]{1,0:T(8,128)(2,1)S(1)}, u32[]{:S(2)}, u32[]{:S(2)}) collective-permute-start(bf16[4096,384]{1,0:T(8,128)(2,1)} %refs_8_.3), channel_id=1, source_target_pairs={{0,1},{1,0},{2,3},{3,2},{4,5},{5,4},{6,7},{7,6},{8,9},{9,8},{10,11... | collective-permute-start | bytes 9437192 | tf_op jit(solution)/shard_map/ppermute | solution.py:58
  5.5 20.7 %collective-permute-start = (bf16[64,4224]{1,0:T(8,128)(2,1)S(1)}, bf16[64,4224]{1,0:T(8,128)(2,1)S(1)}, u32[]{:S(2)}, u32[]{:S(2)}) collective-permute-start(bf16[64,4224]{1,0:T(8,128)(2,1)S(1)} %get-tuple-element.69), channel_id=1, source_target_pairs={{0,8},{1,9},{2,10},{3,11},{4,12},{5,13},{6,14},{7,15},{8,16},{9,17... | collective-permute-start | bytes 1622024 | tf_op jit(solution)/shard_map/ppermute | solution.py:58
  9.5 16.6 %collective-permute-start.5 = (bf16[40,4096]{1,0:T(8,128)(2,1)S(1)}, bf16[40,4096]{1,0:T(8,128)(2,1)S(1)}, u32[]{:S(2)}, u32[]{:S(2)}) collective-permute-start(bf16[40,4096]{1,0:T(8,128)(2,1)S(1)} %get-tuple-element.77), channel_id=1, source_target_pairs={{0,4},{1,5},{2,6},{3,7},{4,0},{5,1},{6,2},{7,3},{8,12},{9,13},{10,... | collective-permute-start | bytes 983048 | tf_op jit(solution)/shard_map/ppermute | solution.py:58
  11.0 15.1 %collective-permute-start.8 = (bf16[40,4096]{1,0:T(8,128)(2,1)S(1)}, bf16[40,4096]{1,0:T(8,128)(2,1)S(1)}, u32[]{:S(2)}, u32[]{:S(2)}) collective-permute-start(bf16[40,4096]{1,0:T(8,128)(2,1)S(1)} %get-tuple-element.82), channel_id=1, source_target_pairs={{0,6},{1,7},{2,4},{3,5},{4,2},{5,3},{6,0},{7,1},{8,14},{9,15},{10,... | collective-permute-start | bytes 983048 | tf_op jit(solution)/shard_map/ppermute | solution.py:58
  26.1 21.5 %collective-permute-start.12 = (bf16[4096,384]{1,0:T(8,128)(2,1)}, bf16[4096,384]{1,0:T(8,128)(2,1)S(1)}, u32[]{:S(2)}, u32[]{:S(2)}) collective-permute-start(bf16[4096,384]{1,0:T(8,128)(2,1)} %refs_10_.3), channel_id=1, source_target_pairs={{0,1},{1,0},{2,3},{3,2},{4,5},{5,4},{6,7},{7,6},{8,9},{9,8},{10,11... | collective-permute-start | bytes 9437192 | tf_op jit(solution)/shard_map/ppermute | solution.py:58
  28.0 19.7 %collective-permute-start.1 = (bf16[64,4224]{1,0:T(8,128)(2,1)S(1)}, bf16[64,4224]{1,0:T(8,128)(2,1)S(1)}, u32[]{:S(2)}, u32[]{:S(2)}) collective-permute-start(bf16[64,4224]{1,0:T(8,128)(2,1)S(1)} %collective-permute-done.block_ref), channel_id=1, source_target_pairs={{0,8},{1,9},{2,10},{3,11},{4,12},{5,13},{6,14},{7,15},{8,16},{9,17... | collective-permute-start | bytes 1622024 | tf_op jit(solution)/shard_map/ppermute | solution.py:58
  32.2 15.5 %collective-permute-start.6 = (bf16[40,4096]{1,0:T(8,128)(2,1)S(1)}, bf16[40,4096]{1,0:T(8,128)(2,1)S(1)}, u32[]{:S(2)}, u32[]{:S(2)}) collective-permute-start(bf16[40,4096]{1,0:T(8,128)(2,1)S(1)} %get-tuple-element.78), channel_id=1, source_target_pairs={{0,4},{1,5},{2,6},{3,7},{4,0},{5,1},{6,2},{7,3},{8,12},{9,13},{10,... | collective-permute-start | bytes 983048 | tf_op jit(solution)/shard_map/ppermute | solution.py:58
  33.1 14.6 %collective-permute-start.9 = (bf16[40,4096]{1,0:T(8,128)(2,1)S(1)}, bf16[40,4096]{1,0:T(8,128)(2,1)S(1)}, u32[]{:S(2)}, u32[]{:S(2)}) collective-permute-start(bf16[40,4096]{1,0:T(8,128)(2,1)S(1)} %get-tuple-element.83), channel_id=1, source_target_pairs={{0,6},{1,7},{2,4},{3,5},{4,2},{5,3},{6,0},{7,1},{8,14},{9,15},{10,... | collective-permute-start | bytes 983048 | tf_op jit(solution)/shard_map/ppermute | solution.py:58
  47.7 35.5 %collective-permute-start.13 = (bf16[384,4096]{1,0:T(8,128)(2,1)}, bf16[384,4096]{1,0:T(8,128)(2,1)}, u32[]{:S(2)}, u32[]{:S(2)}) collective-permute-start(bf16[384,4096]{1,0:T(8,128)(2,1)} %refs_12_.3), channel_id=1, source_target_pairs={{0,1},{1,0},{2,3},{3,2},{4,5},{5,4},{6,7},{7,6},{8,9},{9,8},{10,11... | collective-permute-start | bytes 9437192 | tf_op jit(solution)/shard_map/ppermute | solution.py:58
  53.7 15.9 %collective-permute-start.7 = (bf16[40,4096]{1,0:T(8,128)(2,1)S(1)}, bf16[40,4096]{1,0:T(8,128)(2,1)S(1)}, u32[]{:S(2)}, u32[]{:S(2)}) collective-permute-start(bf16[40,4096]{1,0:T(8,128)(2,1)S(1)} %get-tuple-element.79), channel_id=1, source_target_pairs={{0,4},{1,5},{2,6},{3,7},{4,0},{5,1},{6,2},{7,3},{8,12},{9,13},{10,... | collective-permute-start | bytes 983048 | tf_op jit(solution)/shard_map/ppermute | solution.py:58
  55.2 14.4 %collective-permute-start.10 = (bf16[40,4096]{1,0:T(8,128)(2,1)S(1)}, bf16[40,4096]{1,0:T(8,128)(2,1)S(1)}, u32[]{:S(2)}, u32[]{:S(2)}) collective-permute-start(bf16[40,4096]{1,0:T(8,128)(2,1)S(1)} %get-tuple-element.84), channel_id=1, source_target_pairs={{0,6},{1,7},{2,4},{3,5},{4,2},{5,3},{6,0},{7,1},{8,14},{9,15},{10,... | collective-permute-start | bytes 983048 | tf_op jit(solution)/shard_map/ppermute | solution.py:58
  56.6 14.7 %collective-permute-start.14 = (bf16[64,4224]{1,0:T(8,128)(2,1)S(1)}, bf16[64,4224]{1,0:T(8,128)(2,1)S(1)}, u32[]{:S(2)}, u32[]{:S(2)}) collective-permute-start(bf16[64,4224]{1,0:T(8,128)(2,1)S(1)} %collective-permute-done.1.block_ref), channel_id=1, source_target_pairs={{0,8},{1,9},{2,10},{3,11},{4,12},{5,13},{6,14},{7,15},{8,16},{9,17... | collective-permute-start | bytes 1622024 | tf_op jit(solution)/shard_map/ppermute | solution.py:58
  72.8 28.9 %collective-permute-start.15 = (bf16[40,4096]{1,0:T(8,128)(2,1)S(1)}, bf16[40,4096]{1,0:T(8,128)(2,1)}, u32[]{:S(2)}, u32[]{:S(2)}) collective-permute-start(bf16[40,4096]{1,0:T(8,128)(2,1)S(1)} %get-tuple-element.102), channel_id=1, source_target_pairs={{0,2},{1,3},{2,0},{3,1},{4,6},{5,7},{6,4},{7,5},{8,10},{9,11},{10,... | collective-permute-start | bytes 983048 | tf_op jit(solution)/shard_map/ppermute | solution.py:58
  73.4 27.8 %collective-permute-start.16 = (bf16[40,4096]{1,0:T(8,128)(2,1)S(1)}, bf16[40,4096]{1,0:T(8,128)(2,1)}, u32[]{:S(2)}, u32[]{:S(2)}) collective-permute-start(bf16[40,4096]{1,0:T(8,128)(2,1)S(1)} %get-tuple-element.104), channel_id=1, source_target_pairs={{0,4},{1,5},{2,6},{3,7},{4,0},{5,1},{6,2},{7,3},{8,12},{9,13},{10,... | collective-permute-start | bytes 983048 | tf_op jit(solution)/shard_map/ppermute | solution.py:58
  74.9 23.7 %collective-permute-start.17 = (bf16[40,4096]{1,0:T(8,128)(2,1)S(1)}, bf16[40,4096]{1,0:T(8,128)(2,1)}, u32[]{:S(2)}, u32[]{:S(2)}) collective-permute-start(bf16[40,4096]{1,0:T(8,128)(2,1)S(1)} %get-tuple-element.106), channel_id=1, source_target_pairs={{0,6},{1,7},{2,4},{3,5},{4,2},{5,3},{6,0},{7,1},{8,14},{9,15},{10,... | collective-permute-start | bytes 983048 | tf_op jit(solution)/shard_map/ppermute | solution.py:58
  79.8 60.8 %all-to-all-start = ((bf16[32,2,8256]{2,1,0:T(2,128)(2,1)}), bf16[32,2,8256]{2,1,0:T(2,128)(2,1)}, u32[]{:S(2)}, u32[]{:S(2)}) async-start(bf16[32,2,8256]{2,1,0:T(2,128)(2,1)} %reshape.38), calls=%async_computation | async-start | bytes 2129920 | tf_op jit(solution)/shard_map/all_to_all | solution.py:49
  98.6 18.9 %collective-permute-start.21 = (bf16[40,4096]{1,0:T(8,128)(2,1)}, bf16[40,4096]{1,0:T(8,128)(2,1)S(1)}, u32[]{:S(2)}, u32[]{:S(2)}) collective-permute-start(bf16[40,4096]{1,0:T(8,128)(2,1)} %get-tuple-element.112), channel_id=1, source_target_pairs={{0,6},{1,7},{2,4},{3,5},{4,2},{5,3},{6,0},{7,1},{8,14},{9,15},{10,... | collective-permute-start | bytes 983048 | tf_op jit(solution)/shard_map/ppermute | solution.py:58
  101.2 17.1 %collective-permute-start.18 = (bf16[40,4096]{1,0:T(8,128)(2,1)}, bf16[40,4096]{1,0:T(8,128)(2,1)S(1)}, u32[]{:S(2)}, u32[]{:S(2)}) collective-permute-start(bf16[40,4096]{1,0:T(8,128)(2,1)} %get-tuple-element.108), channel_id=1, source_target_pairs={{0,4},{1,5},{2,6},{3,7},{4,0},{5,1},{6,2},{7,3},{8,12},{9,13},{10,... | collective-permute-start | bytes 983048 | tf_op jit(solution)/shard_map/ppermute | solution.py:58
  101.7 17.0 %collective-permute-start.27 = (bf16[40,4096]{1,0:T(8,128)(2,1)}, bf16[40,4096]{1,0:T(8,128)(2,1)S(1)}, u32[]{:S(2)}, u32[]{:S(2)}) collective-permute-start(bf16[40,4096]{1,0:T(8,128)(2,1)} %get-tuple-element.125), channel_id=1, source_target_pairs={{0,2},{1,3},{2,0},{3,1},{4,6},{5,7},{6,4},{7,5},{8,10},{9,11},{10,... | collective-permute-start | bytes 983048 | tf_op jit(solution)/shard_map/ppermute | solution.py:58
  119.1 20.3 %collective-permute-start.30 = (bf16[64,4096]{1,0:T(8,128)(2,1)S(1)}, bf16[64,4096]{1,0:T(8,128)(2,1)S(1)}, u32[]{:S(2)}, u32[]{:S(2)}) collective-permute-start(bf16[64,4096]{1,0:T(8,128)(2,1)S(1)} %convolution_convert_fusion.2), channel_id=1, source_target_pairs={{0,8},{1,9},{2,10},{3,11},{4,12},{5,13},{6,14},{7,15},{8,16},{9,17... | collective-permute-start | bytes 1572872 | tf_op jit(solution)/shard_map/ppermute | solution.py:58
  121.9 16.1 %collective-permute-start.19 = (bf16[40,4096]{1,0:T(8,128)(2,1)S(1)}, bf16[40,4096]{1,0:T(8,128)(2,1)S(1)}, u32[]{:S(2)}, u32[]{:S(2)}) collective-permute-start(bf16[40,4096]{1,0:T(8,128)(2,1)S(1)} %copy-done.23), channel_id=1, source_target_pairs={{0,6},{1,7},{2,4},{3,5},{4,2},{5,3},{6,0},{7,1},{8,14},{9,15},{10,... | collective-permute-start | bytes 983048 | tf_op jit(solution)/shard_map/ppermute | solution.py:58
  123.6 15.8 %collective-permute-start.28 = (bf16[40,4096]{1,0:T(8,128)(2,1)S(1)}, bf16[40,4096]{1,0:T(8,128)(2,1)S(1)}, u32[]{:S(2)}, u32[]{:S(2)}) collective-permute-start(bf16[40,4096]{1,0:T(8,128)(2,1)S(1)} %copy-done.22), channel_id=1, source_target_pairs={{0,4},{1,5},{2,6},{3,7},{4,0},{5,1},{6,2},{7,3},{8,12},{9,13},{10,... | collective-permute-start | bytes 983048 | tf_op jit(solution)/shard_map/ppermute | solution.py:58
  139.7 21.4 %collective-permute-start.31 = (bf16[64,4096]{1,0:T(8,128)(2,1)S(1)}, bf16[64,4096]{1,0:T(8,128)(2,1)S(1)}, u32[]{:S(2)}, u32[]{:S(2)}) collective-permute-start(bf16[64,4096]{1,0:T(8,128)(2,1)S(1)} %fusion.2), channel_id=1, source_target_pairs={{0,8},{1,9},{2,10},{3,11},{4,12},{5,13},{6,14},{7,15},{8,16},{9,17... | collective-permute-start | bytes 1572872 | tf_op jit(solution)/shard_map/ppermute | solution.py:58
  161.6 14.3 %collective-permute-start.32 = (bf16[64,4096]{1,0:T(8,128)(2,1)S(1)}, bf16[64,4096]{1,0:T(8,128)(2,1)S(1)}, u32[]{:S(2)}, u32[]{:S(2)}) collective-permute-start(bf16[64,4096]{1,0:T(8,128)(2,1)S(1)} %fusion.1), channel_id=1, source_target_pairs={{0,8},{1,9},{2,10},{3,11},{4,12},{5,13},{6,14},{7,15},{8,16},{9,17... | collective-permute-start | bytes 1572872 | tf_op jit(solution)/shard_map/ppermute | solution.py:58
  (39 other events, 324.5 us)

commit v5 on v4

--- a/solution.py
+++ b/solution.py
@@ -11,38 +11,70 @@
 PLANE = 4
 
 
-def slot_ranks(labels, count):
-    onehot = (labels[:, None] == jnp.arange(count, dtype=jnp.int32)[None, :]).astype(jnp.int32)
-    earlier = jnp.cumsum(onehot, axis=0) - onehot
-    return jnp.sum(earlier * onehot, axis=1)
-
-
-def place_pages(arrived, page_count, page_shape):
-    picking = (
-        arrived[:, -1].astype(jnp.float32)[None, :]
-        == jnp.arange(page_count, dtype=jnp.float32)[:, None]
-    ).astype(jnp.bfloat16)
-    landed = jnp.dot(picking, arrived[:, :-128], preferred_element_type=jnp.float32)
-    return landed.astype(jnp.bfloat16).reshape(page_shape)
+LANES = 128
+
+
+def sort_kernel(target_ref, pages_ref, out_ref):
+    count, rows, width = pages_ref.shape
+    if out_ref.shape[0] > count:
+        out_ref[...] = jnp.full(out_ref.shape, -1.0, out_ref.dtype)
+
+    @pl.loop(0, count)
+    def _(p):
+        target = target_ref[p]
+        owner = target // count
+        slot = (target - owner * count).astype(jnp.float32)
+        out_ref[owner, :, :width] = pages_ref[p]
+        out_ref[owner, :, width:] = jnp.full((rows, LANES), slot, jnp.float32).astype(jnp.bfloat16)
 
 
 def sort_pages(kv_pages, page_target):
-    page_count = kv_pages.shape[0]
+    count, rows, width = kv_pages.shape
     owners = lax.axis_size("expert")
-    target_dev = page_target // page_count
-    target_slot = page_target % page_count
-    flat_pages = kv_pages.reshape(page_count, -1)
-    position = target_dev * PCAP + slot_ranks(target_dev, owners)
-    placing = position[:, None] == jnp.arange(owners * PCAP, dtype=jnp.int32)[None, :]
-    outgoing = lax.dot_general(
-        placing.astype(jnp.bfloat16),
-        flat_pages,
-        (((0,), (0,)), ((), ())),
-        preferred_element_type=jnp.float32,
-    ).astype(jnp.bfloat16)
-    labels = jnp.sum(jnp.where(placing, target_slot[:, None] + 1, 0), axis=0) - 1
-    labels = jnp.broadcast_to(labels.astype(jnp.bfloat16)[:, None], (owners * PCAP, 128))
-    return jnp.concatenate([outgoing, labels], axis=1)
+    return pl.pallas_call(
+        sort_kernel,
+        out_shape=jax.ShapeDtypeStruct((owners * PCAP, rows, width + LANES), jnp.bfloat16),
+        in_specs=[
+            pl.BlockSpec(memory_space=pltpu.SMEM),
+            pl.BlockSpec(memory_space=pltpu.VMEM),
+        ],
+        out_specs=pl.BlockSpec(memory_space=pltpu.VMEM),
+        compiler_params=pltpu.CompilerParams(vmem_limit_bytes=16 * 2**20),
+        cost_estimate=pl.CostEstimate(
+            flops=0, bytes_accessed=6 * count * rows * width, transcendentals=0
+        ),
+    )(page_target, kv_pages)
+
+
+def place_kernel(label_ref, arrived_ref, out_ref):
+    sources = arrived_ref.shape[0]
+    width = out_ref.shape[2]
+
+    @pl.loop(0, sources)
+    def _(p):
+        label = label_ref[p]
+
+        @pl.when((label >= 0) & (label < out_ref.shape[0]))
+        def _():
+            out_ref[label] = arrived_ref[p, :, :width]
+
+
+def place_pages(arrived, page_shape):
+    count, rows, width = page_shape
+    labels = arrived[:, 0, width].astype(jnp.int32)
+    return pl.pallas_call(
+        place_kernel,
+        out_shape=jax.ShapeDtypeStruct(page_shape, jnp.bfloat16),
+        in_specs=[
+            pl.BlockSpec(memory_space=pltpu.SMEM),
+            pl.BlockSpec(memory_space=pltpu.VMEM),
+        ],
+        out_specs=pl.BlockSpec(memory_space=pltpu.VMEM),
+        compiler_params=pltpu.CompilerParams(vmem_limit_bytes=16 * 2**20),
+        cost_estimate=pl.CostEstimate(
+            flops=0, bytes_accessed=4 * count * rows * width, transcendentals=0
+        ),
+    )(labels, arrived)
 
 
 def exchange(x):
@@ -278,24 +310,23 @@
         if s + 1 < planes:
             block = send(block, step=stride)
 
-    pairs = [(own, other) for own, other in zip(weights, swapped)]
     for first in range(0, planes, group):
         held = [list(pieces) for pieces in got[first : first + group]]
         following = got[first + group][1:] if first + group < planes else []
         held[0][0] = after(held[0][0], *outs, *following)
-        outs.extend(work(held, *pairs))
-
-    arrived = exchange(after(outgoing, *got[-2][1:], block))
+        outs.extend(work(held, *zip(weights, swapped)))
+
+    arrived = exchange(after(outgoing, outs[0]))
     order = list(range(1, planes)) + [0]
     sent, landed = {}, got[-1][1:]
     for s in order:
         mine = outs[s * PLANE : (s + 1) * PLANE]
         sent[s] = [mine[0]]
         for j in range(1, PLANE):
-            waits = [landed[-3 if s == 1 else -4]] + ([arrived] if s == order[-2] else [])
+            waits = [landed[-3 if s == 1 else -4]] + ([arrived] if s == 0 else [])
             landed.append(send(after(mine[j], *waits), flip=2 * j))
             sent[s].append(landed[-1])
-    handed = place_pages(arrived, kv_pages.shape[0], kv_pages.shape)
+    handed = place_pages(arrived, kv_pages.shape)
     sent[1][0] = after(sent[1][0], outs[-1])
     total = None
     for s in order:

time: 178 us -> 181 us (1.017)
  local copies, waits for them, and re-layouts: 19.1 us -> 10.7 us
  waiting for transfers between devices: 74.4 us -> 82.1 us
  Pallas kernels: 34.1 us -> 38.2 us
  starting transfers between devices: 42.4 us -> 44.7 us
  other arithmetic: 2.8 us -> 0.66 us
    unnamed x65 -> x64, local copies, waits for them, and re-layouts: 18.5 us -> 10.7 us
    ppermute x33, waiting for transfers between devices: 74.4 us -> 82.1 us  [send(): return lax.ppermute(x, 'expert', pairs)]
    pallas_call x0 -> x2, Pallas kernels: none -> 3.98 us  [the longest x1 1.99 us: sort_pages(): pl.pallas_call(sort_kernel, out_shape=jax.ShapeDtypeStruct((owners * PCAP...]
    ppermute x33, starting transfers between devices: 39 us -> 41.2 us  [send(): return lax.ppermute(x, 'expert', pairs)]
  transfers between devices with their start and end apart: 34 -> 34, of which waited for: 17 -> 18; matrix products, arithmetic and copies ran while one was open for 8% -> 1% of each run, Pallas kernels for 19% -> 21%
where the time goes in v5:
time: 181 us
  waiting for transfers between devices  82.1 us (45%)
  starting transfers between devices  44.7 us (25%)
  Pallas kernels  38.2 us (21%)
  local copies, waits for them, and re-layouts  10.7 us (6%)
  matrix products  3.18 us (2%)
    ppermute x33, waiting for transfers between devices, send(): return lax.ppermute(x, 'expert', pairs)  82.1 us
    ppermute x33, starting transfers between devices, send(): return lax.ppermute(x, 'expert', pairs)  41.2 us
    pallas_call x2, Pallas kernels, apply(): pl.pallas_call(functools.partial(expert_kernel, len(pieces), steps), grid...  30.8 us
    unnamed x64, local copies, waits for them, and re-layouts  10.7 us
  transfers between devices with their start and end apart: 34, of which 18 were waited for; matrix products, arithmetic and copies ran while one was open for 1% of the time, Pallas kernels for 21%

profile of v5, /device:TPU:0, one launch (start us, length us, event | category | flops | bytes accessed | tf_op | source)
XLA Modules:
  0.0 180.5 jit_solution(16215839959323598482)
XLA Ops:
  5.5 2.6 %collective-permute-start = (bf16[64,4224]{1,0:T(8,128)(2,1)S(1)}, bf16[64,4224]{1,0:T(8,128)(2,1)S(1)}, u32[]{:S(2)}, u32[]{:S(2)}) collective-permute-start(bf16[64,4224]{1,0:T(8,128)(2,1)S(1)} %get-tuple-element.69), channel_id=1, source_target_pairs={{0,8},{1,9},{2,10},{3,11},{4,12},{5,13},{6,14},{7,15},{8,16},{9,17... | collective-permute-start | bytes 1622024 | tf_op jit(solution)/shard_map/ppermute | solution.py:90
  11.5 7.1 %collective-permute-done.2.refs_1_ = bf16[40,4096]{1,0:T(8,128)(2,1)S(1)} collective-permute-done((bf16[40,4096]{1,0:T(8,128)(2,1)S(1)}, bf16[40,4096]{1,0:T(8,128)(2,1)S(1)}, u32[]{:S(2)}, u32[]{:S(2)}) %collective-permute-start.2) | collective-permute-done | bytes 327712 | tf_op jit(solution)/shard_map/ppermute | solution.py:90
  18.6 7.5 %collective-permute-done.5.refs_2_ = bf16[40,4096]{1,0:T(8,128)(2,1)S(1)} collective-permute-done((bf16[40,4096]{1,0:T(8,128)(2,1)S(1)}, bf16[40,4096]{1,0:T(8,128)(2,1)S(1)}, u32[]{:S(2)}, u32[]{:S(2)}) %collective-permute-start.5) | collective-permute-done | bytes 327712 | tf_op jit(solution)/shard_map/ppermute | solution.py:90
  34.4 7.2 %collective-permute-done.3.refs_5_ = bf16[40,4096]{1,0:T(8,128)(2,1)S(1)} collective-permute-done((bf16[40,4096]{1,0:T(8,128)(2,1)S(1)}, bf16[40,4096]{1,0:T(8,128)(2,1)S(1)}, u32[]{:S(2)}, u32[]{:S(2)}) %collective-permute-start.3) | collective-permute-done | bytes 327712 | tf_op jit(solution)/shard_map/ppermute | solution.py:90
  41.5 6.1 %collective-permute-done.6.refs_6_ = bf16[40,4096]{1,0:T(8,128)(2,1)S(1)} collective-permute-done((bf16[40,4096]{1,0:T(8,128)(2,1)S(1)}, bf16[40,4096]{1,0:T(8,128)(2,1)S(1)}, u32[]{:S(2)}, u32[]{:S(2)}) %collective-permute-start.6) | collective-permute-done | bytes 327712 | tf_op jit(solution)/shard_map/ppermute | solution.py:90
  59.0 3.2 %collective-permute-done.4.refs_1_ = bf16[40,4096]{1,0:T(8,128)(2,1)S(1)} collective-permute-done((bf16[40,4096]{1,0:T(8,128)(2,1)S(1)}, bf16[40,4096]{1,0:T(8,128)(2,1)S(1)}, u32[]{:S(2)}, u32[]{:S(2)}) %collective-permute-start.4) | collective-permute-done | bytes 327712 | tf_op jit(solution)/shard_map/ppermute | solution.py:90
  62.1 6.6 %collective-permute-done.7.refs_2_ = bf16[40,4096]{1,0:T(8,128)(2,1)S(1)} collective-permute-done((bf16[40,4096]{1,0:T(8,128)(2,1)S(1)}, bf16[40,4096]{1,0:T(8,128)(2,1)S(1)}, u32[]{:S(2)}, u32[]{:S(2)}) %collective-permute-start.7) | collective-permute-done | bytes 327712 | tf_op jit(solution)/shard_map/ppermute | solution.py:90
  74.7 15.4 %shard_map.98 = (bf16[40,4096]{1,0:T(8,128)(2,1)}, bf16[40,4096]{1,0:T(8,128)(2,1)}, bf16[40,4096]{1,0:T(8,128)(2,1)}, bf16[40,4096]{1,0:T(8,128)(2,1)}, bf16[40...) custom-call(bf16[40,4096]{1,0:T(8,128)(2,1)} %copy-done.3, ...), custom_call_target="tpu_custom_call" | custom-call | flops 6039797760 | bytes 24117248 | tf_op jit(solution)/shard_map/pallas_call | solution.py:236
  90.1 3.5 %all-to-all-start = ((bf16[32,16,1152]{2,1,0:T(8,128)(2,1)}), bf16[32,16,1152]{2,1,0:T(8,128)(2,1)S(1)}, u32[]{:S(2)}, u32[]{:S(2)}) async-start(bf16[32,16,1152]{2,1,0:T(8,128)(2,1)} %shard_map.101), calls=%async_computation | async-start | bytes 2359296 | tf_op jit(solution)/shard_map/all_to_all | solution.py:81
  93.6 2.7 %collective-permute-start.21 = (bf16[40,4096]{1,0:T(8,128)(2,1)}, bf16[40,4096]{1,0:T(8,128)(2,1)S(1)}, u32[]{:S(2)}, u32[]{:S(2)}) collective-permute-start(bf16[40,4096]{1,0:T(8,128)(2,1)} %get-tuple-element.113), channel_id=1, source_target_pairs={{0,6},{1,7},{2,4},{3,5},{4,2},{5,3},{6,0},{7,1},{8,14},{9,15},{10,... | collective-permute-start | bytes 983048 | tf_op jit(solution)/shard_map/ppermute | solution.py:90
  97.2 15.4 %shard_map.100 = (bf16[40,4096]{1,0:T(8,128)(2,1)}, bf16[40,4096]{1,0:T(8,128)(2,1)}, bf16[40,4096]{1,0:T(8,128)(2,1)}, bf16[40,4096]{1,0:T(8,128)(2,1)}, bf16[4...) custom-call(bf16[40,4096]{1,0:T(8,128)(2,1)} %copy-done.4, ...), custom_call_target="tpu_custom_call" | custom-call | flops 6039797760 | bytes 24117248 | tf_op jit(solution)/shard_map/pallas_call | solution.py:236
  112.6 3.8 %collective-permute-done.21 = bf16[40,4096]{1,0:T(8,128)(2,1)S(1)} collective-permute-done((bf16[40,4096]{1,0:T(8,128)(2,1)}, bf16[40,4096]{1,0:T(8,128)(2,1)S(1)}, u32[]{:S(2)}, u32[]{:S(2)}) %collective-permute-start.21) | collective-permute-done | bytes 327712 | tf_op jit(solution)/shard_map/ppermute | solution.py:90
  116.3 6.8 %collective-permute-done.18 = bf16[40,4096]{1,0:T(8,128)(2,1)S(1)} collective-permute-done((bf16[40,4096]{1,0:T(8,128)(2,1)}, bf16[40,4096]{1,0:T(8,128)(2,1)S(1)}, u32[]{:S(2)}, u32[]{:S(2)}) %collective-permute-start.18) | collective-permute-done | bytes 327712 | tf_op jit(solution)/shard_map/ppermute | solution.py:90
  123.7 2.0 %collective-permute-start.30 = (bf16[64,4096]{1,0:T(8,128)(2,1)S(1)}, bf16[64,4096]{1,0:T(8,128)(2,1)S(1)}, u32[]{:S(2)}, u32[]{:S(2)}) collective-permute-start(bf16[64,4096]{1,0:T(8,128)(2,1)S(1)} %convolution_convert_fusion), channel_id=1, source_target_pairs={{0,8},{1,9},{2,10},{3,11},{4,12},{5,13},{6,14},{7,15},{8,16},{9,17... | collective-permute-start | bytes 1572872 | tf_op jit(solution)/shard_map/ppermute | solution.py:90
  129.2 7.2 %collective-permute-done.24 = bf16[40,4096]{1,0:T(8,128)(2,1)S(1)} collective-permute-done((bf16[40,4096]{1,0:T(8,128)(2,1)S(1)}, bf16[40,4096]{1,0:T(8,128)(2,1)S(1)}, u32[]{:S(2)}, u32[]{:S(2)}) %collective-permute-start.24) | collective-permute-done | bytes 327712 | tf_op jit(solution)/shard_map/ppermute | solution.py:90
  136.4 6.0 %collective-permute-done.19 = bf16[40,4096]{1,0:T(8,128)(2,1)S(1)} collective-permute-done((bf16[40,4096]{1,0:T(8,128)(2,1)S(1)}, bf16[40,4096]{1,0:T(8,128)(2,1)S(1)}, u32[]{:S(2)}, u32[]{:S(2)}) %collective-permute-start.19) | collective-permute-done | bytes 327712 | tf_op jit(solution)/shard_map/ppermute | solution.py:90
  144.1 2.9 %collective-permute-start.31 = (bf16[64,4096]{1,0:T(8,128)(2,1)S(1)}, bf16[64,4096]{1,0:T(8,128)(2,1)S(1)}, u32[]{:S(2)}, u32[]{:S(2)}) collective-permute-start(bf16[64,4096]{1,0:T(8,128)(2,1)S(1)} %fusion.2), channel_id=1, source_target_pairs={{0,8},{1,9},{2,10},{3,11},{4,12},{5,13},{6,14},{7,15},{8,16},{9,17... | collective-permute-start | bytes 1572872 | tf_op jit(solution)/shard_map/ppermute | solution.py:90
  148.0 2.6 %collective-permute-start.29 = (bf16[40,4096]{1,0:T(8,128)(2,1)S(1)}, bf16[40,4096]{1,0:T(8,128)(2,1)S(1)}, u32[]{:S(2)}, u32[]{:S(2)}) collective-permute-start(bf16[40,4096]{1,0:T(8,128)(2,1)S(1)} %copy-done.21), channel_id=1, source_target_pairs={{0,6},{1,7},{2,4},{3,5},{4,2},{5,3},{6,0},{7,1},{8,14},{9,15},{10,... | collective-permute-start | bytes 983048 | tf_op jit(solution)/shard_map/ppermute | solution.py:90
  150.6 7.1 %collective-permute-done.25 = bf16[40,4096]{1,0:T(8,128)(2,1)S(1)} collective-permute-done((bf16[40,4096]{1,0:T(8,128)(2,1)S(1)}, bf16[40,4096]{1,0:T(8,128)(2,1)S(1)}, u32[]{:S(2)}, u32[]{:S(2)}) %collective-permute-start.25) | collective-permute-done | bytes 327712 | tf_op jit(solution)/shard_map/ppermute | solution.py:90
  157.7 4.0 %collective-permute-done.29 = bf16[40,4096]{1,0:T(8,128)(2,1)S(1)} collective-permute-done((bf16[40,4096]{1,0:T(8,128)(2,1)S(1)}, bf16[40,4096]{1,0:T(8,128)(2,1)S(1)}, u32[]{:S(2)}, u32[]{:S(2)}) %collective-permute-start.29) | collective-permute-done | bytes 327712 | tf_op jit(solution)/shard_map/ppermute | solution.py:90
  162.1 2.1 %collective-permute-start.32 = (bf16[64,4096]{1,0:T(8,128)(2,1)S(1)}, bf16[64,4096]{1,0:T(8,128)(2,1)S(1)}, u32[]{:S(2)}, u32[]{:S(2)}) collective-permute-start(bf16[64,4096]{1,0:T(8,128)(2,1)S(1)} %fusion.1), channel_id=1, source_target_pairs={{0,8},{1,9},{2,10},{3,11},{4,12},{5,13},{6,14},{7,15},{8,16},{9,17... | collective-permute-start | bytes 1572872 | tf_op jit(solution)/shard_map/ppermute | solution.py:90
  170.3 3.0 %collective-permute-done.32 = bf16[64,4096]{1,0:T(8,128)(2,1)S(1)} collective-permute-done((bf16[64,4096]{1,0:T(8,128)(2,1)S(1)}, bf16[64,4096]{1,0:T(8,128)(2,1)S(1)}, u32[]{:S(2)}, u32[]{:S(2)}) %collective-permute-start.32) | collective-permute-done | bytes 524320 | tf_op jit(solution)/shard_map/ppermute | solution.py:90
  173.9 3.4 %collective-permute-done.23 = bf16[40,4096]{1,0:T(8,128)(2,1)S(1)} collective-permute-done((bf16[40,4096]{1,0:T(8,128)(2,1)S(1)}, bf16[40,4096]{1,0:T(8,128)(2,1)S(1)}, u32[]{:S(2)}, u32[]{:S(2)}) %collective-permute-start.23) | collective-permute-done | bytes 327712 | tf_op jit(solution)/shard_map/ppermute | solution.py:90
  178.4 2.1 %fusion = bf16[64,4096]{1,0:T(8,128)(2,1)} fusion(bf16[64,160]{1,0:T(8,128)(2,1)S(1)} %get-tuple-element.67, bf16[40,4096]{1,0:T(8,128)(2,1)S(1)} %collective-permute-done.26, bf16[40,4096]{1,0:T(8,128)(2,1)S(1)} %collective-permute-done.23, bf16[40,4096]{1,0:T(8,128)(2,1)S(1)} %collective-permute-done.20, bf16[40,4096]{1,0:T(8,128)(2,1)} %get-tuple-element.90, ...), kind=kOutput, calls=%fused_computation.3 | convolution fusion | flops 89915392 | bytes 2379776 | tf_op jit(solution)/shard_map/dot_general | solution.py:333
  (121 shorter events, 49.6 us)
Async XLA Ops:
  5.0 21.1 %collective-permute-start.11 = (bf16[4096,384]{1,0:T(8,128)(2,1)}, bf16[4096,384]{1,0:T(8,128)(2,1)S(1)}, u32[]{:S(2)}, u32[]{:S(2)}) collective-permute-start(bf16[4096,384]{1,0:T(8,128)(2,1)} %refs_8_.3), channel_id=1, source_target_pairs={{0,1},{1,0},{2,3},{3,2},{4,5},{5,4},{6,7},{7,6},{8,9},{9,8},{10,11... | collective-permute-start | bytes 9437192 | tf_op jit(solution)/shard_map/ppermute | solution.py:90
  5.5 20.7 %collective-permute-start = (bf16[64,4224]{1,0:T(8,128)(2,1)S(1)}, bf16[64,4224]{1,0:T(8,128)(2,1)S(1)}, u32[]{:S(2)}, u32[]{:S(2)}) collective-permute-start(bf16[64,4224]{1,0:T(8,128)(2,1)S(1)} %get-tuple-element.69), channel_id=1, source_target_pairs={{0,8},{1,9},{2,10},{3,11},{4,12},{5,13},{6,14},{7,15},{8,16},{9,17... | collective-permute-start | bytes 1622024 | tf_op jit(solution)/shard_map/ppermute | solution.py:90
  9.5 16.6 %collective-permute-start.5 = (bf16[40,4096]{1,0:T(8,128)(2,1)S(1)}, bf16[40,4096]{1,0:T(8,128)(2,1)S(1)}, u32[]{:S(2)}, u32[]{:S(2)}) collective-permute-start(bf16[40,4096]{1,0:T(8,128)(2,1)S(1)} %get-tuple-element.77), channel_id=1, source_target_pairs={{0,4},{1,5},{2,6},{3,7},{4,0},{5,1},{6,2},{7,3},{8,12},{9,13},{10,... | collective-permute-start | bytes 983048 | tf_op jit(solution)/shard_map/ppermute | solution.py:90
  11.1 15.1 %collective-permute-start.8 = (bf16[40,4096]{1,0:T(8,128)(2,1)S(1)}, bf16[40,4096]{1,0:T(8,128)(2,1)S(1)}, u32[]{:S(2)}, u32[]{:S(2)}) collective-permute-start(bf16[40,4096]{1,0:T(8,128)(2,1)S(1)} %get-tuple-element.82), channel_id=1, source_target_pairs={{0,6},{1,7},{2,4},{3,5},{4,2},{5,3},{6,0},{7,1},{8,14},{9,15},{10,... | collective-permute-start | bytes 983048 | tf_op jit(solution)/shard_map/ppermute | solution.py:90
  26.2 21.5 %collective-permute-start.12 = (bf16[4096,384]{1,0:T(8,128)(2,1)}, bf16[4096,384]{1,0:T(8,128)(2,1)S(1)}, u32[]{:S(2)}, u32[]{:S(2)}) collective-permute-start(bf16[4096,384]{1,0:T(8,128)(2,1)} %refs_10_.3), channel_id=1, source_target_pairs={{0,1},{1,0},{2,3},{3,2},{4,5},{5,4},{6,7},{7,6},{8,9},{9,8},{10,11... | collective-permute-start | bytes 9437192 | tf_op jit(solution)/shard_map/ppermute | solution.py:90
  27.8 19.8 %collective-permute-start.1 = (bf16[64,4224]{1,0:T(8,128)(2,1)S(1)}, bf16[64,4224]{1,0:T(8,128)(2,1)S(1)}, u32[]{:S(2)}, u32[]{:S(2)}) collective-permute-start(bf16[64,4224]{1,0:T(8,128)(2,1)S(1)} %collective-permute-done.block_ref), channel_id=1, source_target_pairs={{0,8},{1,9},{2,10},{3,11},{4,12},{5,13},{6,14},{7,15},{8,16},{9,17... | collective-permute-start | bytes 1622024 | tf_op jit(solution)/shard_map/ppermute | solution.py:90
  32.1 15.5 %collective-permute-start.6 = (bf16[40,4096]{1,0:T(8,128)(2,1)S(1)}, bf16[40,4096]{1,0:T(8,128)(2,1)S(1)}, u32[]{:S(2)}, u32[]{:S(2)}) collective-permute-start(bf16[40,4096]{1,0:T(8,128)(2,1)S(1)} %get-tuple-element.78), channel_id=1, source_target_pairs={{0,4},{1,5},{2,6},{3,7},{4,0},{5,1},{6,2},{7,3},{8,12},{9,13},{10,... | collective-permute-start | bytes 983048 | tf_op jit(solution)/shard_map/ppermute | solution.py:90
  32.9 14.7 %collective-permute-start.9 = (bf16[40,4096]{1,0:T(8,128)(2,1)S(1)}, bf16[40,4096]{1,0:T(8,128)(2,1)S(1)}, u32[]{:S(2)}, u32[]{:S(2)}) collective-permute-start(bf16[40,4096]{1,0:T(8,128)(2,1)S(1)} %get-tuple-element.83), channel_id=1, source_target_pairs={{0,6},{1,7},{2,4},{3,5},{4,2},{5,3},{6,0},{7,1},{8,14},{9,15},{10,... | collective-permute-start | bytes 983048 | tf_op jit(solution)/shard_map/ppermute | solution.py:90
  48.5 26.2 %collective-permute-start.13 = (bf16[384,4096]{1,0:T(8,128)(2,1)}, bf16[384,4096]{1,0:T(8,128)(2,1)}, u32[]{:S(2)}, u32[]{:S(2)}) collective-permute-start(bf16[384,4096]{1,0:T(8,128)(2,1)} %refs_12_.3), channel_id=1, source_target_pairs={{0,1},{1,0},{2,3},{3,2},{4,5},{5,4},{6,7},{7,6},{8,9},{9,8},{10,11... | collective-permute-start | bytes 9437192 | tf_op jit(solution)/shard_map/ppermute | solution.py:90
  48.5 21.1 %collective-permute-start.14 = (bf16[64,4224]{1,0:T(8,128)(2,1)S(1)}, bf16[64,4224]{1,0:T(8,128)(2,1)S(1)}, u32[]{:S(2)}, u32[]{:S(2)}) collective-permute-start(bf16[64,4224]{1,0:T(8,128)(2,1)S(1)} %collective-permute-done.1.block_ref), channel_id=1, source_target_pairs={{0,8},{1,9},{2,10},{3,11},{4,12},{5,13},{6,14},{7,15},{8,16},{9,17... | collective-permute-start | bytes 1622024 | tf_op jit(solution)/shard_map/ppermute | solution.py:90
  52.2 16.6 %collective-permute-start.7 = (bf16[40,4096]{1,0:T(8,128)(2,1)S(1)}, bf16[40,4096]{1,0:T(8,128)(2,1)S(1)}, u32[]{:S(2)}, u32[]{:S(2)}) collective-permute-start(bf16[40,4096]{1,0:T(8,128)(2,1)S(1)} %get-tuple-element.79), channel_id=1, source_target_pairs={{0,4},{1,5},{2,6},{3,7},{4,0},{5,1},{6,2},{7,3},{8,12},{9,13},{10,... | collective-permute-start | bytes 983048 | tf_op jit(solution)/shard_map/ppermute | solution.py:90
  53.6 15.2 %collective-permute-start.10 = (bf16[40,4096]{1,0:T(8,128)(2,1)S(1)}, bf16[40,4096]{1,0:T(8,128)(2,1)S(1)}, u32[]{:S(2)}, u32[]{:S(2)}) collective-permute-start(bf16[40,4096]{1,0:T(8,128)(2,1)S(1)} %get-tuple-element.84), channel_id=1, source_target_pairs={{0,6},{1,7},{2,4},{3,5},{4,2},{5,3},{6,0},{7,1},{8,14},{9,15},{10,... | collective-permute-start | bytes 983048 | tf_op jit(solution)/shard_map/ppermute | solution.py:90
  71.1 25.8 %collective-permute-start.15 = (bf16[40,4096]{1,0:T(8,128)(2,1)S(1)}, bf16[40,4096]{1,0:T(8,128)(2,1)}, u32[]{:S(2)}, u32[]{:S(2)}) collective-permute-start(bf16[40,4096]{1,0:T(8,128)(2,1)S(1)} %get-tuple-element.102), channel_id=1, source_target_pairs={{0,2},{1,3},{2,0},{3,1},{4,6},{5,7},{6,4},{7,5},{8,10},{9,11},{10,... | collective-permute-start | bytes 983048 | tf_op jit(solution)/shard_map/ppermute | solution.py:90
  72.6 23.8 %collective-permute-start.16 = (bf16[40,4096]{1,0:T(8,128)(2,1)S(1)}, bf16[40,4096]{1,0:T(8,128)(2,1)}, u32[]{:S(2)}, u32[]{:S(2)}) collective-permute-start(bf16[40,4096]{1,0:T(8,128)(2,1)S(1)} %get-tuple-element.104), channel_id=1, source_target_pairs={{0,4},{1,5},{2,6},{3,7},{4,0},{5,1},{6,2},{7,3},{8,12},{9,13},{10,... | collective-permute-start | bytes 983048 | tf_op jit(solution)/shard_map/ppermute | solution.py:90
  73.1 20.5 %collective-permute-start.17 = (bf16[40,4096]{1,0:T(8,128)(2,1)S(1)}, bf16[40,4096]{1,0:T(8,128)(2,1)S(1)}, u32[]{:S(2)}, u32[]{:S(2)}) collective-permute-start(bf16[40,4096]{1,0:T(8,128)(2,1)S(1)} %get-tuple-element.106), channel_id=1, source_target_pairs={{0,6},{1,7},{2,4},{3,5},{4,2},{5,3},{6,0},{7,1},{8,14},{9,15},{10,... | collective-permute-start | bytes 983048 | tf_op jit(solution)/shard_map/ppermute | solution.py:90
  90.1 74.1 %all-to-all-start = ((bf16[32,16,1152]{2,1,0:T(8,128)(2,1)}), bf16[32,16,1152]{2,1,0:T(8,128)(2,1)S(1)}, u32[]{:S(2)}, u32[]{:S(2)}) async-start(bf16[32,16,1152]{2,1,0:T(8,128)(2,1)} %shard_map.101), calls=%async_computation | async-start | bytes 2359296 | tf_op jit(solution)/shard_map/all_to_all | solution.py:81
  93.6 22.7 %collective-permute-start.21 = (bf16[40,4096]{1,0:T(8,128)(2,1)}, bf16[40,4096]{1,0:T(8,128)(2,1)S(1)}, u32[]{:S(2)}, u32[]{:S(2)}) collective-permute-start(bf16[40,4096]{1,0:T(8,128)(2,1)} %get-tuple-element.113), channel_id=1, source_target_pairs={{0,6},{1,7},{2,4},{3,5},{4,2},{5,3},{6,0},{7,1},{8,14},{9,15},{10,... | collective-permute-start | bytes 983048 | tf_op jit(solution)/shard_map/ppermute | solution.py:90
  96.4 26.8 %collective-permute-start.18 = (bf16[40,4096]{1,0:T(8,128)(2,1)}, bf16[40,4096]{1,0:T(8,128)(2,1)S(1)}, u32[]{:S(2)}, u32[]{:S(2)}) collective-permute-start(bf16[40,4096]{1,0:T(8,128)(2,1)} %get-tuple-element.108), channel_id=1, source_target_pairs={{0,4},{1,5},{2,6},{3,7},{4,0},{5,1},{6,2},{7,3},{8,12},{9,13},{10,... | collective-permute-start | bytes 983048 | tf_op jit(solution)/shard_map/ppermute | solution.py:90
  96.9 26.5 %collective-permute-start.27 = (bf16[40,4096]{1,0:T(8,128)(2,1)}, bf16[40,4096]{1,0:T(8,128)(2,1)S(1)}, u32[]{:S(2)}, u32[]{:S(2)}) collective-permute-start(bf16[40,4096]{1,0:T(8,128)(2,1)} %get-tuple-element.125), channel_id=1, source_target_pairs={{0,2},{1,3},{2,0},{3,1},{4,6},{5,7},{6,4},{7,5},{8,10},{9,11},{10,... | collective-permute-start | bytes 983048 | tf_op jit(solution)/shard_map/ppermute | solution.py:90
  123.7 20.0 %collective-permute-start.30 = (bf16[64,4096]{1,0:T(8,128)(2,1)S(1)}, bf16[64,4096]{1,0:T(8,128)(2,1)S(1)}, u32[]{:S(2)}, u32[]{:S(2)}) collective-permute-start(bf16[64,4096]{1,0:T(8,128)(2,1)S(1)} %convolution_convert_fusion), channel_id=1, source_target_pairs={{0,8},{1,9},{2,10},{3,11},{4,12},{5,13},{6,14},{7,15},{8,16},{9,17... | collective-permute-start | bytes 1572872 | tf_op jit(solution)/shard_map/ppermute | solution.py:90
  126.5 15.9 %collective-permute-start.19 = (bf16[40,4096]{1,0:T(8,128)(2,1)S(1)}, bf16[40,4096]{1,0:T(8,128)(2,1)S(1)}, u32[]{:S(2)}, u32[]{:S(2)}) collective-permute-start(bf16[40,4096]{1,0:T(8,128)(2,1)S(1)} %copy-done.26), channel_id=1, source_target_pairs={{0,6},{1,7},{2,4},{3,5},{4,2},{5,3},{6,0},{7,1},{8,14},{9,15},{10,... | collective-permute-start | bytes 983048 | tf_op jit(solution)/shard_map/ppermute | solution.py:90
  128.3 15.4 %collective-permute-start.28 = (bf16[40,4096]{1,0:T(8,128)(2,1)S(1)}, bf16[40,4096]{1,0:T(8,128)(2,1)S(1)}, u32[]{:S(2)}, u32[]{:S(2)}) collective-permute-start(bf16[40,4096]{1,0:T(8,128)(2,1)S(1)} %copy-done.25), channel_id=1, source_target_pairs={{0,4},{1,5},{2,6},{3,7},{4,0},{5,1},{6,2},{7,3},{8,12},{9,13},{10,... | collective-permute-start | bytes 983048 | tf_op jit(solution)/shard_map/ppermute | solution.py:90
  144.1 17.6 %collective-permute-start.31 = (bf16[64,4096]{1,0:T(8,128)(2,1)S(1)}, bf16[64,4096]{1,0:T(8,128)(2,1)S(1)}, u32[]{:S(2)}, u32[]{:S(2)}) collective-permute-start(bf16[64,4096]{1,0:T(8,128)(2,1)S(1)} %fusion.2), channel_id=1, source_target_pairs={{0,8},{1,9},{2,10},{3,11},{4,12},{5,13},{6,14},{7,15},{8,16},{9,17... | collective-permute-start | bytes 1572872 | tf_op jit(solution)/shard_map/ppermute | solution.py:90
  148.0 13.7 %collective-permute-start.29 = (bf16[40,4096]{1,0:T(8,128)(2,1)S(1)}, bf16[40,4096]{1,0:T(8,128)(2,1)S(1)}, u32[]{:S(2)}, u32[]{:S(2)}) collective-permute-start(bf16[40,4096]{1,0:T(8,128)(2,1)S(1)} %copy-done.21), channel_id=1, source_target_pairs={{0,6},{1,7},{2,4},{3,5},{4,2},{5,3},{6,0},{7,1},{8,14},{9,15},{10,... | collective-permute-start | bytes 983048 | tf_op jit(solution)/shard_map/ppermute | solution.py:90
  (41 other events, 520.3 us)

commit v6 on v5

--- a/solution.py
+++ b/solution.py
@@ -136,42 +136,42 @@
 
 def pick_kernel(experts, capacity, step, chip_ref, block_ref, *outs):
     width = outs[0].shape[1]
-    blend_ref = outs[PLANE]
+    blend_ref = outs[PLANE - 1]
     placing, blend = slots_of(block_ref[:, width : width + experts], capacity, chip_ref[0])
     blend_ref[...] = blend
     for at in range(0, width, step):
         found = pick(placing, block_ref[:, at : at + step])
-        for j in range(PLANE):
-            outs[j][:, at : at + step] = found[capacity * j : capacity * (j + 1)].astype(
-                jnp.bfloat16
-            )
+        for j in range(1, PLANE):
+            part = found[capacity * j : capacity * (j + 1)]
+            outs[j - 1][:, at : at + step] = part.astype(jnp.bfloat16)
 
 
 def first_kernel(experts, capacity, step, chip_ref, tokens_ref, ids_ref, gates_ref, *outs):
     rows, width = tokens_ref.shape
-    block_ref = outs[PLANE + 1]
-    gates = gates_ref[...]
+    block_ref = outs[PLANE]
+    ids = ids_ref[...].astype(jnp.float32).T.astype(jnp.int32)
+    gates = gates_ref[...].T
     shares = gates / jnp.sum(gates, axis=1, keepdims=True)
     mixing = shares.astype(jnp.bfloat16).astype(jnp.float32)
     lane = lax.broadcasted_iota(jnp.int32, (rows, block_ref.shape[1] - width), 1)
     table = jnp.zeros(lane.shape, jnp.float32)
     for k in range(gates.shape[1]):
-        table = table + jnp.where(ids_ref[:, k : k + 1] == lane, mixing[:, k : k + 1], 0.0)
+        table = table + jnp.where(ids[:, k : k + 1] == lane, mixing[:, k : k + 1], 0.0)
     block_ref[:, width:] = table.astype(jnp.bfloat16)
     block_ref[:, :width] = tokens_ref[...]
-    pick_kernel(experts, capacity, step, chip_ref, block_ref, *outs[: PLANE + 1])
+    pick_kernel(experts, capacity, step, chip_ref, block_ref, *outs[:PLANE])
 
 
 def pick_pieces(chip, block, width, experts, capacity, routing=None):
     rows = block.shape[0]
     piece = jax.ShapeDtypeStruct((capacity, width), jnp.bfloat16)
-    outs = [piece] * PLANE + [jax.ShapeDtypeStruct((rows, PLANE * capacity), jnp.bfloat16)]
+    outs = [piece] * (PLANE - 1) + [jax.ShapeDtypeStruct((rows, PLANE * capacity), jnp.bfloat16)]
     if routing:
         lanes = experts + -experts % 128
         outs.append(jax.ShapeDtypeStruct((rows, width + lanes), jnp.bfloat16))
     body = first_kernel if routing else pick_kernel
-    operands = (block, *routing) if routing else (block,)
-    return pl.pallas_call(
+    operands = (block, routing[0].T, routing[1].T) if routing else (block,)
+    found = pl.pallas_call(
         functools.partial(body, experts, capacity, 512),
         out_shape=outs,
         in_specs=[pl.BlockSpec(memory_space=pltpu.SMEM)]
@@ -184,6 +184,8 @@
             transcendentals=0,
         ),
     )(jnp.reshape(chip, (1,)), *operands)
+    placing = (found[PLANE - 1][:, :capacity] > 0).astype(jnp.bfloat16)
+    return [pick(placing, block[:, :width]).astype(jnp.bfloat16), *found]
 
 
 def expert_kernel(pieces, steps, *refs):
@@ -301,7 +303,7 @@
             )
         blends.append(blend)
         if s < 3:
-            earlier = [block] + (got[s - 1][1:] if s else [])
+            earlier = [block] + (got[s - 1][1:] if s else []) + ([outgoing] if s == 1 else [])
             swapped.append(send(after(weights[s], *swapped, *earlier), flip=1))
         for j in range(1, PLANE):
             piece = after(pieces[j], got[s - 1][j]) if s else pieces[j]
@@ -316,7 +318,7 @@
         held[0][0] = after(held[0][0], *outs, *following)
         outs.extend(work(held, *zip(weights, swapped)))
 
-    arrived = exchange(after(outgoing, outs[0]))
+    arrived = exchange(after(outgoing, *got[-2][1:], block))
     order = list(range(1, planes)) + [0]
     sent, landed = {}, got[-1][1:]
     for s in order:

time: 181 us -> 167 us (0.923)
  waiting for transfers between devices: 82.1 us -> 71.4 us
  local copies, waits for them, and re-layouts: 10.7 us -> 5.14 us
  matrix products: 3.18 us -> 7.31 us
  starting transfers between devices: 44.7 us -> 42.5 us
    ppermute x33, waiting for transfers between devices: 82.1 us -> 71.4 us  [send(): return lax.ppermute(x, 'expert', pairs)]
    unnamed x64 -> x58, local copies, waits for them, and re-layouts: 10.7 us -> 5.14 us
    dot_general x0 -> x4, matrix products: none -> 4.13 us  [pick(): lax.dot_general(placing, rows, (((0,), (0,)), ((), ())), preferred_elemen...]
    ppermute x33, starting transfers between devices: 41.2 us -> 39 us  [send(): return lax.ppermute(x, 'expert', pairs)]
  transfers between devices with their start and end apart: 34 -> 34, of which waited for: 18 -> 16; matrix products, arithmetic and copies ran while one was open for 1% -> 4% of each run, Pallas kernels for 21% -> 22%
where the time goes in v6:
time: 167 us; the launch traced here: 166 us
  waiting for transfers between devices  71.4 us (43%)
  starting transfers between devices  42.5 us (25%)
  Pallas kernels  38.1 us (23%)
  matrix products  7.31 us (4%)
  local copies, waits for them, and re-layouts  5.14 us (3%)
    ppermute x33, waiting for transfers between devices, send(): return lax.ppermute(x, 'expert', pairs)  71.4 us
    ppermute x33, starting transfers between devices, send(): return lax.ppermute(x, 'expert', pairs)  39 us
    pallas_call x2, Pallas kernels, apply(): pl.pallas_call(functools.partial(expert_kernel, len(pieces), steps), grid...  30.7 us
    unnamed x58, local copies, waits for them, and re-layouts  5.14 us
    dot_general x4, matrix products, pick(): lax.dot_general(placing, rows, (((0,), (0,)), ((), ())), preferred_elemen...  4.13 us
    all_to_all x1, starting transfers between devices, exchange(): return lax.all_to_all(x, 'expert', split_axis=0, concat_axis=0, tiled=True)  3.57 us
    pallas_call x4, Pallas kernels, pick_pieces(): pl.pallas_call(functools.partial(body, experts, capacity, 512), out_shape...  3.45 us
  transfers between devices with their start and end apart: 34, of which 16 were waited for; matrix products, arithmetic and copies ran while one was open for 4% of the time, Pallas kernels for 22%

profile of v6, /device:TPU:0, one launch (start us, length us, event | category | flops | bytes accessed | tf_op | source)
XLA Modules:
  0.0 166.1 jit_solution(13767404360672103150)
XLA Ops:
  4.7 2.6 %collective-permute-start = (bf16[64,4224]{1,0:T(8,128)(2,1)S(1)}, bf16[64,4224]{1,0:T(8,128)(2,1)S(1)}, u32[]{:S(2)}, u32[]{:S(2)}) collective-permute-start(bf16[64,4224]{1,0:T(8,128)(2,1)S(1)} %get-tuple-element.64), channel_id=1, source_target_pairs={{0,8},{1,9},{2,10},{3,11},{4,12},{5,13},{6,14},{7,15},{8,16},{9,17... | collective-permute-start | bytes 1622024 | tf_op jit(solution)/shard_map/ppermute | solution.py:90
  12.7 2.0 %shard_map.98 = bf16[32,16,1152]{2,1,0:T(8,128)(2,1)} custom-call(s32[32]{0:T(128)S(1)} %copy-done.5, bf16[32,16,1024]{2,1,0:T(8,128)(2,1)S(1)} %copy-done.2), custom_call_target="tpu_custom_call" | custom-call | bytes 3145728 | tf_op jit(solution)/shard_map/pallas_call | solution.py:34
  14.7 3.2 %collective-permute-done.2.refs_1_ = bf16[40,4096]{1,0:T(8,128)(2,1)S(1)} collective-permute-done((bf16[40,4096]{1,0:T(8,128)(2,1)S(1)}, bf16[40,4096]{1,0:T(8,128)(2,1)S(1)}, u32[]{:S(2)}, u32[]{:S(2)}) %collective-permute-start.2) | collective-permute-done | bytes 327712 | tf_op jit(solution)/shard_map/ppermute | solution.py:90
  17.9 7.5 %collective-permute-done.5.refs_2_ = bf16[40,4096]{1,0:T(8,128)(2,1)S(1)} collective-permute-done((bf16[40,4096]{1,0:T(8,128)(2,1)S(1)}, bf16[40,4096]{1,0:T(8,128)(2,1)S(1)}, u32[]{:S(2)}, u32[]{:S(2)}) %collective-permute-start.5) | collective-permute-done | bytes 327712 | tf_op jit(solution)/shard_map/ppermute | solution.py:90
  32.1 7.1 %collective-permute-done.3.refs_5_ = bf16[40,4096]{1,0:T(8,128)(2,1)S(1)} collective-permute-done((bf16[40,4096]{1,0:T(8,128)(2,1)S(1)}, bf16[40,4096]{1,0:T(8,128)(2,1)S(1)}, u32[]{:S(2)}, u32[]{:S(2)}) %collective-permute-start.3) | collective-permute-done | bytes 327712 | tf_op jit(solution)/shard_map/ppermute | solution.py:90
  39.2 5.6 %collective-permute-done.6.refs_6_ = bf16[40,4096]{1,0:T(8,128)(2,1)S(1)} collective-permute-done((bf16[40,4096]{1,0:T(8,128)(2,1)S(1)}, bf16[40,4096]{1,0:T(8,128)(2,1)S(1)}, u32[]{:S(2)}, u32[]{:S(2)}) %collective-permute-start.6) | collective-permute-done | bytes 327712 | tf_op jit(solution)/shard_map/ppermute | solution.py:90
  55.6 5.0 %collective-permute-done.4.refs_1_ = bf16[40,4096]{1,0:T(8,128)(2,1)S(1)} collective-permute-done((bf16[40,4096]{1,0:T(8,128)(2,1)S(1)}, bf16[40,4096]{1,0:T(8,128)(2,1)S(1)}, u32[]{:S(2)}, u32[]{:S(2)}) %collective-permute-start.4) | collective-permute-done | bytes 327712 | tf_op jit(solution)/shard_map/ppermute | solution.py:90
  60.5 6.8 %collective-permute-done.7.refs_2_ = bf16[40,4096]{1,0:T(8,128)(2,1)S(1)} collective-permute-done((bf16[40,4096]{1,0:T(8,128)(2,1)S(1)}, bf16[40,4096]{1,0:T(8,128)(2,1)S(1)}, u32[]{:S(2)}, u32[]{:S(2)}) %collective-permute-start.7) | collective-permute-done | bytes 327712 | tf_op jit(solution)/shard_map/ppermute | solution.py:90
  71.8 3.6 %all-to-all-start = ((bf16[32,16,1152]{2,1,0:T(8,128)(2,1)}), bf16[32,16,1152]{2,1,0:T(8,128)(2,1)S(1)}, u32[]{:S(2)}, u32[]{:S(2)}) async-start(bf16[32,16,1152]{2,1,0:T(8,128)(2,1)} %shard_map.98), calls=%async_computation | async-start | bytes 2359296 | tf_op jit(solution)/shard_map/all_to_all | solution.py:81
  76.4 15.4 %shard_map.99 = (bf16[40,4096]{1,0:T(8,128)(2,1)}, bf16[40,4096]{1,0:T(8,128)(2,1)}, bf16[40,4096]{1,0:T(8,128)(2,1)}, bf16[40,4096]{1,0:T(8,128)(2,1)}, bf16[40...) custom-call(bf16[40,4096]{1,0:T(8,128)(2,1)} %convolution_convert_fusion.4.re, ...), custom_call_target="tpu_custom_call" | custom-call | flops 6039797760 | bytes 24117248 | tf_op jit(solution)/shard_map/pallas_call | solution.py:238
  91.8 2.4 %collective-permute-done.17.refs_7_ = bf16[40,4096]{1,0:T(8,128)(2,1)} collective-permute-done((bf16[40,4096]{1,0:T(8,128)(2,1)S(1)}, bf16[40,4096]{1,0:T(8,128)(2,1)}, u32[]{:S(2)}, u32[]{:S(2)}) %collective-permute-start.17) | collective-permute-done | bytes 327712 | tf_op jit(solution)/shard_map/ppermute | solution.py:90
  94.2 1.9 %collective-permute-start.21 = (bf16[40,4096]{1,0:T(8,128)(2,1)}, bf16[40,4096]{1,0:T(8,128)(2,1)S(1)}, u32[]{:S(2)}, u32[]{:S(2)}) collective-permute-start(bf16[40,4096]{1,0:T(8,128)(2,1)} %get-tuple-element.108), channel_id=1, source_target_pairs={{0,6},{1,7},{2,4},{3,5},{4,2},{5,3},{6,0},{7,1},{8,14},{9,15},{10,... | collective-permute-start | bytes 983048 | tf_op jit(solution)/shard_map/ppermute | solution.py:90
  97.7 15.3 %shard_map.101 = (bf16[40,4096]{1,0:T(8,128)(2,1)}, bf16[40,4096]{1,0:T(8,128)(2,1)}, bf16[40,4096]{1,0:T(8,128)(2,1)}, bf16[40,4096]{1,0:T(8,128)(2,1)}, bf16[4...) custom-call(bf16[40,4096]{1,0:T(8,128)(2,1)} %convolution_convert_fusion.2.r, ...), custom_call_target="tpu_custom_call" | custom-call | flops 6039797760 | bytes 24117248 | tf_op jit(solution)/shard_map/pallas_call | solution.py:238
  118.2 7.1 %collective-permute-done.24 = bf16[40,4096]{1,0:T(8,128)(2,1)S(1)} collective-permute-done((bf16[40,4096]{1,0:T(8,128)(2,1)S(1)}, bf16[40,4096]{1,0:T(8,128)(2,1)S(1)}, u32[]{:S(2)}, u32[]{:S(2)}) %collective-permute-start.24) | collective-permute-done | bytes 327712 | tf_op jit(solution)/shard_map/ppermute | solution.py:90
  125.4 5.9 %collective-permute-done.19 = bf16[40,4096]{1,0:T(8,128)(2,1)S(1)} collective-permute-done((bf16[40,4096]{1,0:T(8,128)(2,1)S(1)}, bf16[40,4096]{1,0:T(8,128)(2,1)S(1)}, u32[]{:S(2)}, u32[]{:S(2)}) %collective-permute-start.19) | collective-permute-done | bytes 327712 | tf_op jit(solution)/shard_map/ppermute | solution.py:90
  134.5 1.7 collective-permute-start.25
  138.0 6.9 %collective-permute-done.25 = bf16[40,4096]{1,0:T(8,128)(2,1)S(1)} collective-permute-done((bf16[40,4096]{1,0:T(8,128)(2,1)S(1)}, bf16[40,4096]{1,0:T(8,128)(2,1)S(1)}, u32[]{:S(2)}, u32[]{:S(2)}) %collective-permute-start.25) | collective-permute-done | bytes 327712 | tf_op jit(solution)/shard_map/ppermute | solution.py:90
  146.1 3.3 %collective-permute-done.29 = bf16[40,4096]{1,0:T(8,128)(2,1)S(1)} collective-permute-done((bf16[40,4096]{1,0:T(8,128)(2,1)S(1)}, bf16[40,4096]{1,0:T(8,128)(2,1)S(1)}, u32[]{:S(2)}, u32[]{:S(2)}) %collective-permute-start.29) | collective-permute-done | bytes 327712 | tf_op jit(solution)/shard_map/ppermute | solution.py:90
  149.8 1.7 %collective-permute-start.32 = (bf16[64,4096]{1,0:T(8,128)(2,1)S(1)}, bf16[64,4096]{1,0:T(8,128)(2,1)S(1)}, u32[]{:S(2)}, u32[]{:S(2)}) collective-permute-start(bf16[64,4096]{1,0:T(8,128)(2,1)S(1)} %fusion.1), channel_id=1, source_target_pairs={{0,8},{1,9},{2,10},{3,11},{4,12},{5,13},{6,14},{7,15},{8,16},{9,17... | collective-permute-start | bytes 1572872 | tf_op jit(solution)/shard_map/ppermute | solution.py:90
  153.3 1.7 %collective-permute-start.20 = (bf16[40,4096]{1,0:T(8,128)(2,1)S(1)}, bf16[40,4096]{1,0:T(8,128)(2,1)S(1)}, u32[]{:S(2)}, u32[]{:S(2)}) collective-permute-start(bf16[40,4096]{1,0:T(8,128)(2,1)S(1)} %copy-done.8), channel_id=1, source_target_pairs={{0,2},{1,3},{2,0},{3,1},{4,6},{5,7},{6,4},{7,5},{8,10},{9,11},{10,... | collective-permute-start | bytes 983048 | tf_op jit(solution)/shard_map/ppermute | solution.py:90
  155.7 2.0 %shard_map.102 = bf16[32,16,1024]{2,1,0:T(8,128)(2,1)} custom-call(s32[32]{0:T(128)S(1)} %fusion.38.label_ref, bf16[32,16,1152]{2,1,0:T(8,128)(2,1)S(1)} %all-to-all-done.arrived_ref), custom_call_target="tpu_custom_call" | custom-call | bytes 2097152 | tf_op jit(solution)/shard_map/pallas_call | solution.py:65
  157.6 3.0 %collective-permute-done.26 = bf16[40,4096]{1,0:T(8,128)(2,1)S(1)} collective-permute-done((bf16[40,4096]{1,0:T(8,128)(2,1)S(1)}, bf16[40,4096]{1,0:T(8,128)(2,1)S(1)}, u32[]{:S(2)}, u32[]{:S(2)}) %collective-permute-start.26) | collective-permute-done | bytes 327712 | tf_op jit(solution)/shard_map/ppermute | solution.py:90
  160.7 3.3 %collective-permute-done.23 = bf16[40,4096]{1,0:T(8,128)(2,1)S(1)} collective-permute-done((bf16[40,4096]{1,0:T(8,128)(2,1)S(1)}, bf16[40,4096]{1,0:T(8,128)(2,1)S(1)}, u32[]{:S(2)}, u32[]{:S(2)}) %collective-permute-start.23) | collective-permute-done | bytes 327712 | tf_op jit(solution)/shard_map/ppermute | solution.py:90
  164.0 2.1 %fusion = bf16[64,4096]{1,0:T(8,128)(2,1)} fusion(bf16[64,160]{1,0:T(8,128)(2,1)S(1)} %get-tuple-element.63, bf16[40,4096]{1,0:T(8,128)(2,1)S(1)} %collective-permute-done.26, bf16[40,4096]{1,0:T(8,128)(2,1)S(1)} %collective-permute-done.23, bf16[40,4096]{1,0:T(8,128)(2,1)S(1)} %collective-permute-done.20, bf16[40,4096]{1,0:T(8,128)(2,1)} %get-tuple-element.85, ...), kind=kOutput, calls=%fused_computation.3 | convolution fusion | flops 89915392 | bytes 2379776 | tf_op jit(solution)/shard_map/dot_general | solution.py:335
  (119 shorter events, 48.1 us)
Async XLA Ops:
  4.2 21.9 %collective-permute-start.11 = (bf16[4096,384]{1,0:T(8,128)(2,1)}, bf16[4096,384]{1,0:T(8,128)(2,1)S(1)}, u32[]{:S(2)}, u32[]{:S(2)}) collective-permute-start(bf16[4096,384]{1,0:T(8,128)(2,1)} %refs_8_.3), channel_id=1, source_target_pairs={{0,1},{1,0},{2,3},{3,2},{4,5},{5,4},{6,7},{7,6},{8,9},{9,8},{10,11... | collective-permute-start | bytes 9437192 | tf_op jit(solution)/shard_map/ppermute | solution.py:90
  4.7 20.7 %collective-permute-start = (bf16[64,4224]{1,0:T(8,128)(2,1)S(1)}, bf16[64,4224]{1,0:T(8,128)(2,1)S(1)}, u32[]{:S(2)}, u32[]{:S(2)}) collective-permute-start(bf16[64,4224]{1,0:T(8,128)(2,1)S(1)} %get-tuple-element.64), channel_id=1, source_target_pairs={{0,8},{1,9},{2,10},{3,11},{4,12},{5,13},{6,14},{7,15},{8,16},{9,17... | collective-permute-start | bytes 1622024 | tf_op jit(solution)/shard_map/ppermute | solution.py:90
  8.8 16.5 %collective-permute-start.5 = (bf16[40,4096]{1,0:T(8,128)(2,1)S(1)}, bf16[40,4096]{1,0:T(8,128)(2,1)S(1)}, u32[]{:S(2)}, u32[]{:S(2)}) collective-permute-start(bf16[40,4096]{1,0:T(8,128)(2,1)S(1)} %get-tuple-element.72), channel_id=1, source_target_pairs={{0,4},{1,5},{2,6},{3,7},{4,0},{5,1},{6,2},{7,3},{8,12},{9,13},{10,... | collective-permute-start | bytes 983048 | tf_op jit(solution)/shard_map/ppermute | solution.py:90
  10.3 15.0 %collective-permute-start.8 = (bf16[40,4096]{1,0:T(8,128)(2,1)S(1)}, bf16[40,4096]{1,0:T(8,128)(2,1)S(1)}, u32[]{:S(2)}, u32[]{:S(2)}) collective-permute-start(bf16[40,4096]{1,0:T(8,128)(2,1)S(1)} %get-tuple-element.77), channel_id=1, source_target_pairs={{0,6},{1,7},{2,4},{3,5},{4,2},{5,3},{6,0},{7,1},{8,14},{9,15},{10,... | collective-permute-start | bytes 983048 | tf_op jit(solution)/shard_map/ppermute | solution.py:90
  26.1 20.3 %collective-permute-start.12 = (bf16[4096,384]{1,0:T(8,128)(2,1)}, bf16[4096,384]{1,0:T(8,128)(2,1)S(1)}, u32[]{:S(2)}, u32[]{:S(2)}) collective-permute-start(bf16[4096,384]{1,0:T(8,128)(2,1)} %refs_10_.3), channel_id=1, source_target_pairs={{0,1},{1,0},{2,3},{3,2},{4,5},{5,4},{6,7},{7,6},{8,9},{9,8},{10,11... | collective-permute-start | bytes 9437192 | tf_op jit(solution)/shard_map/ppermute | solution.py:90
  26.1 20.3 %collective-permute-start.1 = (bf16[64,4224]{1,0:T(8,128)(2,1)S(1)}, bf16[64,4224]{1,0:T(8,128)(2,1)S(1)}, u32[]{:S(2)}, u32[]{:S(2)}) collective-permute-start(bf16[64,4224]{1,0:T(8,128)(2,1)S(1)} %collective-permute-done.block_ref), channel_id=1, source_target_pairs={{0,8},{1,9},{2,10},{3,11},{4,12},{5,13},{6,14},{7,15},{8,16},{9,17... | collective-permute-start | bytes 1622024 | tf_op jit(solution)/shard_map/ppermute | solution.py:90
  29.8 14.9 %collective-permute-start.6 = (bf16[40,4096]{1,0:T(8,128)(2,1)S(1)}, bf16[40,4096]{1,0:T(8,128)(2,1)S(1)}, u32[]{:S(2)}, u32[]{:S(2)}) collective-permute-start(bf16[40,4096]{1,0:T(8,128)(2,1)S(1)} %get-tuple-element.73), channel_id=1, source_target_pairs={{0,4},{1,5},{2,6},{3,7},{4,0},{5,1},{6,2},{7,3},{8,12},{9,13},{10,... | collective-permute-start | bytes 983048 | tf_op jit(solution)/shard_map/ppermute | solution.py:90
  30.7 15.7 %collective-permute-start.9 = (bf16[40,4096]{1,0:T(8,128)(2,1)S(1)}, bf16[40,4096]{1,0:T(8,128)(2,1)S(1)}, u32[]{:S(2)}, u32[]{:S(2)}) collective-permute-start(bf16[40,4096]{1,0:T(8,128)(2,1)S(1)} %get-tuple-element.78), channel_id=1, source_target_pairs={{0,6},{1,7},{2,4},{3,5},{4,2},{5,3},{6,0},{7,1},{8,14},{9,15},{10,... | collective-permute-start | bytes 983048 | tf_op jit(solution)/shard_map/ppermute | solution.py:90
  46.4 30.0 %collective-permute-start.13 = (bf16[384,4096]{1,0:T(8,128)(2,1)}, bf16[384,4096]{1,0:T(8,128)(2,1)}, u32[]{:S(2)}, u32[]{:S(2)}) collective-permute-start(bf16[384,4096]{1,0:T(8,128)(2,1)} %refs_12_.3), channel_id=1, source_target_pairs={{0,1},{1,0},{2,3},{3,2},{4,5},{5,4},{6,7},{7,6},{8,9},{9,8},{10,11... | collective-permute-start | bytes 9437192 | tf_op jit(solution)/shard_map/ppermute | solution.py:90
  46.5 20.8 %collective-permute-start.14 = (bf16[64,4224]{1,0:T(8,128)(2,1)S(1)}, bf16[64,4224]{1,0:T(8,128)(2,1)S(1)}, u32[]{:S(2)}, u32[]{:S(2)}) collective-permute-start(bf16[64,4224]{1,0:T(8,128)(2,1)S(1)} %collective-permute-done.1.block_ref), channel_id=1, source_target_pairs={{0,8},{1,9},{2,10},{3,11},{4,12},{5,13},{6,14},{7,15},{8,16},{9,17... | collective-permute-start | bytes 1622024 | tf_op jit(solution)/shard_map/ppermute | solution.py:90
  50.8 16.5 %collective-permute-start.7 = (bf16[40,4096]{1,0:T(8,128)(2,1)S(1)}, bf16[40,4096]{1,0:T(8,128)(2,1)S(1)}, u32[]{:S(2)}, u32[]{:S(2)}) collective-permute-start(bf16[40,4096]{1,0:T(8,128)(2,1)S(1)} %get-tuple-element.74), channel_id=1, source_target_pairs={{0,4},{1,5},{2,6},{3,7},{4,0},{5,1},{6,2},{7,3},{8,12},{9,13},{10,... | collective-permute-start | bytes 983048 | tf_op jit(solution)/shard_map/ppermute | solution.py:90
  52.3 15.0 %collective-permute-start.10 = (bf16[40,4096]{1,0:T(8,128)(2,1)S(1)}, bf16[40,4096]{1,0:T(8,128)(2,1)S(1)}, u32[]{:S(2)}, u32[]{:S(2)}) collective-permute-start(bf16[40,4096]{1,0:T(8,128)(2,1)S(1)} %get-tuple-element.79), channel_id=1, source_target_pairs={{0,6},{1,7},{2,4},{3,5},{4,2},{5,3},{6,0},{7,1},{8,14},{9,15},{10,... | collective-permute-start | bytes 983048 | tf_op jit(solution)/shard_map/ppermute | solution.py:90
  68.1 28.0 %collective-permute-start.15 = (bf16[40,4096]{1,0:T(8,128)(2,1)S(1)}, bf16[40,4096]{1,0:T(8,128)(2,1)}, u32[]{:S(2)}, u32[]{:S(2)}) collective-permute-start(bf16[40,4096]{1,0:T(8,128)(2,1)S(1)} %get-tuple-element.97), channel_id=1, source_target_pairs={{0,2},{1,3},{2,0},{3,1},{4,6},{5,7},{6,4},{7,5},{8,10},{9,11},{10,... | collective-permute-start | bytes 983048 | tf_op jit(solution)/shard_map/ppermute | solution.py:90
  69.4 26.7 %collective-permute-start.16 = (bf16[40,4096]{1,0:T(8,128)(2,1)S(1)}, bf16[40,4096]{1,0:T(8,128)(2,1)}, u32[]{:S(2)}, u32[]{:S(2)}) collective-permute-start(bf16[40,4096]{1,0:T(8,128)(2,1)S(1)} %get-tuple-element.99), channel_id=1, source_target_pairs={{0,4},{1,5},{2,6},{3,7},{4,0},{5,1},{6,2},{7,3},{8,12},{9,13},{10,... | collective-permute-start | bytes 983048 | tf_op jit(solution)/shard_map/ppermute | solution.py:90
  70.3 24.0 %collective-permute-start.17 = (bf16[40,4096]{1,0:T(8,128)(2,1)S(1)}, bf16[40,4096]{1,0:T(8,128)(2,1)}, u32[]{:S(2)}, u32[]{:S(2)}) collective-permute-start(bf16[40,4096]{1,0:T(8,128)(2,1)S(1)} %get-tuple-element.101), channel_id=1, source_target_pairs={{0,6},{1,7},{2,4},{3,5},{4,2},{5,3},{6,0},{7,1},{8,14},{9,15},{10,... | collective-permute-start | bytes 983048 | tf_op jit(solution)/shard_map/ppermute | solution.py:90
  71.8 79.7 %all-to-all-start = ((bf16[32,16,1152]{2,1,0:T(8,128)(2,1)}), bf16[32,16,1152]{2,1,0:T(8,128)(2,1)S(1)}, u32[]{:S(2)}, u32[]{:S(2)}) async-start(bf16[32,16,1152]{2,1,0:T(8,128)(2,1)} %shard_map.98), calls=%async_computation | async-start | bytes 2359296 | tf_op jit(solution)/shard_map/all_to_all | solution.py:81
  94.2 18.9 %collective-permute-start.21 = (bf16[40,4096]{1,0:T(8,128)(2,1)}, bf16[40,4096]{1,0:T(8,128)(2,1)S(1)}, u32[]{:S(2)}, u32[]{:S(2)}) collective-permute-start(bf16[40,4096]{1,0:T(8,128)(2,1)} %get-tuple-element.108), channel_id=1, source_target_pairs={{0,6},{1,7},{2,4},{3,5},{4,2},{5,3},{6,0},{7,1},{8,14},{9,15},{10,... | collective-permute-start | bytes 983048 | tf_op jit(solution)/shard_map/ppermute | solution.py:90
  96.1 17.0 %collective-permute-start.18 = (bf16[40,4096]{1,0:T(8,128)(2,1)}, bf16[40,4096]{1,0:T(8,128)(2,1)S(1)}, u32[]{:S(2)}, u32[]{:S(2)}) collective-permute-start(bf16[40,4096]{1,0:T(8,128)(2,1)} %get-tuple-element.103), channel_id=1, source_target_pairs={{0,4},{1,5},{2,6},{3,7},{4,0},{5,1},{6,2},{7,3},{8,12},{9,13},{10,... | collective-permute-start | bytes 983048 | tf_op jit(solution)/shard_map/ppermute | solution.py:90
  96.1 17.0 %collective-permute-start.27 = (bf16[40,4096]{1,0:T(8,128)(2,1)}, bf16[40,4096]{1,0:T(8,128)(2,1)S(1)}, u32[]{:S(2)}, u32[]{:S(2)}) collective-permute-start(bf16[40,4096]{1,0:T(8,128)(2,1)} %get-tuple-element.119), channel_id=1, source_target_pairs={{0,2},{1,3},{2,0},{3,1},{4,6},{5,7},{6,4},{7,5},{8,10},{9,11},{10,... | collective-permute-start | bytes 983048 | tf_op jit(solution)/shard_map/ppermute | solution.py:90
  113.5 19.2 %collective-permute-start.30 = (bf16[64,4096]{1,0:T(8,128)(2,1)S(1)}, bf16[64,4096]{1,0:T(8,128)(2,1)S(1)}, u32[]{:S(2)}, u32[]{:S(2)}) collective-permute-start(bf16[64,4096]{1,0:T(8,128)(2,1)S(1)} %convolution_convert_fusion), channel_id=1, source_target_pairs={{0,8},{1,9},{2,10},{3,11},{4,12},{5,13},{6,14},{7,15},{8,16},{9,17... | collective-permute-start | bytes 1572872 | tf_op jit(solution)/shard_map/ppermute | solution.py:90
  115.9 15.4 %collective-permute-start.19 = (bf16[40,4096]{1,0:T(8,128)(2,1)S(1)}, bf16[40,4096]{1,0:T(8,128)(2,1)S(1)}, u32[]{:S(2)}, u32[]{:S(2)}) collective-permute-start(bf16[40,4096]{1,0:T(8,128)(2,1)S(1)} %copy-done.24), channel_id=1, source_target_pairs={{0,6},{1,7},{2,4},{3,5},{4,2},{5,3},{6,0},{7,1},{8,14},{9,15},{10,... | collective-permute-start | bytes 983048 | tf_op jit(solution)/shard_map/ppermute | solution.py:90
  116.9 15.8 %collective-permute-start.28 = (bf16[40,4096]{1,0:T(8,128)(2,1)S(1)}, bf16[40,4096]{1,0:T(8,128)(2,1)S(1)}, u32[]{:S(2)}, u32[]{:S(2)}) collective-permute-start(bf16[40,4096]{1,0:T(8,128)(2,1)S(1)} %copy-done.23), channel_id=1, source_target_pairs={{0,4},{1,5},{2,6},{3,7},{4,0},{5,1},{6,2},{7,3},{8,12},{9,13},{10,... | collective-permute-start | bytes 983048 | tf_op jit(solution)/shard_map/ppermute | solution.py:90
  133.1 16.4 %collective-permute-start.31 = (bf16[64,4096]{1,0:T(8,128)(2,1)S(1)}, bf16[64,4096]{1,0:T(8,128)(2,1)S(1)}, u32[]{:S(2)}, u32[]{:S(2)}) collective-permute-start(bf16[64,4096]{1,0:T(8,128)(2,1)S(1)} %fusion.2), channel_id=1, source_target_pairs={{0,8},{1,9},{2,10},{3,11},{4,12},{5,13},{6,14},{7,15},{8,16},{9,17... | collective-permute-start | bytes 1572872 | tf_op jit(solution)/shard_map/ppermute | solution.py:90
  149.8 14.2 %collective-permute-start.32 = (bf16[64,4096]{1,0:T(8,128)(2,1)S(1)}, bf16[64,4096]{1,0:T(8,128)(2,1)S(1)}, u32[]{:S(2)}, u32[]{:S(2)}) collective-permute-start(bf16[64,4096]{1,0:T(8,128)(2,1)S(1)} %fusion.1), channel_id=1, source_target_pairs={{0,8},{1,9},{2,10},{3,11},{4,12},{5,13},{6,14},{7,15},{8,16},{9,17... | collective-permute-start | bytes 1572872 | tf_op jit(solution)/shard_map/ppermute | solution.py:90
  (39 other events, 604.7 us)

commit v7 on v6

--- a/solution.py
+++ b/solution.py
@@ -92,6 +92,11 @@
 
 def after(x, *earlier):
     return lax.optimization_barrier((x, *earlier))[0]
+
+
+def gather(weight, dimension):
+    pairs = [[i, i + 1] for i in range(0, lax.axis_size("expert"), 2)]
+    return lax.all_gather(weight, "expert", axis=dimension, tiled=True, axis_index_groups=pairs)
 
 
 def mixing_table(route_ids, route_gates, experts):
@@ -179,7 +184,7 @@
         out_specs=[pl.BlockSpec(memory_space=pltpu.VMEM)] * len(outs),
         compiler_params=pltpu.CompilerParams(vmem_limit_bytes=16 * 2**20),
         cost_estimate=pl.CostEstimate(
-            flops=2 * rows * PLANE * capacity * width,
+            flops=200 * rows * PLANE * capacity * width,
             bytes_accessed=2 * width * (rows + PLANE * capacity),
             transcendentals=0,
         ),
@@ -189,35 +194,30 @@
 
 
 def expert_kernel(pieces, steps, *refs):
-    rows_in, weights = refs[:pieces], refs[pieces : pieces + 6]
-    outs, hidden = refs[pieces + 6 : 2 * pieces + 6], refs[2 * pieces + 6]
-    sums = refs[2 * pieces + 7 :]
+    rows_in, (gate_ref, up_ref, down_ref) = refs[:pieces], refs[pieces : pieces + 3]
+    outs = refs[pieces + 3 : 2 * pieces + 3]
+    rows, hidden = refs[2 * pieces + 3 :]
     i = pl.program_id(0)
-    half = hidden.shape[1] // 2
+    width = rows.shape[1]
+    part = gate_ref.shape[1]
 
     @pl.when(i == 0)
     def _():
-        for total in sums:
-            total[...] = jnp.zeros_like(total)
+        for at in range(0, width, 512):
+            found = [ref[:, at : at + 512].astype(jnp.float32) for ref in rows_in]
+            rows[:, at : at + 512] = jnp.concatenate(found, axis=0).astype(jnp.bfloat16)
 
     @pl.when(i < steps)
     def _():
-        rows = jnp.concatenate([ref[...].astype(jnp.float32) for ref in rows_in], axis=0)
-        rows = rows.astype(jnp.bfloat16)
-        for total, weight in zip(sums, weights[:4]):
-            total[...] += jnp.dot(rows, weight[...], preferred_element_type=jnp.float32)
-
-    @pl.when(i == steps - 1)
-    def _():
-        for n in range(2):
-            gate = sums[n][...]
-            value = gate / (1.0 + jnp.exp(-gate)) * sums[2 + n][...]
-            hidden[:, n * half : (n + 1) * half] = value.astype(jnp.bfloat16)
+        wide = jnp.concatenate([gate_ref[...], up_ref[...]], axis=1)
+        found = jnp.dot(rows[...], wide, preferred_element_type=jnp.float32)
+        gate, up = found[:, :part], found[:, part:]
+        hidden[i] = (gate / (1.0 + jnp.exp(-gate)) * up).astype(jnp.bfloat16)
 
     @pl.when(i >= steps)
     def _():
-        down = jnp.concatenate([weights[4][...], weights[5][...]], axis=0)
-        out = jnp.dot(hidden[...], down, preferred_element_type=jnp.float32)
+        left = jnp.concatenate([hidden[n] for n in range(steps)], axis=1)
+        out = jnp.dot(left, down_ref[...], preferred_element_type=jnp.float32)
         each = out.shape[0] // pieces
         for n in range(pieces):
             outs[n][...] = out[n * each : (n + 1) * each].astype(jnp.bfloat16)
@@ -226,44 +226,44 @@
 def apply(held, gate, up, down):
     pieces = [piece for arrived in held for piece in arrived]
     each, width = pieces[0].shape
-    rows, half = each * len(pieces), gate[0].shape[1]
-    step = 1024
-    steps = width // step
+    rows, units = each * len(pieces), gate.shape[1]
+    part, span = 256, 1024
+    steps = units // part
     read = lambda i: jnp.minimum(i, steps - 1)
     write = lambda i: jnp.maximum(i - steps, 0)
-    piece_in = pl.BlockSpec((each, step), lambda i: (0, read(i)))
-    piece_out = pl.BlockSpec((each, step), lambda i: (0, write(i)))
-    wide = pl.BlockSpec((step, half), lambda i: (read(i), 0))
-    tall = pl.BlockSpec((half, step), lambda i: (0, write(i)))
+    piece_in = pl.BlockSpec((each, width), lambda i: (0, 0))
+    piece_out = pl.BlockSpec((each, span), lambda i: (0, write(i)))
+    wide = pl.BlockSpec((width, part), lambda i: (0, read(i)))
+    tall = pl.BlockSpec((units, span), lambda i: (0, write(i)))
     return pl.pallas_call(
         functools.partial(expert_kernel, len(pieces), steps),
-        grid=(2 * steps,),
+        grid=(steps + width // span,),
         out_shape=[jax.ShapeDtypeStruct((each, width), jnp.bfloat16)] * len(pieces),
-        in_specs=[piece_in] * len(pieces) + [wide] * 4 + [tall] * 2,
+        in_specs=[piece_in] * len(pieces) + [wide] * 2 + [tall],
         out_specs=[piece_out] * len(pieces),
-        scratch_shapes=[pltpu.VMEM((rows, 2 * half), jnp.bfloat16)]
-        + [pltpu.VMEM((rows, half), jnp.float32)] * 4,
+        scratch_shapes=[
+            pltpu.VMEM((rows, width), jnp.bfloat16),
+            pltpu.VMEM((steps, rows, part), jnp.bfloat16),
+        ],
         compiler_params=pltpu.CompilerParams(
             dimension_semantics=("arbitrary",), vmem_limit_bytes=60 * 2**20
         ),
         cost_estimate=pl.CostEstimate(
-            flops=12 * rows * width * half,
-            bytes_accessed=12 * width * half + 4 * rows * width,
-            transcendentals=2 * rows * half,
-        ),
-    )(*pieces, *gate, *up, *down)
-
-
-def apply_plain(held, gate, up, down):
+            flops=6 * rows * width * units,
+            bytes_accessed=6 * width * units + 4 * rows * width,
+            transcendentals=rows * units,
+        ),
+    )(*pieces, gate, up, down)
+
+
+def apply_plain(held, gate_weight, up_weight, down_weight):
     pieces = [piece for arrived in held for piece in arrived]
     rows = jnp.concatenate(pieces, axis=0)
-    total = 0.0
-    for n in range(2):
-        left = jnp.dot(rows, gate[n], preferred_element_type=jnp.float32)
-        right = jnp.dot(rows, up[n], preferred_element_type=jnp.float32)
-        hidden = (jax.nn.silu(left) * right).astype(jnp.bfloat16)
-        total = total + jnp.dot(hidden, down[n], preferred_element_type=jnp.float32)
-    return jnp.split(total.astype(jnp.bfloat16), len(pieces), axis=0)
+    gate = jnp.dot(rows, gate_weight, preferred_element_type=jnp.float32)
+    up = jnp.dot(rows, up_weight, preferred_element_type=jnp.float32)
+    hidden = (jax.nn.silu(gate) * up).astype(jnp.bfloat16)
+    out = jnp.dot(hidden, down_weight, preferred_element_type=jnp.float32)
+    return jnp.split(out.astype(jnp.bfloat16), len(pieces), axis=0)
 
 
 def pick_plain(chip, block, width, experts, capacity, routing=None):
@@ -289,9 +289,9 @@
     chip = lax.axis_index("expert") // 2
     whole = capacity % 8 == 0 and width % 1024 == 0
     choose, work = (pick_pieces, apply) if whole else (pick_plain, apply_plain)
-    weights = (gate_weight, up_weight, down_weight)
+    weights = [gather(gate_weight, 1), gather(up_weight, 1), gather(down_weight, 0)]
     group = 2
-    swapped, blends, got, outs = [], [], [], []
+    blends, got, outs = [], [], []
     outgoing = sort_pages(kv_pages, page_target)
     block = tokens
     for s in range(planes):
@@ -302,9 +302,6 @@
                 chip, tokens, width, experts, capacity, (route_ids, route_gates)
             )
         blends.append(blend)
-        if s < 3:
-            earlier = [block] + (got[s - 1][1:] if s else []) + ([outgoing] if s == 1 else [])
-            swapped.append(send(after(weights[s], *swapped, *earlier), flip=1))
         for j in range(1, PLANE):
             piece = after(pieces[j], got[s - 1][j]) if s else pieces[j]
             pieces[j] = send(piece, flip=2 * j)
@@ -316,9 +313,9 @@
         held = [list(pieces) for pieces in got[first : first + group]]
         following = got[first + group][1:] if first + group < planes else []
         held[0][0] = after(held[0][0], *outs, *following)
-        outs.extend(work(held, *zip(weights, swapped)))
-
-    arrived = exchange(after(outgoing, *got[-2][1:], block))
+        outs.extend(work(held, *weights))
+
+    arrived = exchange(after(outgoing, block))
     order = list(range(1, planes)) + [0]
     sent, landed = {}, got[-1][1:]
     for s in order:

time: 167 us -> 167 us (level)
  between operations: 0.93 us -> 14.1 us
  waiting for transfers between devices: 71.4 us -> 63.7 us
  local copies, waits for them, and re-layouts: 5.14 us -> 1.35 us
    ppermute x33 -> x30, waiting for transfers between devices: 71.4 us -> 61.6 us  [send(): return lax.ppermute(x, 'expert', pairs)]
    unnamed x58 -> x56, local copies, waits for them, and re-layouts: 5.14 us -> 1.35 us
    ppermute x33 -> x30, starting transfers between devices: 39 us -> 36.5 us  [send(): return lax.ppermute(x, 'expert', pairs)]
    unnamed x0 -> x3, waiting for transfers between devices: none -> 2.06 us
    all_to_all x1, starting transfers between devices: 3.57 us -> 5.27 us  [exchange(): return lax.all_to_all(x, 'expert', split_axis=0, concat_axis=0, tiled=True)]
  transfers between devices with their start and end apart: 34 -> 34, of which waited for: 16 -> 11; matrix products, arithmetic and copies ran while one was open for 4% -> 3% of each run, Pallas kernels for 22% -> 23%
where the time goes in v7:
time: 167 us
  waiting for transfers between devices  63.7 us (38%)
  starting transfers between devices  41.9 us (25%)
  Pallas kernels  37.8 us (23%)
  between operations  14.1 us (8%)
  matrix products  7.3 us (4%)
    ppermute x30, waiting for transfers between devices, send(): return lax.ppermute(x, 'expert', pairs)  61.6 us
    ppermute x30, starting transfers between devices, send(): return lax.ppermute(x, 'expert', pairs)  36.5 us
    pallas_call x2, Pallas kernels, apply(): pl.pallas_call(functools.partial(expert_kernel, len(pieces), steps), grid...  30.4 us
    all_to_all x1, starting transfers between devices, exchange(): return lax.all_to_all(x, 'expert', split_axis=0, concat_axis=0, tiled=True)  5.27 us
    dot_general x4, matrix products, pick(): lax.dot_general(placing, rows, (((0,), (0,)), ((), ())), preferred_elemen...  4.12 us
    pallas_call x4, Pallas kernels, pick_pieces(): pl.pallas_call(functools.partial(body, experts, capacity, 512), out_shape...  3.45 us
  transfers between devices with their start and end apart: 34, of which 11 were waited for; matrix products, arithmetic and copies ran while one was open for 3% of the time, Pallas kernels for 23%

profile of v7, /device:TPU:0, one launch (start us, length us, event | category | flops | bytes accessed | tf_op | source)
XLA Modules:
  0.0 166.8 jit_solution(2116097459577282571)
XLA Ops:
  10.6 3.1 %collective-permute-start = (bf16[64,4224]{1,0:T(8,128)(2,1)S(1)}, bf16[64,4224]{1,0:T(8,128)(2,1)S(1)}, u32[]{:S(2)}, u32[]{:S(2)}) collective-permute-start(bf16[64,4224]{1,0:T(8,128)(2,1)S(1)} %get-tuple-element.61), channel_id=1, source_target_pairs={{0,8},{1,9},{2,10},{3,11},{4,12},{5,13},{6,14},{7,15},{8,16},{9,17... | collective-permute-start | bytes 1622024 | tf_op jit(solution)/shard_map/ppermute | solution.py:90
  13.7 2.5 %collective-permute-start.8 = (bf16[40,4096]{1,0:T(8,128)(2,1)S(1)}, bf16[40,4096]{1,0:T(8,128)(2,1)S(1)}, u32[]{:S(2)}, u32[]{:S(2)}) collective-permute-start(bf16[40,4096]{1,0:T(8,128)(2,1)S(1)} %get-tuple-element.74), channel_id=1, source_target_pairs={{0,6},{1,7},{2,4},{3,5},{4,2},{5,3},{6,0},{7,1},{8,14},{9,15},{10,... | collective-permute-start | bytes 983048 | tf_op jit(solution)/shard_map/ppermute | solution.py:90
  17.2 2.0 %shard_map.101 = bf16[32,16,1152]{2,1,0:T(8,128)(2,1)} custom-call(s32[32]{0:T(128)S(1)} %copy-done.2, bf16[32,16,1024]{2,1,0:T(8,128)(2,1)S(1)} %copy-done), custom_call_target="tpu_custom_call" | custom-call | bytes 3145728 | tf_op jit(solution)/shard_map/pallas_call | solution.py:34
  20.2 7.8 %collective-permute-done.block_ref = bf16[64,4224]{1,0:T(8,128)(2,1)S(1)} collective-permute-done((bf16[64,4224]{1,0:T(8,128)(2,1)S(1)}, bf16[64,4224]{1,0:T(8,128)(2,1)S(1)}, u32[]{:S(2)}, u32[]{:S(2)}) %collective-permute-start) | collective-permute-done | bytes 540704 | tf_op jit(solution)/shard_map/ppermute | solution.py:90
  28.8 2.5 %collective-permute-start.9 = (bf16[40,4096]{1,0:T(8,128)(2,1)S(1)}, bf16[40,4096]{1,0:T(8,128)(2,1)S(1)}, u32[]{:S(2)}, u32[]{:S(2)}) collective-permute-start(bf16[40,4096]{1,0:T(8,128)(2,1)S(1)} %get-tuple-element.75), channel_id=1, source_target_pairs={{0,6},{1,7},{2,4},{3,5},{4,2},{5,3},{6,0},{7,1},{8,14},{9,15},{10,... | collective-permute-start | bytes 983048 | tf_op jit(solution)/shard_map/ppermute | solution.py:90
  33.1 10.2 %collective-permute-done.1.block_ref = bf16[64,4224]{1,0:T(8,128)(2,1)S(1)} collective-permute-done((bf16[64,4224]{1,0:T(8,128)(2,1)S(1)}, bf16[64,4224]{1,0:T(8,128)(2,1)S(1)}, u32[]{:S(2)}, u32[]{:S(2)}) %collective-permute-start.1) | collective-permute-done | bytes 540704 | tf_op jit(solution)/shard_map/ppermute | solution.py:90
  44.1 2.3 %collective-permute-start.10 = (bf16[40,4096]{1,0:T(8,128)(2,1)S(1)}, bf16[40,4096]{1,0:T(8,128)(2,1)S(1)}, u32[]{:S(2)}, u32[]{:S(2)}) collective-permute-start(bf16[40,4096]{1,0:T(8,128)(2,1)S(1)} %get-tuple-element.76), channel_id=1, source_target_pairs={{0,6},{1,7},{2,4},{3,5},{4,2},{5,3},{6,0},{7,1},{8,14},{9,15},{10,... | collective-permute-start | bytes 983048 | tf_op jit(solution)/shard_map/ppermute | solution.py:90
  50.5 5.2 %collective-permute-done.10.refs_3_ = bf16[40,4096]{1,0:T(8,128)(2,1)S(1)} collective-permute-done((bf16[40,4096]{1,0:T(8,128)(2,1)S(1)}, bf16[40,4096]{1,0:T(8,128)(2,1)S(1)}, u32[]{:S(2)}, u32[]{:S(2)}) %collective-permute-start.10) | collective-permute-done | bytes 327712 | tf_op jit(solution)/shard_map/ppermute | solution.py:90
  55.7 4.3 %collective-permute-done.7.refs_2_ = bf16[40,4096]{1,0:T(8,128)(2,1)S(1)} collective-permute-done((bf16[40,4096]{1,0:T(8,128)(2,1)S(1)}, bf16[40,4096]{1,0:T(8,128)(2,1)S(1)}, u32[]{:S(2)}, u32[]{:S(2)}) %collective-permute-start.7) | collective-permute-done | bytes 327712 | tf_op jit(solution)/shard_map/ppermute | solution.py:90
  61.7 2.0 %collective-permute-start.14 = (bf16[40,4096]{1,0:T(8,128)(2,1)S(1)}, bf16[40,4096]{1,0:T(8,128)(2,1)S(1)}, u32[]{:S(2)}, u32[]{:S(2)}) collective-permute-start(bf16[40,4096]{1,0:T(8,128)(2,1)S(1)} %get-tuple-element.95), channel_id=1, source_target_pairs={{0,6},{1,7},{2,4},{3,5},{4,2},{5,3},{6,0},{7,1},{8,14},{9,15},{10,... | collective-permute-start | bytes 983048 | tf_op jit(solution)/shard_map/ppermute | solution.py:90
  65.2 5.3 %all-to-all-start = ((bf16[32,16,1152]{2,1,0:T(8,128)(2,1)}), bf16[32,16,1152]{2,1,0:T(8,128)(2,1)S(1)}, u32[]{:S(2)}, u32[]{:S(2)}) async-start(bf16[32,16,1152]{2,1,0:T(8,128)(2,1)} %shard_map.101), calls=%async_computation | async-start | bytes 2359296 | tf_op jit(solution)/shard_map/all_to_all | solution.py:81
  71.6 15.1 %shard_map.98 = (bf16[40,4096]{1,0:T(8,128)(2,1)}, bf16[40,4096]{1,0:T(8,128)(2,1)}, bf16[40,4096]{1,0:T(8,128)(2,1)}, bf16[40,4096]{1,0:T(8,128)(2,1)}, bf16[40...) custom-call(bf16[40,4096]{1,0:T(8,128)(2,1)} %convolution_convert_fusion.4.re, ...), custom_call_target="tpu_custom_call" | custom-call | flops 6039797760 | bytes 24117248 | tf_op jit(solution)/shard_map/pallas_call | solution.py:238
  86.7 1.8 %collective-permute-start.24 = (bf16[40,4096]{1,0:T(8,128)(2,1)}, bf16[40,4096]{1,0:T(8,128)(2,1)S(1)}, u32[]{:S(2)}, u32[]{:S(2)}) collective-permute-start(bf16[40,4096]{1,0:T(8,128)(2,1)} %get-tuple-element.113), channel_id=1, source_target_pairs={{0,2},{1,3},{2,0},{3,1},{4,6},{5,7},{6,4},{7,5},{8,10},{9,11},{10,... | collective-permute-start | bytes 983048 | tf_op jit(solution)/shard_map/ppermute | solution.py:90
  90.8 15.2 %shard_map.100 = (bf16[40,4096]{1,0:T(8,128)(2,1)}, bf16[40,4096]{1,0:T(8,128)(2,1)}, bf16[40,4096]{1,0:T(8,128)(2,1)}, bf16[40,4096]{1,0:T(8,128)(2,1)}, bf16[4...) custom-call(bf16[40,4096]{1,0:T(8,128)(2,1)} %convolution_convert_fusion.2.r, ...), custom_call_target="tpu_custom_call" | custom-call | flops 6039797760 | bytes 24117248 | tf_op jit(solution)/shard_map/pallas_call | solution.py:238
  107.6 1.9 %collective-permute-start.27 = (bf16[64,4096]{1,0:T(8,128)(2,1)S(1)}, bf16[64,4096]{1,0:T(8,128)(2,1)S(1)}, u32[]{:S(2)}, u32[]{:S(2)}) collective-permute-start(bf16[64,4096]{1,0:T(8,128)(2,1)S(1)} %convolution_convert_fusion), channel_id=1, source_target_pairs={{0,8},{1,9},{2,10},{3,11},{4,12},{5,13},{6,14},{7,15},{8,16},{9,17... | collective-permute-start | bytes 1572872 | tf_op jit(solution)/shard_map/ppermute | solution.py:90
  111.2 1.9 %collective-permute-start.16 = (bf16[40,4096]{1,0:T(8,128)(2,1)S(1)}, bf16[40,4096]{1,0:T(8,128)(2,1)S(1)}, u32[]{:S(2)}, u32[]{:S(2)}) collective-permute-start(bf16[40,4096]{1,0:T(8,128)(2,1)S(1)} %copy-done.22), channel_id=1, source_target_pairs={{0,6},{1,7},{2,4},{3,5},{4,2},{5,3},{6,0},{7,1},{8,14},{9,15},{10,... | collective-permute-start | bytes 983048 | tf_op jit(solution)/shard_map/ppermute | solution.py:90
  113.0 7.2 %collective-permute-done.21 = bf16[40,4096]{1,0:T(8,128)(2,1)S(1)} collective-permute-done((bf16[40,4096]{1,0:T(8,128)(2,1)S(1)}, bf16[40,4096]{1,0:T(8,128)(2,1)S(1)}, u32[]{:S(2)}, u32[]{:S(2)}) %collective-permute-start.21) | collective-permute-done | bytes 327712 | tf_op jit(solution)/shard_map/ppermute | solution.py:90
  120.2 6.0 %collective-permute-done.25 = bf16[40,4096]{1,0:T(8,128)(2,1)S(1)} collective-permute-done((bf16[40,4096]{1,0:T(8,128)(2,1)S(1)}, bf16[40,4096]{1,0:T(8,128)(2,1)S(1)}, u32[]{:S(2)}, u32[]{:S(2)}) %collective-permute-start.25) | collective-permute-done | bytes 327712 | tf_op jit(solution)/shard_map/ppermute | solution.py:90
  131.5 7.2 %collective-permute-done.19 = bf16[40,4096]{1,0:T(8,128)(2,1)S(1)} collective-permute-done((bf16[40,4096]{1,0:T(8,128)(2,1)S(1)}, bf16[40,4096]{1,0:T(8,128)(2,1)S(1)}, u32[]{:S(2)}, u32[]{:S(2)}) %collective-permute-start.19) | collective-permute-done | bytes 327712 | tf_op jit(solution)/shard_map/ppermute | solution.py:90
  138.6 4.4 %collective-permute-done.22 = bf16[40,4096]{1,0:T(8,128)(2,1)S(1)} collective-permute-done((bf16[40,4096]{1,0:T(8,128)(2,1)S(1)}, bf16[40,4096]{1,0:T(8,128)(2,1)S(1)}, u32[]{:S(2)}, u32[]{:S(2)}) %collective-permute-start.22) | collective-permute-done | bytes 327712 | tf_op jit(solution)/shard_map/ppermute | solution.py:90
  148.0 2.0 %shard_map.102 = bf16[32,16,1024]{2,1,0:T(8,128)(2,1)} custom-call(s32[32]{0:T(128)S(1)} %fusion.38.label_ref, bf16[32,16,1152]{2,1,0:T(8,128)(2,1)S(1)} %all-to-all-done.arrived_ref), custom_call_target="tpu_custom_call" | custom-call | bytes 2097152 | tf_op jit(solution)/shard_map/pallas_call | solution.py:65
  150.0 3.3 %collective-permute-done.17 = bf16[40,4096]{1,0:T(8,128)(2,1)S(1)} collective-permute-done((bf16[40,4096]{1,0:T(8,128)(2,1)S(1)}, bf16[40,4096]{1,0:T(8,128)(2,1)S(1)}, u32[]{:S(2)}, u32[]{:S(2)}) %collective-permute-start.17) | collective-permute-done | bytes 327712 | tf_op jit(solution)/shard_map/ppermute | solution.py:90
  153.3 4.9 %collective-permute-done.20 = bf16[40,4096]{1,0:T(8,128)(2,1)S(1)} collective-permute-done((bf16[40,4096]{1,0:T(8,128)(2,1)S(1)}, bf16[40,4096]{1,0:T(8,128)(2,1)S(1)}, u32[]{:S(2)}, u32[]{:S(2)}) %collective-permute-start.20) | collective-permute-done | bytes 327712 | tf_op jit(solution)/shard_map/ppermute | solution.py:90
  158.1 2.1 %fusion = bf16[64,4096]{1,0:T(8,128)(2,1)} fusion(bf16[64,160]{1,0:T(8,128)(2,1)S(1)} %get-tuple-element.60, bf16[40,4096]{1,0:T(8,128)(2,1)S(1)} %collective-permute-done.23, bf16[40,4096]{1,0:T(8,128)(2,1)S(1)} %collective-permute-done.20, bf16[40,4096]{1,0:T(8,128)(2,1)S(1)} %collective-permute-done.17, bf16[40,4096]{1,0:T(8,128)(2,1)} %get-tuple-element.79, ...), kind=kOutput, calls=%fused_computation.3 | convolution fusion | flops 89915392 | bytes 2379776 | tf_op jit(solution)/shard_map/dot_general | solution.py:332
  (120 shorter events, 32.7 us)
Async XLA Ops:
  7.2 64.4 %all-gather.4.cloned.1.call-start = ((), (), s32[]{:S(2)}) async-start(), calls=%async_computation.1 | async-start | bytes 9437184 | tf_op jit(solution)/shard_map/all_gather | solution.py:99
  7.9 63.6 %all-gather.6.cloned.1.call-start = ((), (), s32[]{:S(2)}) async-start(), calls=%async_computation.2 | async-start | bytes 9437184 | tf_op jit(solution)/shard_map/all_gather | solution.py:99
  8.7 62.9 %all-gather.8.cloned.1.call-start = ((), (), s32[]{:S(2)}) async-start(), calls=%async_computation.3 | async-start | bytes 9437184 | tf_op jit(solution)/shard_map/all_gather | solution.py:99
  10.6 17.4 %collective-permute-start = (bf16[64,4224]{1,0:T(8,128)(2,1)S(1)}, bf16[64,4224]{1,0:T(8,128)(2,1)S(1)}, u32[]{:S(2)}, u32[]{:S(2)}) collective-permute-start(bf16[64,4224]{1,0:T(8,128)(2,1)S(1)} %get-tuple-element.61), channel_id=1, source_target_pairs={{0,8},{1,9},{2,10},{3,11},{4,12},{5,13},{6,14},{7,15},{8,16},{9,17... | collective-permute-start | bytes 1622024 | tf_op jit(solution)/shard_map/ppermute | solution.py:90
  13.7 15.1 %collective-permute-start.8 = (bf16[40,4096]{1,0:T(8,128)(2,1)S(1)}, bf16[40,4096]{1,0:T(8,128)(2,1)S(1)}, u32[]{:S(2)}, u32[]{:S(2)}) collective-permute-start(bf16[40,4096]{1,0:T(8,128)(2,1)S(1)} %get-tuple-element.74), channel_id=1, source_target_pairs={{0,6},{1,7},{2,4},{3,5},{4,2},{5,3},{6,0},{7,1},{8,14},{9,15},{10,... | collective-permute-start | bytes 983048 | tf_op jit(solution)/shard_map/ppermute | solution.py:90
  16.1 15.2 %collective-permute-start.5 = (bf16[40,4096]{1,0:T(8,128)(2,1)S(1)}, bf16[40,4096]{1,0:T(8,128)(2,1)S(1)}, u32[]{:S(2)}, u32[]{:S(2)}) collective-permute-start(bf16[40,4096]{1,0:T(8,128)(2,1)S(1)} %get-tuple-element.69), channel_id=1, source_target_pairs={{0,4},{1,5},{2,6},{3,7},{4,0},{5,1},{6,2},{7,3},{8,12},{9,13},{10,... | collective-permute-start | bytes 983048 | tf_op jit(solution)/shard_map/ppermute | solution.py:90
  16.6 15.7 %collective-permute-start.2 = (bf16[40,4096]{1,0:T(8,128)(2,1)S(1)}, bf16[40,4096]{1,0:T(8,128)(2,1)S(1)}, u32[]{:S(2)}, u32[]{:S(2)}) collective-permute-start(bf16[40,4096]{1,0:T(8,128)(2,1)S(1)} %get-tuple-element.64), channel_id=1, source_target_pairs={{0,2},{1,3},{2,0},{3,1},{4,6},{5,7},{6,4},{7,5},{8,10},{9,11},{10,... | collective-permute-start | bytes 983048 | tf_op jit(solution)/shard_map/ppermute | solution.py:90
  28.0 15.3 %collective-permute-start.1 = (bf16[64,4224]{1,0:T(8,128)(2,1)S(1)}, bf16[64,4224]{1,0:T(8,128)(2,1)S(1)}, u32[]{:S(2)}, u32[]{:S(2)}) collective-permute-start(bf16[64,4224]{1,0:T(8,128)(2,1)S(1)} %collective-permute-done.block_ref), channel_id=1, source_target_pairs={{0,8},{1,9},{2,10},{3,11},{4,12},{5,13},{6,14},{7,15},{8,16},{9,17... | collective-permute-start | bytes 1622024 | tf_op jit(solution)/shard_map/ppermute | solution.py:90
  28.8 15.3 %collective-permute-start.9 = (bf16[40,4096]{1,0:T(8,128)(2,1)S(1)}, bf16[40,4096]{1,0:T(8,128)(2,1)S(1)}, u32[]{:S(2)}, u32[]{:S(2)}) collective-permute-start(bf16[40,4096]{1,0:T(8,128)(2,1)S(1)} %get-tuple-element.75), channel_id=1, source_target_pairs={{0,6},{1,7},{2,4},{3,5},{4,2},{5,3},{6,0},{7,1},{8,14},{9,15},{10,... | collective-permute-start | bytes 983048 | tf_op jit(solution)/shard_map/ppermute | solution.py:90
  31.3 15.0 %collective-permute-start.6 = (bf16[40,4096]{1,0:T(8,128)(2,1)S(1)}, bf16[40,4096]{1,0:T(8,128)(2,1)S(1)}, u32[]{:S(2)}, u32[]{:S(2)}) collective-permute-start(bf16[40,4096]{1,0:T(8,128)(2,1)S(1)} %get-tuple-element.70), channel_id=1, source_target_pairs={{0,4},{1,5},{2,6},{3,7},{4,0},{5,1},{6,2},{7,3},{8,12},{9,13},{10,... | collective-permute-start | bytes 983048 | tf_op jit(solution)/shard_map/ppermute | solution.py:90
  32.3 14.7 %collective-permute-start.3 = (bf16[40,4096]{1,0:T(8,128)(2,1)S(1)}, bf16[40,4096]{1,0:T(8,128)(2,1)S(1)}, u32[]{:S(2)}, u32[]{:S(2)}) collective-permute-start(bf16[40,4096]{1,0:T(8,128)(2,1)S(1)} %get-tuple-element.65), channel_id=1, source_target_pairs={{0,2},{1,3},{2,0},{3,1},{4,6},{5,7},{6,4},{7,5},{8,10},{9,11},{10,... | collective-permute-start | bytes 983048 | tf_op jit(solution)/shard_map/ppermute | solution.py:90
  43.2 17.6 %collective-permute-start.11 = (bf16[64,4224]{1,0:T(8,128)(2,1)S(1)}, bf16[64,4224]{1,0:T(8,128)(2,1)S(1)}, u32[]{:S(2)}, u32[]{:S(2)}) collective-permute-start(bf16[64,4224]{1,0:T(8,128)(2,1)S(1)} %collective-permute-done.1.block_ref), channel_id=1, source_target_pairs={{0,8},{1,9},{2,10},{3,11},{4,12},{5,13},{6,14},{7,15},{8,16},{9,17... | collective-permute-start | bytes 1622024 | tf_op jit(solution)/shard_map/ppermute | solution.py:90
  61.7 28.4 %collective-permute-start.14 = (bf16[40,4096]{1,0:T(8,128)(2,1)S(1)}, bf16[40,4096]{1,0:T(8,128)(2,1)S(1)}, u32[]{:S(2)}, u32[]{:S(2)}) collective-permute-start(bf16[40,4096]{1,0:T(8,128)(2,1)S(1)} %get-tuple-element.95), channel_id=1, source_target_pairs={{0,6},{1,7},{2,4},{3,5},{4,2},{5,3},{6,0},{7,1},{8,14},{9,15},{10,... | collective-permute-start | bytes 983048 | tf_op jit(solution)/shard_map/ppermute | solution.py:90
  63.7 24.9 %collective-permute-start.13 = (bf16[40,4096]{1,0:T(8,128)(2,1)S(1)}, bf16[40,4096]{1,0:T(8,128)(2,1)S(1)}, u32[]{:S(2)}, u32[]{:S(2)}) collective-permute-start(bf16[40,4096]{1,0:T(8,128)(2,1)S(1)} %get-tuple-element.93), channel_id=1, source_target_pairs={{0,4},{1,5},{2,6},{3,7},{4,0},{5,1},{6,2},{7,3},{8,12},{9,13},{10,... | collective-permute-start | bytes 983048 | tf_op jit(solution)/shard_map/ppermute | solution.py:90
  64.2 22.5 %collective-permute-start.12 = (bf16[40,4096]{1,0:T(8,128)(2,1)S(1)}, bf16[40,4096]{1,0:T(8,128)(2,1)}, u32[]{:S(2)}, u32[]{:S(2)}) collective-permute-start(bf16[40,4096]{1,0:T(8,128)(2,1)S(1)} %get-tuple-element.91), channel_id=1, source_target_pairs={{0,2},{1,3},{2,0},{3,1},{4,6},{5,7},{6,4},{7,5},{8,10},{9,11},{10,... | collective-permute-start | bytes 983048 | tf_op jit(solution)/shard_map/ppermute | solution.py:90
  65.2 78.6 %all-to-all-start = ((bf16[32,16,1152]{2,1,0:T(8,128)(2,1)}), bf16[32,16,1152]{2,1,0:T(8,128)(2,1)S(1)}, u32[]{:S(2)}, u32[]{:S(2)}) async-start(bf16[32,16,1152]{2,1,0:T(8,128)(2,1)} %shard_map.101), calls=%async_computation | async-start | bytes 2359296 | tf_op jit(solution)/shard_map/all_to_all | solution.py:81
  86.7 19.3 %collective-permute-start.24 = (bf16[40,4096]{1,0:T(8,128)(2,1)}, bf16[40,4096]{1,0:T(8,128)(2,1)S(1)}, u32[]{:S(2)}, u32[]{:S(2)}) collective-permute-start(bf16[40,4096]{1,0:T(8,128)(2,1)} %get-tuple-element.113), channel_id=1, source_target_pairs={{0,2},{1,3},{2,0},{3,1},{4,6},{5,7},{6,4},{7,5},{8,10},{9,11},{10,... | collective-permute-start | bytes 983048 | tf_op jit(solution)/shard_map/ppermute | solution.py:90
  88.6 18.7 %collective-permute-start.15 = (bf16[40,4096]{1,0:T(8,128)(2,1)}, bf16[40,4096]{1,0:T(8,128)(2,1)S(1)}, u32[]{:S(2)}, u32[]{:S(2)}) collective-permute-start(bf16[40,4096]{1,0:T(8,128)(2,1)} %get-tuple-element.97), channel_id=1, source_target_pairs={{0,4},{1,5},{2,6},{3,7},{4,0},{5,1},{6,2},{7,3},{8,12},{9,13},{10,... | collective-permute-start | bytes 983048 | tf_op jit(solution)/shard_map/ppermute | solution.py:90
  90.0 17.2 %collective-permute-start.18 = (bf16[40,4096]{1,0:T(8,128)(2,1)}, bf16[40,4096]{1,0:T(8,128)(2,1)S(1)}, u32[]{:S(2)}, u32[]{:S(2)}) collective-permute-start(bf16[40,4096]{1,0:T(8,128)(2,1)} %get-tuple-element.102), channel_id=1, source_target_pairs={{0,6},{1,7},{2,4},{3,5},{4,2},{5,3},{6,0},{7,1},{8,14},{9,15},{10,... | collective-permute-start | bytes 983048 | tf_op jit(solution)/shard_map/ppermute | solution.py:90
  107.6 18.6 %collective-permute-start.27 = (bf16[64,4096]{1,0:T(8,128)(2,1)S(1)}, bf16[64,4096]{1,0:T(8,128)(2,1)S(1)}, u32[]{:S(2)}, u32[]{:S(2)}) collective-permute-start(bf16[64,4096]{1,0:T(8,128)(2,1)S(1)} %convolution_convert_fusion), channel_id=1, source_target_pairs={{0,8},{1,9},{2,10},{3,11},{4,12},{5,13},{6,14},{7,15},{8,16},{9,17... | collective-permute-start | bytes 1572872 | tf_op jit(solution)/shard_map/ppermute | solution.py:90
  110.2 15.9 %collective-permute-start.25 = (bf16[40,4096]{1,0:T(8,128)(2,1)S(1)}, bf16[40,4096]{1,0:T(8,128)(2,1)S(1)}, u32[]{:S(2)}, u32[]{:S(2)}) collective-permute-start(bf16[40,4096]{1,0:T(8,128)(2,1)S(1)} %copy-done.23), channel_id=1, source_target_pairs={{0,4},{1,5},{2,6},{3,7},{4,0},{5,1},{6,2},{7,3},{8,12},{9,13},{10,... | collective-permute-start | bytes 983048 | tf_op jit(solution)/shard_map/ppermute | solution.py:90
  111.2 15.0 %collective-permute-start.16 = (bf16[40,4096]{1,0:T(8,128)(2,1)S(1)}, bf16[40,4096]{1,0:T(8,128)(2,1)S(1)}, u32[]{:S(2)}, u32[]{:S(2)}) collective-permute-start(bf16[40,4096]{1,0:T(8,128)(2,1)S(1)} %copy-done.22), channel_id=1, source_target_pairs={{0,6},{1,7},{2,4},{3,5},{4,2},{5,3},{6,0},{7,1},{8,14},{9,15},{10,... | collective-permute-start | bytes 983048 | tf_op jit(solution)/shard_map/ppermute | solution.py:90
  126.6 16.4 %collective-permute-start.28 = (bf16[64,4096]{1,0:T(8,128)(2,1)S(1)}, bf16[64,4096]{1,0:T(8,128)(2,1)S(1)}, u32[]{:S(2)}, u32[]{:S(2)}) collective-permute-start(bf16[64,4096]{1,0:T(8,128)(2,1)S(1)} %fusion.2), channel_id=1, source_target_pairs={{0,8},{1,9},{2,10},{3,11},{4,12},{5,13},{6,14},{7,15},{8,16},{9,17... | collective-permute-start | bytes 1572872 | tf_op jit(solution)/shard_map/ppermute | solution.py:90
  143.4 14.8 %collective-permute-start.29 = (bf16[64,4096]{1,0:T(8,128)(2,1)S(1)}, bf16[64,4096]{1,0:T(8,128)(2,1)S(1)}, u32[]{:S(2)}, u32[]{:S(2)}) collective-permute-start(bf16[64,4096]{1,0:T(8,128)(2,1)S(1)} %fusion.1), channel_id=1, source_target_pairs={{0,8},{1,9},{2,10},{3,11},{4,12},{5,13},{6,14},{7,15},{8,16},{9,17... | collective-permute-start | bytes 1572872 | tf_op jit(solution)/shard_map/ppermute | solution.py:90
  (38 other events, 416.6 us)
Sparse Core Ops, SparseCore 0:
  9.5 19.2 all-gather.3
  30.4 17.7 all-gather.5
  49.7 17.9 all-gather.7

commit v8 on v6

--- a/solution.py
+++ b/solution.py
@@ -179,7 +179,7 @@
         out_specs=[pl.BlockSpec(memory_space=pltpu.VMEM)] * len(outs),
         compiler_params=pltpu.CompilerParams(vmem_limit_bytes=16 * 2**20),
         cost_estimate=pl.CostEstimate(
-            flops=2 * rows * PLANE * capacity * width,
+            flops=1200 * rows * PLANE * capacity * width,
             bytes_accessed=2 * width * (rows + PLANE * capacity),
             transcendentals=0,
         ),
@@ -303,8 +303,7 @@
             )
         blends.append(blend)
         if s < 3:
-            earlier = [block] + (got[s - 1][1:] if s else []) + ([outgoing] if s == 1 else [])
-            swapped.append(send(after(weights[s], *swapped, *earlier), flip=1))
+            swapped.append(send(after(weights[s], *swapped, block), flip=1))
         for j in range(1, PLANE):
             piece = after(pieces[j], got[s - 1][j]) if s else pieces[j]
             pieces[j] = send(piece, flip=2 * j)
@@ -318,7 +317,7 @@
         held[0][0] = after(held[0][0], *outs, *following)
         outs.extend(work(held, *zip(weights, swapped)))
 
-    arrived = exchange(after(outgoing, *got[-2][1:], block))
+    arrived = exchange(after(outgoing, block))
     order = list(range(1, planes)) + [0]
     sent, landed = {}, got[-1][1:]
     for s in order:

time: 167 us -> 157 us (0.940)
  waiting for transfers between devices: 71.4 us -> 62.6 us
    ppermute x33, waiting for transfers between devices: 71.4 us -> 62.6 us  [send(): return lax.ppermute(x, 'expert', pairs)]
    ppermute x33, starting transfers between devices: 39 us -> 36.8 us  [send(): return lax.ppermute(x, 'expert', pairs)]
    all_to_all x1, starting transfers between devices: 3.57 us -> 5.6 us  [exchange(): return lax.all_to_all(x, 'expert', split_axis=0, concat_axis=0, tiled=True)]
    unnamed x58 -> x68, local copies, waits for them, and re-layouts: 5.14 us -> 4.6 us
  transfers between devices with their start and end apart: 34 -> 34, of which waited for: 16 -> 13; matrix products, arithmetic and copies ran while one was open for 4% -> 4% of each run, Pallas kernels for 22% -> 24%
where the time goes in v8:
time: 157 us
  waiting for transfers between devices  62.6 us (40%)
  starting transfers between devices  42.4 us (27%)
  Pallas kernels  38.2 us (24%)
  matrix products  7.28 us (5%)
  local copies, waits for them, and re-layouts  4.6 us (3%)
    ppermute x33, waiting for transfers between devices, send(): return lax.ppermute(x, 'expert', pairs)  62.6 us
    ppermute x33, starting transfers between devices, send(): return lax.ppermute(x, 'expert', pairs)  36.8 us
    pallas_call x2, Pallas kernels, apply(): pl.pallas_call(functools.partial(expert_kernel, len(pieces), steps), grid...  30.7 us
    all_to_all x1, starting transfers between devices, exchange(): return lax.all_to_all(x, 'expert', split_axis=0, concat_axis=0, tiled=True)  5.6 us
    unnamed x68, local copies, waits for them, and re-layouts  4.6 us
    dot_general x4, matrix products, pick(): lax.dot_general(placing, rows, (((0,), (0,)), ((), ())), preferred_elemen...  4.11 us
    pallas_call x4, Pallas kernels, pick_pieces(): pl.pallas_call(functools.partial(body, experts, capacity, 512), out_shape...  3.45 us
    dot_general x4, matrix products, local(): jnp.dot(blends[s], jnp.concatenate(sent[s], axis=0), preferred_element_ty...  3.18 us
  transfers between devices with their start and end apart: 34, of which 13 were waited for; matrix products, arithmetic and copies ran while one was open for 4% of the time, Pallas kernels for 24%

profile of v8, /device:TPU:0, one launch (start us, length us, event | category | flops | bytes accessed | tf_op | source)
XLA Modules:
  0.0 156.7 jit_solution(853780526276438139)
XLA Ops:
  4.2 3.1 %collective-permute-start = (bf16[64,4224]{1,0:T(8,128)(2,1)S(1)}, bf16[64,4224]{1,0:T(8,128)(2,1)S(1)}, u32[]{:S(2)}, u32[]{:S(2)}) collective-permute-start(bf16[64,4224]{1,0:T(8,128)(2,1)S(1)} %get-tuple-element.64), channel_id=1, source_target_pairs={{0,8},{1,9},{2,10},{3,11},{4,12},{5,13},{6,14},{7,15},{8,16},{9,17... | collective-permute-start | bytes 1622024 | tf_op jit(solution)/shard_map/ppermute | solution.py:90
  7.3 2.4 %collective-permute-start.8 = (bf16[40,4096]{1,0:T(8,128)(2,1)S(1)}, bf16[40,4096]{1,0:T(8,128)(2,1)S(1)}, u32[]{:S(2)}, u32[]{:S(2)}) collective-permute-start(bf16[40,4096]{1,0:T(8,128)(2,1)S(1)} %get-tuple-element.77), channel_id=1, source_target_pairs={{0,6},{1,7},{2,4},{3,5},{4,2},{5,3},{6,0},{7,1},{8,14},{9,15},{10,... | collective-permute-start | bytes 983048 | tf_op jit(solution)/shard_map/ppermute | solution.py:90
  10.8 2.0 %shard_map.101 = bf16[32,16,1152]{2,1,0:T(8,128)(2,1)} custom-call(s32[32]{0:T(128)S(1)} %copy-done.4, bf16[32,16,1024]{2,1,0:T(8,128)(2,1)S(1)} %copy-done), custom_call_target="tpu_custom_call" | custom-call | bytes 3145728 | tf_op jit(solution)/shard_map/pallas_call | solution.py:34
  13.8 7.8 %collective-permute-done.block_ref = bf16[64,4224]{1,0:T(8,128)(2,1)S(1)} collective-permute-done((bf16[64,4224]{1,0:T(8,128)(2,1)S(1)}, bf16[64,4224]{1,0:T(8,128)(2,1)S(1)}, u32[]{:S(2)}, u32[]{:S(2)}) %collective-permute-start) | collective-permute-done | bytes 540704 | tf_op jit(solution)/shard_map/ppermute | solution.py:90
  22.4 2.5 %collective-permute-start.9 = (bf16[40,4096]{1,0:T(8,128)(2,1)S(1)}, bf16[40,4096]{1,0:T(8,128)(2,1)S(1)}, u32[]{:S(2)}, u32[]{:S(2)}) collective-permute-start(bf16[40,4096]{1,0:T(8,128)(2,1)S(1)} %get-tuple-element.78), channel_id=1, source_target_pairs={{0,6},{1,7},{2,4},{3,5},{4,2},{5,3},{6,0},{7,1},{8,14},{9,15},{10,... | collective-permute-start | bytes 983048 | tf_op jit(solution)/shard_map/ppermute | solution.py:90
  25.4 1.8 %collective-permute-start.6 = (bf16[40,4096]{1,0:T(8,128)(2,1)S(1)}, bf16[40,4096]{1,0:T(8,128)(2,1)S(1)}, u32[]{:S(2)}, u32[]{:S(2)}) collective-permute-start(bf16[40,4096]{1,0:T(8,128)(2,1)S(1)} %get-tuple-element.73), channel_id=1, source_target_pairs={{0,4},{1,5},{2,6},{3,7},{4,0},{5,1},{6,2},{7,3},{8,12},{9,13},{10,... | collective-permute-start | bytes 983048 | tf_op jit(solution)/shard_map/ppermute | solution.py:90
  27.6 9.2 %collective-permute-done.1.block_ref = bf16[64,4224]{1,0:T(8,128)(2,1)S(1)} collective-permute-done((bf16[64,4224]{1,0:T(8,128)(2,1)S(1)}, bf16[64,4224]{1,0:T(8,128)(2,1)S(1)}, u32[]{:S(2)}, u32[]{:S(2)}) %collective-permute-start.1) | collective-permute-done | bytes 540704 | tf_op jit(solution)/shard_map/ppermute | solution.py:90
  38.5 2.2 %collective-permute-start.10 = (bf16[40,4096]{1,0:T(8,128)(2,1)S(1)}, bf16[40,4096]{1,0:T(8,128)(2,1)S(1)}, u32[]{:S(2)}, u32[]{:S(2)}) collective-permute-start(bf16[40,4096]{1,0:T(8,128)(2,1)S(1)} %get-tuple-element.79), channel_id=1, source_target_pairs={{0,6},{1,7},{2,4},{3,5},{4,2},{5,3},{6,0},{7,1},{8,14},{9,15},{10,... | collective-permute-start | bytes 983048 | tf_op jit(solution)/shard_map/ppermute | solution.py:90
  44.5 5.5 %collective-permute-done.10.refs_3_ = bf16[40,4096]{1,0:T(8,128)(2,1)S(1)} collective-permute-done((bf16[40,4096]{1,0:T(8,128)(2,1)S(1)}, bf16[40,4096]{1,0:T(8,128)(2,1)S(1)}, u32[]{:S(2)}, u32[]{:S(2)}) %collective-permute-start.10) | collective-permute-done | bytes 327712 | tf_op jit(solution)/shard_map/ppermute | solution.py:90
  50.0 5.9 %collective-permute-done.7.refs_2_ = bf16[40,4096]{1,0:T(8,128)(2,1)S(1)} collective-permute-done((bf16[40,4096]{1,0:T(8,128)(2,1)S(1)}, bf16[40,4096]{1,0:T(8,128)(2,1)S(1)}, u32[]{:S(2)}, u32[]{:S(2)}) %collective-permute-start.7) | collective-permute-done | bytes 327712 | tf_op jit(solution)/shard_map/ppermute | solution.py:90
  57.7 2.2 %collective-permute-start.17 = (bf16[40,4096]{1,0:T(8,128)(2,1)S(1)}, bf16[40,4096]{1,0:T(8,128)(2,1)S(1)}, u32[]{:S(2)}, u32[]{:S(2)}) collective-permute-start(bf16[40,4096]{1,0:T(8,128)(2,1)S(1)} %get-tuple-element.101), channel_id=1, source_target_pairs={{0,6},{1,7},{2,4},{3,5},{4,2},{5,3},{6,0},{7,1},{8,14},{9,15},{10,... | collective-permute-start | bytes 983048 | tf_op jit(solution)/shard_map/ppermute | solution.py:90
  61.2 5.6 %all-to-all-start = ((bf16[32,16,1152]{2,1,0:T(8,128)(2,1)}), bf16[32,16,1152]{2,1,0:T(8,128)(2,1)S(1)}, u32[]{:S(2)}, u32[]{:S(2)}) async-start(bf16[32,16,1152]{2,1,0:T(8,128)(2,1)} %shard_map.101), calls=%async_computation | async-start | bytes 2359296 | tf_op jit(solution)/shard_map/all_to_all | solution.py:81
  67.9 15.4 %shard_map.98 = (bf16[40,4096]{1,0:T(8,128)(2,1)}, bf16[40,4096]{1,0:T(8,128)(2,1)}, bf16[40,4096]{1,0:T(8,128)(2,1)}, bf16[40,4096]{1,0:T(8,128)(2,1)}, bf16[40...) custom-call(bf16[40,4096]{1,0:T(8,128)(2,1)} %convolution_convert_fusion.4.re, ...), custom_call_target="tpu_custom_call" | custom-call | flops 6039797760 | bytes 24117248 | tf_op jit(solution)/shard_map/pallas_call | solution.py:238
  83.3 1.8 %collective-permute-start.27 = (bf16[40,4096]{1,0:T(8,128)(2,1)}, bf16[40,4096]{1,0:T(8,128)(2,1)S(1)}, u32[]{:S(2)}, u32[]{:S(2)}) collective-permute-start(bf16[40,4096]{1,0:T(8,128)(2,1)} %get-tuple-element.119), channel_id=1, source_target_pairs={{0,2},{1,3},{2,0},{3,1},{4,6},{5,7},{6,4},{7,5},{8,10},{9,11},{10,... | collective-permute-start | bytes 983048 | tf_op jit(solution)/shard_map/ppermute | solution.py:90
  87.3 15.4 %shard_map.100 = (bf16[40,4096]{1,0:T(8,128)(2,1)}, bf16[40,4096]{1,0:T(8,128)(2,1)}, bf16[40,4096]{1,0:T(8,128)(2,1)}, bf16[40,4096]{1,0:T(8,128)(2,1)}, bf16[4...) custom-call(bf16[40,4096]{1,0:T(8,128)(2,1)} %convolution_convert_fusion.2.r, ...), custom_call_target="tpu_custom_call" | custom-call | flops 6039797760 | bytes 24117248 | tf_op jit(solution)/shard_map/pallas_call | solution.py:238
  104.1 1.8 %collective-permute-start.30 = (bf16[64,4096]{1,0:T(8,128)(2,1)S(1)}, bf16[64,4096]{1,0:T(8,128)(2,1)S(1)}, u32[]{:S(2)}, u32[]{:S(2)}) collective-permute-start(bf16[64,4096]{1,0:T(8,128)(2,1)S(1)} %convolution_convert_fusion), channel_id=1, source_target_pairs={{0,8},{1,9},{2,10},{3,11},{4,12},{5,13},{6,14},{7,15},{8,16},{9,17... | collective-permute-start | bytes 1572872 | tf_op jit(solution)/shard_map/ppermute | solution.py:90
  109.5 7.1 %collective-permute-done.24 = bf16[40,4096]{1,0:T(8,128)(2,1)S(1)} collective-permute-done((bf16[40,4096]{1,0:T(8,128)(2,1)S(1)}, bf16[40,4096]{1,0:T(8,128)(2,1)S(1)}, u32[]{:S(2)}, u32[]{:S(2)}) %collective-permute-start.24) | collective-permute-done | bytes 327712 | tf_op jit(solution)/shard_map/ppermute | solution.py:90
  116.7 5.4 %collective-permute-done.19 = bf16[40,4096]{1,0:T(8,128)(2,1)S(1)} collective-permute-done((bf16[40,4096]{1,0:T(8,128)(2,1)S(1)}, bf16[40,4096]{1,0:T(8,128)(2,1)S(1)}, u32[]{:S(2)}, u32[]{:S(2)}) %collective-permute-start.19) | collective-permute-done | bytes 327712 | tf_op jit(solution)/shard_map/ppermute | solution.py:90
  127.6 7.2 %collective-permute-done.22 = bf16[40,4096]{1,0:T(8,128)(2,1)S(1)} collective-permute-done((bf16[40,4096]{1,0:T(8,128)(2,1)S(1)}, bf16[40,4096]{1,0:T(8,128)(2,1)S(1)}, u32[]{:S(2)}, u32[]{:S(2)}) %collective-permute-start.22) | collective-permute-done | bytes 327712 | tf_op jit(solution)/shard_map/ppermute | solution.py:90
  134.8 5.0 %collective-permute-done.25 = bf16[40,4096]{1,0:T(8,128)(2,1)S(1)} collective-permute-done((bf16[40,4096]{1,0:T(8,128)(2,1)S(1)}, bf16[40,4096]{1,0:T(8,128)(2,1)S(1)}, u32[]{:S(2)}, u32[]{:S(2)}) %collective-permute-start.25) | collective-permute-done | bytes 327712 | tf_op jit(solution)/shard_map/ppermute | solution.py:90
  144.7 2.0 %shard_map.102 = bf16[32,16,1024]{2,1,0:T(8,128)(2,1)} custom-call(s32[32]{0:T(128)S(1)} %fusion.38.label_ref, bf16[32,16,1152]{2,1,0:T(8,128)(2,1)S(1)} %all-to-all-done.arrived_ref), custom_call_target="tpu_custom_call" | custom-call | bytes 2097152 | tf_op jit(solution)/shard_map/pallas_call | solution.py:65
  146.7 3.7 %collective-permute-done.20 = bf16[40,4096]{1,0:T(8,128)(2,1)S(1)} collective-permute-done((bf16[40,4096]{1,0:T(8,128)(2,1)S(1)}, bf16[40,4096]{1,0:T(8,128)(2,1)S(1)}, u32[]{:S(2)}, u32[]{:S(2)}) %collective-permute-start.20) | collective-permute-done | bytes 327712 | tf_op jit(solution)/shard_map/ppermute | solution.py:90
  150.3 4.2 %collective-permute-done.23 = bf16[40,4096]{1,0:T(8,128)(2,1)S(1)} collective-permute-done((bf16[40,4096]{1,0:T(8,128)(2,1)S(1)}, bf16[40,4096]{1,0:T(8,128)(2,1)S(1)}, u32[]{:S(2)}, u32[]{:S(2)}) %collective-permute-start.23) | collective-permute-done | bytes 327712 | tf_op jit(solution)/shard_map/ppermute | solution.py:90
  154.5 2.1 %fusion = bf16[64,4096]{1,0:T(8,128)(2,1)} fusion(bf16[64,160]{1,0:T(8,128)(2,1)S(1)} %copy-done.3, bf16[40,4096]{1,0:T(8,128)(2,1)S(1)} %collective-permute-done.26, bf16[40,4096]{1,0:T(8,128)(2,1)S(1)} %collective-permute-done.23, bf16[40,4096]{1,0:T(8,128)(2,1)S(1)} %collective-permute-done.20, bf16[40,4096]{1,0:T(8,128)(2,1)} %get-tuple-element.85, ...), kind=kOutput, calls=%fused_computation.3 | convolution fusion | flops 89915392 | bytes 2379776 | tf_op jit(solution)/shard_map/dot_general | solution.py:334
  (129 shorter events, 34.3 us)
Async XLA Ops:
  4.2 17.4 %collective-permute-start = (bf16[64,4224]{1,0:T(8,128)(2,1)S(1)}, bf16[64,4224]{1,0:T(8,128)(2,1)S(1)}, u32[]{:S(2)}, u32[]{:S(2)}) collective-permute-start(bf16[64,4224]{1,0:T(8,128)(2,1)S(1)} %get-tuple-element.64), channel_id=1, source_target_pairs={{0,8},{1,9},{2,10},{3,11},{4,12},{5,13},{6,14},{7,15},{8,16},{9,17... | collective-permute-start | bytes 1622024 | tf_op jit(solution)/shard_map/ppermute | solution.py:90
  7.3 29.6 %collective-permute-start.11 = (bf16[4096,384]{1,0:T(8,128)(2,1)S(1)}, bf16[4096,384]{1,0:T(8,128)(2,1)S(1)}, u32[]{:S(2)}, u32[]{:S(2)}) collective-permute-start(bf16[4096,384]{1,0:T(8,128)(2,1)S(1)} %copy-done.7), channel_id=1, source_target_pairs={{0,1},{1,0},{2,3},{3,2},{4,5},{5,4},{6,7},{7,6},{8,9},{9,8},{10,11... | collective-permute-start | bytes 9437192 | tf_op jit(solution)/shard_map/ppermute | solution.py:90
  7.3 15.1 %collective-permute-start.8 = (bf16[40,4096]{1,0:T(8,128)(2,1)S(1)}, bf16[40,4096]{1,0:T(8,128)(2,1)S(1)}, u32[]{:S(2)}, u32[]{:S(2)}) collective-permute-start(bf16[40,4096]{1,0:T(8,128)(2,1)S(1)} %get-tuple-element.77), channel_id=1, source_target_pairs={{0,6},{1,7},{2,4},{3,5},{4,2},{5,3},{6,0},{7,1},{8,14},{9,15},{10,... | collective-permute-start | bytes 983048 | tf_op jit(solution)/shard_map/ppermute | solution.py:90
  9.7 15.6 %collective-permute-start.5 = (bf16[40,4096]{1,0:T(8,128)(2,1)S(1)}, bf16[40,4096]{1,0:T(8,128)(2,1)S(1)}, u32[]{:S(2)}, u32[]{:S(2)}) collective-permute-start(bf16[40,4096]{1,0:T(8,128)(2,1)S(1)} %get-tuple-element.72), channel_id=1, source_target_pairs={{0,4},{1,5},{2,6},{3,7},{4,0},{5,1},{6,2},{7,3},{8,12},{9,13},{10,... | collective-permute-start | bytes 983048 | tf_op jit(solution)/shard_map/ppermute | solution.py:90
  10.2 17.0 %collective-permute-start.2 = (bf16[40,4096]{1,0:T(8,128)(2,1)S(1)}, bf16[40,4096]{1,0:T(8,128)(2,1)S(1)}, u32[]{:S(2)}, u32[]{:S(2)}) collective-permute-start(bf16[40,4096]{1,0:T(8,128)(2,1)S(1)} %get-tuple-element.67), channel_id=1, source_target_pairs={{0,2},{1,3},{2,0},{3,1},{4,6},{5,7},{6,4},{7,5},{8,10},{9,11},{10,... | collective-permute-start | bytes 983048 | tf_op jit(solution)/shard_map/ppermute | solution.py:90
  21.6 15.3 %collective-permute-start.1 = (bf16[64,4224]{1,0:T(8,128)(2,1)S(1)}, bf16[64,4224]{1,0:T(8,128)(2,1)S(1)}, u32[]{:S(2)}, u32[]{:S(2)}) collective-permute-start(bf16[64,4224]{1,0:T(8,128)(2,1)S(1)} %collective-permute-done.block_ref), channel_id=1, source_target_pairs={{0,8},{1,9},{2,10},{3,11},{4,12},{5,13},{6,14},{7,15},{8,16},{9,17... | collective-permute-start | bytes 1622024 | tf_op jit(solution)/shard_map/ppermute | solution.py:90
  22.4 16.1 %collective-permute-start.9 = (bf16[40,4096]{1,0:T(8,128)(2,1)S(1)}, bf16[40,4096]{1,0:T(8,128)(2,1)S(1)}, u32[]{:S(2)}, u32[]{:S(2)}) collective-permute-start(bf16[40,4096]{1,0:T(8,128)(2,1)S(1)} %get-tuple-element.78), channel_id=1, source_target_pairs={{0,6},{1,7},{2,4},{3,5},{4,2},{5,3},{6,0},{7,1},{8,14},{9,15},{10,... | collective-permute-start | bytes 983048 | tf_op jit(solution)/shard_map/ppermute | solution.py:90
  25.4 15.3 %collective-permute-start.6 = (bf16[40,4096]{1,0:T(8,128)(2,1)S(1)}, bf16[40,4096]{1,0:T(8,128)(2,1)S(1)}, u32[]{:S(2)}, u32[]{:S(2)}) collective-permute-start(bf16[40,4096]{1,0:T(8,128)(2,1)S(1)} %get-tuple-element.73), channel_id=1, source_target_pairs={{0,4},{1,5},{2,6},{3,7},{4,0},{5,1},{6,2},{7,3},{8,12},{9,13},{10,... | collective-permute-start | bytes 983048 | tf_op jit(solution)/shard_map/ppermute | solution.py:90
  36.8 19.2 %collective-permute-start.14 = (bf16[64,4224]{1,0:T(8,128)(2,1)S(1)}, bf16[64,4224]{1,0:T(8,128)(2,1)S(1)}, u32[]{:S(2)}, u32[]{:S(2)}) collective-permute-start(bf16[64,4224]{1,0:T(8,128)(2,1)S(1)} %collective-permute-done.1.block_ref), channel_id=1, source_target_pairs={{0,8},{1,9},{2,10},{3,11},{4,12},{5,13},{6,14},{7,15},{8,16},{9,17... | collective-permute-start | bytes 1622024 | tf_op jit(solution)/shard_map/ppermute | solution.py:90
  36.9 19.0 %collective-permute-start.12 = (bf16[4096,384]{1,0:T(8,128)(2,1)S(1)}, bf16[4096,384]{1,0:T(8,128)(2,1)S(1)}, u32[]{:S(2)}, u32[]{:S(2)}) collective-permute-start(bf16[4096,384]{1,0:T(8,128)(2,1)S(1)} %copy-done.8), channel_id=1, source_target_pairs={{0,1},{1,0},{2,3},{3,2},{4,5},{5,4},{6,7},{7,6},{8,9},{9,8},{10,11... | collective-permute-start | bytes 9437192 | tf_op jit(solution)/shard_map/ppermute | solution.py:90
  40.7 15.2 %collective-permute-start.7 = (bf16[40,4096]{1,0:T(8,128)(2,1)S(1)}, bf16[40,4096]{1,0:T(8,128)(2,1)S(1)}, u32[]{:S(2)}, u32[]{:S(2)}) collective-permute-start(bf16[40,4096]{1,0:T(8,128)(2,1)S(1)} %get-tuple-element.74), channel_id=1, source_target_pairs={{0,4},{1,5},{2,6},{3,7},{4,0},{5,1},{6,2},{7,3},{8,12},{9,13},{10,... | collective-permute-start | bytes 983048 | tf_op jit(solution)/shard_map/ppermute | solution.py:90
  41.2 14.7 %collective-permute-start.4 = (bf16[40,4096]{1,0:T(8,128)(2,1)S(1)}, bf16[40,4096]{1,0:T(8,128)(2,1)S(1)}, u32[]{:S(2)}, u32[]{:S(2)}) collective-permute-start(bf16[40,4096]{1,0:T(8,128)(2,1)S(1)} %get-tuple-element.69), channel_id=1, source_target_pairs={{0,2},{1,3},{2,0},{3,1},{4,6},{5,7},{6,4},{7,5},{8,10},{9,11},{10,... | collective-permute-start | bytes 983048 | tf_op jit(solution)/shard_map/ppermute | solution.py:90
  57.7 28.8 %collective-permute-start.17 = (bf16[40,4096]{1,0:T(8,128)(2,1)S(1)}, bf16[40,4096]{1,0:T(8,128)(2,1)S(1)}, u32[]{:S(2)}, u32[]{:S(2)}) collective-permute-start(bf16[40,4096]{1,0:T(8,128)(2,1)S(1)} %get-tuple-element.101), channel_id=1, source_target_pairs={{0,6},{1,7},{2,4},{3,5},{4,2},{5,3},{6,0},{7,1},{8,14},{9,15},{10,... | collective-permute-start | bytes 983048 | tf_op jit(solution)/shard_map/ppermute | solution.py:90
  59.9 25.2 %collective-permute-start.16 = (bf16[40,4096]{1,0:T(8,128)(2,1)S(1)}, bf16[40,4096]{1,0:T(8,128)(2,1)S(1)}, u32[]{:S(2)}, u32[]{:S(2)}) collective-permute-start(bf16[40,4096]{1,0:T(8,128)(2,1)S(1)} %get-tuple-element.99), channel_id=1, source_target_pairs={{0,4},{1,5},{2,6},{3,7},{4,0},{5,1},{6,2},{7,3},{8,12},{9,13},{10,... | collective-permute-start | bytes 983048 | tf_op jit(solution)/shard_map/ppermute | solution.py:90
  60.5 22.8 %collective-permute-start.15 = (bf16[40,4096]{1,0:T(8,128)(2,1)S(1)}, bf16[40,4096]{1,0:T(8,128)(2,1)}, u32[]{:S(2)}, u32[]{:S(2)}) collective-permute-start(bf16[40,4096]{1,0:T(8,128)(2,1)S(1)} %get-tuple-element.97), channel_id=1, source_target_pairs={{0,2},{1,3},{2,0},{3,1},{4,6},{5,7},{6,4},{7,5},{8,10},{9,11},{10,... | collective-permute-start | bytes 983048 | tf_op jit(solution)/shard_map/ppermute | solution.py:90
  61.2 79.3 %all-to-all-start = ((bf16[32,16,1152]{2,1,0:T(8,128)(2,1)}), bf16[32,16,1152]{2,1,0:T(8,128)(2,1)S(1)}, u32[]{:S(2)}, u32[]{:S(2)}) async-start(bf16[32,16,1152]{2,1,0:T(8,128)(2,1)} %shard_map.101), calls=%async_computation | async-start | bytes 2359296 | tf_op jit(solution)/shard_map/all_to_all | solution.py:81
  83.3 19.4 %collective-permute-start.27 = (bf16[40,4096]{1,0:T(8,128)(2,1)}, bf16[40,4096]{1,0:T(8,128)(2,1)S(1)}, u32[]{:S(2)}, u32[]{:S(2)}) collective-permute-start(bf16[40,4096]{1,0:T(8,128)(2,1)} %get-tuple-element.119), channel_id=1, source_target_pairs={{0,2},{1,3},{2,0},{3,1},{4,6},{5,7},{6,4},{7,5},{8,10},{9,11},{10,... | collective-permute-start | bytes 983048 | tf_op jit(solution)/shard_map/ppermute | solution.py:90
  85.1 18.7 %collective-permute-start.18 = (bf16[40,4096]{1,0:T(8,128)(2,1)}, bf16[40,4096]{1,0:T(8,128)(2,1)S(1)}, u32[]{:S(2)}, u32[]{:S(2)}) collective-permute-start(bf16[40,4096]{1,0:T(8,128)(2,1)} %get-tuple-element.103), channel_id=1, source_target_pairs={{0,4},{1,5},{2,6},{3,7},{4,0},{5,1},{6,2},{7,3},{8,12},{9,13},{10,... | collective-permute-start | bytes 983048 | tf_op jit(solution)/shard_map/ppermute | solution.py:90
  86.6 17.2 %collective-permute-start.21 = (bf16[40,4096]{1,0:T(8,128)(2,1)}, bf16[40,4096]{1,0:T(8,128)(2,1)S(1)}, u32[]{:S(2)}, u32[]{:S(2)}) collective-permute-start(bf16[40,4096]{1,0:T(8,128)(2,1)} %get-tuple-element.108), channel_id=1, source_target_pairs={{0,6},{1,7},{2,4},{3,5},{4,2},{5,3},{6,0},{7,1},{8,14},{9,15},{10,... | collective-permute-start | bytes 983048 | tf_op jit(solution)/shard_map/ppermute | solution.py:90
  104.1 18.0 %collective-permute-start.30 = (bf16[64,4096]{1,0:T(8,128)(2,1)S(1)}, bf16[64,4096]{1,0:T(8,128)(2,1)S(1)}, u32[]{:S(2)}, u32[]{:S(2)}) collective-permute-start(bf16[64,4096]{1,0:T(8,128)(2,1)S(1)} %convolution_convert_fusion), channel_id=1, source_target_pairs={{0,8},{1,9},{2,10},{3,11},{4,12},{5,13},{6,14},{7,15},{8,16},{9,17... | collective-permute-start | bytes 1572872 | tf_op jit(solution)/shard_map/ppermute | solution.py:90
  107.7 14.4 %collective-permute-start.19 = (bf16[40,4096]{1,0:T(8,128)(2,1)S(1)}, bf16[40,4096]{1,0:T(8,128)(2,1)S(1)}, u32[]{:S(2)}, u32[]{:S(2)}) collective-permute-start(bf16[40,4096]{1,0:T(8,128)(2,1)S(1)} %copy-done.28), channel_id=1, source_target_pairs={{0,6},{1,7},{2,4},{3,5},{4,2},{5,3},{6,0},{7,1},{8,14},{9,15},{10,... | collective-permute-start | bytes 983048 | tf_op jit(solution)/shard_map/ppermute | solution.py:90
  122.5 17.2 %collective-permute-start.31 = (bf16[64,4096]{1,0:T(8,128)(2,1)S(1)}, bf16[64,4096]{1,0:T(8,128)(2,1)S(1)}, u32[]{:S(2)}, u32[]{:S(2)}) collective-permute-start(bf16[64,4096]{1,0:T(8,128)(2,1)S(1)} %fusion.2), channel_id=1, source_target_pairs={{0,8},{1,9},{2,10},{3,11},{4,12},{5,13},{6,14},{7,15},{8,16},{9,17... | collective-permute-start | bytes 1572872 | tf_op jit(solution)/shard_map/ppermute | solution.py:90
  125.7 14.1 %collective-permute-start.25 = (bf16[40,4096]{1,0:T(8,128)(2,1)S(1)}, bf16[40,4096]{1,0:T(8,128)(2,1)S(1)}, u32[]{:S(2)}, u32[]{:S(2)}) collective-permute-start(bf16[40,4096]{1,0:T(8,128)(2,1)S(1)} %copy-done.24), channel_id=1, source_target_pairs={{0,4},{1,5},{2,6},{3,7},{4,0},{5,1},{6,2},{7,3},{8,12},{9,13},{10,... | collective-permute-start | bytes 983048 | tf_op jit(solution)/shard_map/ppermute | solution.py:90
  140.1 14.4 %collective-permute-start.32 = (bf16[64,4096]{1,0:T(8,128)(2,1)S(1)}, bf16[64,4096]{1,0:T(8,128)(2,1)S(1)}, u32[]{:S(2)}, u32[]{:S(2)}) collective-permute-start(bf16[64,4096]{1,0:T(8,128)(2,1)S(1)} %fusion.1), channel_id=1, source_target_pairs={{0,8},{1,9},{2,10},{3,11},{4,12},{5,13},{6,14},{7,15},{8,16},{9,17... | collective-permute-start | bytes 1572872 | tf_op jit(solution)/shard_map/ppermute | solution.py:90
  (44 other events, 476.6 us)

commit v9 on v8

--- a/solution.py
+++ b/solution.py
@@ -204,8 +204,10 @@
     def _():
         rows = jnp.concatenate([ref[...].astype(jnp.float32) for ref in rows_in], axis=0)
         rows = rows.astype(jnp.bfloat16)
-        for total, weight in zip(sums, weights[:4]):
-            total[...] += jnp.dot(rows, weight[...], preferred_element_type=jnp.float32)
+        wide = jnp.concatenate([weight[...] for weight in weights[:4]], axis=1)
+        found = jnp.dot(rows, wide, preferred_element_type=jnp.float32)
+        for n, total in enumerate(sums):
+            total[...] += found[:, n * half : (n + 1) * half]
 
     @pl.when(i == steps - 1)
     def _():
@@ -227,7 +229,7 @@
     pieces = [piece for arrived in held for piece in arrived]
     each, width = pieces[0].shape
     rows, half = each * len(pieces), gate[0].shape[1]
-    step = 1024
+    step = 2048
     steps = width // step
     read = lambda i: jnp.minimum(i, steps - 1)
     write = lambda i: jnp.maximum(i - steps, 0)
@@ -287,7 +289,7 @@
     stride = 2 * PLANE
     capacity = min(tok_rows, 5 * tok_rows * chosen // (4 * experts))
     chip = lax.axis_index("expert") // 2
-    whole = capacity % 8 == 0 and width % 1024 == 0
+    whole = capacity % 8 == 0 and width % 2048 == 0
     choose, work = (pick_pieces, apply) if whole else (pick_plain, apply_plain)
     weights = (gate_weight, up_weight, down_weight)
     group = 2

time: 157 us -> 158 us (level)
  Pallas kernels: 38.2 us -> 34.4 us
  waiting for transfers between devices: 62.6 us -> 65.9 us
  starting transfers between devices: 42.4 us -> 44.2 us
    pallas_call x2, Pallas kernels: 30.7 us -> 27 us  [apply(): pl.pallas_call(functools.partial(expert_kernel, len(pieces), steps), grid...]
    ppermute x33, waiting for transfers between devices: 62.6 us -> 65.9 us  [send(): return lax.ppermute(x, 'expert', pairs)]
    ppermute x33, starting transfers between devices: 36.8 us -> 38.6 us  [send(): return lax.ppermute(x, 'expert', pairs)]
  transfers between devices with their start and end apart: 34 -> 34, of which waited for: 13 -> 14; matrix products, arithmetic and copies ran while one was open for 4% -> 4% of each run, Pallas kernels for 24% -> 21%
where the time goes in v9:
time: 158 us
  waiting for transfers between devices  65.9 us (42%)
  starting transfers between devices  44.2 us (28%)
  Pallas kernels  34.4 us (22%)
  matrix products  7.26 us (5%)
  local copies, waits for them, and re-layouts  4.14 us (3%)
    ppermute x33, waiting for transfers between devices, send(): return lax.ppermute(x, 'expert', pairs)  65.9 us
    ppermute x33, starting transfers between devices, send(): return lax.ppermute(x, 'expert', pairs)  38.6 us
    pallas_call x2, Pallas kernels, apply(): pl.pallas_call(functools.partial(expert_kernel, len(pieces), steps), grid...  27 us
    all_to_all x1, starting transfers between devices, exchange(): return lax.all_to_all(x, 'expert', split_axis=0, concat_axis=0, tiled=True)  5.6 us
    unnamed x68, local copies, waits for them, and re-layouts  4.14 us
    dot_general x4, matrix products, pick(): lax.dot_general(placing, rows, (((0,), (0,)), ((), ())), preferred_elemen...  4.11 us
    pallas_call x4, Pallas kernels, pick_pieces(): pl.pallas_call(functools.partial(body, experts, capacity, 512), out_shape...  3.45 us
  transfers between devices with their start and end apart: 34, of which 14 were waited for; matrix products, arithmetic and copies ran while one was open for 4% of the time, Pallas kernels for 21%

profile of v9, /device:TPU:0, one launch (start us, length us, event | category | flops | bytes accessed | tf_op | source)
XLA Modules:
  0.0 157.7 jit_solution(11203885419723257852)
XLA Ops:
  4.2 3.1 %collective-permute-start = (bf16[64,4224]{1,0:T(8,128)(2,1)S(1)}, bf16[64,4224]{1,0:T(8,128)(2,1)S(1)}, u32[]{:S(2)}, u32[]{:S(2)}) collective-permute-start(bf16[64,4224]{1,0:T(8,128)(2,1)S(1)} %get-tuple-element.64), channel_id=1, source_target_pairs={{0,8},{1,9},{2,10},{3,11},{4,12},{5,13},{6,14},{7,15},{8,16},{9,17... | collective-permute-start | bytes 1622024 | tf_op jit(solution)/shard_map/ppermute | solution.py:90
  7.3 2.4 %collective-permute-start.8 = (bf16[40,4096]{1,0:T(8,128)(2,1)S(1)}, bf16[40,4096]{1,0:T(8,128)(2,1)S(1)}, u32[]{:S(2)}, u32[]{:S(2)}) collective-permute-start(bf16[40,4096]{1,0:T(8,128)(2,1)S(1)} %get-tuple-element.77), channel_id=1, source_target_pairs={{0,6},{1,7},{2,4},{3,5},{4,2},{5,3},{6,0},{7,1},{8,14},{9,15},{10,... | collective-permute-start | bytes 983048 | tf_op jit(solution)/shard_map/ppermute | solution.py:90
  10.8 2.0 %shard_map.101 = bf16[32,16,1152]{2,1,0:T(8,128)(2,1)} custom-call(s32[32]{0:T(128)S(1)} %copy-done.4, bf16[32,16,1024]{2,1,0:T(8,128)(2,1)S(1)} %copy-done), custom_call_target="tpu_custom_call" | custom-call | bytes 3145728 | tf_op jit(solution)/shard_map/pallas_call | solution.py:34
  13.8 7.8 %collective-permute-done.block_ref = bf16[64,4224]{1,0:T(8,128)(2,1)S(1)} collective-permute-done((bf16[64,4224]{1,0:T(8,128)(2,1)S(1)}, bf16[64,4224]{1,0:T(8,128)(2,1)S(1)}, u32[]{:S(2)}, u32[]{:S(2)}) %collective-permute-start) | collective-permute-done | bytes 540704 | tf_op jit(solution)/shard_map/ppermute | solution.py:90
  22.4 2.5 %collective-permute-start.9 = (bf16[40,4096]{1,0:T(8,128)(2,1)S(1)}, bf16[40,4096]{1,0:T(8,128)(2,1)S(1)}, u32[]{:S(2)}, u32[]{:S(2)}) collective-permute-start(bf16[40,4096]{1,0:T(8,128)(2,1)S(1)} %get-tuple-element.78), channel_id=1, source_target_pairs={{0,6},{1,7},{2,4},{3,5},{4,2},{5,3},{6,0},{7,1},{8,14},{9,15},{10,... | collective-permute-start | bytes 983048 | tf_op jit(solution)/shard_map/ppermute | solution.py:90
  27.6 9.2 %collective-permute-done.1.block_ref = bf16[64,4224]{1,0:T(8,128)(2,1)S(1)} collective-permute-done((bf16[64,4224]{1,0:T(8,128)(2,1)S(1)}, bf16[64,4224]{1,0:T(8,128)(2,1)S(1)}, u32[]{:S(2)}, u32[]{:S(2)}) %collective-permute-start.1) | collective-permute-done | bytes 540704 | tf_op jit(solution)/shard_map/ppermute | solution.py:90
  38.5 2.2 %collective-permute-start.10 = (bf16[40,4096]{1,0:T(8,128)(2,1)S(1)}, bf16[40,4096]{1,0:T(8,128)(2,1)S(1)}, u32[]{:S(2)}, u32[]{:S(2)}) collective-permute-start(bf16[40,4096]{1,0:T(8,128)(2,1)S(1)} %get-tuple-element.79), channel_id=1, source_target_pairs={{0,6},{1,7},{2,4},{3,5},{4,2},{5,3},{6,0},{7,1},{8,14},{9,15},{10,... | collective-permute-start | bytes 983048 | tf_op jit(solution)/shard_map/ppermute | solution.py:90
  44.5 5.5 %collective-permute-done.10.refs_3_ = bf16[40,4096]{1,0:T(8,128)(2,1)S(1)} collective-permute-done((bf16[40,4096]{1,0:T(8,128)(2,1)S(1)}, bf16[40,4096]{1,0:T(8,128)(2,1)S(1)}, u32[]{:S(2)}, u32[]{:S(2)}) %collective-permute-start.10) | collective-permute-done | bytes 327712 | tf_op jit(solution)/shard_map/ppermute | solution.py:90
  50.0 5.9 %collective-permute-done.7.refs_2_ = bf16[40,4096]{1,0:T(8,128)(2,1)S(1)} collective-permute-done((bf16[40,4096]{1,0:T(8,128)(2,1)S(1)}, bf16[40,4096]{1,0:T(8,128)(2,1)S(1)}, u32[]{:S(2)}, u32[]{:S(2)}) %collective-permute-start.7) | collective-permute-done | bytes 327712 | tf_op jit(solution)/shard_map/ppermute | solution.py:90
  57.7 2.2 %collective-permute-start.17 = (bf16[40,4096]{1,0:T(8,128)(2,1)S(1)}, bf16[40,4096]{1,0:T(8,128)(2,1)S(1)}, u32[]{:S(2)}, u32[]{:S(2)}) collective-permute-start(bf16[40,4096]{1,0:T(8,128)(2,1)S(1)} %get-tuple-element.101), channel_id=1, source_target_pairs={{0,6},{1,7},{2,4},{3,5},{4,2},{5,3},{6,0},{7,1},{8,14},{9,15},{10,... | collective-permute-start | bytes 983048 | tf_op jit(solution)/shard_map/ppermute | solution.py:90
  61.2 5.6 %all-to-all-start = ((bf16[32,16,1152]{2,1,0:T(8,128)(2,1)}), bf16[32,16,1152]{2,1,0:T(8,128)(2,1)S(1)}, u32[]{:S(2)}, u32[]{:S(2)}) async-start(bf16[32,16,1152]{2,1,0:T(8,128)(2,1)} %shard_map.101), calls=%async_computation | async-start | bytes 2359296 | tf_op jit(solution)/shard_map/all_to_all | solution.py:81
  67.9 13.5 %shard_map.98 = (bf16[40,4096]{1,0:T(8,128)(2,1)}, bf16[40,4096]{1,0:T(8,128)(2,1)}, bf16[40,4096]{1,0:T(8,128)(2,1)}, bf16[40,4096]{1,0:T(8,128)(2,1)}, bf16[40...) custom-call(bf16[40,4096]{1,0:T(8,128)(2,1)} %convolution_convert_fusion.4.re, ...), custom_call_target="tpu_custom_call" | custom-call | flops 6039797760 | bytes 24117248 | tf_op jit(solution)/shard_map/pallas_call | solution.py:240
  81.6 2.5 %collective-permute-start.27 = (bf16[40,4096]{1,0:T(8,128)(2,1)}, bf16[40,4096]{1,0:T(8,128)(2,1)S(1)}, u32[]{:S(2)}, u32[]{:S(2)}) collective-permute-start(bf16[40,4096]{1,0:T(8,128)(2,1)} %get-tuple-element.119), channel_id=1, source_target_pairs={{0,2},{1,3},{2,0},{3,1},{4,6},{5,7},{6,4},{7,5},{8,10},{9,11},{10,... | collective-permute-start | bytes 983048 | tf_op jit(solution)/shard_map/ppermute | solution.py:90
  85.7 13.5 %shard_map.100 = (bf16[40,4096]{1,0:T(8,128)(2,1)}, bf16[40,4096]{1,0:T(8,128)(2,1)}, bf16[40,4096]{1,0:T(8,128)(2,1)}, bf16[40,4096]{1,0:T(8,128)(2,1)}, bf16[4...) custom-call(bf16[40,4096]{1,0:T(8,128)(2,1)} %convolution_convert_fusion.2.r, ...), custom_call_target="tpu_custom_call" | custom-call | flops 6039797760 | bytes 24117248 | tf_op jit(solution)/shard_map/pallas_call | solution.py:240
  99.2 3.4 %collective-permute-done.18 = bf16[40,4096]{1,0:T(8,128)(2,1)S(1)} collective-permute-done((bf16[40,4096]{1,0:T(8,128)(2,1)}, bf16[40,4096]{1,0:T(8,128)(2,1)S(1)}, u32[]{:S(2)}, u32[]{:S(2)}) %collective-permute-start.18) | collective-permute-done | bytes 327712 | tf_op jit(solution)/shard_map/ppermute | solution.py:90
  102.9 2.0 %collective-permute-start.30 = (bf16[64,4096]{1,0:T(8,128)(2,1)S(1)}, bf16[64,4096]{1,0:T(8,128)(2,1)S(1)}, u32[]{:S(2)}, u32[]{:S(2)}) collective-permute-start(bf16[64,4096]{1,0:T(8,128)(2,1)S(1)} %convolution_convert_fusion), channel_id=1, source_target_pairs={{0,8},{1,9},{2,10},{3,11},{4,12},{5,13},{6,14},{7,15},{8,16},{9,17... | collective-permute-start | bytes 1572872 | tf_op jit(solution)/shard_map/ppermute | solution.py:90
  105.9 2.6 %collective-permute-start.19 = (bf16[40,4096]{1,0:T(8,128)(2,1)S(1)}, bf16[40,4096]{1,0:T(8,128)(2,1)S(1)}, u32[]{:S(2)}, u32[]{:S(2)}) collective-permute-start(bf16[40,4096]{1,0:T(8,128)(2,1)S(1)} %copy-done.28), channel_id=1, source_target_pairs={{0,6},{1,7},{2,4},{3,5},{4,2},{5,3},{6,0},{7,1},{8,14},{9,15},{10,... | collective-permute-start | bytes 983048 | tf_op jit(solution)/shard_map/ppermute | solution.py:90
  108.5 7.1 %collective-permute-done.24 = bf16[40,4096]{1,0:T(8,128)(2,1)S(1)} collective-permute-done((bf16[40,4096]{1,0:T(8,128)(2,1)S(1)}, bf16[40,4096]{1,0:T(8,128)(2,1)S(1)}, u32[]{:S(2)}, u32[]{:S(2)}) %collective-permute-start.24) | collective-permute-done | bytes 327712 | tf_op jit(solution)/shard_map/ppermute | solution.py:90
  115.6 5.5 %collective-permute-done.28 = bf16[40,4096]{1,0:T(8,128)(2,1)S(1)} collective-permute-done((bf16[40,4096]{1,0:T(8,128)(2,1)S(1)}, bf16[40,4096]{1,0:T(8,128)(2,1)S(1)}, u32[]{:S(2)}, u32[]{:S(2)}) %collective-permute-start.28) | collective-permute-done | bytes 327712 | tf_op jit(solution)/shard_map/ppermute | solution.py:90
  127.0 7.2 %collective-permute-done.22 = bf16[40,4096]{1,0:T(8,128)(2,1)S(1)} collective-permute-done((bf16[40,4096]{1,0:T(8,128)(2,1)S(1)}, bf16[40,4096]{1,0:T(8,128)(2,1)S(1)}, u32[]{:S(2)}, u32[]{:S(2)}) %collective-permute-start.22) | collective-permute-done | bytes 327712 | tf_op jit(solution)/shard_map/ppermute | solution.py:90
  134.4 4.5 %collective-permute-done.29 = bf16[40,4096]{1,0:T(8,128)(2,1)S(1)} collective-permute-done((bf16[40,4096]{1,0:T(8,128)(2,1)S(1)}, bf16[40,4096]{1,0:T(8,128)(2,1)S(1)}, u32[]{:S(2)}, u32[]{:S(2)}) %collective-permute-start.29) | collective-permute-done | bytes 327712 | tf_op jit(solution)/shard_map/ppermute | solution.py:90
  146.5 4.0 %collective-permute-done.20 = bf16[40,4096]{1,0:T(8,128)(2,1)S(1)} collective-permute-done((bf16[40,4096]{1,0:T(8,128)(2,1)S(1)}, bf16[40,4096]{1,0:T(8,128)(2,1)S(1)}, u32[]{:S(2)}, u32[]{:S(2)}) %collective-permute-start.20) | collective-permute-done | bytes 327712 | tf_op jit(solution)/shard_map/ppermute | solution.py:90
  150.5 5.0 %collective-permute-done.23 = bf16[40,4096]{1,0:T(8,128)(2,1)S(1)} collective-permute-done((bf16[40,4096]{1,0:T(8,128)(2,1)S(1)}, bf16[40,4096]{1,0:T(8,128)(2,1)S(1)}, u32[]{:S(2)}, u32[]{:S(2)}) %collective-permute-start.23) | collective-permute-done | bytes 327712 | tf_op jit(solution)/shard_map/ppermute | solution.py:90
  155.5 2.1 %fusion = bf16[64,4096]{1,0:T(8,128)(2,1)} fusion(bf16[64,160]{1,0:T(8,128)(2,1)S(1)} %copy-done.3, bf16[40,4096]{1,0:T(8,128)(2,1)S(1)} %collective-permute-done.26, bf16[40,4096]{1,0:T(8,128)(2,1)S(1)} %collective-permute-done.23, bf16[40,4096]{1,0:T(8,128)(2,1)S(1)} %collective-permute-done.20, bf16[40,4096]{1,0:T(8,128)(2,1)} %get-tuple-element.85, ...), kind=kOutput, calls=%fused_computation.3 | convolution fusion | flops 89915392 | bytes 2379776 | tf_op jit(solution)/shard_map/dot_general | solution.py:336
  (129 shorter events, 35.3 us)
Async XLA Ops:
  4.2 17.4 %collective-permute-start = (bf16[64,4224]{1,0:T(8,128)(2,1)S(1)}, bf16[64,4224]{1,0:T(8,128)(2,1)S(1)}, u32[]{:S(2)}, u32[]{:S(2)}) collective-permute-start(bf16[64,4224]{1,0:T(8,128)(2,1)S(1)} %get-tuple-element.64), channel_id=1, source_target_pairs={{0,8},{1,9},{2,10},{3,11},{4,12},{5,13},{6,14},{7,15},{8,16},{9,17... | collective-permute-start | bytes 1622024 | tf_op jit(solution)/shard_map/ppermute | solution.py:90
  7.3 29.6 %collective-permute-start.11 = (bf16[4096,384]{1,0:T(8,128)(2,1)S(1)}, bf16[4096,384]{1,0:T(8,128)(2,1)S(1)}, u32[]{:S(2)}, u32[]{:S(2)}) collective-permute-start(bf16[4096,384]{1,0:T(8,128)(2,1)S(1)} %copy-done.7), channel_id=1, source_target_pairs={{0,1},{1,0},{2,3},{3,2},{4,5},{5,4},{6,7},{7,6},{8,9},{9,8},{10,11... | collective-permute-start | bytes 9437192 | tf_op jit(solution)/shard_map/ppermute | solution.py:90
  7.3 15.1 %collective-permute-start.8 = (bf16[40,4096]{1,0:T(8,128)(2,1)S(1)}, bf16[40,4096]{1,0:T(8,128)(2,1)S(1)}, u32[]{:S(2)}, u32[]{:S(2)}) collective-permute-start(bf16[40,4096]{1,0:T(8,128)(2,1)S(1)} %get-tuple-element.77), channel_id=1, source_target_pairs={{0,6},{1,7},{2,4},{3,5},{4,2},{5,3},{6,0},{7,1},{8,14},{9,15},{10,... | collective-permute-start | bytes 983048 | tf_op jit(solution)/shard_map/ppermute | solution.py:90
  9.7 15.6 %collective-permute-start.5 = (bf16[40,4096]{1,0:T(8,128)(2,1)S(1)}, bf16[40,4096]{1,0:T(8,128)(2,1)S(1)}, u32[]{:S(2)}, u32[]{:S(2)}) collective-permute-start(bf16[40,4096]{1,0:T(8,128)(2,1)S(1)} %get-tuple-element.72), channel_id=1, source_target_pairs={{0,4},{1,5},{2,6},{3,7},{4,0},{5,1},{6,2},{7,3},{8,12},{9,13},{10,... | collective-permute-start | bytes 983048 | tf_op jit(solution)/shard_map/ppermute | solution.py:90
  10.2 17.0 %collective-permute-start.2 = (bf16[40,4096]{1,0:T(8,128)(2,1)S(1)}, bf16[40,4096]{1,0:T(8,128)(2,1)S(1)}, u32[]{:S(2)}, u32[]{:S(2)}) collective-permute-start(bf16[40,4096]{1,0:T(8,128)(2,1)S(1)} %get-tuple-element.67), channel_id=1, source_target_pairs={{0,2},{1,3},{2,0},{3,1},{4,6},{5,7},{6,4},{7,5},{8,10},{9,11},{10,... | collective-permute-start | bytes 983048 | tf_op jit(solution)/shard_map/ppermute | solution.py:90
  21.6 15.3 %collective-permute-start.1 = (bf16[64,4224]{1,0:T(8,128)(2,1)S(1)}, bf16[64,4224]{1,0:T(8,128)(2,1)S(1)}, u32[]{:S(2)}, u32[]{:S(2)}) collective-permute-start(bf16[64,4224]{1,0:T(8,128)(2,1)S(1)} %collective-permute-done.block_ref), channel_id=1, source_target_pairs={{0,8},{1,9},{2,10},{3,11},{4,12},{5,13},{6,14},{7,15},{8,16},{9,17... | collective-permute-start | bytes 1622024 | tf_op jit(solution)/shard_map/ppermute | solution.py:90
  22.4 16.1 %collective-permute-start.9 = (bf16[40,4096]{1,0:T(8,128)(2,1)S(1)}, bf16[40,4096]{1,0:T(8,128)(2,1)S(1)}, u32[]{:S(2)}, u32[]{:S(2)}) collective-permute-start(bf16[40,4096]{1,0:T(8,128)(2,1)S(1)} %get-tuple-element.78), channel_id=1, source_target_pairs={{0,6},{1,7},{2,4},{3,5},{4,2},{5,3},{6,0},{7,1},{8,14},{9,15},{10,... | collective-permute-start | bytes 983048 | tf_op jit(solution)/shard_map/ppermute | solution.py:90
  25.4 15.3 %collective-permute-start.6 = (bf16[40,4096]{1,0:T(8,128)(2,1)S(1)}, bf16[40,4096]{1,0:T(8,128)(2,1)S(1)}, u32[]{:S(2)}, u32[]{:S(2)}) collective-permute-start(bf16[40,4096]{1,0:T(8,128)(2,1)S(1)} %get-tuple-element.73), channel_id=1, source_target_pairs={{0,4},{1,5},{2,6},{3,7},{4,0},{5,1},{6,2},{7,3},{8,12},{9,13},{10,... | collective-permute-start | bytes 983048 | tf_op jit(solution)/shard_map/ppermute | solution.py:90
  36.8 19.2 %collective-permute-start.14 = (bf16[64,4224]{1,0:T(8,128)(2,1)S(1)}, bf16[64,4224]{1,0:T(8,128)(2,1)S(1)}, u32[]{:S(2)}, u32[]{:S(2)}) collective-permute-start(bf16[64,4224]{1,0:T(8,128)(2,1)S(1)} %collective-permute-done.1.block_ref), channel_id=1, source_target_pairs={{0,8},{1,9},{2,10},{3,11},{4,12},{5,13},{6,14},{7,15},{8,16},{9,17... | collective-permute-start | bytes 1622024 | tf_op jit(solution)/shard_map/ppermute | solution.py:90
  36.9 19.0 %collective-permute-start.12 = (bf16[4096,384]{1,0:T(8,128)(2,1)S(1)}, bf16[4096,384]{1,0:T(8,128)(2,1)S(1)}, u32[]{:S(2)}, u32[]{:S(2)}) collective-permute-start(bf16[4096,384]{1,0:T(8,128)(2,1)S(1)} %copy-done.8), channel_id=1, source_target_pairs={{0,1},{1,0},{2,3},{3,2},{4,5},{5,4},{6,7},{7,6},{8,9},{9,8},{10,11... | collective-permute-start | bytes 9437192 | tf_op jit(solution)/shard_map/ppermute | solution.py:90
  40.7 15.2 %collective-permute-start.7 = (bf16[40,4096]{1,0:T(8,128)(2,1)S(1)}, bf16[40,4096]{1,0:T(8,128)(2,1)S(1)}, u32[]{:S(2)}, u32[]{:S(2)}) collective-permute-start(bf16[40,4096]{1,0:T(8,128)(2,1)S(1)} %get-tuple-element.74), channel_id=1, source_target_pairs={{0,4},{1,5},{2,6},{3,7},{4,0},{5,1},{6,2},{7,3},{8,12},{9,13},{10,... | collective-permute-start | bytes 983048 | tf_op jit(solution)/shard_map/ppermute | solution.py:90
  41.2 14.7 %collective-permute-start.4 = (bf16[40,4096]{1,0:T(8,128)(2,1)S(1)}, bf16[40,4096]{1,0:T(8,128)(2,1)S(1)}, u32[]{:S(2)}, u32[]{:S(2)}) collective-permute-start(bf16[40,4096]{1,0:T(8,128)(2,1)S(1)} %get-tuple-element.69), channel_id=1, source_target_pairs={{0,2},{1,3},{2,0},{3,1},{4,6},{5,7},{6,4},{7,5},{8,10},{9,11},{10,... | collective-permute-start | bytes 983048 | tf_op jit(solution)/shard_map/ppermute | solution.py:90
  57.7 27.0 %collective-permute-start.17 = (bf16[40,4096]{1,0:T(8,128)(2,1)S(1)}, bf16[40,4096]{1,0:T(8,128)(2,1)S(1)}, u32[]{:S(2)}, u32[]{:S(2)}) collective-permute-start(bf16[40,4096]{1,0:T(8,128)(2,1)S(1)} %get-tuple-element.101), channel_id=1, source_target_pairs={{0,6},{1,7},{2,4},{3,5},{4,2},{5,3},{6,0},{7,1},{8,14},{9,15},{10,... | collective-permute-start | bytes 983048 | tf_op jit(solution)/shard_map/ppermute | solution.py:90
  59.9 24.2 %collective-permute-start.16 = (bf16[40,4096]{1,0:T(8,128)(2,1)S(1)}, bf16[40,4096]{1,0:T(8,128)(2,1)S(1)}, u32[]{:S(2)}, u32[]{:S(2)}) collective-permute-start(bf16[40,4096]{1,0:T(8,128)(2,1)S(1)} %get-tuple-element.99), channel_id=1, source_target_pairs={{0,4},{1,5},{2,6},{3,7},{4,0},{5,1},{6,2},{7,3},{8,12},{9,13},{10,... | collective-permute-start | bytes 983048 | tf_op jit(solution)/shard_map/ppermute | solution.py:90
  60.5 21.2 %collective-permute-start.15 = (bf16[40,4096]{1,0:T(8,128)(2,1)S(1)}, bf16[40,4096]{1,0:T(8,128)(2,1)}, u32[]{:S(2)}, u32[]{:S(2)}) collective-permute-start(bf16[40,4096]{1,0:T(8,128)(2,1)S(1)} %get-tuple-element.97), channel_id=1, source_target_pairs={{0,2},{1,3},{2,0},{3,1},{4,6},{5,7},{6,4},{7,5},{8,10},{9,11},{10,... | collective-permute-start | bytes 983048 | tf_op jit(solution)/shard_map/ppermute | solution.py:90
  61.2 79.2 %all-to-all-start = ((bf16[32,16,1152]{2,1,0:T(8,128)(2,1)}), bf16[32,16,1152]{2,1,0:T(8,128)(2,1)S(1)}, u32[]{:S(2)}, u32[]{:S(2)}) async-start(bf16[32,16,1152]{2,1,0:T(8,128)(2,1)} %shard_map.101), calls=%async_computation | async-start | bytes 2359296 | tf_op jit(solution)/shard_map/all_to_all | solution.py:81
  81.6 17.6 %collective-permute-start.27 = (bf16[40,4096]{1,0:T(8,128)(2,1)}, bf16[40,4096]{1,0:T(8,128)(2,1)S(1)}, u32[]{:S(2)}, u32[]{:S(2)}) collective-permute-start(bf16[40,4096]{1,0:T(8,128)(2,1)} %get-tuple-element.119), channel_id=1, source_target_pairs={{0,2},{1,3},{2,0},{3,1},{4,6},{5,7},{6,4},{7,5},{8,10},{9,11},{10,... | collective-permute-start | bytes 983048 | tf_op jit(solution)/shard_map/ppermute | solution.py:90
  84.1 18.4 %collective-permute-start.18 = (bf16[40,4096]{1,0:T(8,128)(2,1)}, bf16[40,4096]{1,0:T(8,128)(2,1)S(1)}, u32[]{:S(2)}, u32[]{:S(2)}) collective-permute-start(bf16[40,4096]{1,0:T(8,128)(2,1)} %get-tuple-element.103), channel_id=1, source_target_pairs={{0,4},{1,5},{2,6},{3,7},{4,0},{5,1},{6,2},{7,3},{8,12},{9,13},{10,... | collective-permute-start | bytes 983048 | tf_op jit(solution)/shard_map/ppermute | solution.py:90
  84.7 17.9 %collective-permute-start.21 = (bf16[40,4096]{1,0:T(8,128)(2,1)}, bf16[40,4096]{1,0:T(8,128)(2,1)S(1)}, u32[]{:S(2)}, u32[]{:S(2)}) collective-permute-start(bf16[40,4096]{1,0:T(8,128)(2,1)} %get-tuple-element.108), channel_id=1, source_target_pairs={{0,6},{1,7},{2,4},{3,5},{4,2},{5,3},{6,0},{7,1},{8,14},{9,15},{10,... | collective-permute-start | bytes 983048 | tf_op jit(solution)/shard_map/ppermute | solution.py:90
  102.9 18.2 %collective-permute-start.30 = (bf16[64,4096]{1,0:T(8,128)(2,1)S(1)}, bf16[64,4096]{1,0:T(8,128)(2,1)S(1)}, u32[]{:S(2)}, u32[]{:S(2)}) collective-permute-start(bf16[64,4096]{1,0:T(8,128)(2,1)S(1)} %convolution_convert_fusion), channel_id=1, source_target_pairs={{0,8},{1,9},{2,10},{3,11},{4,12},{5,13},{6,14},{7,15},{8,16},{9,17... | collective-permute-start | bytes 1572872 | tf_op jit(solution)/shard_map/ppermute | solution.py:90
  105.5 15.6 %collective-permute-start.28 = (bf16[40,4096]{1,0:T(8,128)(2,1)S(1)}, bf16[40,4096]{1,0:T(8,128)(2,1)S(1)}, u32[]{:S(2)}, u32[]{:S(2)}) collective-permute-start(bf16[40,4096]{1,0:T(8,128)(2,1)S(1)} %copy-done.29), channel_id=1, source_target_pairs={{0,4},{1,5},{2,6},{3,7},{4,0},{5,1},{6,2},{7,3},{8,12},{9,13},{10,... | collective-permute-start | bytes 983048 | tf_op jit(solution)/shard_map/ppermute | solution.py:90
  105.9 15.3 %collective-permute-start.19 = (bf16[40,4096]{1,0:T(8,128)(2,1)S(1)}, bf16[40,4096]{1,0:T(8,128)(2,1)S(1)}, u32[]{:S(2)}, u32[]{:S(2)}) collective-permute-start(bf16[40,4096]{1,0:T(8,128)(2,1)S(1)} %copy-done.28), channel_id=1, source_target_pairs={{0,6},{1,7},{2,4},{3,5},{4,2},{5,3},{6,0},{7,1},{8,14},{9,15},{10,... | collective-permute-start | bytes 983048 | tf_op jit(solution)/shard_map/ppermute | solution.py:90
  121.5 17.3 %collective-permute-start.31 = (bf16[64,4096]{1,0:T(8,128)(2,1)S(1)}, bf16[64,4096]{1,0:T(8,128)(2,1)S(1)}, u32[]{:S(2)}, u32[]{:S(2)}) collective-permute-start(bf16[64,4096]{1,0:T(8,128)(2,1)S(1)} %fusion.2), channel_id=1, source_target_pairs={{0,8},{1,9},{2,10},{3,11},{4,12},{5,13},{6,14},{7,15},{8,16},{9,17... | collective-permute-start | bytes 1572872 | tf_op jit(solution)/shard_map/ppermute | solution.py:90
  139.3 16.3 %collective-permute-start.32 = (bf16[64,4096]{1,0:T(8,128)(2,1)S(1)}, bf16[64,4096]{1,0:T(8,128)(2,1)S(1)}, u32[]{:S(2)}, u32[]{:S(2)}) collective-permute-start(bf16[64,4096]{1,0:T(8,128)(2,1)S(1)} %fusion.1), channel_id=1, source_target_pairs={{0,8},{1,9},{2,10},{3,11},{4,12},{5,13},{6,14},{7,15},{8,16},{9,17... | collective-permute-start | bytes 1572872 | tf_op jit(solution)/shard_map/ppermute | solution.py:90
  (44 other events, 495.5 us)

commit v10 on v9

--- a/solution.py
+++ b/solution.py
@@ -315,8 +315,7 @@
 
     for first in range(0, planes, group):
         held = [list(pieces) for pieces in got[first : first + group]]
-        following = got[first + group][1:] if first + group < planes else []
-        held[0][0] = after(held[0][0], *outs, *following)
+        held[0][0] = after(held[0][0], *outs)
         outs.extend(work(held, *zip(weights, swapped)))
 
     arrived = exchange(after(outgoing, block))

time: 158 us -> 156 us (0.987)
  starting transfers between devices: 44.2 us -> 41.9 us
    ppermute x33, starting transfers between devices: 38.6 us -> 36.9 us  [send(): return lax.ppermute(x, 'expert', pairs)]
    unnamed x68 -> x64, local copies, waits for them, and re-layouts: 4.14 us -> 3.99 us
where the time goes in v10:
time: 156 us
  waiting for transfers between devices  66.6 us (43%)
  starting transfers between devices  41.9 us (27%)
  Pallas kernels  34.3 us (22%)
  matrix products  7.3 us (5%)
  local copies, waits for them, and re-layouts  3.99 us (3%)
    ppermute x33, waiting for transfers between devices, send(): return lax.ppermute(x, 'expert', pairs)  66.6 us
    ppermute x33, starting transfers between devices, send(): return lax.ppermute(x, 'expert', pairs)  36.9 us
    pallas_call x2, Pallas kernels, apply(): pl.pallas_call(functools.partial(expert_kernel, len(pieces), steps), grid...  26.9 us
    all_to_all x1, starting transfers between devices, exchange(): return lax.all_to_all(x, 'expert', split_axis=0, concat_axis=0, tiled=True)  4.99 us
    dot_general x4, matrix products, pick(): lax.dot_general(placing, rows, (((0,), (0,)), ((), ())), preferred_elemen...  4.12 us
    unnamed x64, local copies, waits for them, and re-layouts  3.99 us
    pallas_call x4, Pallas kernels, pick_pieces(): pl.pallas_call(functools.partial(body, experts, capacity, 512), out_shape...  3.45 us
    dot_general x4, matrix products, local(): jnp.dot(blends[s], jnp.concatenate(sent[s], axis=0), preferred_element_ty...  3.18 us
  transfers between devices with their start and end apart: 34, of which 14 were waited for; matrix products, arithmetic and copies ran while one was open for 4% of the time, Pallas kernels for 21%

profile of v10, /device:TPU:0, one launch (start us, length us, event | category | flops | bytes accessed | tf_op | source)
XLA Modules:
  0.0 155.7 jit_solution(9465242560171321502)
XLA Ops:
  4.2 3.1 %collective-permute-start.3 = (bf16[64,4224]{1,0:T(8,128)(2,1)S(1)}, bf16[64,4224]{1,0:T(8,128)(2,1)S(1)}, u32[]{:S(2)}, u32[]{:S(2)}) collective-permute-start(bf16[64,4224]{1,0:T(8,128)(2,1)S(1)} %get-tuple-element.66), channel_id=1, source_target_pairs={{0,8},{1,9},{2,10},{3,11},{4,12},{5,13},{6,14},{7,15},{8,16},{9,17... | collective-permute-start | bytes 1622024 | tf_op jit(solution)/shard_map/ppermute | solution.py:90
  11.8 2.0 %shard_map.101 = bf16[32,16,1152]{2,1,0:T(8,128)(2,1)} custom-call(s32[32]{0:T(128)S(1)} %copy-done.4, bf16[32,16,1024]{2,1,0:T(8,128)(2,1)S(1)} %copy-done), custom_call_target="tpu_custom_call" | custom-call | bytes 3145728 | tf_op jit(solution)/shard_map/pallas_call | solution.py:34
  13.8 7.8 %collective-permute-done.3.block_ref = bf16[64,4224]{1,0:T(8,128)(2,1)S(1)} collective-permute-done((bf16[64,4224]{1,0:T(8,128)(2,1)S(1)}, bf16[64,4224]{1,0:T(8,128)(2,1)S(1)}, u32[]{:S(2)}, u32[]{:S(2)}) %collective-permute-start.3) | collective-permute-done | bytes 540704 | tf_op jit(solution)/shard_map/ppermute | solution.py:90
  22.3 2.1 %collective-permute-done.1.refs_2_ = bf16[40,4096]{1,0:T(8,128)(2,1)S(1)} collective-permute-done((bf16[40,4096]{1,0:T(8,128)(2,1)S(1)}, bf16[40,4096]{1,0:T(8,128)(2,1)S(1)}, u32[]{:S(2)}, u32[]{:S(2)}) %collective-permute-start.1) | collective-permute-done | bytes 327712 | tf_op jit(solution)/shard_map/ppermute | solution.py:90
  28.9 7.9 %collective-permute-done.9.block_ref = bf16[64,4224]{1,0:T(8,128)(2,1)S(1)} collective-permute-done((bf16[64,4224]{1,0:T(8,128)(2,1)S(1)}, bf16[64,4224]{1,0:T(8,128)(2,1)S(1)}, u32[]{:S(2)}, u32[]{:S(2)}) %collective-permute-start.9) | collective-permute-done | bytes 540704 | tf_op jit(solution)/shard_map/ppermute | solution.py:90
  38.5 2.3 %collective-permute-done.5.refs_6_ = bf16[40,4096]{1,0:T(8,128)(2,1)S(1)} collective-permute-done((bf16[40,4096]{1,0:T(8,128)(2,1)S(1)}, bf16[40,4096]{1,0:T(8,128)(2,1)S(1)}, u32[]{:S(2)}, u32[]{:S(2)}) %collective-permute-start.5) | collective-permute-done | bytes 327712 | tf_op jit(solution)/shard_map/ppermute | solution.py:90
  45.4 5.8 %collective-permute-done.14.block_ref = bf16[64,4224]{1,0:T(8,128)(2,1)S(1)} collective-permute-done((bf16[64,4224]{1,0:T(8,128)(2,1)S(1)}, bf16[64,4224]{1,0:T(8,128)(2,1)S(1)}, u32[]{:S(2)}, u32[]{:S(2)}) %collective-permute-start.14) | collective-permute-done | bytes 540704 | tf_op jit(solution)/shard_map/ppermute | solution.py:90
  52.0 4.3 %collective-permute-done.12.refs_2_ = bf16[40,4096]{1,0:T(8,128)(2,1)S(1)} collective-permute-done((bf16[40,4096]{1,0:T(8,128)(2,1)S(1)}, bf16[40,4096]{1,0:T(8,128)(2,1)S(1)}, u32[]{:S(2)}, u32[]{:S(2)}) %collective-permute-start.12) | collective-permute-done | bytes 327712 | tf_op jit(solution)/shard_map/ppermute | solution.py:90
  60.5 5.0 %all-to-all-start = ((bf16[32,16,1152]{2,1,0:T(8,128)(2,1)}), bf16[32,16,1152]{2,1,0:T(8,128)(2,1)S(1)}, u32[]{:S(2)}, u32[]{:S(2)}) async-start(bf16[32,16,1152]{2,1,0:T(8,128)(2,1)} %shard_map.101), calls=%async_computation | async-start | bytes 2359296 | tf_op jit(solution)/shard_map/all_to_all | solution.py:81
  66.5 13.5 %shard_map.97 = (bf16[40,4096]{1,0:T(8,128)(2,1)}, bf16[40,4096]{1,0:T(8,128)(2,1)}, bf16[40,4096]{1,0:T(8,128)(2,1)}, bf16[40,4096]{1,0:T(8,128)(2,1)}, bf16[40...) custom-call(bf16[40,4096]{1,0:T(8,128)(2,1)} %convolution_convert_fusion.4.re, ...), custom_call_target="tpu_custom_call" | custom-call | flops 6039797760 | bytes 24117248 | tf_op jit(solution)/shard_map/pallas_call | solution.py:240
  80.1 2.3 %collective-permute-start.27 = (bf16[40,4096]{1,0:T(8,128)(2,1)}, bf16[40,4096]{1,0:T(8,128)(2,1)S(1)}, u32[]{:S(2)}, u32[]{:S(2)}) collective-permute-start(bf16[40,4096]{1,0:T(8,128)(2,1)} %get-tuple-element.117), channel_id=1, source_target_pairs={{0,2},{1,3},{2,0},{3,1},{4,6},{5,7},{6,4},{7,5},{8,10},{9,11},{10,... | collective-permute-start | bytes 983048 | tf_op jit(solution)/shard_map/ppermute | solution.py:90
  82.3 2.5 %collective-permute-start.18 = (bf16[40,4096]{1,0:T(8,128)(2,1)}, bf16[40,4096]{1,0:T(8,128)(2,1)S(1)}, u32[]{:S(2)}, u32[]{:S(2)}) collective-permute-start(bf16[40,4096]{1,0:T(8,128)(2,1)} %get-tuple-element.101), channel_id=1, source_target_pairs={{0,4},{1,5},{2,6},{3,7},{4,0},{5,1},{6,2},{7,3},{8,12},{9,13},{10,... | collective-permute-start | bytes 983048 | tf_op jit(solution)/shard_map/ppermute | solution.py:90
  84.8 13.4 %shard_map.100 = (bf16[40,4096]{1,0:T(8,128)(2,1)}, bf16[40,4096]{1,0:T(8,128)(2,1)}, bf16[40,4096]{1,0:T(8,128)(2,1)}, bf16[40,4096]{1,0:T(8,128)(2,1)}, bf16[4...) custom-call(bf16[40,4096]{1,0:T(8,128)(2,1)} %convolution_convert_fusion.2.r, ...), custom_call_target="tpu_custom_call" | custom-call | flops 6039797760 | bytes 24117248 | tf_op jit(solution)/shard_map/pallas_call | solution.py:240
  98.3 3.0 %collective-permute-done.18 = bf16[40,4096]{1,0:T(8,128)(2,1)S(1)} collective-permute-done((bf16[40,4096]{1,0:T(8,128)(2,1)}, bf16[40,4096]{1,0:T(8,128)(2,1)S(1)}, u32[]{:S(2)}, u32[]{:S(2)}) %collective-permute-start.18) | collective-permute-done | bytes 327712 | tf_op jit(solution)/shard_map/ppermute | solution.py:90
  101.6 2.0 %collective-permute-start.30 = (bf16[64,4096]{1,0:T(8,128)(2,1)S(1)}, bf16[64,4096]{1,0:T(8,128)(2,1)S(1)}, u32[]{:S(2)}, u32[]{:S(2)}) collective-permute-start(bf16[64,4096]{1,0:T(8,128)(2,1)S(1)} %convolution_convert_fusion), channel_id=1, source_target_pairs={{0,8},{1,9},{2,10},{3,11},{4,12},{5,13},{6,14},{7,15},{8,16},{9,17... | collective-permute-start | bytes 1572872 | tf_op jit(solution)/shard_map/ppermute | solution.py:90
  104.6 2.6 %collective-permute-start.19 = (bf16[40,4096]{1,0:T(8,128)(2,1)S(1)}, bf16[40,4096]{1,0:T(8,128)(2,1)S(1)}, u32[]{:S(2)}, u32[]{:S(2)}) collective-permute-start(bf16[40,4096]{1,0:T(8,128)(2,1)S(1)} %copy-done.26), channel_id=1, source_target_pairs={{0,6},{1,7},{2,4},{3,5},{4,2},{5,3},{6,0},{7,1},{8,14},{9,15},{10,... | collective-permute-start | bytes 983048 | tf_op jit(solution)/shard_map/ppermute | solution.py:90
  107.1 7.1 %collective-permute-done.24 = bf16[40,4096]{1,0:T(8,128)(2,1)S(1)} collective-permute-done((bf16[40,4096]{1,0:T(8,128)(2,1)S(1)}, bf16[40,4096]{1,0:T(8,128)(2,1)S(1)}, u32[]{:S(2)}, u32[]{:S(2)}) %collective-permute-start.24) | collective-permute-done | bytes 327712 | tf_op jit(solution)/shard_map/ppermute | solution.py:90
  114.3 5.5 %collective-permute-done.28 = bf16[40,4096]{1,0:T(8,128)(2,1)S(1)} collective-permute-done((bf16[40,4096]{1,0:T(8,128)(2,1)S(1)}, bf16[40,4096]{1,0:T(8,128)(2,1)S(1)}, u32[]{:S(2)}, u32[]{:S(2)}) %collective-permute-start.28) | collective-permute-done | bytes 327712 | tf_op jit(solution)/shard_map/ppermute | solution.py:90
  125.7 7.2 %collective-permute-done.22 = bf16[40,4096]{1,0:T(8,128)(2,1)S(1)} collective-permute-done((bf16[40,4096]{1,0:T(8,128)(2,1)S(1)}, bf16[40,4096]{1,0:T(8,128)(2,1)S(1)}, u32[]{:S(2)}, u32[]{:S(2)}) %collective-permute-start.22) | collective-permute-done | bytes 327712 | tf_op jit(solution)/shard_map/ppermute | solution.py:90
  133.0 4.6 %collective-permute-done.29 = bf16[40,4096]{1,0:T(8,128)(2,1)S(1)} collective-permute-done((bf16[40,4096]{1,0:T(8,128)(2,1)S(1)}, bf16[40,4096]{1,0:T(8,128)(2,1)S(1)}, u32[]{:S(2)}, u32[]{:S(2)}) %collective-permute-start.29) | collective-permute-done | bytes 327712 | tf_op jit(solution)/shard_map/ppermute | solution.py:90
  142.7 2.0 %shard_map.102 = bf16[32,16,1024]{2,1,0:T(8,128)(2,1)} custom-call(s32[32]{0:T(128)S(1)} %fusion.38.label_ref, bf16[32,16,1152]{2,1,0:T(8,128)(2,1)S(1)} %all-to-all-done.arrived_ref), custom_call_target="tpu_custom_call" | custom-call | bytes 2097152 | tf_op jit(solution)/shard_map/pallas_call | solution.py:65
  144.7 4.0 %collective-permute-done.20 = bf16[40,4096]{1,0:T(8,128)(2,1)S(1)} collective-permute-done((bf16[40,4096]{1,0:T(8,128)(2,1)S(1)}, bf16[40,4096]{1,0:T(8,128)(2,1)S(1)}, u32[]{:S(2)}, u32[]{:S(2)}) %collective-permute-start.20) | collective-permute-done | bytes 327712 | tf_op jit(solution)/shard_map/ppermute | solution.py:90
  148.7 4.8 %collective-permute-done.23 = bf16[40,4096]{1,0:T(8,128)(2,1)S(1)} collective-permute-done((bf16[40,4096]{1,0:T(8,128)(2,1)S(1)}, bf16[40,4096]{1,0:T(8,128)(2,1)S(1)}, u32[]{:S(2)}, u32[]{:S(2)}) %collective-permute-start.23) | collective-permute-done | bytes 327712 | tf_op jit(solution)/shard_map/ppermute | solution.py:90
  153.6 2.1 %fusion = bf16[64,4096]{1,0:T(8,128)(2,1)} fusion(bf16[64,160]{1,0:T(8,128)(2,1)S(1)} %copy-done.3, bf16[40,4096]{1,0:T(8,128)(2,1)S(1)} %collective-permute-done.26, bf16[40,4096]{1,0:T(8,128)(2,1)S(1)} %collective-permute-done.23, bf16[40,4096]{1,0:T(8,128)(2,1)S(1)} %collective-permute-done.20, bf16[40,4096]{1,0:T(8,128)(2,1)} %get-tuple-element.77, ...), kind=kOutput, calls=%fused_computation.3 | convolution fusion | flops 89915392 | bytes 2379776 | tf_op jit(solution)/shard_map/dot_general | solution.py:335
  (125 shorter events, 38.0 us)
Async XLA Ops:
  4.2 17.4 %collective-permute-start.3 = (bf16[64,4224]{1,0:T(8,128)(2,1)S(1)}, bf16[64,4224]{1,0:T(8,128)(2,1)S(1)}, u32[]{:S(2)}, u32[]{:S(2)}) collective-permute-start(bf16[64,4224]{1,0:T(8,128)(2,1)S(1)} %get-tuple-element.66), channel_id=1, source_target_pairs={{0,8},{1,9},{2,10},{3,11},{4,12},{5,13},{6,14},{7,15},{8,16},{9,17... | collective-permute-start | bytes 1622024 | tf_op jit(solution)/shard_map/ppermute | solution.py:90
  7.3 29.6 %collective-permute-start.7 = (bf16[4096,384]{1,0:T(8,128)(2,1)S(1)}, bf16[4096,384]{1,0:T(8,128)(2,1)S(1)}, u32[]{:S(2)}, u32[]{:S(2)}) collective-permute-start(bf16[4096,384]{1,0:T(8,128)(2,1)S(1)} %copy-done.7), channel_id=1, source_target_pairs={{0,1},{1,0},{2,3},{3,2},{4,5},{5,4},{6,7},{7,6},{8,9},{9,8},{10,11... | collective-permute-start | bytes 9437192 | tf_op jit(solution)/shard_map/ppermute | solution.py:90
  7.3 17.1 %collective-permute-start.1 = (bf16[40,4096]{1,0:T(8,128)(2,1)S(1)}, bf16[40,4096]{1,0:T(8,128)(2,1)S(1)}, u32[]{:S(2)}, u32[]{:S(2)}) collective-permute-start(bf16[40,4096]{1,0:T(8,128)(2,1)S(1)} %get-tuple-element.64), channel_id=1, source_target_pairs={{0,4},{1,5},{2,6},{3,7},{4,0},{5,1},{6,2},{7,3},{8,12},{9,13},{10,... | collective-permute-start | bytes 983048 | tf_op jit(solution)/shard_map/ppermute | solution.py:90
  8.8 17.1 %collective-permute-start.2 = (bf16[40,4096]{1,0:T(8,128)(2,1)S(1)}, bf16[40,4096]{1,0:T(8,128)(2,1)S(1)}, u32[]{:S(2)}, u32[]{:S(2)}) collective-permute-start(bf16[40,4096]{1,0:T(8,128)(2,1)S(1)} %get-tuple-element.65), channel_id=1, source_target_pairs={{0,6},{1,7},{2,4},{3,5},{4,2},{5,3},{6,0},{7,1},{8,14},{9,15},{10,... | collective-permute-start | bytes 983048 | tf_op jit(solution)/shard_map/ppermute | solution.py:90
  10.2 17.2 %collective-permute-start = (bf16[40,4096]{1,0:T(8,128)(2,1)S(1)}, bf16[40,4096]{1,0:T(8,128)(2,1)S(1)}, u32[]{:S(2)}, u32[]{:S(2)}) collective-permute-start(bf16[40,4096]{1,0:T(8,128)(2,1)S(1)} %get-tuple-element.63), channel_id=1, source_target_pairs={{0,2},{1,3},{2,0},{3,1},{4,6},{5,7},{6,4},{7,5},{8,10},{9,11},{10,... | collective-permute-start | bytes 983048 | tf_op jit(solution)/shard_map/ppermute | solution.py:90
  21.6 15.3 %collective-permute-start.9 = (bf16[64,4224]{1,0:T(8,128)(2,1)S(1)}, bf16[64,4224]{1,0:T(8,128)(2,1)S(1)}, u32[]{:S(2)}, u32[]{:S(2)}) collective-permute-start(bf16[64,4224]{1,0:T(8,128)(2,1)S(1)} %collective-permute-done.3.block_ref), channel_id=1, source_target_pairs={{0,8},{1,9},{2,10},{3,11},{4,12},{5,13},{6,14},{7,15},{8,16},{9,17... | collective-permute-start | bytes 1622024 | tf_op jit(solution)/shard_map/ppermute | solution.py:90
  24.4 16.4 %collective-permute-start.5 = (bf16[40,4096]{1,0:T(8,128)(2,1)S(1)}, bf16[40,4096]{1,0:T(8,128)(2,1)S(1)}, u32[]{:S(2)}, u32[]{:S(2)}) collective-permute-start(bf16[40,4096]{1,0:T(8,128)(2,1)S(1)} %get-tuple-element.71), channel_id=1, source_target_pairs={{0,4},{1,5},{2,6},{3,7},{4,0},{5,1},{6,2},{7,3},{8,12},{9,13},{10,... | collective-permute-start | bytes 983048 | tf_op jit(solution)/shard_map/ppermute | solution.py:90
  25.9 16.4 %collective-permute-start.6 = (bf16[40,4096]{1,0:T(8,128)(2,1)S(1)}, bf16[40,4096]{1,0:T(8,128)(2,1)S(1)}, u32[]{:S(2)}, u32[]{:S(2)}) collective-permute-start(bf16[40,4096]{1,0:T(8,128)(2,1)S(1)} %get-tuple-element.73), channel_id=1, source_target_pairs={{0,6},{1,7},{2,4},{3,5},{4,2},{5,3},{6,0},{7,1},{8,14},{9,15},{10,... | collective-permute-start | bytes 983048 | tf_op jit(solution)/shard_map/ppermute | solution.py:90
  27.4 16.4 %collective-permute-start.4 = (bf16[40,4096]{1,0:T(8,128)(2,1)S(1)}, bf16[40,4096]{1,0:T(8,128)(2,1)S(1)}, u32[]{:S(2)}, u32[]{:S(2)}) collective-permute-start(bf16[40,4096]{1,0:T(8,128)(2,1)S(1)} %get-tuple-element.69), channel_id=1, source_target_pairs={{0,2},{1,3},{2,0},{3,1},{4,6},{5,7},{6,4},{7,5},{8,10},{9,11},{10,... | collective-permute-start | bytes 983048 | tf_op jit(solution)/shard_map/ppermute | solution.py:90
  40.8 15.5 %collective-permute-start.12 = (bf16[40,4096]{1,0:T(8,128)(2,1)S(1)}, bf16[40,4096]{1,0:T(8,128)(2,1)S(1)}, u32[]{:S(2)}, u32[]{:S(2)}) collective-permute-start(bf16[40,4096]{1,0:T(8,128)(2,1)S(1)} %get-tuple-element.90), channel_id=1, source_target_pairs={{0,4},{1,5},{2,6},{3,7},{4,0},{5,1},{6,2},{7,3},{8,12},{9,13},{10,... | collective-permute-start | bytes 983048 | tf_op jit(solution)/shard_map/ppermute | solution.py:90
  42.3 15.5 %collective-permute-start.13 = (bf16[40,4096]{1,0:T(8,128)(2,1)S(1)}, bf16[40,4096]{1,0:T(8,128)(2,1)S(1)}, u32[]{:S(2)}, u32[]{:S(2)}) collective-permute-start(bf16[40,4096]{1,0:T(8,128)(2,1)S(1)} %get-tuple-element.92), channel_id=1, source_target_pairs={{0,6},{1,7},{2,4},{3,5},{4,2},{5,3},{6,0},{7,1},{8,14},{9,15},{10,... | collective-permute-start | bytes 983048 | tf_op jit(solution)/shard_map/ppermute | solution.py:90
  43.7 15.5 %collective-permute-start.11 = (bf16[40,4096]{1,0:T(8,128)(2,1)S(1)}, bf16[40,4096]{1,0:T(8,128)(2,1)S(1)}, u32[]{:S(2)}, u32[]{:S(2)}) collective-permute-start(bf16[40,4096]{1,0:T(8,128)(2,1)S(1)} %get-tuple-element.88), channel_id=1, source_target_pairs={{0,2},{1,3},{2,0},{3,1},{4,6},{5,7},{6,4},{7,5},{8,10},{9,11},{10,... | collective-permute-start | bytes 983048 | tf_op jit(solution)/shard_map/ppermute | solution.py:90
  45.3 21.2 %collective-permute-start.10 = (bf16[384,4096]{1,0:T(8,128)(2,1)}, bf16[384,4096]{1,0:T(8,128)(2,1)}, u32[]{:S(2)}, u32[]{:S(2)}) collective-permute-start(bf16[384,4096]{1,0:T(8,128)(2,1)} %refs_12_.3), channel_id=1, source_target_pairs={{0,1},{1,0},{2,3},{3,2},{4,5},{5,4},{6,7},{7,6},{8,9},{9,8},{10,11... | collective-permute-start | bytes 9437192 | tf_op jit(solution)/shard_map/ppermute | solution.py:90
  56.3 26.1 %collective-permute-start.16 = (bf16[40,4096]{1,0:T(8,128)(2,1)S(1)}, bf16[40,4096]{1,0:T(8,128)(2,1)}, u32[]{:S(2)}, u32[]{:S(2)}) collective-permute-start(bf16[40,4096]{1,0:T(8,128)(2,1)S(1)} %get-tuple-element.97), channel_id=1, source_target_pairs={{0,4},{1,5},{2,6},{3,7},{4,0},{5,1},{6,2},{7,3},{8,12},{9,13},{10,... | collective-permute-start | bytes 983048 | tf_op jit(solution)/shard_map/ppermute | solution.py:90
  57.8 27.0 %collective-permute-start.17 = (bf16[40,4096]{1,0:T(8,128)(2,1)S(1)}, bf16[40,4096]{1,0:T(8,128)(2,1)}, u32[]{:S(2)}, u32[]{:S(2)}) collective-permute-start(bf16[40,4096]{1,0:T(8,128)(2,1)S(1)} %get-tuple-element.99), channel_id=1, source_target_pairs={{0,6},{1,7},{2,4},{3,5},{4,2},{5,3},{6,0},{7,1},{8,14},{9,15},{10,... | collective-permute-start | bytes 983048 | tf_op jit(solution)/shard_map/ppermute | solution.py:90
  60.0 20.1 %collective-permute-start.15 = (bf16[40,4096]{1,0:T(8,128)(2,1)S(1)}, bf16[40,4096]{1,0:T(8,128)(2,1)}, u32[]{:S(2)}, u32[]{:S(2)}) collective-permute-start(bf16[40,4096]{1,0:T(8,128)(2,1)S(1)} %get-tuple-element.95), channel_id=1, source_target_pairs={{0,2},{1,3},{2,0},{3,1},{4,6},{5,7},{6,4},{7,5},{8,10},{9,11},{10,... | collective-permute-start | bytes 983048 | tf_op jit(solution)/shard_map/ppermute | solution.py:90
  60.5 78.1 %all-to-all-start = ((bf16[32,16,1152]{2,1,0:T(8,128)(2,1)}), bf16[32,16,1152]{2,1,0:T(8,128)(2,1)S(1)}, u32[]{:S(2)}, u32[]{:S(2)}) async-start(bf16[32,16,1152]{2,1,0:T(8,128)(2,1)} %shard_map.101), calls=%async_computation | async-start | bytes 2359296 | tf_op jit(solution)/shard_map/all_to_all | solution.py:81
  80.1 18.2 %collective-permute-start.27 = (bf16[40,4096]{1,0:T(8,128)(2,1)}, bf16[40,4096]{1,0:T(8,128)(2,1)S(1)}, u32[]{:S(2)}, u32[]{:S(2)}) collective-permute-start(bf16[40,4096]{1,0:T(8,128)(2,1)} %get-tuple-element.117), channel_id=1, source_target_pairs={{0,2},{1,3},{2,0},{3,1},{4,6},{5,7},{6,4},{7,5},{8,10},{9,11},{10,... | collective-permute-start | bytes 983048 | tf_op jit(solution)/shard_map/ppermute | solution.py:90
  82.3 18.9 %collective-permute-start.18 = (bf16[40,4096]{1,0:T(8,128)(2,1)}, bf16[40,4096]{1,0:T(8,128)(2,1)S(1)}, u32[]{:S(2)}, u32[]{:S(2)}) collective-permute-start(bf16[40,4096]{1,0:T(8,128)(2,1)} %get-tuple-element.101), channel_id=1, source_target_pairs={{0,4},{1,5},{2,6},{3,7},{4,0},{5,1},{6,2},{7,3},{8,12},{9,13},{10,... | collective-permute-start | bytes 983048 | tf_op jit(solution)/shard_map/ppermute | solution.py:90
  84.8 16.5 %collective-permute-start.21 = (bf16[40,4096]{1,0:T(8,128)(2,1)}, bf16[40,4096]{1,0:T(8,128)(2,1)S(1)}, u32[]{:S(2)}, u32[]{:S(2)}) collective-permute-start(bf16[40,4096]{1,0:T(8,128)(2,1)} %get-tuple-element.106), channel_id=1, source_target_pairs={{0,6},{1,7},{2,4},{3,5},{4,2},{5,3},{6,0},{7,1},{8,14},{9,15},{10,... | collective-permute-start | bytes 983048 | tf_op jit(solution)/shard_map/ppermute | solution.py:90
  101.6 18.2 %collective-permute-start.30 = (bf16[64,4096]{1,0:T(8,128)(2,1)S(1)}, bf16[64,4096]{1,0:T(8,128)(2,1)S(1)}, u32[]{:S(2)}, u32[]{:S(2)}) collective-permute-start(bf16[64,4096]{1,0:T(8,128)(2,1)S(1)} %convolution_convert_fusion), channel_id=1, source_target_pairs={{0,8},{1,9},{2,10},{3,11},{4,12},{5,13},{6,14},{7,15},{8,16},{9,17... | collective-permute-start | bytes 1572872 | tf_op jit(solution)/shard_map/ppermute | solution.py:90
  104.2 15.6 %collective-permute-start.28 = (bf16[40,4096]{1,0:T(8,128)(2,1)S(1)}, bf16[40,4096]{1,0:T(8,128)(2,1)S(1)}, u32[]{:S(2)}, u32[]{:S(2)}) collective-permute-start(bf16[40,4096]{1,0:T(8,128)(2,1)S(1)} %copy-done.27), channel_id=1, source_target_pairs={{0,4},{1,5},{2,6},{3,7},{4,0},{5,1},{6,2},{7,3},{8,12},{9,13},{10,... | collective-permute-start | bytes 983048 | tf_op jit(solution)/shard_map/ppermute | solution.py:90
  120.2 17.4 %collective-permute-start.31 = (bf16[64,4096]{1,0:T(8,128)(2,1)S(1)}, bf16[64,4096]{1,0:T(8,128)(2,1)S(1)}, u32[]{:S(2)}, u32[]{:S(2)}) collective-permute-start(bf16[64,4096]{1,0:T(8,128)(2,1)S(1)} %fusion.2), channel_id=1, source_target_pairs={{0,8},{1,9},{2,10},{3,11},{4,12},{5,13},{6,14},{7,15},{8,16},{9,17... | collective-permute-start | bytes 1572872 | tf_op jit(solution)/shard_map/ppermute | solution.py:90
  137.9 15.6 %collective-permute-start.32 = (bf16[64,4096]{1,0:T(8,128)(2,1)S(1)}, bf16[64,4096]{1,0:T(8,128)(2,1)S(1)}, u32[]{:S(2)}, u32[]{:S(2)}) collective-permute-start(bf16[64,4096]{1,0:T(8,128)(2,1)S(1)} %fusion.1), channel_id=1, source_target_pairs={{0,8},{1,9},{2,10},{3,11},{4,12},{5,13},{6,14},{7,15},{8,16},{9,17... | collective-permute-start | bytes 1572872 | tf_op jit(solution)/shard_map/ppermute | solution.py:90
  (42 other events, 487.4 us)

commit v11 on v10

--- a/solution.py
+++ b/solution.py
@@ -146,9 +146,17 @@
             outs[j - 1][:, at : at + step] = part.astype(jnp.bfloat16)
 
 
-def first_kernel(experts, capacity, step, chip_ref, tokens_ref, ids_ref, gates_ref, *outs):
-    rows, width = tokens_ref.shape
-    block_ref = outs[PLANE]
+def first_kernel(experts, capacity, step, chip_ref, tokens_hbm, ids_hbm, gates_hbm, *outs):
+    rows, width = tokens_hbm.shape
+    block_ref, ids_ref, gates_ref, sems = outs[PLANE:]
+    ids_copy = pltpu.make_async_copy(ids_hbm, ids_ref, sems.at[0])
+    gates_copy = pltpu.make_async_copy(gates_hbm, gates_ref, sems.at[1])
+    tokens_copy = pltpu.make_async_copy(tokens_hbm, block_ref.at[:, :width], sems.at[2])
+    ids_copy.start()
+    gates_copy.start()
+    tokens_copy.start()
+    ids_copy.wait()
+    gates_copy.wait()
     ids = ids_ref[...].astype(jnp.float32).T.astype(jnp.int32)
     gates = gates_ref[...].T
     shares = gates / jnp.sum(gates, axis=1, keepdims=True)
@@ -158,7 +166,7 @@
     for k in range(gates.shape[1]):
         table = table + jnp.where(ids[:, k : k + 1] == lane, mixing[:, k : k + 1], 0.0)
     block_ref[:, width:] = table.astype(jnp.bfloat16)
-    block_ref[:, :width] = tokens_ref[...]
+    tokens_copy.wait()
     pick_kernel(experts, capacity, step, chip_ref, block_ref, *outs[:PLANE])
 
 
@@ -171,13 +179,21 @@
         outs.append(jax.ShapeDtypeStruct((rows, width + lanes), jnp.bfloat16))
     body = first_kernel if routing else pick_kernel
     operands = (block, routing[0].T, routing[1].T) if routing else (block,)
+    space = pl.ANY if routing else pltpu.VMEM
     found = pl.pallas_call(
         functools.partial(body, experts, capacity, 512),
         out_shape=outs,
         in_specs=[pl.BlockSpec(memory_space=pltpu.SMEM)]
-        + [pl.BlockSpec(memory_space=pltpu.VMEM)] * len(operands),
+        + [pl.BlockSpec(memory_space=space)] * len(operands),
+        scratch_shapes=[
+            pltpu.VMEM(operands[1].shape, jnp.int32),
+            pltpu.VMEM(operands[2].shape, jnp.float32),
+            pltpu.SemaphoreType.DMA((3,)),
+        ]
+        if routing
+        else [],
         out_specs=[pl.BlockSpec(memory_space=pltpu.VMEM)] * len(outs),
-        compiler_params=pltpu.CompilerParams(vmem_limit_bytes=16 * 2**20),
+        compiler_params=pltpu.CompilerParams(vmem_limit_bytes=(60 if routing else 16) * 2**20),
         cost_estimate=pl.CostEstimate(
             flops=1200 * rows * PLANE * capacity * width,
             bytes_accessed=2 * width * (rows + PLANE * capacity),

time: 156 us -> 154 us (0.987)
  local copies, waits for them, and re-layouts: 3.99 us -> 1.03 us
  Pallas kernels: 34.3 us -> 36.2 us
    unnamed x64 -> x56, local copies, waits for them, and re-layouts: 3.99 us -> 1.03 us
    pallas_call x4, Pallas kernels: 3.45 us -> 5.36 us  [pick_pieces(): pl.pallas_call(functools.partial(body, experts, capacity, 512), out_shape...]
  transfers between devices with their start and end apart: 34 -> 34, of which waited for: 14 -> 14; matrix products, arithmetic and copies ran while one was open for 4% -> 4% of each run, Pallas kernels for 21% -> 22%
where the time goes in v11:
time: 154 us; the launch traced here: 153 us
  waiting for transfers between devices  65.6 us (43%)
  starting transfers between devices  40.8 us (26%)
  Pallas kernels  36.2 us (24%)
  matrix products  8 us (5%)
    ppermute x33, waiting for transfers between devices, send(): return lax.ppermute(x, 'expert', pairs)  65.6 us
    ppermute x33, starting transfers between devices, send(): return lax.ppermute(x, 'expert', pairs)  36.2 us
    pallas_call x2, Pallas kernels, apply(): pl.pallas_call(functools.partial(expert_kernel, len(pieces), steps), grid...  26.9 us
    pallas_call x4, Pallas kernels, pick_pieces(): pl.pallas_call(functools.partial(body, experts, capacity, 512), out_shape...  5.36 us
    dot_general x4, matrix products, pick(): lax.dot_general(placing, rows, (((0,), (0,)), ((), ())), preferred_elemen...  4.85 us
    all_to_all x1, starting transfers between devices, exchange(): return lax.all_to_all(x, 'expert', split_axis=0, concat_axis=0, tiled=True)  4.65 us
    dot_general x4, matrix products, local(): jnp.dot(blends[s], jnp.concatenate(sent[s], axis=0), preferred_element_ty...  3.16 us
  transfers between devices with their start and end apart: 34, of which 14 were waited for; matrix products, arithmetic and copies ran while one was open for 4% of the time, Pallas kernels for 22%

profile of v11, /device:TPU:0, one launch (start us, length us, event | category | flops | bytes accessed | tf_op | source)
XLA Modules:
  0.0 153.3 jit_solution(4173653378724709735)
XLA Ops:
  0.7 3.0 %shard_map.95 = (bf16[40,4096]{1,0:T(8,128)(2,1)}, bf16[40,4096]{1,0:T(8,128)(2,1)}, bf16[40,4096]{1,0:T(8,128)(2,1)}, bf16[64,160]{1,0:T(8,128)(2,1)}, bf16[64,4224]{1,0:T(8,128)(2,1)}) custom-call(s32[1]{0:T(128)} %bitcast.chip_ref, bf16[64,4096]{1,0:T(8,128)(2,1)} %tokens_hbm.1, s32[8,64]{1,0:T(8,128)} %bitcast.8, f32[8,64]{1,0:T(8,128)} %bitcast.9), custom_call_target="tpu_custom_call" | custom-call | flops 50331648000 | bytes 1835008 | tf_op jit(solution)/shard_map/pallas_call | solution.py:183
  3.7 3.1 %collective-permute-start.3 = (bf16[64,4224]{1,0:T(8,128)(2,1)}, bf16[64,4224]{1,0:T(8,128)(2,1)S(1)}, u32[]{:S(2)}, u32[]{:S(2)}) collective-permute-start(bf16[64,4224]{1,0:T(8,128)(2,1)} %get-tuple-element.66), channel_id=1, source_target_pairs={{0,8},{1,9},{2,10},{3,11},{4,12},{5,13},{6,14},{7,15},{8,16},{9,17... | collective-permute-start | bytes 1622024 | tf_op jit(solution)/shard_map/ppermute | solution.py:90
  12.0 2.0 %shard_map.101 = bf16[32,16,1152]{2,1,0:T(8,128)(2,1)} custom-call(s32[32]{0:T(128)S(1)} %copy-done.1, bf16[32,16,1024]{2,1,0:T(8,128)(2,1)S(1)} %copy-done), custom_call_target="tpu_custom_call" | custom-call | bytes 3145728 | tf_op jit(solution)/shard_map/pallas_call | solution.py:34
  14.0 7.3 %collective-permute-done.3.block_ref = bf16[64,4224]{1,0:T(8,128)(2,1)S(1)} collective-permute-done((bf16[64,4224]{1,0:T(8,128)(2,1)}, bf16[64,4224]{1,0:T(8,128)(2,1)S(1)}, u32[]{:S(2)}, u32[]{:S(2)}) %collective-permute-start.3) | collective-permute-done | bytes 540704 | tf_op jit(solution)/shard_map/ppermute | solution.py:90
  22.1 2.1 %collective-permute-done.1.refs_2_ = bf16[40,4096]{1,0:T(8,128)(2,1)S(1)} collective-permute-done((bf16[40,4096]{1,0:T(8,128)(2,1)}, bf16[40,4096]{1,0:T(8,128)(2,1)S(1)}, u32[]{:S(2)}, u32[]{:S(2)}) %collective-permute-start.1) | collective-permute-done | bytes 327712 | tf_op jit(solution)/shard_map/ppermute | solution.py:90
  28.7 7.9 %collective-permute-done.9.block_ref = bf16[64,4224]{1,0:T(8,128)(2,1)S(1)} collective-permute-done((bf16[64,4224]{1,0:T(8,128)(2,1)S(1)}, bf16[64,4224]{1,0:T(8,128)(2,1)S(1)}, u32[]{:S(2)}, u32[]{:S(2)}) %collective-permute-start.9) | collective-permute-done | bytes 540704 | tf_op jit(solution)/shard_map/ppermute | solution.py:90
  38.2 2.3 %collective-permute-done.5.refs_6_ = bf16[40,4096]{1,0:T(8,128)(2,1)S(1)} collective-permute-done((bf16[40,4096]{1,0:T(8,128)(2,1)S(1)}, bf16[40,4096]{1,0:T(8,128)(2,1)S(1)}, u32[]{:S(2)}, u32[]{:S(2)}) %collective-permute-start.5) | collective-permute-done | bytes 327712 | tf_op jit(solution)/shard_map/ppermute | solution.py:90
  45.1 5.8 %collective-permute-done.14.block_ref = bf16[64,4224]{1,0:T(8,128)(2,1)S(1)} collective-permute-done((bf16[64,4224]{1,0:T(8,128)(2,1)S(1)}, bf16[64,4224]{1,0:T(8,128)(2,1)S(1)}, u32[]{:S(2)}, u32[]{:S(2)}) %collective-permute-start.14) | collective-permute-done | bytes 540704 | tf_op jit(solution)/shard_map/ppermute | solution.py:90
  51.7 4.3 %collective-permute-done.12.refs_2_ = bf16[40,4096]{1,0:T(8,128)(2,1)S(1)} collective-permute-done((bf16[40,4096]{1,0:T(8,128)(2,1)S(1)}, bf16[40,4096]{1,0:T(8,128)(2,1)S(1)}, u32[]{:S(2)}, u32[]{:S(2)}) %collective-permute-start.12) | collective-permute-done | bytes 327712 | tf_op jit(solution)/shard_map/ppermute | solution.py:90
  59.7 4.6 %all-to-all-start = ((bf16[32,16,1152]{2,1,0:T(8,128)(2,1)}), bf16[32,16,1152]{2,1,0:T(8,128)(2,1)S(1)}, u32[]{:S(2)}, u32[]{:S(2)}) async-start(bf16[32,16,1152]{2,1,0:T(8,128)(2,1)} %shard_map.101), calls=%async_computation | async-start | bytes 2359296 | tf_op jit(solution)/shard_map/all_to_all | solution.py:81
  65.4 13.5 %shard_map.97 = (bf16[40,4096]{1,0:T(8,128)(2,1)}, bf16[40,4096]{1,0:T(8,128)(2,1)}, bf16[40,4096]{1,0:T(8,128)(2,1)}, bf16[40,4096]{1,0:T(8,128)(2,1)}, bf16[40...) custom-call(bf16[40,4096]{1,0:T(8,128)(2,1)} %convolution_convert_fusion.4.re, ...), custom_call_target="tpu_custom_call" | custom-call | flops 6039797760 | bytes 24117248 | tf_op jit(solution)/shard_map/pallas_call | solution.py:256
  78.9 2.1 %collective-permute-done.15.refs_5_ = bf16[40,4096]{1,0:T(8,128)(2,1)} collective-permute-done((bf16[40,4096]{1,0:T(8,128)(2,1)S(1)}, bf16[40,4096]{1,0:T(8,128)(2,1)}, u32[]{:S(2)}, u32[]{:S(2)}) %collective-permute-start.15) | collective-permute-done | bytes 327712 | tf_op jit(solution)/shard_map/ppermute | solution.py:90
  82.4 2.9 %collective-permute-start.18 = (bf16[40,4096]{1,0:T(8,128)(2,1)}, bf16[40,4096]{1,0:T(8,128)(2,1)S(1)}, u32[]{:S(2)}, u32[]{:S(2)}) collective-permute-start(bf16[40,4096]{1,0:T(8,128)(2,1)} %get-tuple-element.101), channel_id=1, source_target_pairs={{0,4},{1,5},{2,6},{3,7},{4,0},{5,1},{6,2},{7,3},{8,12},{9,13},{10,... | collective-permute-start | bytes 983048 | tf_op jit(solution)/shard_map/ppermute | solution.py:90
  85.3 13.4 %shard_map.100 = (bf16[40,4096]{1,0:T(8,128)(2,1)}, bf16[40,4096]{1,0:T(8,128)(2,1)}, bf16[40,4096]{1,0:T(8,128)(2,1)}, bf16[40,4096]{1,0:T(8,128)(2,1)}, bf16[4...) custom-call(bf16[40,4096]{1,0:T(8,128)(2,1)} %convolution_convert_fusion.2.r, ...), custom_call_target="tpu_custom_call" | custom-call | flops 6039797760 | bytes 24117248 | tf_op jit(solution)/shard_map/pallas_call | solution.py:256
  100.8 2.0 %collective-permute-start.30 = (bf16[64,4096]{1,0:T(8,128)(2,1)S(1)}, bf16[64,4096]{1,0:T(8,128)(2,1)S(1)}, u32[]{:S(2)}, u32[]{:S(2)}) collective-permute-start(bf16[64,4096]{1,0:T(8,128)(2,1)S(1)} %convolution_convert_fusion), channel_id=1, source_target_pairs={{0,8},{1,9},{2,10},{3,11},{4,12},{5,13},{6,14},{7,15},{8,16},{9,17... | collective-permute-start | bytes 1572872 | tf_op jit(solution)/shard_map/ppermute | solution.py:90
  104.2 2.2 %collective-permute-start.19 = (bf16[40,4096]{1,0:T(8,128)(2,1)S(1)}, bf16[40,4096]{1,0:T(8,128)(2,1)S(1)}, u32[]{:S(2)}, u32[]{:S(2)}) collective-permute-start(bf16[40,4096]{1,0:T(8,128)(2,1)S(1)} %copy-done.22), channel_id=1, source_target_pairs={{0,6},{1,7},{2,4},{3,5},{4,2},{5,3},{6,0},{7,1},{8,14},{9,15},{10,... | collective-permute-start | bytes 983048 | tf_op jit(solution)/shard_map/ppermute | solution.py:90
  106.4 7.1 %collective-permute-done.24 = bf16[40,4096]{1,0:T(8,128)(2,1)S(1)} collective-permute-done((bf16[40,4096]{1,0:T(8,128)(2,1)S(1)}, bf16[40,4096]{1,0:T(8,128)(2,1)S(1)}, u32[]{:S(2)}, u32[]{:S(2)}) %collective-permute-start.24) | collective-permute-done | bytes 327712 | tf_op jit(solution)/shard_map/ppermute | solution.py:90
  113.5 5.5 %collective-permute-done.28 = bf16[40,4096]{1,0:T(8,128)(2,1)S(1)} collective-permute-done((bf16[40,4096]{1,0:T(8,128)(2,1)S(1)}, bf16[40,4096]{1,0:T(8,128)(2,1)S(1)}, u32[]{:S(2)}, u32[]{:S(2)}) %collective-permute-start.28) | collective-permute-done | bytes 327712 | tf_op jit(solution)/shard_map/ppermute | solution.py:90
  124.8 7.2 %collective-permute-done.22 = bf16[40,4096]{1,0:T(8,128)(2,1)S(1)} collective-permute-done((bf16[40,4096]{1,0:T(8,128)(2,1)S(1)}, bf16[40,4096]{1,0:T(8,128)(2,1)S(1)}, u32[]{:S(2)}, u32[]{:S(2)}) %collective-permute-start.22) | collective-permute-done | bytes 327712 | tf_op jit(solution)/shard_map/ppermute | solution.py:90
  131.9 4.5 %collective-permute-done.25 = bf16[40,4096]{1,0:T(8,128)(2,1)S(1)} collective-permute-done((bf16[40,4096]{1,0:T(8,128)(2,1)S(1)}, bf16[40,4096]{1,0:T(8,128)(2,1)S(1)}, u32[]{:S(2)}, u32[]{:S(2)}) %collective-permute-start.25) | collective-permute-done | bytes 327712 | tf_op jit(solution)/shard_map/ppermute | solution.py:90
  141.4 2.0 %shard_map.102 = bf16[32,16,1024]{2,1,0:T(8,128)(2,1)} custom-call(s32[32]{0:T(128)S(1)} %fusion.38.label_ref, bf16[32,16,1152]{2,1,0:T(8,128)(2,1)S(1)} %all-to-all-done.arrived_ref), custom_call_target="tpu_custom_call" | custom-call | bytes 2097152 | tf_op jit(solution)/shard_map/pallas_call | solution.py:65
  143.4 3.2 %collective-permute-done.20 = bf16[40,4096]{1,0:T(8,128)(2,1)S(1)} collective-permute-done((bf16[40,4096]{1,0:T(8,128)(2,1)S(1)}, bf16[40,4096]{1,0:T(8,128)(2,1)S(1)}, u32[]{:S(2)}, u32[]{:S(2)}) %collective-permute-start.20) | collective-permute-done | bytes 327712 | tf_op jit(solution)/shard_map/ppermute | solution.py:90
  146.6 4.6 %collective-permute-done.23 = bf16[40,4096]{1,0:T(8,128)(2,1)S(1)} collective-permute-done((bf16[40,4096]{1,0:T(8,128)(2,1)S(1)}, bf16[40,4096]{1,0:T(8,128)(2,1)S(1)}, u32[]{:S(2)}, u32[]{:S(2)}) %collective-permute-start.23) | collective-permute-done | bytes 327712 | tf_op jit(solution)/shard_map/ppermute | solution.py:90
  151.2 2.1 %fusion = bf16[64,4096]{1,0:T(8,128)(2,1)} fusion(bf16[64,160]{1,0:T(8,128)(2,1)S(1)} %copy-done.3, bf16[40,4096]{1,0:T(8,128)(2,1)S(1)} %collective-permute-done.26, bf16[40,4096]{1,0:T(8,128)(2,1)S(1)} %collective-permute-done.23, bf16[40,4096]{1,0:T(8,128)(2,1)S(1)} %collective-permute-done.20, bf16[40,4096]{1,0:T(8,128)(2,1)} %get-tuple-element.77, ...), kind=kOutput, calls=%fused_computation.3 | convolution fusion | flops 89915392 | bytes 2379776 | tf_op jit(solution)/shard_map/dot_general | solution.py:351
  (117 shorter events, 37.7 us)
Async XLA Ops:
  3.7 17.6 %collective-permute-start.3 = (bf16[64,4224]{1,0:T(8,128)(2,1)}, bf16[64,4224]{1,0:T(8,128)(2,1)S(1)}, u32[]{:S(2)}, u32[]{:S(2)}) collective-permute-start(bf16[64,4224]{1,0:T(8,128)(2,1)} %get-tuple-element.66), channel_id=1, source_target_pairs={{0,8},{1,9},{2,10},{3,11},{4,12},{5,13},{6,14},{7,15},{8,16},{9,17... | collective-permute-start | bytes 1622024 | tf_op jit(solution)/shard_map/ppermute | solution.py:90
  6.8 29.8 %collective-permute-start.7 = (bf16[4096,384]{1,0:T(8,128)(2,1)}, bf16[4096,384]{1,0:T(8,128)(2,1)S(1)}, u32[]{:S(2)}, u32[]{:S(2)}) collective-permute-start(bf16[4096,384]{1,0:T(8,128)(2,1)} %refs_8_.3), channel_id=1, source_target_pairs={{0,1},{1,0},{2,3},{3,2},{4,5},{5,4},{6,7},{7,6},{8,9},{9,8},{10,11... | collective-permute-start | bytes 9437192 | tf_op jit(solution)/shard_map/ppermute | solution.py:90
  6.8 17.4 %collective-permute-start.1 = (bf16[40,4096]{1,0:T(8,128)(2,1)}, bf16[40,4096]{1,0:T(8,128)(2,1)S(1)}, u32[]{:S(2)}, u32[]{:S(2)}) collective-permute-start(bf16[40,4096]{1,0:T(8,128)(2,1)} %get-tuple-element.64), channel_id=1, source_target_pairs={{0,4},{1,5},{2,6},{3,7},{4,0},{5,1},{6,2},{7,3},{8,12},{9,13},{10,... | collective-permute-start | bytes 983048 | tf_op jit(solution)/shard_map/ppermute | solution.py:90
  8.3 17.4 %collective-permute-start.2 = (bf16[40,4096]{1,0:T(8,128)(2,1)}, bf16[40,4096]{1,0:T(8,128)(2,1)S(1)}, u32[]{:S(2)}, u32[]{:S(2)}) collective-permute-start(bf16[40,4096]{1,0:T(8,128)(2,1)} %get-tuple-element.65), channel_id=1, source_target_pairs={{0,6},{1,7},{2,4},{3,5},{4,2},{5,3},{6,0},{7,1},{8,14},{9,15},{10,... | collective-permute-start | bytes 983048 | tf_op jit(solution)/shard_map/ppermute | solution.py:90
  9.7 17.4 %collective-permute-start = (bf16[40,4096]{1,0:T(8,128)(2,1)}, bf16[40,4096]{1,0:T(8,128)(2,1)S(1)}, u32[]{:S(2)}, u32[]{:S(2)}) collective-permute-start(bf16[40,4096]{1,0:T(8,128)(2,1)} %get-tuple-element.63), channel_id=1, source_target_pairs={{0,2},{1,3},{2,0},{3,1},{4,6},{5,7},{6,4},{7,5},{8,10},{9,11},{10,... | collective-permute-start | bytes 983048 | tf_op jit(solution)/shard_map/ppermute | solution.py:90
  21.3 15.3 %collective-permute-start.9 = (bf16[64,4224]{1,0:T(8,128)(2,1)S(1)}, bf16[64,4224]{1,0:T(8,128)(2,1)S(1)}, u32[]{:S(2)}, u32[]{:S(2)}) collective-permute-start(bf16[64,4224]{1,0:T(8,128)(2,1)S(1)} %collective-permute-done.3.block_ref), channel_id=1, source_target_pairs={{0,8},{1,9},{2,10},{3,11},{4,12},{5,13},{6,14},{7,15},{8,16},{9,17... | collective-permute-start | bytes 1622024 | tf_op jit(solution)/shard_map/ppermute | solution.py:90
  24.1 16.4 %collective-permute-start.5 = (bf16[40,4096]{1,0:T(8,128)(2,1)S(1)}, bf16[40,4096]{1,0:T(8,128)(2,1)S(1)}, u32[]{:S(2)}, u32[]{:S(2)}) collective-permute-start(bf16[40,4096]{1,0:T(8,128)(2,1)S(1)} %get-tuple-element.71), channel_id=1, source_target_pairs={{0,4},{1,5},{2,6},{3,7},{4,0},{5,1},{6,2},{7,3},{8,12},{9,13},{10,... | collective-permute-start | bytes 983048 | tf_op jit(solution)/shard_map/ppermute | solution.py:90
  25.7 16.4 %collective-permute-start.6 = (bf16[40,4096]{1,0:T(8,128)(2,1)S(1)}, bf16[40,4096]{1,0:T(8,128)(2,1)S(1)}, u32[]{:S(2)}, u32[]{:S(2)}) collective-permute-start(bf16[40,4096]{1,0:T(8,128)(2,1)S(1)} %get-tuple-element.73), channel_id=1, source_target_pairs={{0,6},{1,7},{2,4},{3,5},{4,2},{5,3},{6,0},{7,1},{8,14},{9,15},{10,... | collective-permute-start | bytes 983048 | tf_op jit(solution)/shard_map/ppermute | solution.py:90
  27.1 16.4 %collective-permute-start.4 = (bf16[40,4096]{1,0:T(8,128)(2,1)S(1)}, bf16[40,4096]{1,0:T(8,128)(2,1)S(1)}, u32[]{:S(2)}, u32[]{:S(2)}) collective-permute-start(bf16[40,4096]{1,0:T(8,128)(2,1)S(1)} %get-tuple-element.69), channel_id=1, source_target_pairs={{0,2},{1,3},{2,0},{3,1},{4,6},{5,7},{6,4},{7,5},{8,10},{9,11},{10,... | collective-permute-start | bytes 983048 | tf_op jit(solution)/shard_map/ppermute | solution.py:90
  40.5 15.5 %collective-permute-start.12 = (bf16[40,4096]{1,0:T(8,128)(2,1)S(1)}, bf16[40,4096]{1,0:T(8,128)(2,1)S(1)}, u32[]{:S(2)}, u32[]{:S(2)}) collective-permute-start(bf16[40,4096]{1,0:T(8,128)(2,1)S(1)} %get-tuple-element.90), channel_id=1, source_target_pairs={{0,4},{1,5},{2,6},{3,7},{4,0},{5,1},{6,2},{7,3},{8,12},{9,13},{10,... | collective-permute-start | bytes 983048 | tf_op jit(solution)/shard_map/ppermute | solution.py:90
  42.0 15.5 %collective-permute-start.13 = (bf16[40,4096]{1,0:T(8,128)(2,1)S(1)}, bf16[40,4096]{1,0:T(8,128)(2,1)S(1)}, u32[]{:S(2)}, u32[]{:S(2)}) collective-permute-start(bf16[40,4096]{1,0:T(8,128)(2,1)S(1)} %get-tuple-element.92), channel_id=1, source_target_pairs={{0,6},{1,7},{2,4},{3,5},{4,2},{5,3},{6,0},{7,1},{8,14},{9,15},{10,... | collective-permute-start | bytes 983048 | tf_op jit(solution)/shard_map/ppermute | solution.py:90
  43.5 15.5 %collective-permute-start.11 = (bf16[40,4096]{1,0:T(8,128)(2,1)S(1)}, bf16[40,4096]{1,0:T(8,128)(2,1)S(1)}, u32[]{:S(2)}, u32[]{:S(2)}) collective-permute-start(bf16[40,4096]{1,0:T(8,128)(2,1)S(1)} %get-tuple-element.88), channel_id=1, source_target_pairs={{0,2},{1,3},{2,0},{3,1},{4,6},{5,7},{6,4},{7,5},{8,10},{9,11},{10,... | collective-permute-start | bytes 983048 | tf_op jit(solution)/shard_map/ppermute | solution.py:90
  45.1 20.3 %collective-permute-start.10 = (bf16[384,4096]{1,0:T(8,128)(2,1)}, bf16[384,4096]{1,0:T(8,128)(2,1)}, u32[]{:S(2)}, u32[]{:S(2)}) collective-permute-start(bf16[384,4096]{1,0:T(8,128)(2,1)} %refs_12_.3), channel_id=1, source_target_pairs={{0,1},{1,0},{2,3},{3,2},{4,5},{5,4},{6,7},{7,6},{8,9},{9,8},{10,11... | collective-permute-start | bytes 9437192 | tf_op jit(solution)/shard_map/ppermute | solution.py:90
  56.0 26.5 %collective-permute-start.16 = (bf16[40,4096]{1,0:T(8,128)(2,1)S(1)}, bf16[40,4096]{1,0:T(8,128)(2,1)}, u32[]{:S(2)}, u32[]{:S(2)}) collective-permute-start(bf16[40,4096]{1,0:T(8,128)(2,1)S(1)} %get-tuple-element.97), channel_id=1, source_target_pairs={{0,4},{1,5},{2,6},{3,7},{4,0},{5,1},{6,2},{7,3},{8,12},{9,13},{10,... | collective-permute-start | bytes 983048 | tf_op jit(solution)/shard_map/ppermute | solution.py:90
  57.5 27.8 %collective-permute-start.17 = (bf16[40,4096]{1,0:T(8,128)(2,1)S(1)}, bf16[40,4096]{1,0:T(8,128)(2,1)}, u32[]{:S(2)}, u32[]{:S(2)}) collective-permute-start(bf16[40,4096]{1,0:T(8,128)(2,1)S(1)} %get-tuple-element.99), channel_id=1, source_target_pairs={{0,6},{1,7},{2,4},{3,5},{4,2},{5,3},{6,0},{7,1},{8,14},{9,15},{10,... | collective-permute-start | bytes 983048 | tf_op jit(solution)/shard_map/ppermute | solution.py:90
  59.0 22.0 %collective-permute-start.15 = (bf16[40,4096]{1,0:T(8,128)(2,1)S(1)}, bf16[40,4096]{1,0:T(8,128)(2,1)}, u32[]{:S(2)}, u32[]{:S(2)}) collective-permute-start(bf16[40,4096]{1,0:T(8,128)(2,1)S(1)} %get-tuple-element.95), channel_id=1, source_target_pairs={{0,2},{1,3},{2,0},{3,1},{4,6},{5,7},{6,4},{7,5},{8,10},{9,11},{10,... | collective-permute-start | bytes 983048 | tf_op jit(solution)/shard_map/ppermute | solution.py:90
  59.7 77.6 %all-to-all-start = ((bf16[32,16,1152]{2,1,0:T(8,128)(2,1)}), bf16[32,16,1152]{2,1,0:T(8,128)(2,1)S(1)}, u32[]{:S(2)}, u32[]{:S(2)}) async-start(bf16[32,16,1152]{2,1,0:T(8,128)(2,1)} %shard_map.101), calls=%async_computation | async-start | bytes 2359296 | tf_op jit(solution)/shard_map/all_to_all | solution.py:81
  81.0 17.8 %collective-permute-start.27 = (bf16[40,4096]{1,0:T(8,128)(2,1)}, bf16[40,4096]{1,0:T(8,128)(2,1)S(1)}, u32[]{:S(2)}, u32[]{:S(2)}) collective-permute-start(bf16[40,4096]{1,0:T(8,128)(2,1)} %get-tuple-element.117), channel_id=1, source_target_pairs={{0,2},{1,3},{2,0},{3,1},{4,6},{5,7},{6,4},{7,5},{8,10},{9,11},{10,... | collective-permute-start | bytes 983048 | tf_op jit(solution)/shard_map/ppermute | solution.py:90
  82.4 18.0 %collective-permute-start.18 = (bf16[40,4096]{1,0:T(8,128)(2,1)}, bf16[40,4096]{1,0:T(8,128)(2,1)S(1)}, u32[]{:S(2)}, u32[]{:S(2)}) collective-permute-start(bf16[40,4096]{1,0:T(8,128)(2,1)} %get-tuple-element.101), channel_id=1, source_target_pairs={{0,4},{1,5},{2,6},{3,7},{4,0},{5,1},{6,2},{7,3},{8,12},{9,13},{10,... | collective-permute-start | bytes 983048 | tf_op jit(solution)/shard_map/ppermute | solution.py:90
  85.3 15.2 %collective-permute-start.21 = (bf16[40,4096]{1,0:T(8,128)(2,1)}, bf16[40,4096]{1,0:T(8,128)(2,1)S(1)}, u32[]{:S(2)}, u32[]{:S(2)}) collective-permute-start(bf16[40,4096]{1,0:T(8,128)(2,1)} %get-tuple-element.106), channel_id=1, source_target_pairs={{0,6},{1,7},{2,4},{3,5},{4,2},{5,3},{6,0},{7,1},{8,14},{9,15},{10,... | collective-permute-start | bytes 983048 | tf_op jit(solution)/shard_map/ppermute | solution.py:90
  100.8 18.2 %collective-permute-start.30 = (bf16[64,4096]{1,0:T(8,128)(2,1)S(1)}, bf16[64,4096]{1,0:T(8,128)(2,1)S(1)}, u32[]{:S(2)}, u32[]{:S(2)}) collective-permute-start(bf16[64,4096]{1,0:T(8,128)(2,1)S(1)} %convolution_convert_fusion), channel_id=1, source_target_pairs={{0,8},{1,9},{2,10},{3,11},{4,12},{5,13},{6,14},{7,15},{8,16},{9,17... | collective-permute-start | bytes 1572872 | tf_op jit(solution)/shard_map/ppermute | solution.py:90
  103.8 15.2 %collective-permute-start.28 = (bf16[40,4096]{1,0:T(8,128)(2,1)S(1)}, bf16[40,4096]{1,0:T(8,128)(2,1)S(1)}, u32[]{:S(2)}, u32[]{:S(2)}) collective-permute-start(bf16[40,4096]{1,0:T(8,128)(2,1)S(1)} %copy-done.23), channel_id=1, source_target_pairs={{0,4},{1,5},{2,6},{3,7},{4,0},{5,1},{6,2},{7,3},{8,12},{9,13},{10,... | collective-permute-start | bytes 983048 | tf_op jit(solution)/shard_map/ppermute | solution.py:90
  104.2 14.9 %collective-permute-start.19 = (bf16[40,4096]{1,0:T(8,128)(2,1)S(1)}, bf16[40,4096]{1,0:T(8,128)(2,1)S(1)}, u32[]{:S(2)}, u32[]{:S(2)}) collective-permute-start(bf16[40,4096]{1,0:T(8,128)(2,1)S(1)} %copy-done.22), channel_id=1, source_target_pairs={{0,6},{1,7},{2,4},{3,5},{4,2},{5,3},{6,0},{7,1},{8,14},{9,15},{10,... | collective-permute-start | bytes 983048 | tf_op jit(solution)/shard_map/ppermute | solution.py:90
  119.5 17.0 %collective-permute-start.31 = (bf16[64,4096]{1,0:T(8,128)(2,1)S(1)}, bf16[64,4096]{1,0:T(8,128)(2,1)S(1)}, u32[]{:S(2)}, u32[]{:S(2)}) collective-permute-start(bf16[64,4096]{1,0:T(8,128)(2,1)S(1)} %fusion.2), channel_id=1, source_target_pairs={{0,8},{1,9},{2,10},{3,11},{4,12},{5,13},{6,14},{7,15},{8,16},{9,17... | collective-permute-start | bytes 1572872 | tf_op jit(solution)/shard_map/ppermute | solution.py:90
  (38 other events, 464.0 us)

commit v12 on v11

--- a/solution.py
+++ b/solution.py
@@ -270,6 +270,36 @@
             transcendentals=2 * rows * half,
         ),
     )(*pieces, *gate, *up, *down)
+
+
+def blend_kernel(blend_ref, *refs):
+    *inputs, out_ref = refs
+    pieces, earlier = inputs[:PLANE], inputs[PLANE:]
+    step = 512
+    for at in range(0, out_ref.shape[1], step):
+        rows = [ref[:, at : at + step].astype(jnp.float32) for ref in pieces]
+        rows = jnp.concatenate(rows, axis=0).astype(jnp.bfloat16)
+        total = jnp.dot(blend_ref[...], rows, preferred_element_type=jnp.float32)
+        for ref in earlier:
+            total = total + ref[:, at : at + step].astype(jnp.float32)
+        out_ref[:, at : at + step] = total
+
+
+def blend_pieces(blend, pieces, earlier):
+    rows, width = blend.shape[0], pieces[0].shape[1]
+    operands = (blend, *pieces, *earlier)
+    return pl.pallas_call(
+        blend_kernel,
+        out_shape=jax.ShapeDtypeStruct((rows, width), jnp.float32),
+        in_specs=[pl.BlockSpec(memory_space=pltpu.VMEM)] * len(operands),
+        out_specs=pl.BlockSpec(memory_space=pltpu.VMEM),
+        compiler_params=pltpu.CompilerParams(vmem_limit_bytes=16 * 2**20),
+        cost_estimate=pl.CostEstimate(
+            flops=100 * rows * blend.shape[1] * width,
+            bytes_accessed=2 * width * (2 * rows + blend.shape[1]),
+            transcendentals=0,
+        ),
+    )(*operands)
 
 
 def apply_plain(held, gate, up, down):
@@ -341,16 +371,19 @@
         mine = outs[s * PLANE : (s + 1) * PLANE]
         sent[s] = [mine[0]]
         for j in range(1, PLANE):
-            waits = [landed[-3 if s == 1 else -4]] + ([arrived] if s == 0 else [])
+            waits = [landed[-3 if s == 1 else -4]] + ([arrived] if s == order[1] else [])
             landed.append(send(after(mine[j], *waits), flip=2 * j))
             sent[s].append(landed[-1])
     handed = place_pages(arrived, kv_pages.shape)
     sent[1][0] = after(sent[1][0], outs[-1])
     total = None
     for s in order:
-        part = jnp.dot(
-            blends[s], jnp.concatenate(sent[s], axis=0), preferred_element_type=jnp.float32
-        )
+        if whole and s not in (1, 0):
+            part = blend_pieces(blends[s], sent[s], [])
+        else:
+            part = jnp.dot(
+                blends[s], jnp.concatenate(sent[s], axis=0), preferred_element_type=jnp.float32
+            )
         if total is not None:
             part = part + send(total, step=stride).astype(jnp.float32)
         total = part.astype(jnp.bfloat16)

time: 154 us -> 149 us (0.968)
  waiting for transfers between devices: 65.6 us -> 55.8 us
  starting transfers between devices: 40.8 us -> 45.5 us
    ppermute x33, waiting for transfers between devices: 65.6 us -> 55.8 us  [send(): return lax.ppermute(x, 'expert', pairs)]
    ppermute x33, starting transfers between devices: 36.2 us -> 42.9 us  [send(): return lax.ppermute(x, 'expert', pairs)]
    all_to_all x1, starting transfers between devices: 4.65 us -> 2.66 us  [exchange(): return lax.all_to_all(x, 'expert', split_axis=0, concat_axis=0, tiled=True)]
    dot_general x4 -> x2, matrix products: 3.16 us -> 2.67 us  [local(): jnp.dot(blends[s], jnp.concatenate(sent[s], axis=0), preferred_element_ty...]
  transfers between devices with their start and end apart: 34 -> 34, of which waited for: 14 -> 15; matrix products, arithmetic and copies ran while one was open for 4% -> 5% of each run, Pallas kernels for 22% -> 23%
where the time goes in v12:
time: 149 us
  waiting for transfers between devices  55.8 us (37%)
  starting transfers between devices  45.5 us (31%)
  Pallas kernels  36.8 us (25%)
  matrix products  7.52 us (5%)
  local copies, waits for them, and re-layouts  1.53 us (1%)
    ppermute x33, waiting for transfers between devices, send(): return lax.ppermute(x, 'expert', pairs)  55.8 us
    ppermute x33, starting transfers between devices, send(): return lax.ppermute(x, 'expert', pairs)  42.9 us
    pallas_call x2, Pallas kernels, apply(): pl.pallas_call(functools.partial(expert_kernel, len(pieces), steps), grid...  26.8 us
    pallas_call x4, Pallas kernels, pick_pieces(): pl.pallas_call(functools.partial(body, experts, capacity, 512), out_shape...  5.38 us
    dot_general x4, matrix products, pick(): lax.dot_general(placing, rows, (((0,), (0,)), ((), ())), preferred_elemen...  4.85 us
  transfers between devices with their start and end apart: 34, of which 15 were waited for; matrix products, arithmetic and copies ran while one was open for 5% of the time, Pallas kernels for 23%

profile of v12, /device:TPU:0, one launch (start us, length us, event | category | flops | bytes accessed | tf_op | source)
XLA Modules:
  0.0 148.9 jit_solution(11554621875566478635)
XLA Ops:
  0.7 3.0 %shard_map.95 = (bf16[40,4096]{1,0:T(8,128)(2,1)}, bf16[40,4096]{1,0:T(8,128)(2,1)}, bf16[40,4096]{1,0:T(8,128)(2,1)}, bf16[64,160]{1,0:T(8,128)(2,1)}, bf16[64,4224]{1,0:T(8,128)(2,1)}) custom-call(s32[1]{0:T(128)} %bitcast.chip_ref, bf16[64,4096]{1,0:T(8,128)(2,1)} %tokens_hbm.1, s32[8,64]{1,0:T(8,128)} %bitcast.6, f32[8,64]{1,0:T(8,128)} %bitcast.7), custom_call_target="tpu_custom_call" | custom-call | flops 50331648000 | bytes 1835008 | tf_op jit(solution)/shard_map/pallas_call | solution.py:183
  3.7 3.1 %collective-permute-start.3 = (bf16[64,4224]{1,0:T(8,128)(2,1)}, bf16[64,4224]{1,0:T(8,128)(2,1)S(1)}, u32[]{:S(2)}, u32[]{:S(2)}) collective-permute-start(bf16[64,4224]{1,0:T(8,128)(2,1)} %get-tuple-element.66), channel_id=1, source_target_pairs={{0,8},{1,9},{2,10},{3,11},{4,12},{5,13},{6,14},{7,15},{8,16},{9,17... | collective-permute-start | bytes 1622024 | tf_op jit(solution)/shard_map/ppermute | solution.py:90
  12.0 2.0 %shard_map.101 = bf16[32,16,1152]{2,1,0:T(8,128)(2,1)} custom-call(s32[32]{0:T(128)S(1)} %copy-done.1, bf16[32,16,1024]{2,1,0:T(8,128)(2,1)S(1)} %copy-done), custom_call_target="tpu_custom_call" | custom-call | bytes 3145728 | tf_op jit(solution)/shard_map/pallas_call | solution.py:34
  14.0 7.3 %collective-permute-done.3.block_ref = bf16[64,4224]{1,0:T(8,128)(2,1)S(1)} collective-permute-done((bf16[64,4224]{1,0:T(8,128)(2,1)}, bf16[64,4224]{1,0:T(8,128)(2,1)S(1)}, u32[]{:S(2)}, u32[]{:S(2)}) %collective-permute-start.3) | collective-permute-done | bytes 540704 | tf_op jit(solution)/shard_map/ppermute | solution.py:90
  22.1 2.1 %collective-permute-done.1.refs_2_ = bf16[40,4096]{1,0:T(8,128)(2,1)S(1)} collective-permute-done((bf16[40,4096]{1,0:T(8,128)(2,1)}, bf16[40,4096]{1,0:T(8,128)(2,1)S(1)}, u32[]{:S(2)}, u32[]{:S(2)}) %collective-permute-start.1) | collective-permute-done | bytes 327712 | tf_op jit(solution)/shard_map/ppermute | solution.py:90
  28.7 7.9 %collective-permute-done.9.block_ref = bf16[64,4224]{1,0:T(8,128)(2,1)S(1)} collective-permute-done((bf16[64,4224]{1,0:T(8,128)(2,1)S(1)}, bf16[64,4224]{1,0:T(8,128)(2,1)S(1)}, u32[]{:S(2)}, u32[]{:S(2)}) %collective-permute-start.9) | collective-permute-done | bytes 540704 | tf_op jit(solution)/shard_map/ppermute | solution.py:90
  38.2 2.3 %collective-permute-done.5.refs_6_ = bf16[40,4096]{1,0:T(8,128)(2,1)S(1)} collective-permute-done((bf16[40,4096]{1,0:T(8,128)(2,1)S(1)}, bf16[40,4096]{1,0:T(8,128)(2,1)S(1)}, u32[]{:S(2)}, u32[]{:S(2)}) %collective-permute-start.5) | collective-permute-done | bytes 327712 | tf_op jit(solution)/shard_map/ppermute | solution.py:90
  45.1 5.8 %collective-permute-done.14.block_ref = bf16[64,4224]{1,0:T(8,128)(2,1)S(1)} collective-permute-done((bf16[64,4224]{1,0:T(8,128)(2,1)S(1)}, bf16[64,4224]{1,0:T(8,128)(2,1)S(1)}, u32[]{:S(2)}, u32[]{:S(2)}) %collective-permute-start.14) | collective-permute-done | bytes 540704 | tf_op jit(solution)/shard_map/ppermute | solution.py:90
  50.9 2.7 %all-to-all-start = ((bf16[32,16,1152]{2,1,0:T(8,128)(2,1)}), bf16[32,16,1152]{2,1,0:T(8,128)(2,1)S(1)}, u32[]{:S(2)}, u32[]{:S(2)}) async-start(bf16[32,16,1152]{2,1,0:T(8,128)(2,1)} %shard_map.101), calls=%async_computation | async-start | bytes 2359296 | tf_op jit(solution)/shard_map/all_to_all | solution.py:81
  56.1 2.3 %collective-permute-start.16 = (bf16[40,4096]{1,0:T(8,128)(2,1)S(1)}, bf16[40,4096]{1,0:T(8,128)(2,1)S(1)}, u32[]{:S(2)}, u32[]{:S(2)}) collective-permute-start(bf16[40,4096]{1,0:T(8,128)(2,1)S(1)} %get-tuple-element.97), channel_id=1, source_target_pairs={{0,4},{1,5},{2,6},{3,7},{4,0},{5,1},{6,2},{7,3},{8,12},{9,13},{10,... | collective-permute-start | bytes 983048 | tf_op jit(solution)/shard_map/ppermute | solution.py:90
  58.4 4.1 %collective-permute-start.17 = (bf16[40,4096]{1,0:T(8,128)(2,1)S(1)}, bf16[40,4096]{1,0:T(8,128)(2,1)S(1)}, u32[]{:S(2)}, u32[]{:S(2)}) collective-permute-start(bf16[40,4096]{1,0:T(8,128)(2,1)S(1)} %get-tuple-element.99), channel_id=1, source_target_pairs={{0,6},{1,7},{2,4},{3,5},{4,2},{5,3},{6,0},{7,1},{8,14},{9,15},{10,... | collective-permute-start | bytes 983048 | tf_op jit(solution)/shard_map/ppermute | solution.py:90
  62.6 2.5 %collective-permute-start.15 = (bf16[40,4096]{1,0:T(8,128)(2,1)S(1)}, bf16[40,4096]{1,0:T(8,128)(2,1)S(1)}, u32[]{:S(2)}, u32[]{:S(2)}) collective-permute-start(bf16[40,4096]{1,0:T(8,128)(2,1)S(1)} %get-tuple-element.95), channel_id=1, source_target_pairs={{0,2},{1,3},{2,0},{3,1},{4,6},{5,7},{6,4},{7,5},{8,10},{9,11},{10,... | collective-permute-start | bytes 983048 | tf_op jit(solution)/shard_map/ppermute | solution.py:90
  66.1 13.4 %shard_map.97 = (bf16[40,4096]{1,0:T(8,128)(2,1)}, bf16[40,4096]{1,0:T(8,128)(2,1)}, bf16[40,4096]{1,0:T(8,128)(2,1)}, bf16[40,4096]{1,0:T(8,128)(2,1)}, bf16[40...) custom-call(bf16[40,4096]{1,0:T(8,128)(2,1)} %convolution_convert_fusion.4.re, ...), custom_call_target="tpu_custom_call" | custom-call | flops 6039797760 | bytes 24117248 | tf_op jit(solution)/shard_map/pallas_call | solution.py:256
  79.6 4.5 %collective-permute-done.15.refs_5_ = bf16[40,4096]{1,0:T(8,128)(2,1)S(1)} collective-permute-done((bf16[40,4096]{1,0:T(8,128)(2,1)S(1)}, bf16[40,4096]{1,0:T(8,128)(2,1)S(1)}, u32[]{:S(2)}, u32[]{:S(2)}) %collective-permute-start.15) | collective-permute-done | bytes 327712 | tf_op jit(solution)/shard_map/ppermute | solution.py:90
  85.4 2.3 %collective-permute-start.18 = (bf16[40,4096]{1,0:T(8,128)(2,1)}, bf16[40,4096]{1,0:T(8,128)(2,1)}, u32[]{:S(2)}, u32[]{:S(2)}) collective-permute-start(bf16[40,4096]{1,0:T(8,128)(2,1)} %get-tuple-element.101), channel_id=1, source_target_pairs={{0,4},{1,5},{2,6},{3,7},{4,0},{5,1},{6,2},{7,3},{8,12},{9,13},{10,... | collective-permute-start | bytes 983048 | tf_op jit(solution)/shard_map/ppermute | solution.py:90
  88.4 13.4 %shard_map.100 = (bf16[40,4096]{1,0:T(8,128)(2,1)}, bf16[40,4096]{1,0:T(8,128)(2,1)}, bf16[40,4096]{1,0:T(8,128)(2,1)}, bf16[40,4096]{1,0:T(8,128)(2,1)}, bf16[4...) custom-call(bf16[40,4096]{1,0:T(8,128)(2,1)} %convolution_convert_fusion.2.r, ...), custom_call_target="tpu_custom_call" | custom-call | flops 6039797760 | bytes 24117248 | tf_op jit(solution)/shard_map/pallas_call | solution.py:256
  109.4 3.4 %collective-permute-done.24.refs_1_ = bf16[40,4096]{1,0:T(8,128)(2,1)S(1)} collective-permute-done((bf16[40,4096]{1,0:T(8,128)(2,1)}, bf16[40,4096]{1,0:T(8,128)(2,1)S(1)}, u32[]{:S(2)}, u32[]{:S(2)}) %collective-permute-start.24) | collective-permute-done | bytes 327712 | tf_op jit(solution)/shard_map/ppermute | solution.py:90
  113.9 4.0 %collective-permute-done.28.refs_2_ = bf16[40,4096]{1,0:T(8,128)(2,1)S(1)} collective-permute-done((bf16[40,4096]{1,0:T(8,128)(2,1)}, bf16[40,4096]{1,0:T(8,128)(2,1)S(1)}, u32[]{:S(2)}, u32[]{:S(2)}) %collective-permute-start.28) | collective-permute-done | bytes 327712 | tf_op jit(solution)/shard_map/ppermute | solution.py:90
  117.8 4.2 %collective-permute-start.29 = (bf16[40,4096]{1,0:T(8,128)(2,1)S(1)}, bf16[40,4096]{1,0:T(8,128)(2,1)S(1)}, u32[]{:S(2)}, u32[]{:S(2)}) collective-permute-start(bf16[40,4096]{1,0:T(8,128)(2,1)S(1)} %copy-done.16), channel_id=1, source_target_pairs={{0,6},{1,7},{2,4},{3,5},{4,2},{5,3},{6,0},{7,1},{8,14},{9,15},{10,... | collective-permute-start | bytes 983048 | tf_op jit(solution)/shard_map/ppermute | solution.py:90
  123.8 3.0 %collective-permute-done.22.refs_1_ = bf16[40,4096]{1,0:T(8,128)(2,1)S(1)} collective-permute-done((bf16[40,4096]{1,0:T(8,128)(2,1)S(1)}, bf16[40,4096]{1,0:T(8,128)(2,1)S(1)}, u32[]{:S(2)}, u32[]{:S(2)}) %collective-permute-start.22) | collective-permute-done | bytes 327712 | tf_op jit(solution)/shard_map/ppermute | solution.py:90
  126.9 3.5 %collective-permute-done.25.refs_2_ = bf16[40,4096]{1,0:T(8,128)(2,1)S(1)} collective-permute-done((bf16[40,4096]{1,0:T(8,128)(2,1)S(1)}, bf16[40,4096]{1,0:T(8,128)(2,1)S(1)}, u32[]{:S(2)}, u32[]{:S(2)}) %collective-permute-start.25) | collective-permute-done | bytes 327712 | tf_op jit(solution)/shard_map/ppermute | solution.py:90
  138.1 2.0 %shard_map.104 = bf16[32,16,1024]{2,1,0:T(8,128)(2,1)} custom-call(s32[32]{0:T(128)S(1)} %fusion.22.label_ref, bf16[32,16,1152]{2,1,0:T(8,128)(2,1)S(1)} %all-to-all-done.arrived_ref), custom_call_target="tpu_custom_call" | custom-call | bytes 2097152 | tf_op jit(solution)/shard_map/pallas_call | solution.py:65
  140.1 4.1 %collective-permute-done.20 = bf16[40,4096]{1,0:T(8,128)(2,1)S(1)} collective-permute-done((bf16[40,4096]{1,0:T(8,128)(2,1)S(1)}, bf16[40,4096]{1,0:T(8,128)(2,1)S(1)}, u32[]{:S(2)}, u32[]{:S(2)}) %collective-permute-start.20) | collective-permute-done | bytes 327712 | tf_op jit(solution)/shard_map/ppermute | solution.py:90
  144.1 3.6 %collective-permute-done.23 = bf16[40,4096]{1,0:T(8,128)(2,1)S(1)} collective-permute-done((bf16[40,4096]{1,0:T(8,128)(2,1)S(1)}, bf16[40,4096]{1,0:T(8,128)(2,1)S(1)}, u32[]{:S(2)}, u32[]{:S(2)}) %collective-permute-start.23) | collective-permute-done | bytes 327712 | tf_op jit(solution)/shard_map/ppermute | solution.py:90
  (109 shorter events, 41.6 us)
Async XLA Ops:
  3.7 17.6 %collective-permute-start.3 = (bf16[64,4224]{1,0:T(8,128)(2,1)}, bf16[64,4224]{1,0:T(8,128)(2,1)S(1)}, u32[]{:S(2)}, u32[]{:S(2)}) collective-permute-start(bf16[64,4224]{1,0:T(8,128)(2,1)} %get-tuple-element.66), channel_id=1, source_target_pairs={{0,8},{1,9},{2,10},{3,11},{4,12},{5,13},{6,14},{7,15},{8,16},{9,17... | collective-permute-start | bytes 1622024 | tf_op jit(solution)/shard_map/ppermute | solution.py:90
  6.8 29.8 %collective-permute-start.7 = (bf16[4096,384]{1,0:T(8,128)(2,1)}, bf16[4096,384]{1,0:T(8,128)(2,1)S(1)}, u32[]{:S(2)}, u32[]{:S(2)}) collective-permute-start(bf16[4096,384]{1,0:T(8,128)(2,1)} %refs_8_.3), channel_id=1, source_target_pairs={{0,1},{1,0},{2,3},{3,2},{4,5},{5,4},{6,7},{7,6},{8,9},{9,8},{10,11... | collective-permute-start | bytes 9437192 | tf_op jit(solution)/shard_map/ppermute | solution.py:90
  6.8 17.4 %collective-permute-start.1 = (bf16[40,4096]{1,0:T(8,128)(2,1)}, bf16[40,4096]{1,0:T(8,128)(2,1)S(1)}, u32[]{:S(2)}, u32[]{:S(2)}) collective-permute-start(bf16[40,4096]{1,0:T(8,128)(2,1)} %get-tuple-element.64), channel_id=1, source_target_pairs={{0,4},{1,5},{2,6},{3,7},{4,0},{5,1},{6,2},{7,3},{8,12},{9,13},{10,... | collective-permute-start | bytes 983048 | tf_op jit(solution)/shard_map/ppermute | solution.py:90
  8.3 17.4 %collective-permute-start.2 = (bf16[40,4096]{1,0:T(8,128)(2,1)}, bf16[40,4096]{1,0:T(8,128)(2,1)S(1)}, u32[]{:S(2)}, u32[]{:S(2)}) collective-permute-start(bf16[40,4096]{1,0:T(8,128)(2,1)} %get-tuple-element.65), channel_id=1, source_target_pairs={{0,6},{1,7},{2,4},{3,5},{4,2},{5,3},{6,0},{7,1},{8,14},{9,15},{10,... | collective-permute-start | bytes 983048 | tf_op jit(solution)/shard_map/ppermute | solution.py:90
  9.7 17.4 %collective-permute-start = (bf16[40,4096]{1,0:T(8,128)(2,1)}, bf16[40,4096]{1,0:T(8,128)(2,1)S(1)}, u32[]{:S(2)}, u32[]{:S(2)}) collective-permute-start(bf16[40,4096]{1,0:T(8,128)(2,1)} %get-tuple-element.63), channel_id=1, source_target_pairs={{0,2},{1,3},{2,0},{3,1},{4,6},{5,7},{6,4},{7,5},{8,10},{9,11},{10,... | collective-permute-start | bytes 983048 | tf_op jit(solution)/shard_map/ppermute | solution.py:90
  21.3 15.3 %collective-permute-start.9 = (bf16[64,4224]{1,0:T(8,128)(2,1)S(1)}, bf16[64,4224]{1,0:T(8,128)(2,1)S(1)}, u32[]{:S(2)}, u32[]{:S(2)}) collective-permute-start(bf16[64,4224]{1,0:T(8,128)(2,1)S(1)} %collective-permute-done.3.block_ref), channel_id=1, source_target_pairs={{0,8},{1,9},{2,10},{3,11},{4,12},{5,13},{6,14},{7,15},{8,16},{9,17... | collective-permute-start | bytes 1622024 | tf_op jit(solution)/shard_map/ppermute | solution.py:90
  24.2 16.4 %collective-permute-start.5 = (bf16[40,4096]{1,0:T(8,128)(2,1)S(1)}, bf16[40,4096]{1,0:T(8,128)(2,1)S(1)}, u32[]{:S(2)}, u32[]{:S(2)}) collective-permute-start(bf16[40,4096]{1,0:T(8,128)(2,1)S(1)} %get-tuple-element.71), channel_id=1, source_target_pairs={{0,4},{1,5},{2,6},{3,7},{4,0},{5,1},{6,2},{7,3},{8,12},{9,13},{10,... | collective-permute-start | bytes 983048 | tf_op jit(solution)/shard_map/ppermute | solution.py:90
  25.7 16.4 %collective-permute-start.6 = (bf16[40,4096]{1,0:T(8,128)(2,1)S(1)}, bf16[40,4096]{1,0:T(8,128)(2,1)S(1)}, u32[]{:S(2)}, u32[]{:S(2)}) collective-permute-start(bf16[40,4096]{1,0:T(8,128)(2,1)S(1)} %get-tuple-element.73), channel_id=1, source_target_pairs={{0,6},{1,7},{2,4},{3,5},{4,2},{5,3},{6,0},{7,1},{8,14},{9,15},{10,... | collective-permute-start | bytes 983048 | tf_op jit(solution)/shard_map/ppermute | solution.py:90
  27.1 16.4 %collective-permute-start.4 = (bf16[40,4096]{1,0:T(8,128)(2,1)S(1)}, bf16[40,4096]{1,0:T(8,128)(2,1)S(1)}, u32[]{:S(2)}, u32[]{:S(2)}) collective-permute-start(bf16[40,4096]{1,0:T(8,128)(2,1)S(1)} %get-tuple-element.69), channel_id=1, source_target_pairs={{0,2},{1,3},{2,0},{3,1},{4,6},{5,7},{6,4},{7,5},{8,10},{9,11},{10,... | collective-permute-start | bytes 983048 | tf_op jit(solution)/shard_map/ppermute | solution.py:90
  36.6 17.0 %collective-permute-start.8 = (bf16[4096,384]{1,0:T(8,128)(2,1)}, bf16[4096,384]{1,0:T(8,128)(2,1)}, u32[]{:S(2)}, u32[]{:S(2)}) collective-permute-start(bf16[4096,384]{1,0:T(8,128)(2,1)} %refs_10_.3), channel_id=1, source_target_pairs={{0,1},{1,0},{2,3},{3,2},{4,5},{5,4},{6,7},{7,6},{8,9},{9,8},{10,11... | collective-permute-start | bytes 9437192 | tf_op jit(solution)/shard_map/ppermute | solution.py:90
  40.5 15.6 %collective-permute-start.12 = (bf16[40,4096]{1,0:T(8,128)(2,1)S(1)}, bf16[40,4096]{1,0:T(8,128)(2,1)}, u32[]{:S(2)}, u32[]{:S(2)}) collective-permute-start(bf16[40,4096]{1,0:T(8,128)(2,1)S(1)} %get-tuple-element.90), channel_id=1, source_target_pairs={{0,4},{1,5},{2,6},{3,7},{4,0},{5,1},{6,2},{7,3},{8,12},{9,13},{10,... | collective-permute-start | bytes 983048 | tf_op jit(solution)/shard_map/ppermute | solution.py:90
  42.0 16.4 %collective-permute-start.13 = (bf16[40,4096]{1,0:T(8,128)(2,1)S(1)}, bf16[40,4096]{1,0:T(8,128)(2,1)}, u32[]{:S(2)}, u32[]{:S(2)}) collective-permute-start(bf16[40,4096]{1,0:T(8,128)(2,1)S(1)} %get-tuple-element.92), channel_id=1, source_target_pairs={{0,6},{1,7},{2,4},{3,5},{4,2},{5,3},{6,0},{7,1},{8,14},{9,15},{10,... | collective-permute-start | bytes 983048 | tf_op jit(solution)/shard_map/ppermute | solution.py:90
  43.5 19.1 %collective-permute-start.11 = (bf16[40,4096]{1,0:T(8,128)(2,1)S(1)}, bf16[40,4096]{1,0:T(8,128)(2,1)}, u32[]{:S(2)}, u32[]{:S(2)}) collective-permute-start(bf16[40,4096]{1,0:T(8,128)(2,1)S(1)} %get-tuple-element.88), channel_id=1, source_target_pairs={{0,2},{1,3},{2,0},{3,1},{4,6},{5,7},{6,4},{7,5},{8,10},{9,11},{10,... | collective-permute-start | bytes 983048 | tf_op jit(solution)/shard_map/ppermute | solution.py:90
  50.9 51.0 %all-to-all-start = ((bf16[32,16,1152]{2,1,0:T(8,128)(2,1)}), bf16[32,16,1152]{2,1,0:T(8,128)(2,1)S(1)}, u32[]{:S(2)}, u32[]{:S(2)}) async-start(bf16[32,16,1152]{2,1,0:T(8,128)(2,1)} %shard_map.101), calls=%async_computation | async-start | bytes 2359296 | tf_op jit(solution)/shard_map/all_to_all | solution.py:81
  56.1 29.3 %collective-permute-start.16 = (bf16[40,4096]{1,0:T(8,128)(2,1)S(1)}, bf16[40,4096]{1,0:T(8,128)(2,1)S(1)}, u32[]{:S(2)}, u32[]{:S(2)}) collective-permute-start(bf16[40,4096]{1,0:T(8,128)(2,1)S(1)} %get-tuple-element.97), channel_id=1, source_target_pairs={{0,4},{1,5},{2,6},{3,7},{4,0},{5,1},{6,2},{7,3},{8,12},{9,13},{10,... | collective-permute-start | bytes 983048 | tf_op jit(solution)/shard_map/ppermute | solution.py:90
  58.4 29.3 %collective-permute-start.17 = (bf16[40,4096]{1,0:T(8,128)(2,1)S(1)}, bf16[40,4096]{1,0:T(8,128)(2,1)S(1)}, u32[]{:S(2)}, u32[]{:S(2)}) collective-permute-start(bf16[40,4096]{1,0:T(8,128)(2,1)S(1)} %get-tuple-element.99), channel_id=1, source_target_pairs={{0,6},{1,7},{2,4},{3,5},{4,2},{5,3},{6,0},{7,1},{8,14},{9,15},{10,... | collective-permute-start | bytes 983048 | tf_op jit(solution)/shard_map/ppermute | solution.py:90
  62.6 21.5 %collective-permute-start.15 = (bf16[40,4096]{1,0:T(8,128)(2,1)S(1)}, bf16[40,4096]{1,0:T(8,128)(2,1)S(1)}, u32[]{:S(2)}, u32[]{:S(2)}) collective-permute-start(bf16[40,4096]{1,0:T(8,128)(2,1)S(1)} %get-tuple-element.95), channel_id=1, source_target_pairs={{0,2},{1,3},{2,0},{3,1},{4,6},{5,7},{6,4},{7,5},{8,10},{9,11},{10,... | collective-permute-start | bytes 983048 | tf_op jit(solution)/shard_map/ppermute | solution.py:90
  84.1 18.7 %collective-permute-start.27 = (bf16[40,4096]{1,0:T(8,128)(2,1)}, bf16[40,4096]{1,0:T(8,128)(2,1)S(1)}, u32[]{:S(2)}, u32[]{:S(2)}) collective-permute-start(bf16[40,4096]{1,0:T(8,128)(2,1)} %get-tuple-element.117), channel_id=1, source_target_pairs={{0,2},{1,3},{2,0},{3,1},{4,6},{5,7},{6,4},{7,5},{8,10},{9,11},{10,... | collective-permute-start | bytes 983048 | tf_op jit(solution)/shard_map/ppermute | solution.py:90
  85.4 19.3 %collective-permute-start.18 = (bf16[40,4096]{1,0:T(8,128)(2,1)}, bf16[40,4096]{1,0:T(8,128)(2,1)}, u32[]{:S(2)}, u32[]{:S(2)}) collective-permute-start(bf16[40,4096]{1,0:T(8,128)(2,1)} %get-tuple-element.101), channel_id=1, source_target_pairs={{0,4},{1,5},{2,6},{3,7},{4,0},{5,1},{6,2},{7,3},{8,12},{9,13},{10,... | collective-permute-start | bytes 983048 | tf_op jit(solution)/shard_map/ppermute | solution.py:90
  87.7 17.7 %collective-permute-start.21 = (bf16[40,4096]{1,0:T(8,128)(2,1)}, bf16[40,4096]{1,0:T(8,128)(2,1)}, u32[]{:S(2)}, u32[]{:S(2)}) collective-permute-start(bf16[40,4096]{1,0:T(8,128)(2,1)} %get-tuple-element.106), channel_id=1, source_target_pairs={{0,6},{1,7},{2,4},{3,5},{4,2},{5,3},{6,0},{7,1},{8,14},{9,15},{10,... | collective-permute-start | bytes 983048 | tf_op jit(solution)/shard_map/ppermute | solution.py:90
  104.7 17.3 %collective-permute-start.19 = (bf16[40,4096]{1,0:T(8,128)(2,1)}, bf16[40,4096]{1,0:T(8,128)(2,1)S(1)}, u32[]{:S(2)}, u32[]{:S(2)}) collective-permute-start(bf16[40,4096]{1,0:T(8,128)(2,1)} %get-tuple-element.103), channel_id=1, source_target_pairs={{0,6},{1,7},{2,4},{3,5},{4,2},{5,3},{6,0},{7,1},{8,14},{9,15},{10,... | collective-permute-start | bytes 983048 | tf_op jit(solution)/shard_map/ppermute | solution.py:90
  107.0 15.4 %collective-permute-start.30 = (bf16[64,4096]{1,0:T(8,128)(2,1)S(1)}, bf16[64,4096]{1,0:T(8,128)(2,1)S(1)}, u32[]{:S(2)}, u32[]{:S(2)}) collective-permute-start(bf16[64,4096]{1,0:T(8,128)(2,1)S(1)} %convolution_convert_fusion), channel_id=1, source_target_pairs={{0,8},{1,9},{2,10},{3,11},{4,12},{5,13},{6,14},{7,15},{8,16},{9,17... | collective-permute-start | bytes 1572872 | tf_op jit(solution)/shard_map/ppermute | solution.py:90
  108.6 18.3 %collective-permute-start.22 = (bf16[40,4096]{1,0:T(8,128)(2,1)S(1)}, bf16[40,4096]{1,0:T(8,128)(2,1)S(1)}, u32[]{:S(2)}, u32[]{:S(2)}) collective-permute-start(bf16[40,4096]{1,0:T(8,128)(2,1)S(1)} %copy-done.18), channel_id=1, source_target_pairs={{0,2},{1,3},{2,0},{3,1},{4,6},{5,7},{6,4},{7,5},{8,10},{9,11},{10,... | collective-permute-start | bytes 983048 | tf_op jit(solution)/shard_map/ppermute | solution.py:90
  112.8 17.5 %collective-permute-start.25 = (bf16[40,4096]{1,0:T(8,128)(2,1)S(1)}, bf16[40,4096]{1,0:T(8,128)(2,1)S(1)}, u32[]{:S(2)}, u32[]{:S(2)}) collective-permute-start(bf16[40,4096]{1,0:T(8,128)(2,1)S(1)} %copy-done.17), channel_id=1, source_target_pairs={{0,4},{1,5},{2,6},{3,7},{4,0},{5,1},{6,2},{7,3},{8,12},{9,13},{10,... | collective-permute-start | bytes 983048 | tf_op jit(solution)/shard_map/ppermute | solution.py:90
  (33 other events, 290.2 us)
